TPU v7x, 32 devices: a whole 2x2x4 slice. The times are simulated.
32 devices in a mesh: rep: 4 (over y, x), exp: 8 (over z, core).
Axes of the slice: x: 2, y: 2, z: 4, core: 2. Of those that a mesh axis runs over, the one named last changes fastest.
Arguments:
- tokens: bfloat16 [1024, 2048], P('exp', 'rep'), may hold values from -6 to 6
- expert_ids: int32 [1024, 8], P('exp'), may hold values from 0 to 127, all different within a row; in each aligned block of 128 rows (0 to 127, 128 to 255, ...) at most 12 rows name the same one
- route_weights: float32 [1024, 8], P('exp'), may hold values from 0.05 to 1
- w_gate: bfloat16 [128, 768, 2048], P('exp', None, 'rep'), may hold values from -0.125 to 0.125
- w_up: bfloat16 [128, 768, 2048], P('exp', None, 'rep'), may hold values from -0.125 to 0.125
- w_down: bfloat16 [128, 768, 2048], P('exp', None, 'rep'), may hold values from -0.21875 to 0.21875
Outputs:
- mixed: bfloat16 [1024, 2048], P('exp', 'rep')
Inputs may be any that keep to these rules, and one draw needn't show every extreme that they name: `expert_ids`: each token names 8 different experts. Within the rows of one index of exp (aligned blocks of 128 tokens) no expert is named more than 12 times, a bound that some block reaches.
All inputs are finite; a program needn't handle non-finite values.
Results may differ from a plain program's by a relative error of at most 0.0058.
Values may be sent and summed in bfloat16 or wider, within the bound.
No kernel may reach another device: no remote copies, remote signals or barrier semaphores. Data moves between devices by JAX's collectives and lax.ppermute only.
A program may use at most 256 MiB of HBM per device.

v0:
```python
import jax
import jax.numpy as jnp
from jax import lax
from jax.sharding import PartitionSpec as P

EXPERTS = 128


def local(tokens, expert_ids, route_weights, w_gate, w_up, w_down):
    tok_rows = expert_ids.shape[0]
    top_count = expert_ids.shape[1]
    local_experts = w_gate.shape[0]
    replicas = lax.axis_size("rep")
    replica_index = lax.axis_index("rep")
    full_cap = replicas * max(1, tok_rows * top_count * 3 // (8 * EXPERTS))
    slot_cap = full_cap // replicas
    assigned = expert_ids.reshape(-1)
    onehot = (assigned[:, None] == jnp.arange(EXPERTS, dtype=jnp.int32)[None, :]).astype(jnp.int32)
    before = jnp.cumsum(onehot, axis=0) - onehot
    slot_ids = jnp.sum(before * onehot, axis=1)
    owned = slot_ids % replicas == replica_index
    target = assigned * slot_cap + slot_ids // replicas
    destination = jnp.where(owned, target, EXPERTS * slot_cap)
    probs = route_weights / jnp.sum(route_weights, axis=1, keepdims=True)
    full_rows = lax.all_gather(tokens, "rep", axis=1, tiled=True)
    width = full_rows.shape[1]
    repeated = jnp.repeat(full_rows, top_count, axis=0)
    outgoing = (
        jnp.zeros((EXPERTS * slot_cap, width), jnp.bfloat16)
        .at[destination]
        .set(repeated, mode="drop")
    )
    outgoing = outgoing.reshape(EXPERTS, slot_cap, width)
    arrived = lax.all_to_all(outgoing, "exp", split_axis=0, concat_axis=1, tiled=True)
    gate_sum = jnp.einsum(
        "esd,efd->esf",
        arrived,
        lax.all_gather(w_gate, "rep", axis=2, tiled=True),
        preferred_element_type=jnp.float32,
    )
    up_sum = jnp.einsum(
        "esd,efd->esf",
        arrived,
        lax.all_gather(w_up, "rep", axis=2, tiled=True),
        preferred_element_type=jnp.float32,
    )
    hidden = (jax.nn.silu(gate_sum) * up_sum).astype(jnp.bfloat16)
    expert_out = jnp.einsum(
        "esf,efd->esd",
        hidden,
        lax.all_gather(w_down, "rep", axis=2, tiled=True),
        preferred_element_type=jnp.float32,
    ).astype(jnp.bfloat16)
    owners = expert_out.shape[1] // slot_cap
    share = width // replicas
    split_out = expert_out.reshape(local_experts, owners, slot_cap, replicas, share)
    homed = lax.all_to_all(
        lax.all_to_all(split_out, "rep", split_axis=3, concat_axis=3, tiled=True),
        "exp",
        split_axis=1,
        concat_axis=1,
        tiled=True,
    )
    ordered = jnp.swapaxes(homed, 0, 1).reshape(EXPERTS * full_cap, share)
    picked = ordered[assigned * full_cap + slot_ids].astype(jnp.float32)
    weighted = picked.reshape(tok_rows, top_count, share) * probs[:, :, None]
    return jnp.sum(weighted, axis=1).astype(jnp.bfloat16)


def solution(mesh):
    return jax.shard_map(
        local,
        mesh=mesh,
        in_specs=(
            P("exp", "rep"),
            P("exp", None),
            P("exp", None),
            P("exp", None, "rep"),
            P("exp", None, "rep"),
            P("exp", None, "rep"),
        ),
        out_specs=P("exp", "rep"),
        check_vma=False,
    )
```

profile of v0, /device:TPU:0, one launch (start us, length us, event | category | flops | bytes accessed | tf_op | source)
XLA Modules:
  0.0 1441.8 jit_solution(10839095468992084778)
XLA Ops:
  6.5 0.0 all-gather.4.cloned.1.call-start
  6.5 0.7 all-gather.4.cloned.1.call-update
  7.3 0.0 all-gather.6.cloned.1.call-start
  7.3 0.7 all-gather.6.cloned.1.call-update
  8.0 0.0 copy-start.1
  8.0 0.0 all-gather.8.cloned.1.call-start
  8.1 0.7 all-gather.8.cloned.1.call-update
  8.8 0.0 copy-done.1
  8.8 0.1 copy.33
  8.9 0.1 eq.44
  9.0 0.0 copy-start
  9.0 0.1 eq.40
  9.1 0.1 copy.35
  9.2 0.2 fusion.25
  9.5 0.1 copy.36
  9.6 0.1 copy.37
  9.7 0.1 mul.50
  9.8 0.1 copy.44
  9.9 0.1 mul.55
  10.0 0.0 copy-done
  10.0 11.5 all_gather.12
  21.5 0.4 fusion.24
  21.9 7.6 scatter_custom_fusion
  29.6 4.1 reshape.164
  33.7 53.8 %all_to_all.28 = bf16[128,3,2048]{2,1,0:T(4,128)(2,1)S(1)} all-to-all(bf16[128,3,2048]{2,1,0:T(4,128)(2,1)S(1)} %reshape.164), channel_id=1, replica_groups=mesh['rep'=4,'exp'=8] {'exp'}, dimensions={0} | all-to-all | bytes 3145728 | tf_op jit(solution)/shard_map/all_to_all | solution.py:34
  87.5 1.1 copy.38
  88.6 0.1 copy.39
  88.7 360.1 %all-gather.4.cloned.1.call-done = bf16[16,768,2048]{2,1,0:T(8,128)(2,1)} async-done(((bf16[16,768,512]{2,1,0:T(8,128)(2,1)}), bf16[16,768,2048]{2,1,0:T(8,128)(2,1)}) %all-gather.4.cloned.1.call-update) | async-done | bytes 50331664 | tf_op jit(solution)/shard_map/all_gather | solution.py:38
  448.8 28.4 %fusion.6 = f32[16,24,768]{2,1,0:T(8,128)} fusion(bf16[16,768,2048]{2,1,0:T(8,128)(2,1)} %all-gather.4.cloned.1.call-done, bf16[16,24,2048]{2,0,1:T(8,128)(2,1)S(1)} %bitcast.27), kind=kOutput, calls=%fused_computation.10 | convolution fusion | flops 1207959552 | bytes 53084160 | tf_op jit(solution)/shard_map/esd,efd->esf/dot_general | solution.py:35
  477.2 410.3 %all-gather.6.cloned.1.call-done = bf16[16,768,2048]{2,1,0:T(8,128)(2,1)} async-done(((bf16[16,768,512]{2,1,0:T(8,128)(2,1)}), bf16[16,768,2048]{2,1,0:T(8,128)(2,1)}) %all-gather.6.cloned.1.call-update) | async-done | bytes 50331664 | tf_op jit(solution)/shard_map/all_gather | solution.py:44
  887.6 438.8 %all-gather.8.cloned.1.call-done = bf16[16,768,2048]{2,1,0:T(8,128)(2,1)} async-done(((bf16[16,768,512]{2,1,0:T(8,128)(2,1)}), bf16[16,768,2048]{2,1,0:T(8,128)(2,1)}) %all-gather.8.cloned.1.call-update) | async-done | bytes 50331664 | tf_op jit(solution)/shard_map/all_gather | solution.py:51
  1326.3 34.3 %convolution_convert_fusion = bf16[16,24,2048]{2,1,0:T(8,128)(2,1)S(1)} fusion(bf16[16,768,2048]{2,1,0:T(8,128)(2,1)} %all-gather.8.cloned.1.call-done, bf16[16,768,2048]{2,1,0:T(8,128)(2,1)} %all-gather.6.cloned.1.call-done, bf16[16,24,2048]{2,0,1:T(8,128)(2,1)S(1)} %bitcast.28, f32[16,24,768]{2,1,0:T(8,128)} %fusion.6), kind=kOutput, calls=%fused_computation.4 | convolution fusion | flops 2418475008 | bytes 104988672 | tf_op jit(solution)/shard_map/esf,efd->esd/dot_general | solution.py:48
  1360.6 1.2 reshape.165
  1361.8 0.3 copy.42
  1362.1 22.5 %all_to_all.29 = bf16[16,8,3,4,512]{4,1,2,0,3:T(8,128)(2,1)S(1)} all-to-all(bf16[16,8,3,4,512]{4,1,2,0,3:T(8,128)(2,1)S(1)} %copy.42), channel_id=1, replica_groups=mesh['rep'=4,'exp'=8] {'rep'}, dimensions={3} | all-to-all | bytes 3145728 | tf_op jit(solution)/shard_map/all_to_all | solution.py:58
  1384.6 2.4 copy.43
  1386.9 0.0 copy-start.2
  1386.9 4.7 all-to-all-start.2
  1391.7 0.0 copy-done.2
  1391.7 0.1 copy.45
  1391.8 37.7 %all-to-all-done.2 = bf16[16,8,3,4,512]{4,3,2,0,1:T(4,128)(2,1)S(1)} async-done(((bf16[16,8,3,4,512]{4,3,2,0,1:T(4,128)(2,1)}), bf16[16,8,3,4,512]{4,3,2,0,1:T(4,128)(2,1)S(1)}, u32[]{:S(2)}, u32[]{:S(2)}) %all-to-all-start.2) | async-done | bytes 1572896 | tf_op jit(solution)/shard_map/all_to_all | solution.py:57
  1429.5 0.4 reshape.166
  1429.9 4.0 gather_fusion
  1433.9 1.3 fusion.2
  (9 shorter events, 0.2 us)
Async XLA Ops:
  6.5 442.3 %all-gather.4.cloned.1.call-start = ((), (), s32[]{:S(2)}) async-start(), calls=%async_computation.3 | async-start | bytes 62914560 | tf_op jit(solution)/shard_map/all_gather | solution.py:38
  7.3 880.3 %all-gather.6.cloned.1.call-start = ((), (), s32[]{:S(2)}) async-start(), calls=%async_computation.4 | async-start | bytes 62914560 | tf_op jit(solution)/shard_map/all_gather | solution.py:44
  8.0 0.7 copy-start.1
  8.0 1318.3 %all-gather.8.cloned.1.call-start = ((), (), s32[]{:S(2)}) async-start(), calls=%async_computation.5 | async-start | bytes 62914560 | tf_op jit(solution)/shard_map/all_gather | solution.py:51
  9.0 1.0 copy-start
  1386.9 4.7 copy-start.2
  1386.9 42.6 %all-to-all-start.2 = ((bf16[16,8,3,4,512]{4,3,2,0,1:T(4,128)(2,1)}), bf16[16,8,3,4,512]{4,3,2,0,1:T(4,128)(2,1)S(1)}, u32[]{:S(2)}, u32[]{:S(2)}) async-start(bf16[16,8,3,4,512]{4,3,2,0,1:T(4,128)(2,1)} %copy.43), calls=%async_computation.2 | async-start | bytes 3145728 | tf_op jit(solution)/shard_map/all_to_all | solution.py:57
Sparse Core Ops, SparseCore 0:
  9.2 439.5 all-gather.3
  450.6 436.8 all-gather.5
  889.4 436.8 all-gather.7
where the time goes:
time: 1440 us
  waiting for transfers between devices  1250 us (87%)
  blocking collectives  87.8 us (6%)
  matrix products  62.7 us (4%)
  local copies, waits for them, and re-layouts  22.3 us (2%)
    all_gather x1, waiting for transfers between devices, local(): lax.all_gather(w_down, 'rep', axis=2, tiled=True)  439 us
    all_gather x1, waiting for transfers between devices, local(): lax.all_gather(w_up, 'rep', axis=2, tiled=True)  410 us
    all_gather x1, waiting for transfers between devices, local(): lax.all_gather(w_gate, 'rep', axis=2, tiled=True)  360 us
    all_to_all x1, blocking collectives, local(): lax.all_to_all(outgoing, 'exp', split_axis=0, concat_axis=1, tiled=True)  53.8 us
    all_to_all x1, waiting for transfers between devices, local(): lax.all_to_all(lax.all_to_all(split_out, 'rep', split_axis=3, concat_axis...  37.7 us
    dot_general x1, matrix products, local(): jnp.einsum('esf,efd->esd', hidden, lax.all_gather(w_down, 'rep', axis=2,...  34.3 us
  transfers between devices with their start and end apart: 4, of which 4 were waited for; matrix products, arithmetic and copies ran while one was open for 3% of the time, Pallas kernels for 0%

commit v1 on v0

v1 whole, which is shorter than its diff:
```python
import functools

import jax
import jax.numpy as jnp
from jax import lax
from jax.experimental import pallas as pl
from jax.experimental.pallas import tpu as pltpu
from jax.sharding import PartitionSpec as P

EXPERTS = 128
F32 = jnp.float32
BF16 = jnp.bfloat16
VMEM_LIMIT = 56 * 2**20
ALIGN = 16
META = 16


def ceil_to(value, unit):
    return -(-value // unit) * unit


def vmem():
    return pl.BlockSpec(memory_space=pltpu.VMEM)


def smem():
    return pl.BlockSpec(memory_space=pltpu.SMEM)


def hbm():
    return pl.BlockSpec(memory_space=pl.ANY)


def params():
    return pltpu.CompilerParams(vmem_limit_bytes=VMEM_LIMIT)


def cost(flops, moved):
    return pl.CostEstimate(flops=int(flops), bytes_accessed=int(moved), transcendentals=0)


def route(dims, base, gathered, rowid, probs, rowk, offs):
    blocks, rows, top, experts = dims["blocks"], dims["rows"], dims["top"], dims["experts"]
    expert_at = lax.broadcasted_iota(jnp.int32, (experts, rows), 0) + base
    upper = (
        lax.broadcasted_iota(jnp.int32, (rows, rows), 0)
        <= lax.broadcasted_iota(jnp.int32, (rows, rows), 1)
    ).astype(BF16)

    def count(block, seen):
        meta = gathered[block, rows : rows + META, :].astype(F32)
        ids = meta[:top, :rows].astype(jnp.int32)
        chance = meta[:top, rows : 2 * rows] + meta[:top, 2 * rows : 3 * rows]
        chance = chance + meta[:top, 3 * rows : 4 * rows]
        member = jnp.zeros((experts, rows), F32)
        share = jnp.zeros((experts, rows), F32)
        for k in range(top):
            hit = ids[k : k + 1, :] == expert_at
            member = member + hit.astype(F32)
            share = share + jnp.where(hit, chance[k : k + 1, :], 0.0)
        upto = jnp.dot(member.astype(BF16), upper, preferred_element_type=F32)
        rowid[block] = jnp.where(member > 0, seen + upto - 1.0, -1e6)
        probs[block] = share
        return seen + upto[:, rows - 1 : rows]

    total = lax.fori_loop(0, blocks, count, jnp.zeros((experts, rows), F32))
    starts, before = [], jnp.zeros((1, rows), F32)
    for e in range(experts):
        starts.append(before)
        before = before + total[e : e + 1, :]
    start = jnp.concatenate(starts, axis=0) if experts > 1 else starts[0]

    def place(block, carry):
        ids = gathered[block, rows : rows + META, :][:top, :rows].astype(F32).astype(jnp.int32)
        at = rowid[block] + start
        rowid[block] = at
        chosen = []
        for k in range(top):
            hit = ids[k : k + 1, :] == expert_at
            chosen.append(jnp.max(jnp.where(hit, at, -1e6), axis=0, keepdims=True))
        rowk[block] = jnp.concatenate(chosen, axis=0)
        return carry

    lax.fori_loop(0, blocks, place, 0)
    offs[0] = start.astype(jnp.int32)
    offs[1] = total.astype(jnp.int32)
    return start


def window_hits(dims, rowid, block, e, start):
    at = lax.broadcasted_iota(jnp.int32, (dims["window"], dims["rows"]), 0) + start
    return rowid[block, e : e + 1, :].astype(jnp.int32) == at


def dispatch_kernel(dims, base_ref, gathered, x, rowid, probs, rowk, offs, select, total):
    blocks, rows, experts, window = dims["blocks"], dims["rows"], dims["experts"], dims["window"]
    group = dims["group"]
    start = route(dims, base_ref[0], gathered, rowid, probs, rowk, offs).astype(jnp.int32)
    starts = [start[e, 0] for e in range(experts)]

    def body(step, carry):
        select[...] = jnp.zeros_like(select)
        for e in range(experts):
            first = pl.multiple_of(starts[e] // ALIGN * ALIGN, ALIGN)
            at = pl.ds(first, window)
            for inner in range(group):
                cols = slice(inner * rows, (inner + 1) * rows)
                hit = window_hits(dims, rowid, step * group + inner, e, first)
                select[at, cols] = select[at, cols] + hit.astype(F32).astype(BF16)
        width = x.shape[1]
        part = gathered[pl.ds(step * group, group), :rows, :].reshape(group * rows, width)
        tile = dims["tile"]
        for r in range(0, x.shape[0], tile):
            size = min(tile, x.shape[0] - r)
            got = jnp.dot(select[r : r + size, :], part, preferred_element_type=F32)
            if blocks > group:
                got = got + jnp.where(step == 0, 0.0, total[r : r + size, :])
                total[r : r + size, :] = got
            x[r : r + size, :] = got.astype(BF16)
        return carry

    if blocks > group:
        total[...] = jnp.zeros_like(total)
        lax.fori_loop(0, blocks // group, body, 0)
    else:
        body(0, 0)


def dispatch(dims, base, gathered):
    blocks, rows, top, experts = dims["blocks"], dims["rows"], dims["top"], dims["experts"]
    width, padded = gathered.shape[2], dims["padded"]
    acc_rows = padded if blocks > dims["group"] else 8
    return pl.pallas_call(
        functools.partial(dispatch_kernel, dims),
        out_shape=(
            jax.ShapeDtypeStruct((padded, width), BF16),
            jax.ShapeDtypeStruct((blocks, experts, rows), F32),
            jax.ShapeDtypeStruct((blocks, experts, rows), F32),
            jax.ShapeDtypeStruct((blocks, top, rows), F32),
            jax.ShapeDtypeStruct((2, experts, rows), jnp.int32),
        ),
        in_specs=[smem(), vmem()],
        out_specs=(vmem(),) * 5,
        scratch_shapes=[
            pltpu.VMEM((padded, dims["group"] * rows), BF16),
            pltpu.VMEM((acc_rows, width), F32),
        ],
        compiler_params=params(),
        cost_estimate=cost(2 * padded * blocks * rows * width, 2 * blocks * rows * width * 2),
        name="dispatch",
    )(base, gathered)


def row_mask(dims, first, offs, e):
    at = lax.broadcasted_iota(jnp.int32, (dims["window"], 1), 0) + first
    begin = offs[0, e]
    return (at >= begin) & (at < begin + offs[1, e])


def gate_up_kernel(dims, c, me_ref, offs, x, w_gate, w_up, gx, uy, g2, u1, g0, u0, gate_w, up_w, gate, up, sems):
    experts, window, part, quarter = dims["experts"], dims["window"], dims["part"], dims["quarter"]
    units = pl.ds(c * part, part)

    def copies(e):
        return (
            pltpu.make_async_copy(w_gate.at[e, units, :], gate_w.at[e], sems.at[0, e]),
            pltpu.make_async_copy(w_up.at[e, units, :], up_w.at[e], sems.at[1, e]),
        )

    for e in range(experts):
        for copy in copies(e):
            copy.start()
    gate[...] = jnp.zeros_like(gate)
    up[...] = jnp.zeros_like(up)
    contract = (((1,), (1,)), ((), ()))
    for e in range(experts):
        first = pl.multiple_of(offs[0, e] // ALIGN * ALIGN, ALIGN)
        at = pl.ds(first, window)
        rows = x[at, :]
        mask = row_mask(dims, first, offs, e)
        for copy, held, into in zip(copies(e), (gate_w, up_w), (gate, up)):
            copy.wait()
            got = lax.dot_general(rows, held[e], contract, preferred_element_type=F32)
            into[at, :] = jnp.where(mask, got, into[at, :])
    me = me_ref[0]

    def piece(total, j):
        return total[pl.ds(pl.multiple_of((me ^ j) * quarter, ALIGN), quarter), :]

    gx[0] = piece(gate, 1).astype(BF16)
    gx[1] = piece(gate, 3).astype(BF16)
    uy[0] = piece(up, 2).astype(BF16)
    uy[1] = piece(up, 3).astype(BF16)
    g2[...] = piece(gate, 2)
    u1[...] = piece(up, 1)
    g0[...] = piece(gate, 0)
    u0[...] = piece(up, 0)


def gate_up(dims, c, me, offs, x, w_gate, w_up):
    experts, part, quarter, padded = dims["experts"], dims["part"], dims["quarter"], dims["padded"]
    width = x.shape[1]
    half = jax.ShapeDtypeStruct((2, quarter, part), BF16)
    own = jax.ShapeDtypeStruct((quarter, part), F32)
    return pl.pallas_call(
        functools.partial(gate_up_kernel, dims, c),
        out_shape=(half, half, own, own, own, own),
        in_specs=[smem(), smem(), vmem(), hbm(), hbm()],
        out_specs=(vmem(),) * 6,
        scratch_shapes=[
            pltpu.VMEM((experts, part, width), BF16),
            pltpu.VMEM((experts, part, width), BF16),
            pltpu.VMEM((padded, part), F32),
            pltpu.VMEM((padded, part), F32),
            pltpu.SemaphoreType.DMA((2, experts)),
        ],
        compiler_params=params(),
        cost_estimate=cost(4 * padded * width * part, 4 * experts * part * width + 2 * padded * width),
        name="gate_up",
    )(me, offs, x, w_gate, w_up)


def gather_hidden(dims, me, pieces, hidden):
    quarter, half = dims["quarter"], dims["part"] // 2
    for c, chunk in enumerate(pieces):
        for j, halves in enumerate(chunk):
            at = pl.ds(pl.multiple_of((me ^ j) * quarter, ALIGN), quarter)
            for side, held in enumerate(halves):
                col = c * dims["part"] + side * half
                hidden[at, col : col + half] = held[...]


def unpack(refs, chunks):
    pieces = [[refs[c * 8 + j * 2 : c * 8 + j * 2 + 2] for j in range(4)] for c in range(chunks)]
    return pieces, refs[chunks * 8 :]


def choose(dims, rowk, block):
    at = lax.broadcasted_iota(jnp.int32, (dims["rows"], dims["total"]), 1)
    rows_of = rowk[block].T.astype(jnp.int32)
    hit = rows_of[:, 0:1] == at
    for k in range(1, dims["top"]):
        hit = hit | (rows_of[:, k : k + 1] == at)
    return hit.astype(F32).astype(BF16)


def down_first_kernel(dims, chunks, me_ref, offs, rowid, probs, rowk, w_down, *refs):
    experts, window = dims["experts"], dims["window"]
    pieces, (y, scale, chosen, held, hidden, sems) = unpack(refs, chunks)
    units = pl.ds(0, chunks * dims["part"])

    def copy(e):
        return pltpu.make_async_copy(w_down.at[e, units, :], held.at[e], sems.at[e])

    for e in range(experts):
        copy(e).start()
    hidden[...] = jnp.zeros_like(hidden)
    gather_hidden(dims, me_ref[0], pieces, hidden)
    y[...] = jnp.zeros_like(y)
    scale[...] = jnp.zeros_like(scale)
    if dims["early"]:
        def early(block, carry):
            chosen[block] = choose(dims, rowk, block)
            return carry

        lax.fori_loop(0, dims["blocks"], early, 0)
    else:
        chosen[...] = jnp.zeros_like(chosen)
    for e in range(experts):
        first = pl.multiple_of(offs[0, e] // ALIGN * ALIGN, ALIGN)
        at = pl.ds(first, window)
        mask = row_mask(dims, first, offs, e)

        def share(block, carry):
            hit = window_hits(dims, rowid, block, e, first)
            return carry + jnp.where(hit, probs[block, e : e + 1, :], 0.0)

        shares = lax.fori_loop(
            0, dims["blocks"], share, jnp.zeros((window, dims["rows"]), F32)
        )
        wide = jnp.broadcast_to(jnp.sum(shares, axis=1, keepdims=True), (window, scale.shape[1]))
        scale[at, :] = jnp.where(mask, wide, scale[at, :])
        copy(e).wait()
        got = jnp.dot(hidden[at, :], held[e], preferred_element_type=F32)
        y[at, :] = jnp.where(mask, got, y[at, :])


def down_last_kernel(dims, c, me_ref, offs, y, scale, chosen, rowk, w_down, *refs):
    experts, window, part = dims["experts"], dims["window"], dims["part"]
    pieces, (out, held, hidden, scaled, sems) = unpack(refs, 1)
    units = pl.ds(c * part, part)

    def copy(e):
        return pltpu.make_async_copy(w_down.at[e, units, :], held.at[e], sems.at[e])

    for e in range(experts):
        copy(e).start()
    hidden[...] = jnp.zeros_like(hidden)
    scaled[...] = jnp.zeros_like(scaled)
    gather_hidden(dims, me_ref[0], pieces, hidden)
    width = y.shape[1]
    for e in range(experts):
        first = pl.multiple_of(offs[0, e] // ALIGN * ALIGN, ALIGN)
        at = pl.ds(first, window)
        mask = row_mask(dims, first, offs, e)
        copy(e).wait()
        got = jnp.dot(hidden[at, :], held[e], preferred_element_type=F32) + y[at, :]
        got = got * scale[at, 0:1]
        scaled[at, :] = jnp.where(mask, got, scaled[at, :].astype(F32)).astype(BF16)
    rows, group, total = dims["rows"], dims["group"], dims["total"]

    def combine(step, carry):
        many = min(4, group)
        for inner in range(0, group, many):
            if dims["early"]:
                picked = chosen[pl.ds(step * group + inner, many)].reshape(many * rows, total)
            else:
                picked = jnp.concatenate(
                    [choose(dims, rowk, step * group + inner + i) for i in range(many)], axis=0
                )
            summed = jnp.dot(picked, scaled[:total, :], preferred_element_type=F32)
            out[pl.ds(step * group + inner, many)] = summed.astype(BF16).reshape(many, rows, width)
        return carry

    if dims["blocks"] > group:
        lax.fori_loop(0, dims["blocks"] // group, combine, 0)
    else:
        combine(0, 0)


def flat(pieces):
    return [held for chunk in pieces for halves in chunk for held in halves]


def down_first(dims, me, offs, rowid, probs, rowk, w_down, pieces):
    experts, padded, part = dims["experts"], dims["padded"], dims["part"]
    chunks, width = len(pieces), w_down.shape[2]
    picked = (dims["blocks"], dims["rows"], dims["total"]) if dims["early"] else (1, ALIGN, 128)
    return pl.pallas_call(
        functools.partial(down_first_kernel, dims, chunks),
        out_shape=(
            jax.ShapeDtypeStruct((padded, width), F32),
            jax.ShapeDtypeStruct((padded, 128), F32),
            jax.ShapeDtypeStruct(picked, BF16),
        ),
        in_specs=[smem(), smem(), vmem(), vmem(), vmem(), hbm()] + [vmem()] * (8 * chunks),
        out_specs=(vmem(),) * 3,
        scratch_shapes=[
            pltpu.VMEM((experts, chunks * part, width), BF16),
            pltpu.VMEM((padded, chunks * part), BF16),
            pltpu.SemaphoreType.DMA((experts,)),
        ],
        compiler_params=params(),
        cost_estimate=cost(
            2 * padded * width * part * chunks, 2 * experts * part * chunks * width + 8 * padded * width
        ),
        name="down_first",
    )(me, offs, rowid, probs, rowk, w_down, *flat(pieces))


def down_last(dims, c, me, offs, y, scale, chosen, rowk, w_down, pieces):
    experts, padded, part = dims["experts"], dims["padded"], dims["part"]
    width = w_down.shape[2]
    return pl.pallas_call(
        functools.partial(down_last_kernel, dims, c),
        out_shape=jax.ShapeDtypeStruct((dims["blocks"], dims["rows"], width), BF16),
        in_specs=[smem(), smem()] + [vmem()] * 4 + [hbm()] + [vmem()] * 8,
        out_specs=vmem(),
        scratch_shapes=[
            pltpu.VMEM((experts, part, width), BF16),
            pltpu.VMEM((padded, part), BF16),
            pltpu.VMEM((padded, width), BF16),
            pltpu.SemaphoreType.DMA((experts,)),
        ],
        compiler_params=params(),
        cost_estimate=cost(4 * padded * width * part, 2 * experts * part * width + 8 * padded * width),
        name="down_last",
    )(me, offs, y, scale, chosen, rowk, w_down, *flat([pieces]))


def swap(value, bit):
    count = lax.axis_size("rep")
    return lax.ppermute(value, "rep", [(i, i ^ bit) for i in range(count)])


def reduce_chunk(parts):
    gx, uy, g2, u1, g0, u0 = parts
    from_x = swap(gx, 1)
    from_y = swap(uy, 2)
    gate_rest = swap((g2 + from_x[1].astype(F32)).astype(BF16), 2)
    up_rest = swap((u1 + from_y[1].astype(F32)).astype(BF16), 1)
    gate = g0 + from_x[0].astype(F32) + gate_rest.astype(F32)
    up = u0 + from_y[0].astype(F32) + up_rest.astype(F32)
    hidden = (jax.nn.silu(gate) * up).astype(BF16)
    half = hidden.shape[1] // 2
    return hidden[:, :half], hidden[:, half:]


def spread_chunk(left, right):
    x = (swap(left, 1), swap(right, 1))
    y = (swap(left, 2), swap(right, 2))
    corner = (swap(x[0], 2), swap(y[1], 1))
    return [(left, right), x, y, corner]


def local(tokens, expert_ids, route_weights, w_gate, w_up, w_down):
    rows, top = expert_ids.shape
    width = tokens.shape[1]
    experts, units, _ = w_gate.shape
    blocks = lax.axis_size("exp")
    replicas = lax.axis_size("rep")
    cap = replicas * max(1, rows * top * 3 // (8 * EXPERTS))
    total = ceil_to(experts * blocks * cap, replicas * 128)
    window = ceil_to(blocks * cap, ALIGN) + ALIGN
    part = 256
    dims = dict(
        blocks=blocks,
        rows=rows,
        top=top,
        experts=experts,
        window=window,
        total=total,
        quarter=total // replicas,
        padded=total + window,
        part=part,
        group=min(blocks, 8),
        tile=512,
        early=blocks * rows * total <= 4 * 2**20,
    )
    me = lax.axis_index("rep").astype(jnp.int32).reshape(1)
    base = (lax.axis_index("exp") * experts).astype(jnp.int32).reshape(1)

    chance = (route_weights / jnp.sum(route_weights, axis=1, keepdims=True)).T
    high = lax.reduce_precision(chance, 8, 7)
    middle = lax.reduce_precision(chance - high, 8, 7)
    low = chance - high - middle
    chance = jnp.concatenate([high, middle, low], axis=1).astype(BF16)
    meta = jnp.concatenate([expert_ids.T.astype(BF16), chance], axis=1)
    meta = jnp.pad(meta, ((0, META - top), (0, width - meta.shape[1])))
    packed = jnp.concatenate([tokens, meta], axis=0)
    gathered = lax.all_gather(packed, "exp", axis=0)

    x, rowid, probs, rowk, offs_wide = dispatch(dims, base, gathered)
    offs = offs_wide[:, :, 0]

    pieces = []
    for c in range(units // part):
        left, right = reduce_chunk(gate_up(dims, c, me, offs, x, w_gate, w_up))
        pieces.append(spread_chunk(left, right))
    y, scale, chosen = down_first(dims, me, offs, rowid, probs, rowk, w_down, pieces[:-1])
    last = len(pieces) - 1
    mixed = down_last(dims, last, me, offs, y, scale, chosen, rowk, w_down, pieces[-1])
    return lax.psum_scatter(mixed, "exp", scatter_dimension=0, tiled=False)


def solution(mesh):
    return jax.shard_map(
        local,
        mesh=mesh,
        in_specs=(
            P("exp", "rep"),
            P("exp", None),
            P("exp", None),
            P("exp", None, "rep"),
            P("exp", None, "rep"),
            P("exp", None, "rep"),
        ),
        out_specs=P("exp", "rep"),
        check_vma=False,
    )
```

time: 1440 us -> 206 us (0.14)
  waiting for transfers between devices: 1250 us -> 75.2 us
  blocking collectives: 87.8 us -> 0 us
  Pallas kernels: 0 us -> 78.4 us
  matrix products: 62.7 us -> 0 us
  starting transfers between devices: 4.82 us -> 31.1 us
  local copies, waits for them, and re-layouts: 22.3 us -> 2.76 us
    all_gather x3 -> x1, waiting for transfers between devices: 1210 us -> 25.5 us  [local(): gathered = lax.all_gather(packed, 'exp', axis=0)]
    pallas_call x0 -> x6, Pallas kernels: none -> 78.4 us  [the longest x3 39.7 us: gate_up(): pl.pallas_call(functools.partial(gate_up_kernel, dims, c), out_shape=(hal...]
    all_to_all x2 -> x0, blocking collectives: 76.3 us -> none  [the longest x1 53.8 us: local(): lax.all_to_all(outgoing, 'exp', split_axis=0, concat_axis=1, tiled=True)]
    dot_general x2 -> x0, matrix products: 62.7 us -> none  [the longest x1 34.3 us: local(): jnp.einsum('esf,efd->esd', hidden, lax.all_gather(w_down, 'rep', axis=2,...]
    all_to_all x1 -> x0, waiting for transfers between devices: 37.7 us -> none  [local(): lax.all_to_all(lax.all_to_all(split_out, 'rep', split_axis=3, concat_axis...]
    reduce_scatter x0 -> x1, waiting for transfers between devices: none -> 31.3 us  [local(): return lax.psum_scatter(mixed, 'exp', scatter_dimension=0, tiled=False)]
    ppermute x0 -> x30, starting transfers between devices: none -> 31 us  [swap(): return lax.ppermute(value, 'rep', [(i, i ^ bit) for i in range(count)])]
    ppermute x0 -> x30, waiting for transfers between devices: none -> 18.4 us  [swap(): return lax.ppermute(value, 'rep', [(i, i ^ bit) for i in range(count)])]
  transfers between devices with their start and end apart: 4 -> 32, of which waited for: 4 -> 11; matrix products, arithmetic and copies ran while one was open for 3% -> 0% of each run, Pallas kernels for 0% -> 23%
where the time goes in v1:
time: 206 us
  Pallas kernels  78.4 us (38%)
  waiting for transfers between devices  75.2 us (37%)
  starting transfers between devices  31.1 us (15%)
  between operations  13.9 us (7%)
  other arithmetic  4.53 us (2%)
  local copies, waits for them, and re-layouts  2.76 us (1%)
    pallas_call x3, Pallas kernels, gate_up(): pl.pallas_call(functools.partial(gate_up_kernel, dims, c), out_shape=(hal...  39.7 us
    reduce_scatter x1, waiting for transfers between devices, local(): return lax.psum_scatter(mixed, 'exp', scatter_dimension=0, tiled=False)  31.3 us
    ppermute x30, starting transfers between devices, swap(): return lax.ppermute(value, 'rep', [(i, i ^ bit) for i in range(count)])  31 us
    all_gather x1, waiting for transfers between devices, local(): gathered = lax.all_gather(packed, 'exp', axis=0)  25.5 us
    pallas_call x1, Pallas kernels, down_first(): pl.pallas_call(functools.partial(down_first_kernel, dims, chunks), out_sh...  20.6 us
    ppermute x30, waiting for transfers between devices, swap(): return lax.ppermute(value, 'rep', [(i, i ^ bit) for i in range(count)])  18.4 us
    pallas_call x1, Pallas kernels, down_last(): pl.pallas_call(functools.partial(down_last_kernel, dims, c), out_shape=ja...  10.3 us
    pallas_call x1, Pallas kernels, dispatch(): pl.pallas_call(functools.partial(dispatch_kernel, dims), out_shape=(jax.S...  7.84 us
  transfers between devices with their start and end apart: 32, of which 11 were waited for; matrix products, arithmetic and copies ran while one was open for 0% of the time, Pallas kernels for 23%

profile of v1, /device:TPU:0, one launch (start us, length us, event | category | flops | bytes accessed | tf_op | source)
XLA Modules:
  0.0 205.8 jit_solution(3403902010914130155)
XLA Ops:
  6.5 0.7 convert_bitcast_fusion
  7.2 0.7 reduce_sum.9
  7.9 0.7 reduce-precision_convert_fusion.1
  8.6 1.6 pad_maximum_fusion
  10.2 0.0 reduce-scatter.2.cloned.1.call-start
  10.3 25.5 %all-gather.3.cloned.1.call-done = bf16[1152,512]{1,0:T(8,128)(2,1)} async-done(((bf16[144,512]{1,0:T(8,128)(2,1)}), bf16[1152,512]{1,0:T(8,128)(2,1)}) %all-gather.3.cloned.1.call-update) | async-done | bytes 1179664 | tf_op jit(solution)/shard_map/all_gather | solution.py:441
  35.7 7.8 %dispatch.1 = (bf16[1648,512]{1,0:T(8,128)(2,1)}, f32[8,16,128]{2,1,0:T(8,128)}, f32[8,16,128]{2,1,0:T(8,128)}, f32[8,8,128]{2,1,0:T(8,128)}, s32[2,16,128]{2,1,0:T(8,128)}) custom-call(s32[1]{0:T(128)} %bitcast.1.base_ref, bf16[8,144,512]{2,1,0:T(8,128)(2,1)} %bitcast.73), custom_call_target="tpu_custom_call" | custom-call | flops 1728053248 | bytes 2097152 | tf_op jit(solution)/shard_map/dispatch/pallas_call | solution.py:133
  43.6 1.4 slice_reduce_fusion.offs
  45.0 13.2 %gate_up.5 = (bf16[2,384,256]{2,1,0:T(8,128)(2,1)}, bf16[2,384,256]{2,1,0:T(8,128)(2,1)}, f32[384,256]{1,0:T(8,128)}, f32[384,256]{1,0:T(8,128)}, f32[384,256]{1,0:T(8,128)}, /*index=5*/f32[384,256]{1,0:T(8,128)}) custom-call(s32[1]{0:T(128)} %bitcast.me_ref, s32[2,16]{1,0:T(2,128)} %slice_reduce_fusion.offs, bf16[1648,512]{1,0:T(8,128)(2,1)} %get-tuple-element.35.x, ...), custom_call_target="tpu_custom_call" | custom-call | flops 864026624 | bytes 10076160 | tf_op jit(solution)/shard_map/gate_up/pallas_call | solution.py:205
  58.2 1.5 collective-permute-start.20
  59.7 1.5 collective-permute-start.22
  61.2 13.2 %gate_up.4 = (bf16[2,384,256]{2,1,0:T(8,128)(2,1)}, bf16[2,384,256]{2,1,0:T(8,128)(2,1)}, f32[384,256]{1,0:T(8,128)}, f32[384,256]{1,0:T(8,128)}, f32[384,256]{1,0:T(8,128)}, /*index=5*/f32[384,256]{1,0:T(8,128)}) custom-call(s32[1]{0:T(128)} %bitcast.me_ref, s32[2,16]{1,0:T(2,128)} %slice_reduce_fusion.offs, bf16[1648,512]{1,0:T(8,128)(2,1)} %get-tuple-element.35.x, ...), custom_call_target="tpu_custom_call" | custom-call | flops 864026624 | bytes 10076160 | tf_op jit(solution)/shard_map/gate_up/pallas_call | solution.py:205
  74.4 0.6 collective-permute-start.10
  75.0 0.6 collective-permute-start.12
  75.6 13.3 %gate_up.3 = (bf16[2,384,256]{2,1,0:T(8,128)(2,1)}, bf16[2,384,256]{2,1,0:T(8,128)(2,1)}, f32[384,256]{1,0:T(8,128)}, f32[384,256]{1,0:T(8,128)}, f32[384,256]{1,0:T(8,128)}, /*index=5*/f32[384,256]{1,0:T(8,128)}) custom-call(s32[1]{0:T(128)} %bitcast.me_ref, s32[2,16]{1,0:T(2,128)} %slice_reduce_fusion.offs, bf16[1648,512]{1,0:T(8,128)(2,1)} %get-tuple-element.35.x, ...), custom_call_target="tpu_custom_call" | custom-call | flops 864026624 | bytes 10076160 | tf_op jit(solution)/shard_map/gate_up/pallas_call | solution.py:205
  89.0 1.5 collective-permute-start
  90.5 1.5 collective-permute-start.2
  92.0 0.6 collective-permute-start.21
  92.7 0.6 collective-permute-start.23
  93.4 1.6 collective-permute-start.11
  95.1 6.3 %collective-permute-done = bf16[2,384,256]{2,1,0:T(8,128)(2,1)S(1)} collective-permute-done((bf16[2,384,256]{2,1,0:T(8,128)(2,1)}, bf16[2,384,256]{2,1,0:T(8,128)(2,1)S(1)}, u32[]{:S(2)}, u32[]{:S(2)}) %collective-permute-start) | collective-permute-done | bytes 393248 | tf_op jit(solution)/shard_map/ppermute | solution.py:383
  101.3 1.5 collective-permute-start.13
  102.8 0.1 fusion.16
  102.8 1.5 collective-permute-start.1
  104.4 0.1 fusion.12
  104.4 6.8 %collective-permute-done.11 = bf16[384,256]{1,0:T(8,128)(2,1)S(1)} collective-permute-done((bf16[384,256]{1,0:T(8,128)(2,1)S(1)}, bf16[384,256]{1,0:T(8,128)(2,1)S(1)}, u32[]{:S(2)}, u32[]{:S(2)}) %collective-permute-start.11) | collective-permute-done | bytes 196640 | tf_op jit(solution)/shard_map/ppermute | solution.py:383
  111.2 0.6 collective-permute-start.3
  111.8 0.2 fusion.9
  112.0 1.5 collective-permute-start.17
  113.5 1.5 collective-permute-start.15
  115.0 0.2 fusion.3
  115.3 0.6 collective-permute-start.27
  115.9 0.6 collective-permute-start.24
  116.5 0.6 collective-permute-done.3
  117.1 1.2 collective-permute-start.16
  118.4 0.2 fusion.15
  118.6 1.9 collective-permute-done.27.refs_5_
  120.5 0.5 collective-permute-start.14
  121.1 0.5 collective-permute-done.24.refs_2_
  121.6 1.5 collective-permute-start.7
  123.1 0.2 collective-permute-start.5
  123.3 1.8 collective-permute-start.4
  125.2 0.5 collective-permute-start.6
  125.6 0.4 collective-permute-done.14.refs_10_
  126.0 0.6 collective-permute-start.19
  126.6 0.5 collective-permute-done.7.refs_5_
  127.2 1.5 collective-permute-start.18
  128.7 0.2 collective-permute-done.5.refs_3_
  128.9 0.4 collective-permute-start.9
  129.2 1.2 collective-permute-done.4.refs_2_
  130.4 0.8 collective-permute-start.8
  131.2 1.1 collective-permute-start.25
  132.3 0.9 collective-permute-start.26
  133.2 1.3 collective-permute-start.29
  134.5 0.8 collective-permute-start.28
  135.4 0.5 copy-done.34
  135.9 20.6 %down_first.1 = (f32[1648,512]{1,0:T(8,128)}, f32[1648,128]{1,0:T(8,128)}, bf16[8,128,1536]{2,1,0:T(8,128)(2,1)}) custom-call(s32[1]{0:T(128)} %bitcast.me_ref, s32[2,16]{1,0:T(2,128)} %slice_reduce_fusion.offs, f32[8,16,128]{2,1,0:T(8,128)} %get-tuple-element.32.rowid, f32[8,16,128]{2,1,0:T(8,128)} %get-tuple-element.33.probs, ...), custom_call_target="tpu_custom_call" | custom-call | flops 864026624 | bytes 15138816 | tf_op jit(solution)/shard_map/down_first/pallas_call | solution.py:339
  156.6 0.6 copy-done.29
  157.2 0.0 copy-done.31
  157.2 0.0 copy-done.33
  157.2 0.0 copy-done.35
  157.3 10.3 %down_last.1 = bf16[8,128,512]{2,1,0:T(8,128)(2,1)} custom-call(s32[1]{0:T(128)} %bitcast.me_ref, s32[2,16]{1,0:T(2,128)} %slice_reduce_fusion.offs, f32[1648,512]{1,0:T(8,128)} %get-tuple-element.48.y, f32[1648,128]{1,0:T(8,128)} %get-tuple-element.49.scale, bf16[8,128,1536]{2,1,0:T(8,128)(2,1)} %get-tuple-element.50.chosen, ...), custom_call_target="tpu_custom_call" | custom-call | flops 864026624 | bytes 10944512 | tf_op jit(solution)/shard_map/down_last/pallas_call | solution.py:364
  167.6 0.0 reduce-scatter.2.cloned.1.call-update
  167.6 31.3 %reduce-scatter.2.cloned.1.call-done = bf16[1,128,512]{2,1,0:T(8,128)(2,1)} async-done(((bf16[8,128,512]{2,1,0:T(8,128)(2,1)}), bf16[1,128,512]{2,1,0:T(8,128)(2,1)}) %reduce-scatter.2.cloned.1.call-update) | async-done | bytes 131088 | tf_op jit(solution)/shard_map/reduce_scatter | solution.py:453
  (98 shorter events, 0.4 us)
Async XLA Ops:
  6.5 29.2 %all-gather.3.cloned.1.call-start = ((), (), s32[]{:S(2)}) async-start(), calls=%async_computation.2 | async-start | bytes 1327104 | tf_op jit(solution)/shard_map/all_gather | solution.py:441
  10.2 188.7 %reduce-scatter.2.cloned.1.call-start = ((), (), s32[]{:S(2)}) async-start(), calls=%async_computation.1 | async-start | bytes 1179648 | tf_op jit(solution)/shard_map/reduce_scatter | solution.py:453
  58.2 32.4 %collective-permute-start.20 = (bf16[2,384,256]{2,1,0:T(8,128)(2,1)}, bf16[2,384,256]{2,1,0:T(8,128)(2,1)S(1)}, u32[]{:S(2)}, u32[]{:S(2)}) collective-permute-start(bf16[2,384,256]{2,1,0:T(8,128)(2,1)} %get-tuple-element.52), channel_id=1, source_target_pairs={{0,8},{8,0},{16,24},{24,16},{1,9},{9,1},{17,25},{25,17},{2,10},{10... | collective-permute-start | bytes 1179656 | tf_op jit(solution)/shard_map/ppermute | solution.py:383
  59.7 32.4 %collective-permute-start.22 = (bf16[2,384,256]{2,1,0:T(8,128)(2,1)}, bf16[2,384,256]{2,1,0:T(8,128)(2,1)S(1)}, u32[]{:S(2)}, u32[]{:S(2)}) collective-permute-start(bf16[2,384,256]{2,1,0:T(8,128)(2,1)} %get-tuple-element.55), channel_id=1, source_target_pairs={{0,16},{8,24},{16,0},{24,8},{1,17},{9,25},{17,1},{25,9},{2,18},{10... | collective-permute-start | bytes 1179656 | tf_op jit(solution)/shard_map/ppermute | solution.py:383
  74.4 18.4 %collective-permute-start.10 = (bf16[2,384,256]{2,1,0:T(8,128)(2,1)}, bf16[2,384,256]{2,1,0:T(8,128)(2,1)S(1)}, u32[]{:S(2)}, u32[]{:S(2)}) collective-permute-start(bf16[2,384,256]{2,1,0:T(8,128)(2,1)} %get-tuple-element.43), channel_id=1, source_target_pairs={{0,8},{8,0},{16,24},{24,16},{1,9},{9,1},{17,25},{25,17},{2,10},{10... | collective-permute-start | bytes 1179656 | tf_op jit(solution)/shard_map/ppermute | solution.py:383
  75.0 17.0 %copy-start.17 = (f32[384,256]{1,0:T(8,128)S(1)}, f32[384,256]{1,0:T(8,128)}, u32[]{:S(2)}) copy-start(f32[384,256]{1,0:T(8,128)} %get-tuple-element.53) | copy-start | bytes 1179652
  75.0 17.7 %copy-start.15 = (f32[384,256]{1,0:T(8,128)S(1)}, f32[384,256]{1,0:T(8,128)}, u32[]{:S(2)}) copy-start(f32[384,256]{1,0:T(8,128)} %get-tuple-element.56) | copy-start | bytes 1179652
  75.0 18.4 %copy-start.16 = (f32[384,256]{1,0:T(8,128)S(1)}, f32[384,256]{1,0:T(8,128)}, u32[]{:S(2)}) copy-start(f32[384,256]{1,0:T(8,128)} %get-tuple-element.44) | copy-start | bytes 1179652
  75.0 20.0 %copy-start.13 = (f32[384,256]{1,0:T(8,128)S(1)}, f32[384,256]{1,0:T(8,128)}, u32[]{:S(2)}) copy-start(f32[384,256]{1,0:T(8,128)} %get-tuple-element.47) | copy-start | bytes 1179652
  75.0 18.4 %collective-permute-start.12 = (bf16[2,384,256]{2,1,0:T(8,128)(2,1)}, bf16[2,384,256]{2,1,0:T(8,128)(2,1)S(1)}, u32[]{:S(2)}, u32[]{:S(2)}) collective-permute-start(bf16[2,384,256]{2,1,0:T(8,128)(2,1)} %get-tuple-element.46), channel_id=1, source_target_pairs={{0,16},{8,24},{16,0},{24,8},{1,17},{9,25},{17,1},{25,9},{2,18},{10... | collective-permute-start | bytes 1179656 | tf_op jit(solution)/shard_map/ppermute | solution.py:383
  88.9 13.8 %copy-start.14 = (f32[384,256]{1,0:T(8,128)S(1)}, f32[384,256]{1,0:T(8,128)}, u32[]{:S(2)}) copy-start(f32[384,256]{1,0:T(8,128)} %get-tuple-element.38) | copy-start | bytes 1179652
  88.9 15.4 %copy-start.12 = (f32[384,256]{1,0:T(8,128)S(1)}, f32[384,256]{1,0:T(8,128)}, u32[]{:S(2)}) copy-start(f32[384,256]{1,0:T(8,128)} %get-tuple-element.41) | copy-start | bytes 1179652
  89.0 22.8 %copy-start.10 = (f32[384,256]{1,0:T(8,128)S(1)}, f32[384,256]{1,0:T(8,128)}, u32[]{:S(2)}) copy-start(f32[384,256]{1,0:T(8,128)} %get-tuple-element.42) | copy-start | bytes 1179652
  89.0 22.8 %copy-start.11 = (f32[384,256]{1,0:T(8,128)S(1)}, f32[384,256]{1,0:T(8,128)}, u32[]{:S(2)}) copy-start(f32[384,256]{1,0:T(8,128)} %get-tuple-element.45) | copy-start | bytes 1179652
  89.0 12.3 %collective-permute-start = (bf16[2,384,256]{2,1,0:T(8,128)(2,1)}, bf16[2,384,256]{2,1,0:T(8,128)(2,1)S(1)}, u32[]{:S(2)}, u32[]{:S(2)}) collective-permute-start(bf16[2,384,256]{2,1,0:T(8,128)(2,1)} %get-tuple-element.37), channel_id=1, source_target_pairs={{0,8},{8,0},{16,24},{24,16},{1,9},{9,1},{17,25},{25,17},{2,10},{10... | collective-permute-start | bytes 1179656 | tf_op jit(solution)/shard_map/ppermute | solution.py:383
  90.5 12.3 %collective-permute-start.2 = (bf16[2,384,256]{2,1,0:T(8,128)(2,1)}, bf16[2,384,256]{2,1,0:T(8,128)(2,1)S(1)}, u32[]{:S(2)}, u32[]{:S(2)}) collective-permute-start(bf16[2,384,256]{2,1,0:T(8,128)(2,1)} %get-tuple-element.40), channel_id=1, source_target_pairs={{0,16},{8,24},{16,0},{24,8},{1,17},{9,25},{17,1},{25,9},{2,18},{10... | collective-permute-start | bytes 1179656 | tf_op jit(solution)/shard_map/ppermute | solution.py:383
  92.0 23.0 %copy-start.8 = (f32[384,256]{1,0:T(8,128)S(1)}, f32[384,256]{1,0:T(8,128)}, u32[]{:S(2)}) copy-start(f32[384,256]{1,0:T(8,128)} %get-tuple-element.51) | copy-start | bytes 1179652
  92.0 23.1 %copy-start.9 = (f32[384,256]{1,0:T(8,128)S(1)}, f32[384,256]{1,0:T(8,128)}, u32[]{:S(2)}) copy-start(f32[384,256]{1,0:T(8,128)} %get-tuple-element.54) | copy-start | bytes 1179652
  92.0 21.4 %collective-permute-start.21 = (bf16[384,256]{1,0:T(8,128)(2,1)S(1)}, bf16[384,256]{1,0:T(8,128)(2,1)S(1)}, u32[]{:S(2)}, u32[]{:S(2)}) collective-permute-start(bf16[384,256]{1,0:T(8,128)(2,1)S(1)} %fusion.4), channel_id=1, source_target_pairs={{0,16},{8,24},{16,0},{24,8},{1,17},{9,25},{17,1},{25,9},{2,18},{10... | collective-permute-start | bytes 589832 | tf_op jit(solution)/shard_map/ppermute | solution.py:383
  92.7 22.3 %collective-permute-start.23 = (bf16[384,256]{1,0:T(8,128)(2,1)S(1)}, bf16[384,256]{1,0:T(8,128)(2,1)S(1)}, u32[]{:S(2)}, u32[]{:S(2)}) collective-permute-start(bf16[384,256]{1,0:T(8,128)(2,1)S(1)} %fusion), channel_id=1, source_target_pairs={{0,8},{8,0},{16,24},{24,16},{1,9},{9,1},{17,25},{25,17},{2,10},{10... | collective-permute-start | bytes 589832 | tf_op jit(solution)/shard_map/ppermute | solution.py:383
  93.4 25.0 %copy-start.6 = (f32[384,256]{1,0:T(8,128)S(1)}, f32[384,256]{1,0:T(8,128)}, u32[]{:S(2)}) copy-start(f32[384,256]{1,0:T(8,128)} %get-tuple-element.36) | copy-start | bytes 1179652
  93.4 24.9 %copy-start.7 = (f32[384,256]{1,0:T(8,128)S(1)}, f32[384,256]{1,0:T(8,128)}, u32[]{:S(2)}) copy-start(f32[384,256]{1,0:T(8,128)} %get-tuple-element.39) | copy-start | bytes 1179652
  93.4 17.8 %collective-permute-start.11 = (bf16[384,256]{1,0:T(8,128)(2,1)S(1)}, bf16[384,256]{1,0:T(8,128)(2,1)S(1)}, u32[]{:S(2)}, u32[]{:S(2)}) collective-permute-start(bf16[384,256]{1,0:T(8,128)(2,1)S(1)} %fusion.10), channel_id=1, source_target_pairs={{0,16},{8,24},{16,0},{24,8},{1,17},{9,25},{17,1},{25,9},{2,18},{10... | collective-permute-start | bytes 589832 | tf_op jit(solution)/shard_map/ppermute | solution.py:383
  101.3 10.5 %collective-permute-start.13 = (bf16[384,256]{1,0:T(8,128)(2,1)S(1)}, bf16[384,256]{1,0:T(8,128)(2,1)S(1)}, u32[]{:S(2)}, u32[]{:S(2)}) collective-permute-start(bf16[384,256]{1,0:T(8,128)(2,1)S(1)} %fusion.6), channel_id=1, source_target_pairs={{0,8},{8,0},{16,24},{24,16},{1,9},{9,1},{17,25},{25,17},{2,10},{10... | collective-permute-start | bytes 589832 | tf_op jit(solution)/shard_map/ppermute | solution.py:383
  102.8 13.1 %collective-permute-start.1 = (bf16[384,256]{1,0:T(8,128)(2,1)S(1)}, bf16[384,256]{1,0:T(8,128)(2,1)S(1)}, u32[]{:S(2)}, u32[]{:S(2)}) collective-permute-start(bf16[384,256]{1,0:T(8,128)(2,1)S(1)} %fusion.16), channel_id=1, source_target_pairs={{0,16},{8,24},{16,0},{24,8},{1,17},{9,25},{17,1},{25,9},{2,18},{10... | collective-permute-start | bytes 589832 | tf_op jit(solution)/shard_map/ppermute | solution.py:383
  111.2 5.9 %collective-permute-start.3 = (bf16[384,256]{1,0:T(8,128)(2,1)S(1)}, bf16[384,256]{1,0:T(8,128)(2,1)S(1)}, u32[]{:S(2)}, u32[]{:S(2)}) collective-permute-start(bf16[384,256]{1,0:T(8,128)(2,1)S(1)} %fusion.12), channel_id=1, source_target_pairs={{0,8},{8,0},{16,24},{24,16},{1,9},{9,1},{17,25},{25,17},{2,10},{10... | collective-permute-start | bytes 589832 | tf_op jit(solution)/shard_map/ppermute | solution.py:383
  112.0 23.3 %copy-start.2 = (bf16[384,128]{1,0:T(8,128)(2,1)}, bf16[384,128]{1,0:T(8,128)(2,1)S(1)}, u32[]{:S(2)}) copy-start(bf16[384,128]{1,0:T(8,128)(2,1)S(1)} %get-tuple-element.59.refs_9_) | copy-start | bytes 294916
  112.0 23.3 %copy-start.3 = (bf16[384,128]{1,0:T(8,128)(2,1)}, bf16[384,128]{1,0:T(8,128)(2,1)S(1)}, u32[]{:S(2)}) copy-start(bf16[384,128]{1,0:T(8,128)(2,1)S(1)} %get-tuple-element.60.refs_8_) | copy-start | bytes 294916
  112.0 11.1 %collective-permute-start.17 = (bf16[384,128]{1,0:T(8,128)(2,1)S(1)}, bf16[384,128]{1,0:T(8,128)(2,1)S(1)}, u32[]{:S(2)}, u32[]{:S(2)}) collective-permute-start(bf16[384,128]{1,0:T(8,128)(2,1)S(1)} %get-tuple-element.59.refs_9_), channel_id=1, source_target_pairs={{0,16},{8,24},{16,0},{24,8},{1,17},{9,25},{17,1},{25,9},{2,18},{10... | collective-permute-start | bytes 294920 | tf_op jit(solution)/shard_map/ppermute | solution.py:383
  113.5 9.9 %collective-permute-start.15 = (bf16[384,128]{1,0:T(8,128)(2,1)S(1)}, bf16[384,128]{1,0:T(8,128)(2,1)S(1)}, u32[]{:S(2)}, u32[]{:S(2)}) collective-permute-start(bf16[384,128]{1,0:T(8,128)(2,1)S(1)} %get-tuple-element.59.refs_9_), channel_id=1, source_target_pairs={{0,8},{8,0},{16,24},{24,16},{1,9},{9,1},{17,25},{25,17},{2,10},{10... | collective-permute-start | bytes 294920 | tf_op jit(solution)/shard_map/ppermute | solution.py:383
  115.3 41.2 %copy-start = (bf16[384,128]{1,0:T(8,128)(2,1)}, bf16[384,128]{1,0:T(8,128)(2,1)S(1)}, u32[]{:S(2)}) copy-start(bf16[384,128]{1,0:T(8,128)(2,1)S(1)} %get-tuple-element.57.refs_1_) | copy-start | bytes 294916
  115.3 41.2 %copy-start.1 = (bf16[384,128]{1,0:T(8,128)(2,1)}, bf16[384,128]{1,0:T(8,128)(2,1)S(1)}, u32[]{:S(2)}) copy-start(bf16[384,128]{1,0:T(8,128)(2,1)S(1)} %get-tuple-element.58.refs_0_) | copy-start | bytes 294916
  115.3 5.2 %collective-permute-start.27 = (bf16[384,128]{1,0:T(8,128)(2,1)S(1)}, bf16[384,128]{1,0:T(8,128)(2,1)S(1)}, u32[]{:S(2)}, u32[]{:S(2)}) collective-permute-start(bf16[384,128]{1,0:T(8,128)(2,1)S(1)} %get-tuple-element.57.refs_1_), channel_id=1, source_target_pairs={{0,16},{8,24},{16,0},{24,8},{1,17},{9,25},{17,1},{25,9},{2,18},{10... | collective-permute-start | bytes 294920 | tf_op jit(solution)/shard_map/ppermute | solution.py:383
  115.9 5.7 %collective-permute-start.24 = (bf16[384,128]{1,0:T(8,128)(2,1)S(1)}, bf16[384,128]{1,0:T(8,128)(2,1)S(1)}, u32[]{:S(2)}, u32[]{:S(2)}) collective-permute-start(bf16[384,128]{1,0:T(8,128)(2,1)S(1)} %get-tuple-element.58.refs_0_), channel_id=1, source_target_pairs={{0,8},{8,0},{16,24},{24,16},{1,9},{9,1},{17,25},{25,17},{2,10},{10... | collective-permute-start | bytes 294920 | tf_op jit(solution)/shard_map/ppermute | solution.py:383
  117.1 8.1 %collective-permute-start.16 = (bf16[384,128]{1,0:T(8,128)(2,1)S(1)}, bf16[384,128]{1,0:T(8,128)(2,1)S(1)}, u32[]{:S(2)}, u32[]{:S(2)}) collective-permute-start(bf16[384,128]{1,0:T(8,128)(2,1)S(1)} %get-tuple-element.60.refs_8_), channel_id=1, source_target_pairs={{0,16},{8,24},{16,0},{24,8},{1,17},{9,25},{17,1},{25,9},{2,18},{10... | collective-permute-start | bytes 294920 | tf_op jit(solution)/shard_map/ppermute | solution.py:383
  118.6 16.7 %copy-start.4 = (bf16[384,128]{1,0:T(8,128)(2,1)}, bf16[384,128]{1,0:T(8,128)(2,1)S(1)}, u32[]{:S(2)}) copy-start(bf16[384,128]{1,0:T(8,128)(2,1)S(1)} %get-tuple-element.61.refs_1_) | copy-start | bytes 294916
  118.6 16.7 %copy-start.5 = (bf16[384,128]{1,0:T(8,128)(2,1)}, bf16[384,128]{1,0:T(8,128)(2,1)S(1)}, u32[]{:S(2)}) copy-start(bf16[384,128]{1,0:T(8,128)(2,1)S(1)} %get-tuple-element.62.refs_0_) | copy-start | bytes 294916
  120.5 36.0 %copy-start.18 = (bf16[384,128]{1,0:T(8,128)(2,1)}, bf16[384,128]{1,0:T(8,128)(2,1)S(1)}, u32[]{:S(2)}) copy-start(bf16[384,128]{1,0:T(8,128)(2,1)S(1)} %collective-permute-done.27.refs_5_) | copy-start | bytes 294916
  120.5 5.5 %collective-permute-start.14 = (bf16[384,128]{1,0:T(8,128)(2,1)S(1)}, bf16[384,128]{1,0:T(8,128)(2,1)S(1)}, u32[]{:S(2)}, u32[]{:S(2)}) collective-permute-start(bf16[384,128]{1,0:T(8,128)(2,1)S(1)} %get-tuple-element.60.refs_8_), channel_id=1, source_target_pairs={{0,8},{8,0},{16,24},{24,16},{1,9},{9,1},{17,25},{25,17},{2,10},{10... | collective-permute-start | bytes 294920 | tf_op jit(solution)/shard_map/ppermute | solution.py:383
  121.6 35.0 %copy-start.20 = (bf16[384,128]{1,0:T(8,128)(2,1)}, bf16[384,128]{1,0:T(8,128)(2,1)S(1)}, u32[]{:S(2)}) copy-start(bf16[384,128]{1,0:T(8,128)(2,1)S(1)} %collective-permute-done.24.refs_2_) | copy-start | bytes 294916
  121.6 5.6 %collective-permute-start.7 = (bf16[384,128]{1,0:T(8,128)(2,1)S(1)}, bf16[384,128]{1,0:T(8,128)(2,1)S(1)}, u32[]{:S(2)}, u32[]{:S(2)}) collective-permute-start(bf16[384,128]{1,0:T(8,128)(2,1)S(1)} %get-tuple-element.61.refs_1_), channel_id=1, source_target_pairs={{0,16},{8,24},{16,0},{24,8},{1,17},{9,25},{17,1},{25,9},{2,18},{10... | collective-permute-start | bytes 294920 | tf_op jit(solution)/shard_map/ppermute | solution.py:383
  123.1 12.2 %copy-start.19 = (bf16[384,128]{1,0:T(8,128)(2,1)}, bf16[384,128]{1,0:T(8,128)(2,1)S(1)}, u32[]{:S(2)}) copy-start(bf16[384,128]{1,0:T(8,128)(2,1)S(1)} %collective-permute-done.17.refs_13_) | copy-start | bytes 294916
  123.1 5.7 %collective-permute-start.5 = (bf16[384,128]{1,0:T(8,128)(2,1)S(1)}, bf16[384,128]{1,0:T(8,128)(2,1)S(1)}, u32[]{:S(2)}, u32[]{:S(2)}) collective-permute-start(bf16[384,128]{1,0:T(8,128)(2,1)S(1)} %get-tuple-element.61.refs_1_), channel_id=1, source_target_pairs={{0,8},{8,0},{16,24},{24,16},{1,9},{9,1},{17,25},{25,17},{2,10},{10... | collective-permute-start | bytes 294920 | tf_op jit(solution)/shard_map/ppermute | solution.py:383
  123.3 12.0 %copy-start.21 = (bf16[384,128]{1,0:T(8,128)(2,1)}, bf16[384,128]{1,0:T(8,128)(2,1)S(1)}, u32[]{:S(2)}) copy-start(bf16[384,128]{1,0:T(8,128)(2,1)S(1)} %collective-permute-done.15.refs_11_) | copy-start | bytes 294916
  123.3 7.1 %collective-permute-start.4 = (bf16[384,128]{1,0:T(8,128)(2,1)S(1)}, bf16[384,128]{1,0:T(8,128)(2,1)S(1)}, u32[]{:S(2)}, u32[]{:S(2)}) collective-permute-start(bf16[384,128]{1,0:T(8,128)(2,1)S(1)} %get-tuple-element.62.refs_0_), channel_id=1, source_target_pairs={{0,8},{8,0},{16,24},{24,16},{1,9},{9,1},{17,25},{25,17},{2,10},{10... | collective-permute-start | bytes 294920 | tf_op jit(solution)/shard_map/ppermute | solution.py:383
  125.2 10.2 %copy-start.22 = (bf16[384,128]{1,0:T(8,128)(2,1)}, bf16[384,128]{1,0:T(8,128)(2,1)S(1)}, u32[]{:S(2)}) copy-start(bf16[384,128]{1,0:T(8,128)(2,1)S(1)} %collective-permute-done.16.refs_12_) | copy-start | bytes 294916
  125.2 6.0 %collective-permute-start.6 = (bf16[384,128]{1,0:T(8,128)(2,1)S(1)}, bf16[384,128]{1,0:T(8,128)(2,1)S(1)}, u32[]{:S(2)}, u32[]{:S(2)}) collective-permute-start(bf16[384,128]{1,0:T(8,128)(2,1)S(1)} %get-tuple-element.62.refs_0_), channel_id=1, source_target_pairs={{0,16},{8,24},{16,0},{24,8},{1,17},{9,25},{17,1},{25,9},{2,18},{10... | collective-permute-start | bytes 294920 | tf_op jit(solution)/shard_map/ppermute | solution.py:383
  126.0 9.3 %copy-start.23 = (bf16[384,128]{1,0:T(8,128)(2,1)}, bf16[384,128]{1,0:T(8,128)(2,1)S(1)}, u32[]{:S(2)}) copy-start(bf16[384,128]{1,0:T(8,128)(2,1)S(1)} %collective-permute-done.14.refs_10_) | copy-start | bytes 294916
  126.0 6.2 %collective-permute-start.19 = (bf16[384,128]{1,0:T(8,128)(2,1)S(1)}, bf16[384,128]{1,0:T(8,128)(2,1)S(1)}, u32[]{:S(2)}, u32[]{:S(2)}) collective-permute-start(bf16[384,128]{1,0:T(8,128)(2,1)S(1)} %collective-permute-done.17.refs_13_), channel_id=1, source_target_pairs={{0,8},{8,0},{16,24},{24,16},{1,9},{9,1},{17,25},{25,17},{2,10},{10... | collective-permute-start | bytes 294920 | tf_op jit(solution)/shard_map/ppermute | solution.py:383
  127.2 8.2 %copy-start.24 = (bf16[384,128]{1,0:T(8,128)(2,1)}, bf16[384,128]{1,0:T(8,128)(2,1)S(1)}, u32[]{:S(2)}) copy-start(bf16[384,128]{1,0:T(8,128)(2,1)S(1)} %collective-permute-done.7.refs_5_) | copy-start | bytes 294916
  127.2 6.0 %collective-permute-start.18 = (bf16[384,128]{1,0:T(8,128)(2,1)S(1)}, bf16[384,128]{1,0:T(8,128)(2,1)S(1)}, u32[]{:S(2)}, u32[]{:S(2)}) collective-permute-start(bf16[384,128]{1,0:T(8,128)(2,1)S(1)} %collective-permute-done.14.refs_10_), channel_id=1, source_target_pairs={{0,16},{8,24},{16,0},{24,8},{1,17},{9,25},{17,1},{25,9},{2,18},{10... | collective-permute-start | bytes 294920 | tf_op jit(solution)/shard_map/ppermute | solution.py:383
  128.9 6.5 %copy-start.25 = (bf16[384,128]{1,0:T(8,128)(2,1)}, bf16[384,128]{1,0:T(8,128)(2,1)S(1)}, u32[]{:S(2)}) copy-start(bf16[384,128]{1,0:T(8,128)(2,1)S(1)} %collective-permute-done.5.refs_3_) | copy-start | bytes 294916
  128.9 5.6 %collective-permute-start.9 = (bf16[384,128]{1,0:T(8,128)(2,1)S(1)}, bf16[384,128]{1,0:T(8,128)(2,1)S(1)}, u32[]{:S(2)}, u32[]{:S(2)}) collective-permute-start(bf16[384,128]{1,0:T(8,128)(2,1)S(1)} %collective-permute-done.7.refs_5_), channel_id=1, source_target_pairs={{0,8},{8,0},{16,24},{24,16},{1,9},{9,1},{17,25},{25,17},{2,10},{10... | collective-permute-start | bytes 294920 | tf_op jit(solution)/shard_map/ppermute | solution.py:383
  130.4 4.9 %copy-start.26 = (bf16[384,128]{1,0:T(8,128)(2,1)}, bf16[384,128]{1,0:T(8,128)(2,1)S(1)}, u32[]{:S(2)}) copy-start(bf16[384,128]{1,0:T(8,128)(2,1)S(1)} %collective-permute-done.4.refs_2_) | copy-start | bytes 294916
  130.4 4.8 %collective-permute-start.8 = (bf16[384,128]{1,0:T(8,128)(2,1)S(1)}, bf16[384,128]{1,0:T(8,128)(2,1)S(1)}, u32[]{:S(2)}, u32[]{:S(2)}) collective-permute-start(bf16[384,128]{1,0:T(8,128)(2,1)S(1)} %collective-permute-done.4.refs_2_), channel_id=1, source_target_pairs={{0,16},{8,24},{16,0},{24,8},{1,17},{9,25},{17,1},{25,9},{2,18},{10... | collective-permute-start | bytes 294920 | tf_op jit(solution)/shard_map/ppermute | solution.py:383
  131.2 4.2 %copy-start.27 = (bf16[384,128]{1,0:T(8,128)(2,1)}, bf16[384,128]{1,0:T(8,128)(2,1)S(1)}, u32[]{:S(2)}) copy-start(bf16[384,128]{1,0:T(8,128)(2,1)S(1)} %collective-permute-done.6.refs_4_) | copy-start | bytes 294916
  131.2 25.3 %collective-permute-start.25 = (bf16[384,128]{1,0:T(8,128)(2,1)S(1)}, bf16[384,128]{1,0:T(8,128)(2,1)S(1)}, u32[]{:S(2)}, u32[]{:S(2)}) collective-permute-start(bf16[384,128]{1,0:T(8,128)(2,1)S(1)} %get-tuple-element.57.refs_1_), channel_id=1, source_target_pairs={{0,8},{8,0},{16,24},{24,16},{1,9},{9,1},{17,25},{25,17},{2,10},{10... | collective-permute-start | bytes 294920 | tf_op jit(solution)/shard_map/ppermute | solution.py:383
  132.3 3.1 %copy-start.28 = (bf16[384,128]{1,0:T(8,128)(2,1)}, bf16[384,128]{1,0:T(8,128)(2,1)S(1)}, u32[]{:S(2)}) copy-start(bf16[384,128]{1,0:T(8,128)(2,1)S(1)} %collective-permute-done.19.refs_15_) | copy-start | bytes 294916
  132.3 24.3 %collective-permute-start.26 = (bf16[384,128]{1,0:T(8,128)(2,1)S(1)}, bf16[384,128]{1,0:T(8,128)(2,1)S(1)}, u32[]{:S(2)}, u32[]{:S(2)}) collective-permute-start(bf16[384,128]{1,0:T(8,128)(2,1)S(1)} %get-tuple-element.58.refs_0_), channel_id=1, source_target_pairs={{0,16},{8,24},{16,0},{24,8},{1,17},{9,25},{17,1},{25,9},{2,18},{10... | collective-permute-start | bytes 294920 | tf_op jit(solution)/shard_map/ppermute | solution.py:383
  133.2 2.2 %copy-start.30 = (bf16[384,128]{1,0:T(8,128)(2,1)}, bf16[384,128]{1,0:T(8,128)(2,1)S(1)}, u32[]{:S(2)}) copy-start(bf16[384,128]{1,0:T(8,128)(2,1)S(1)} %collective-permute-done.18.refs_14_) | copy-start | bytes 294916
  133.2 23.4 %collective-permute-start.29 = (bf16[384,128]{1,0:T(8,128)(2,1)S(1)}, bf16[384,128]{1,0:T(8,128)(2,1)S(1)}, u32[]{:S(2)}, u32[]{:S(2)}) collective-permute-start(bf16[384,128]{1,0:T(8,128)(2,1)S(1)} %collective-permute-done.27.refs_5_), channel_id=1, source_target_pairs={{0,8},{8,0},{16,24},{24,16},{1,9},{9,1},{17,25},{25,17},{2,10},{10... | collective-permute-start | bytes 294920 | tf_op jit(solution)/shard_map/ppermute | solution.py:383
  134.5 0.9 copy-start.32
  134.5 22.1 %collective-permute-start.28 = (bf16[384,128]{1,0:T(8,128)(2,1)S(1)}, bf16[384,128]{1,0:T(8,128)(2,1)S(1)}, u32[]{:S(2)}, u32[]{:S(2)}) collective-permute-start(bf16[384,128]{1,0:T(8,128)(2,1)S(1)} %collective-permute-done.24.refs_2_), channel_id=1, source_target_pairs={{0,16},{8,24},{16,0},{24,8},{1,17},{9,25},{17,1},{25,9},{2,18},{10... | collective-permute-start | bytes 294920 | tf_op jit(solution)/shard_map/ppermute | solution.py:383
  156.6 0.7 copy-start.35
  (4 other events, 2.6 us)
Sparse Core Ops, SparseCore 0:
  10.3 25.3 all-gather.2
  167.7 31.1 reduce-scatter.1

commit v2 on v0

v2 whole, which is shorter than its diff:
```python
import functools

import jax
import jax.numpy as jnp
from jax import lax
from jax.experimental import pallas as pl
from jax.experimental.pallas import tpu as pltpu
from jax.sharding import PartitionSpec as P

EXPERTS = 128
F32 = jnp.float32
BF16 = jnp.bfloat16
VMEM_LIMIT = 56 * 2**20
ALIGN = 16
META = 16


def ceil_to(value, unit):
    return -(-value // unit) * unit


def vmem():
    return pl.BlockSpec(memory_space=pltpu.VMEM)


def smem():
    return pl.BlockSpec(memory_space=pltpu.SMEM)


def hbm():
    return pl.BlockSpec(memory_space=pl.ANY)


def params():
    return pltpu.CompilerParams(vmem_limit_bytes=VMEM_LIMIT)


def cost(flops, moved):
    return pl.CostEstimate(flops=int(flops), bytes_accessed=int(moved), transcendentals=0)


def prepare_kernel(dims, ids, weights, meta):
    rows, top = dims["rows"], dims["top"]
    chance = weights[...]
    chance = (chance / jnp.sum(chance, axis=1, keepdims=True)).T
    high = chance.astype(BF16)
    rest = chance - high.astype(F32)
    middle = rest.astype(BF16)
    low = (rest - middle.astype(F32)).astype(BF16)
    meta[...] = jnp.zeros_like(meta)
    parts = (ids[...].astype(F32).T, high.astype(F32), middle.astype(F32), low.astype(F32))
    for i, part in enumerate(parts):
        block = jnp.concatenate([part, jnp.zeros((META - top, rows), F32)], axis=0)
        meta[:, i * rows : (i + 1) * rows] = block.astype(BF16)


def prepare(dims, ids, weights):
    return pl.pallas_call(
        functools.partial(prepare_kernel, dims),
        out_shape=jax.ShapeDtypeStruct((META, 4 * dims["rows"]), BF16),
        in_specs=[vmem(), vmem()],
        out_specs=vmem(),
        compiler_params=params(),
        name="prepare",
    )(ids, weights)


def loop(count, body, carry):
    if count > 8:
        return lax.fori_loop(0, count, body, carry)
    for i in range(count):
        carry = body(i, carry)
    return carry


def route(dims, base, meta, rowid, probs, rowk):
    blocks, rows, top, experts = dims["blocks"], dims["rows"], dims["top"], dims["experts"]
    expert_at = lax.broadcasted_iota(jnp.int32, (experts, rows), 0) + base
    upper = (
        lax.broadcasted_iota(jnp.int32, (rows, rows), 0)
        <= lax.broadcasted_iota(jnp.int32, (rows, rows), 1)
    ).astype(BF16)

    def chosen_ids(block):
        return meta[block, :, :rows].astype(F32)[:top].astype(jnp.int32)

    def count(block, seen):
        held = meta[block].astype(F32)[:top]
        ids = held[:, :rows].astype(jnp.int32)
        chance = held[:, rows : 2 * rows] + held[:, 2 * rows : 3 * rows]
        chance = chance + held[:, 3 * rows : 4 * rows]
        member = jnp.zeros((experts, rows), F32)
        share = jnp.zeros((experts, rows), F32)
        for k in range(top):
            hit = ids[k : k + 1, :] == expert_at
            member = member + hit.astype(F32)
            share = share + jnp.where(hit, chance[k : k + 1, :], 0.0)
        upto = jnp.dot(member.astype(BF16), upper, preferred_element_type=F32)
        rowid[block] = jnp.where(member > 0, seen + upto - 1.0, -1e6).astype(jnp.int32)
        probs[block] = share
        return seen + upto[:, rows - 1 : rows]

    total = loop(blocks, count, jnp.zeros((experts, rows), F32))
    starts, before = [], jnp.zeros((1, rows), F32)
    for e in range(experts):
        starts.append(before)
        before = before + total[e : e + 1, :]
    start = jnp.concatenate(starts, axis=0) if experts > 1 else starts[0]
    start, total = start.astype(jnp.int32), total.astype(jnp.int32)

    def place(block, carry):
        ids = chosen_ids(block)
        at = rowid[block] + start
        rowid[block] = at
        found = []
        for k in range(top):
            hit = ids[k : k + 1, :] == expert_at
            found.append(jnp.max(jnp.where(hit, at, -1), axis=0, keepdims=True))
        rowk[block] = jnp.concatenate(found, axis=0)
        return carry

    loop(blocks, place, 0)
    return start, total


def window_hits(dims, rowid, block, e, start):
    at = lax.broadcasted_iota(jnp.int32, (dims["window"], dims["rows"]), 0) + start
    return rowid[block, e : e + 1, :] == at


def aligned(value):
    return pl.multiple_of(value // ALIGN * ALIGN, ALIGN)


def fill_select(dims, rowid, starts, select, step):
    rows = dims["rows"]
    select[...] = jnp.zeros_like(select)
    for e in range(dims["experts"]):
        first = aligned(starts[e])
        at = pl.ds(first, dims["window"])
        for inner in range(dims["group"]):
            cols = slice(inner * rows, (inner + 1) * rows)
            hit = window_hits(dims, rowid, step * dims["group"] + inner, e, first)
            select[at, cols] = select[at, cols] + hit.astype(F32).astype(BF16)


def publish(dims, offs, start, total):
    starts = [start[e, 0] for e in range(dims["experts"])]
    for e in range(dims["experts"]):
        offs[0, e] = starts[e]
        offs[1, e] = total[e, 0]
    return starts


def route_kernel(dims, me_ref, meta, rowid, probs, rowk, select, offs):
    start, total = route(dims, me_ref[1] * dims["experts"], meta, rowid, probs, rowk)
    fill_select(dims, rowid, publish(dims, offs, start, total), select, 0)


def dispatch_kernel(dims, me_ref, meta, gathered, rowid, probs, rowk, x, offs, select, total):
    blocks, rows, group, tile = dims["blocks"], dims["rows"], dims["group"], dims["tile"]
    start, count = route(dims, me_ref[1] * dims["experts"], meta, rowid, probs, rowk)
    starts = publish(dims, offs, start, count)
    total[...] = jnp.zeros_like(total)

    def body(step, carry):
        fill_select(dims, rowid, starts, select, step)
        part = gathered[pl.ds(step * group, group)].reshape(group * rows, x.shape[1])
        for r in range(0, x.shape[0], tile):
            size = min(tile, x.shape[0] - r)
            got = jnp.dot(select[r : r + size, :], part, preferred_element_type=F32)
            got = got + total[r : r + size, :]
            total[r : r + size, :] = got
            x[r : r + size, :] = got.astype(BF16)
        return carry

    lax.fori_loop(0, blocks // group, body, 0)


def route_shapes(dims):
    blocks, rows, top, experts = dims["blocks"], dims["rows"], dims["top"], dims["experts"]
    return (
        jax.ShapeDtypeStruct((blocks, experts, rows), jnp.int32),
        jax.ShapeDtypeStruct((blocks, experts, rows), F32),
        jax.ShapeDtypeStruct((blocks, top, rows), jnp.int32),
    ), jax.ShapeDtypeStruct((2, experts), jnp.int32)


def route_rows(dims, me, meta):
    shapes, offs = route_shapes(dims)
    select = jax.ShapeDtypeStruct((dims["padded"], dims["blocks"] * dims["rows"]), BF16)
    return pl.pallas_call(
        functools.partial(route_kernel, dims),
        out_shape=shapes + (select, offs),
        in_specs=[smem(), vmem()],
        out_specs=(vmem(),) * 4 + (smem(),),
        compiler_params=params(),
        cost_estimate=cost(4e9, 4e6),
        name="route",
    )(me, meta)


def dispatch(dims, me, meta, gathered):
    shapes, offs = route_shapes(dims)
    width, padded = gathered.shape[2], dims["padded"]
    return pl.pallas_call(
        functools.partial(dispatch_kernel, dims),
        out_shape=shapes + (jax.ShapeDtypeStruct((padded, width), BF16), offs),
        in_specs=[smem(), vmem(), vmem()],
        out_specs=(vmem(),) * 4 + (smem(),),
        scratch_shapes=[
            pltpu.VMEM((padded, dims["group"] * dims["rows"]), BF16),
            pltpu.VMEM((padded, width), F32),
        ],
        compiler_params=params(),
        name="dispatch",
    )(me, meta, gathered)


def choose(dims, rowk, block):
    at = lax.broadcasted_iota(jnp.int32, (dims["rows"], dims["total"]), 1)
    rows_of = rowk[block].astype(F32).T.astype(jnp.int32)
    hit = rows_of[:, 0:1] == at
    for k in range(1, dims["top"]):
        hit = hit | (rows_of[:, k : k + 1] == at)
    return hit.astype(F32).astype(BF16)


def weigh_kernel(dims, offs, rowid, probs, rowk, scale, chosen):
    if dims["small"]:
        def pick(block, carry):
            chosen[block] = choose(dims, rowk, block)
            return carry

        lax.fori_loop(0, dims["blocks"], pick, 0)
    else:
        chosen[...] = jnp.zeros_like(chosen)
    for e in range(dims["experts"]):
        first = aligned(offs[0, e])
        at = pl.ds(first, dims["window"])

        def share(block, carry):
            hit = window_hits(dims, rowid, block, e, first)
            return carry + jnp.where(hit, probs[block, e : e + 1, :], 0.0)

        shares = loop(dims["blocks"], share, jnp.zeros((dims["window"], dims["rows"]), F32))
        wide = jnp.sum(shares, axis=1, keepdims=True)
        wide = jnp.broadcast_to(wide, (dims["window"], scale.shape[1]))
        scale[at, :] = jnp.where(row_mask(dims, first, offs, e), wide, scale[at, :])


def weigh(dims, offs, rowid, probs, rowk):
    picked = (dims["blocks"], dims["rows"], dims["total"]) if dims["small"] else (1, ALIGN, 128)
    return pl.pallas_call(
        functools.partial(weigh_kernel, dims),
        out_shape=(
            jax.ShapeDtypeStruct((dims["padded"], 128), F32),
            jax.ShapeDtypeStruct(picked, BF16),
        ),
        in_specs=[smem(), vmem(), vmem(), vmem()],
        out_specs=(vmem(), vmem()),
        compiler_params=params(),
        cost_estimate=cost(6e9, 8e6),
        name="weigh",
    )(offs, rowid, probs, rowk)


def row_mask(dims, first, offs, e):
    at = lax.broadcasted_iota(jnp.int32, (dims["window"], 1), 0) + first
    begin = offs[0, e]
    return (at >= begin) & (at < begin + offs[1, e])


def batches(experts):
    return [range(b, min(b + 4, experts)) for b in range(0, experts, 4)]


def gate_up_kernel(dims, c, first_part, me_ref, offs, *refs):
    experts, window, part, quarter = dims["experts"], dims["window"], dims["part"], dims["quarter"]
    if first_part:
        blocks, rows = dims["blocks"], dims["rows"]
        select, tokens, refs = refs[0], refs[1 : 1 + blocks], refs[1 + blocks :]
        w_gate, w_up, x, gx, uy, g2, u1, g0, u0, gate_w, up_w, gate, up, sems, table = refs
    else:
        x, w_gate, w_up, gx, uy, g2, u1, g0, u0, gate_w, up_w, gate, up, sems = refs
    units = pl.ds(c * part, part)

    def copies(e):
        return (
            pltpu.make_async_copy(w_gate.at[e, units, :], gate_w.at[e], sems.at[0, e]),
            pltpu.make_async_copy(w_up.at[e, units, :], up_w.at[e], sems.at[1, e]),
        )

    for e in range(experts):
        for copy in copies(e):
            copy.start()
    if first_part:
        for j, held in enumerate(tokens):
            table[pl.ds(pl.multiple_of((me_ref[1] ^ j) * rows, rows), rows), :] = held[...]
        for r in range(0, x.shape[0], dims["tile"]):
            size = min(dims["tile"], x.shape[0] - r)
            got = jnp.dot(select[r : r + size, :], table[...], preferred_element_type=F32)
            x[r : r + size, :] = got.astype(BF16)
    contract = (((1,), (1,)), ((), ()))
    for batch in batches(experts):
        for e in batch:
            for copy in copies(e):
                copy.wait()
        for e in batch:
            first = aligned(offs[0, e])
            rows_in = x[pl.ds(first, window), :]
            keep = (lax.broadcasted_iota(jnp.int32, (ALIGN, 1), 0) + first) >= offs[0, e]
            edge, rest = pl.ds(first, ALIGN), pl.ds(first + ALIGN, window - ALIGN)
            for held, into in ((gate_w, gate), (up_w, up)):
                got = lax.dot_general(rows_in, held[e], contract, preferred_element_type=F32)
                into[edge, :] = jnp.where(keep, got[:ALIGN], into[edge, :])
                into[rest, :] = got[ALIGN:]
    me = me_ref[0]

    def piece(total, j):
        return total[pl.ds(pl.multiple_of((me ^ j) * quarter, ALIGN), quarter), :]

    gx[0] = piece(gate, 1).astype(BF16)
    gx[1] = piece(gate, 3).astype(BF16)
    uy[0] = piece(up, 2).astype(BF16)
    uy[1] = piece(up, 3).astype(BF16)
    g2[...] = piece(gate, 2)
    u1[...] = piece(up, 1)
    g0[...] = piece(gate, 0)
    u0[...] = piece(up, 0)


def gate_up(dims, c, me, offs, rows_of, w_gate, w_up):
    experts, part, quarter, padded = dims["experts"], dims["part"], dims["quarter"], dims["padded"]
    width = w_gate.shape[2]
    half = jax.ShapeDtypeStruct((2, quarter, part), BF16)
    own = jax.ShapeDtypeStruct((quarter, part), F32)
    first_part = len(rows_of) > 1
    outs = (half, half, own, own, own, own)
    scratch = [
        pltpu.VMEM((experts, part, width), BF16),
        pltpu.VMEM((experts, part, width), BF16),
        pltpu.VMEM((padded, part), F32),
        pltpu.VMEM((padded, part), F32),
        pltpu.SemaphoreType.DMA((2, experts)),
    ]
    if first_part:
        outs = (jax.ShapeDtypeStruct((padded, width), BF16),) + outs
        scratch.append(pltpu.VMEM((dims["blocks"] * dims["rows"], width), BF16))
    return pl.pallas_call(
        functools.partial(gate_up_kernel, dims, c, first_part),
        out_shape=outs,
        in_specs=[smem(), smem()] + [vmem()] * len(rows_of) + [hbm(), hbm()],
        out_specs=(vmem(),) * len(outs),
        scratch_shapes=scratch,
        compiler_params=params(),
        cost_estimate=cost(4 * padded * width * part, 4 * experts * part * width + 2 * padded * width),
        name="gate_up",
    )(me, offs, *rows_of, w_gate, w_up)


def gather_hidden(dims, me, pieces, hidden):
    quarter, half = dims["quarter"], dims["part"] // 2
    for j in range(4):
        at = pl.ds(pl.multiple_of((me ^ j) * quarter, ALIGN), quarter)
        for side in range(2):
            hidden[at, side * half : (side + 1) * half] = pieces[2 * j + side][...]


def down_kernel(dims, c, last, me_ref, offs, w_down, *refs):
    experts, window, part = dims["experts"], dims["window"], dims["part"]
    pieces, refs = refs[:8], refs[8:]
    y_in = None
    if c > 0:
        y_in, refs = refs[0], refs[1:]
    if last:
        scale, chosen, rowk, refs = refs[0], refs[1], refs[2], refs[3:]
        if dims["small"]:
            stay, away, held, hidden, sems, y_out = refs
        else:
            out, held, hidden, sems, y_out = refs
        y_out[...] = jnp.zeros_like(y_out)
    else:
        y_out, held, hidden, sems = refs
    units = pl.ds(c * part, part)

    def copy(e):
        return pltpu.make_async_copy(w_down.at[e, units, :], held.at[e], sems.at[e])

    for e in range(experts):
        copy(e).start()
    gather_hidden(dims, me_ref[0], pieces, hidden)
    for batch in batches(experts):
        for e in batch:
            copy(e).wait()
        for e in batch:
            first = aligned(offs[0, e])
            at = pl.ds(first, window)
            got = jnp.dot(hidden[at, :], held[e], preferred_element_type=F32)
            if y_in is not None:
                got = got + y_in[at, :]
            mask = row_mask(dims, first, offs, e)
            if last:
                got = got * scale[at, 0:1]
                y_out[at, :] = jnp.where(mask, got, y_out[at, :].astype(F32)).astype(BF16)
            else:
                y_out[at, :] = jnp.where(mask, got, y_out[at, :])
    if not last:
        return
    rows, total, width = dims["rows"], dims["total"], w_down.shape[2]
    blocks, many = dims["blocks"], min(4, dims["blocks"])
    if dims["small"]:
        order = halving_order(blocks)
        for side, into in enumerate((stay, away)):
            for p in range(0, blocks // 2, many):
                at = [me_ref[1] ^ order[side * (blocks // 2) + p + i] for i in range(many)]
                picked = jnp.concatenate([chosen[i] for i in at], axis=0)
                summed = jnp.dot(picked, y_out[:total, :], preferred_element_type=F32)
                into[p : p + many] = summed.astype(BF16).reshape(many, rows, width)
        return

    def combine(step, carry):
        picked = [choose(dims, rowk, step * many + i) for i in range(many)]
        summed = jnp.dot(
            jnp.concatenate(picked, axis=0), y_out[:total, :], preferred_element_type=F32
        )
        out[pl.ds(step * many, many)] = summed.astype(BF16).reshape(many, rows, width)
        return carry

    lax.fori_loop(0, blocks // many, combine, 0)


def halving_order(blocks):
    bits = blocks.bit_length() - 1
    return [sum(((i >> b) & 1) << (bits - 1 - b) for b in range(bits)) for i in range(blocks)]


def down(dims, c, last, me, offs, w_down, pieces, y, extra):
    experts, padded, part = dims["experts"], dims["padded"], dims["part"]
    width = w_down.shape[2]
    operands = list(pieces) + ([y] if c > 0 else []) + list(extra)
    blocks, rows = dims["blocks"], dims["rows"]
    scratch = [
        pltpu.VMEM((experts, part, width), BF16),
        pltpu.VMEM((padded, part), BF16),
        pltpu.SemaphoreType.DMA((experts,)),
    ]
    if not last:
        outs = (jax.ShapeDtypeStruct((padded, width), F32),)
    else:
        scratch.append(pltpu.VMEM((padded, width), BF16))
        if dims["small"]:
            outs = (jax.ShapeDtypeStruct((blocks // 2, rows, width), BF16),) * 2
        else:
            outs = (jax.ShapeDtypeStruct((blocks, rows, width), BF16),)
    return pl.pallas_call(
        functools.partial(down_kernel, dims, c, last),
        out_shape=outs,
        in_specs=[smem(), smem(), hbm()] + [vmem()] * len(operands),
        out_specs=(vmem(),) * len(outs),
        scratch_shapes=scratch,
        compiler_params=params(),
        cost_estimate=cost(4 * padded * width * part, 2 * experts * part * width + 8 * padded * width),
        name="down",
    )(me, offs, w_down, *operands)


def swap(value, axis, bit):
    count = lax.axis_size(axis)
    return lax.ppermute(value, axis, [(i, i ^ bit) for i in range(count)])


def reduce_chunk(parts):
    gx, uy, g2, u1, g0, u0 = parts
    from_x = swap(gx, "rep", 1)
    from_y = swap(uy, "rep", 2)
    gate_rest = swap((g2 + from_x[1].astype(F32)).astype(BF16), "rep", 2)
    up_rest = swap((u1 + from_y[1].astype(F32)).astype(BF16), "rep", 1)
    gate = g0 + from_x[0].astype(F32) + gate_rest.astype(F32)
    up = u0 + from_y[0].astype(F32) + up_rest.astype(F32)
    hidden = (jax.nn.silu(gate) * up).astype(BF16)
    half = hidden.shape[1] // 2
    return hidden[:, :half], hidden[:, half:]


def spread_chunk(left, right):
    x = (swap(left, "rep", 1), swap(right, "rep", 1))
    y = (swap(left, "rep", 2), swap(right, "rep", 2))
    corner = (swap(x[0], "rep", 2), swap(y[1], "rep", 1))
    return [left, right, *x, *y, *corner]


def gather_tokens(tokens):
    held = {0: tokens}
    bit = lax.axis_size("exp") // 2
    while bit:
        for known in list(held):
            held[known | bit] = swap(held[known], "exp", bit)
        bit //= 2
    return [held[j] for j in range(len(held))]


def sum_over_exp(stay, away):
    bit = 1
    while True:
        came = swap(away, "exp", bit)
        total = stay.astype(F32) + came.astype(F32)
        count = total.shape[0] // 2
        if count == 0:
            return total[0].astype(BF16)
        stay, away = total[:count], total[count:].astype(BF16)
        bit *= 2


def local(tokens, expert_ids, route_weights, w_gate, w_up, w_down):
    rows, top = expert_ids.shape
    width = tokens.shape[1]
    experts, units, _ = w_gate.shape
    blocks = lax.axis_size("exp")
    replicas = lax.axis_size("rep")
    cap = replicas * max(1, rows * top * 3 // (8 * EXPERTS))
    total = ceil_to(experts * blocks * cap, replicas * 128)
    window = ceil_to(blocks * cap, ALIGN) + ALIGN
    part = 256
    small = blocks * rows * total <= 4 * 2**20
    dims = dict(
        blocks=blocks,
        rows=rows,
        top=top,
        experts=experts,
        window=window,
        total=total,
        quarter=total // replicas,
        padded=total + window,
        part=part,
        group=min(blocks, 8),
        tile=512,
        small=small,
    )
    me = jnp.stack([lax.axis_index("rep"), lax.axis_index("exp")]).astype(jnp.int32)
    meta = lax.all_gather(prepare(dims, expert_ids, route_weights), "exp", axis=0)
    if small:
        held = gather_tokens(tokens)
        rowid, probs, rowk, select, offs = route_rows(dims, me, meta)
        sources = [select, *held]
    else:
        gathered = lax.all_gather(tokens, "exp", axis=0)
        rowid, probs, rowk, x, offs = dispatch(dims, me, meta, gathered)
        sources = [x]
    scale, chosen = weigh(dims, offs, rowid, probs, rowk)

    pieces = []
    for c in range(units // part):
        parts = gate_up(dims, c, me, offs, sources, w_gate, w_up)
        if len(sources) > 1:
            sources, parts = [parts[0]], parts[1:]
        pieces.append(spread_chunk(*reduce_chunk(parts)))
    y = None
    last = len(pieces) - 1
    for c in range(last):
        y = down(dims, c, False, me, offs, w_down, pieces[c], y, ())[0]
    mixed = down(dims, last, True, me, offs, w_down, pieces[last], y, (scale, chosen, rowk))
    if small:
        return sum_over_exp(*mixed)
    return lax.psum_scatter(mixed[0], "exp", scatter_dimension=0, tiled=False)


def solution(mesh):
    return jax.shard_map(
        local,
        mesh=mesh,
        in_specs=(
            P("exp", "rep"),
            P("exp", None),
            P("exp", None),
            P("exp", None, "rep"),
            P("exp", None, "rep"),
            P("exp", None, "rep"),
        ),
        out_specs=P("exp", "rep"),
        check_vma=False,
    )
```

time: 1440 us -> 164 us (0.11)
  waiting for transfers between devices: 1250 us -> 31.5 us
  blocking collectives: 87.8 us -> 16.1 us
  Pallas kernels: 0 us -> 65.2 us
  matrix products: 62.7 us -> 0 us
  starting transfers between devices: 4.82 us -> 41.2 us
  local copies, waits for them, and re-layouts: 22.3 us -> 5.1 us
    all_gather x3 -> x0, waiting for transfers between devices: 1210 us -> none  [the longest x1 439 us: local(): lax.all_gather(w_down, 'rep', axis=2, tiled=True)]
    all_to_all x2 -> x0, blocking collectives: 76.3 us -> none  [the longest x1 53.8 us: local(): lax.all_to_all(outgoing, 'exp', split_axis=0, concat_axis=1, tiled=True)]
    pallas_call x0 -> x9, Pallas kernels: none -> 65.2 us  [the longest x3 25.4 us: gate_up(): pl.pallas_call(functools.partial(gate_up_kernel, dims, c, first_part), ou...]
    dot_general x2 -> x0, matrix products: 62.7 us -> none  [the longest x1 34.3 us: local(): jnp.einsum('esf,efd->esd', hidden, lax.all_gather(w_down, 'rep', axis=2,...]
    ppermute x0 -> x40, starting transfers between devices: none -> 41.2 us  [swap(): return lax.ppermute(value, axis, [(i, i ^ bit) for i in range(count)])]
    all_to_all x1 -> x0, waiting for transfers between devices: 37.7 us -> none  [local(): lax.all_to_all(lax.all_to_all(split_out, 'rep', split_axis=3, concat_axis...]
    ppermute x0 -> x40, waiting for transfers between devices: none -> 31.5 us  [swap(): return lax.ppermute(value, axis, [(i, i ^ bit) for i in range(count)])]
  transfers between devices with their start and end apart: 4 -> 40, of which waited for: 4 -> 9; matrix products, arithmetic and copies ran while one was open for 3% -> 3% of each run, Pallas kernels for 0% -> 29%
where the time goes in v2:
time: 164 us; the launch traced here: 163 us
  Pallas kernels  65.2 us (40%)
  starting transfers between devices  41.2 us (25%)
  waiting for transfers between devices  31.5 us (19%)
  blocking collectives  16.1 us (10%)
  local copies, waits for them, and re-layouts  5.1 us (3%)
  other arithmetic  3.4 us (2%)
    ppermute x40, starting transfers between devices, swap(): return lax.ppermute(value, axis, [(i, i ^ bit) for i in range(count)])  41.2 us
    ppermute x40, waiting for transfers between devices, swap(): return lax.ppermute(value, axis, [(i, i ^ bit) for i in range(count)])  31.5 us
    pallas_call x3, Pallas kernels, gate_up(): pl.pallas_call(functools.partial(gate_up_kernel, dims, c, first_part), ou...  25.4 us
    pallas_call x3, Pallas kernels, down(): pl.pallas_call(functools.partial(down_kernel, dims, c, last), out_shape=o...  21.1 us
    all_gather x1, blocking collectives, local(): lax.all_gather(prepare(dims, expert_ids, route_weights), 'exp', axis=0)  16.1 us
    pallas_call x1, Pallas kernels, weigh(): pl.pallas_call(functools.partial(weigh_kernel, dims), out_shape=(jax.Shap...  12.7 us
    unnamed x88, local copies, waits for them, and re-layouts  5 us
    pallas_call x1, Pallas kernels, route_rows(): pl.pallas_call(functools.partial(route_kernel, dims), out_shape=shapes +...  4.36 us
  transfers between devices with their start and end apart: 40, of which 9 were waited for; matrix products, arithmetic and copies ran while one was open for 3% of the time, Pallas kernels for 29%

profile of v2, /device:TPU:0, one launch (start us, length us, event | category | flops | bytes accessed | tf_op | source)
XLA Modules:
  0.0 163.3 jit_solution(16034660077605301110)
XLA Ops:
  0.0 4.0 %collective-permute-start.3 = (bf16[128,512]{1,0:T(8,128)(2,1)}, bf16[128,512]{1,0:T(8,128)(2,1)S(1)}, u32[]{:S(2)}, u32[]{:S(2)}) collective-permute-start(bf16[128,512]{1,0:T(8,128)(2,1)} %refs_1_.3), channel_id=1, source_target_pairs={{0,4},{1,5},{2,6},{3,7},{4,0},{5,1},{6,2},{7,3},{8,12},{9,13},{10,... | collective-permute-start | bytes 393224 | tf_op jit(solution)/shard_map/ppermute | solution.py:470
  4.0 1.6 collective-permute-start.1
  5.6 1.4 copy.7.ids
  7.0 1.4 copy.8.weights
  8.4 1.6 prepare.1
  10.1 0.6 collective-permute-done.3.refs_5_
  10.7 0.7 collective-permute-start.5
  11.4 16.1 %all-gather = bf16[128,512]{1,0:T(8,128)(2,1)} all-gather(bf16[16,512]{1,0:T(8,128)(2,1)} %prepare.1), channel_id=2, replica_groups=mesh['rep'=4,'exp'=8] {'exp'}, dimensions={0}, use_global_device_ids=true | all-gather | bytes 147456 | tf_op jit(solution)/shard_map/all_gather | solution.py:541
  27.5 0.6 pad_add_fusion.me_ref
  28.1 0.3 collective-permute-start.4
  28.6 0.3 collective-permute-start.6
  29.0 4.4 %route.1 = (s32[8,16,128]{2,1,0:T(8,128)}, f32[8,16,128]{2,1,0:T(8,128)}, s32[8,8,128]{2,1,0:T(8,128)}, bf16[1648,1024]{1,0:T(8,128)(2,1)}, s32[2,16]{1,0:T(2,128)}) custom-call(s32[2]{0:T(128)} %pad_add_fusion.me_ref, bf16[8,16,512]{2,1,0:T(8,128)(2,1)} %bitcast.65), custom_call_target="tpu_custom_call" | custom-call | flops 4000000000 | bytes 4000000 | tf_op jit(solution)/shard_map/route/pallas_call | solution.py:192
  33.4 0.6 copy-done.20
  34.2 9.7 %gate_up.3 = (bf16[1648,512]{1,0:T(8,128)(2,1)}, bf16[2,384,256]{2,1,0:T(8,128)(2,1)}, bf16[2,384,256]{2,1,0:T(8,128)(2,1)}, f32[384,256]{1,0:T(8,128)}, f32[384...) custom-call(s32[2]{0:T(128)} %pad_add_fusion.me_ref, s32[2,16]{1,0:T(2,128)} %get-tuple-element.33.offs, ...), custom_call_target="tpu_custom_call" | custom-call | flops 864026624 | bytes 10076160 | tf_op jit(solution)/shard_map/gate_up/pallas_call | solution.py:350
  43.9 1.6 collective-permute-start.27
  45.5 1.5 collective-permute-start.29
  47.0 7.8 %gate_up.5 = (bf16[2,384,256]{2,1,0:T(8,128)(2,1)}, bf16[2,384,256]{2,1,0:T(8,128)(2,1)}, f32[384,256]{1,0:T(8,128)}, f32[384,256]{1,0:T(8,128)}, f32[384,256]{1,0:T(8,128)}, /*index=5*/f32[384,256]{1,0:T(8,128)}) custom-call(s32[2]{0:T(128)} %pad_add_fusion.me_ref, s32[2,16]{1,0:T(2,128)} %get-tuple-element.33.offs, ...), custom_call_target="tpu_custom_call" | custom-call | flops 864026624 | bytes 10076160 | tf_op jit(solution)/shard_map/gate_up/pallas_call | solution.py:350
  54.8 0.6 collective-permute-start.17
  55.4 0.6 collective-permute-start.19
  56.0 7.9 %gate_up.4 = (bf16[2,384,256]{2,1,0:T(8,128)(2,1)}, bf16[2,384,256]{2,1,0:T(8,128)(2,1)}, f32[384,256]{1,0:T(8,128)}, f32[384,256]{1,0:T(8,128)}, f32[384,256]{1,0:T(8,128)}, /*index=5*/f32[384,256]{1,0:T(8,128)}) custom-call(s32[2]{0:T(128)} %pad_add_fusion.me_ref, s32[2,16]{1,0:T(2,128)} %get-tuple-element.33.offs, ...), custom_call_target="tpu_custom_call" | custom-call | flops 864026624 | bytes 10076160 | tf_op jit(solution)/shard_map/gate_up/pallas_call | solution.py:350
  63.9 1.6 collective-permute-start.7
  65.5 1.5 collective-permute-start.9
  67.1 0.6 collective-permute-start.28
  67.7 0.6 collective-permute-start.30
  68.4 1.6 collective-permute-start.18
  70.0 6.2 %collective-permute-done.7 = bf16[2,384,256]{2,1,0:T(8,128)(2,1)S(1)} collective-permute-done((bf16[2,384,256]{2,1,0:T(8,128)(2,1)}, bf16[2,384,256]{2,1,0:T(8,128)(2,1)S(1)}, u32[]{:S(2)}, u32[]{:S(2)}) %collective-permute-start.7) | collective-permute-done | bytes 393248 | tf_op jit(solution)/shard_map/ppermute | solution.py:470
  76.2 1.5 collective-permute-start.20
  77.8 1.6 collective-permute-start.8
  79.5 2.5 %collective-permute-done.28 = bf16[384,256]{1,0:T(8,128)(2,1)S(1)} collective-permute-done((bf16[384,256]{1,0:T(8,128)(2,1)S(1)}, bf16[384,256]{1,0:T(8,128)(2,1)S(1)}, u32[]{:S(2)}, u32[]{:S(2)}) %collective-permute-start.28) | collective-permute-done | bytes 196640 | tf_op jit(solution)/shard_map/ppermute | solution.py:470
  82.0 0.5 collective-permute-start.10
  82.5 0.2 fusion.3
  82.8 1.6 collective-permute-start.34
  84.3 1.8 %collective-permute-done.18 = bf16[384,256]{1,0:T(8,128)(2,1)S(1)} collective-permute-done((bf16[384,256]{1,0:T(8,128)(2,1)S(1)}, bf16[384,256]{1,0:T(8,128)(2,1)S(1)}, u32[]{:S(2)}, u32[]{:S(2)}) %collective-permute-start.18) | collective-permute-done | bytes 196640 | tf_op jit(solution)/shard_map/ppermute | solution.py:470
  86.2 0.5 collective-permute-start.32
  86.7 1.5 collective-permute-start.33
  88.2 0.2 fusion.9
  88.5 1.9 %collective-permute-done.8 = bf16[384,256]{1,0:T(8,128)(2,1)S(1)} collective-permute-done((bf16[384,256]{1,0:T(8,128)(2,1)S(1)}, bf16[384,256]{1,0:T(8,128)(2,1)S(1)}, u32[]{:S(2)}, u32[]{:S(2)}) %collective-permute-start.8) | collective-permute-done | bytes 196640 | tf_op jit(solution)/shard_map/ppermute | solution.py:470
  90.4 0.5 collective-permute-start.31
  90.9 1.5 collective-permute-start.24
  92.7 1.6 collective-permute-start.22
  94.3 0.5 collective-permute-start.23
  94.8 1.3 collective-permute-start.21
  96.1 0.8 collective-permute-start.14
  96.9 1.5 collective-permute-start.11
  98.4 0.9 collective-permute-start.36
  99.4 1.0 collective-permute-start.35
  100.5 1.3 collective-permute-start.26
  101.8 0.7 collective-permute-start.25
  102.5 12.7 %weigh.1 = (f32[1648,128]{1,0:T(8,128)}, bf16[8,128,1536]{2,1,0:T(8,128)(2,1)}) custom-call(s32[2,16]{1,0:T(2,128)} %get-tuple-element.33.offs, s32[8,16,128]{2,1,0:T(8,128)} %get-tuple-element.54.rowid, f32[8,16,128]{2,1,0:T(8,128)} %get-tuple-element.55.probs, s32[8,8,128]{2,1,0:T(8,128)} %get-tuple-element.56.rowk.refs_11_), custom_call_target="tpu_custom_call" | custom-call | flops 6000000000 | bytes 8000000 | tf_op jit(solution)/shard_map/weigh/pallas_call | solution.py:254
  115.3 1.4 collective-permute-start.12
  116.8 0.8 collective-permute-start.13
  117.5 1.3 collective-permute-start.16
  118.9 0.7 collective-permute-start.15
  119.6 5.5 %down.3.refs_8_ = f32[1648,512]{1,0:T(8,128)} custom-call(s32[2]{0:T(128)} %pad_add_fusion.me_ref, s32[2,16]{1,0:T(2,128)} %get-tuple-element.33.offs, bf16[16,768,512]{2,1,0:T(8,128)(2,1)} %w_down.5, bf16[384,128]{1,0:T(8,128)(2,1)} %copy-done.1, bf16[384,128]{1,0:T(8,128)(2,1)} %copy-done, bf16[384,128]{1,0:T(8,128)(2,1)} %copy-done.29, ...), custom_call_target="tpu_custom_call" | custom-call | flops 864026624 | bytes 10944512 | tf_op jit(solution)/shard_map/down/pallas_call | solution.py:456
  125.2 0.6 copy-done.41
  125.8 6.7 %down.4.refs_8_ = f32[1648,512]{1,0:T(8,128)} custom-call(s32[2]{0:T(128)} %pad_add_fusion.me_ref, s32[2,16]{1,0:T(2,128)} %get-tuple-element.33.offs, bf16[16,768,512]{2,1,0:T(8,128)(2,1)} %w_down.5, bf16[384,128]{1,0:T(8,128)(2,1)} %copy-done.3, bf16[384,128]{1,0:T(8,128)(2,1)} %copy-done.2, bf16[384,128]{1,0:T(8,128)(2,1)} %copy-done.34, ...), custom_call_target="tpu_custom_call" | custom-call | flops 864026624 | bytes 10944512 | tf_op jit(solution)/shard_map/down/pallas_call | solution.py:456
  132.6 0.6 copy-done.35
  133.3 8.9 %down.5 = (bf16[4,128,512]{2,1,0:T(8,128)(2,1)}, bf16[4,128,512]{2,1,0:T(8,128)(2,1)}) custom-call(s32[2]{0:T(128)} %pad_add_fusion.me_ref, s32[2,16]{1,0:T(2,128)} %get-tuple-element.33.offs, bf16[16,768,512]{2,1,0:T(8,128)(2,1)} %w_down.5, bf16[384,128]{1,0:T(8,128)(2,1)} %copy-done.5, bf16[384,128]{1,0:T(8,128)(2,1)} %copy-done.4, ...), custom_call_target="tpu_custom_call" | custom-call | flops 864026624 | bytes 10944512 | tf_op jit(solution)/shard_map/down/pallas_call | solution.py:456
  142.2 2.1 %collective-permute-done.37 = bf16[4,128,512]{2,1,0:T(8,128)(2,1)S(1)} collective-permute-done((bf16[4,128,512]{2,1,0:T(8,128)(2,1)}, bf16[4,128,512]{2,1,0:T(8,128)(2,1)S(1)}, u32[]{:S(2)}, u32[]{:S(2)}) %collective-permute-start.37) | collective-permute-done | bytes 524320 | tf_op jit(solution)/shard_map/ppermute | solution.py:470
  144.3 1.2 convert_add_fusion
  145.7 8.3 %collective-permute-done.38 = bf16[2,128,512]{2,1,0:T(8,128)(2,1)S(1)} collective-permute-done((bf16[2,128,512]{2,1,0:T(8,128)(2,1)S(1)}, bf16[2,128,512]{2,1,0:T(8,128)(2,1)S(1)}, u32[]{:S(2)}, u32[]{:S(2)}) %collective-permute-start.38) | collective-permute-done | bytes 262176 | tf_op jit(solution)/shard_map/ppermute | solution.py:470
  154.1 0.7 collective-permute-start.39
  154.8 7.8 %collective-permute-done.39 = bf16[1,128,512]{2,1,0:T(8,128)(2,1)S(1)} collective-permute-done((bf16[1,128,512]{2,1,0:T(8,128)(2,1)S(1)}, bf16[1,128,512]{2,1,0:T(8,128)(2,1)S(1)}, u32[]{:S(2)}, u32[]{:S(2)}) %collective-permute-start.39) | collective-permute-done | bytes 131104 | tf_op jit(solution)/shard_map/ppermute | solution.py:470
  162.6 0.7 fusion.19
  (132 shorter events, 1.6 us)
Async XLA Ops:
  0.0 10.7 %collective-permute-start.3 = (bf16[128,512]{1,0:T(8,128)(2,1)}, bf16[128,512]{1,0:T(8,128)(2,1)S(1)}, u32[]{:S(2)}, u32[]{:S(2)}) collective-permute-start(bf16[128,512]{1,0:T(8,128)(2,1)} %refs_1_.3), channel_id=1, source_target_pairs={{0,4},{1,5},{2,6},{3,7},{4,0},{5,1},{6,2},{7,3},{8,12},{9,13},{10,... | collective-permute-start | bytes 393224 | tf_op jit(solution)/shard_map/ppermute | solution.py:470
  4.0 24.4 %collective-permute-start.1 = (bf16[128,512]{1,0:T(8,128)(2,1)}, bf16[128,512]{1,0:T(8,128)(2,1)S(1)}, u32[]{:S(2)}, u32[]{:S(2)}) collective-permute-start(bf16[128,512]{1,0:T(8,128)(2,1)} %refs_1_.3), channel_id=1, source_target_pairs={{0,2},{1,3},{2,0},{3,1},{4,6},{5,7},{6,4},{7,5},{8,10},{9,11},{10,... | collective-permute-start | bytes 393224 | tf_op jit(solution)/shard_map/ppermute | solution.py:470
  5.6 27.8 %collective-permute-start = (bf16[128,512]{1,0:T(8,128)(2,1)}, bf16[128,512]{1,0:T(8,128)(2,1)S(1)}, u32[]{:S(2)}, u32[]{:S(2)}) collective-permute-start(bf16[128,512]{1,0:T(8,128)(2,1)} %refs_1_.3), channel_id=1, source_target_pairs={{0,1},{1,0},{2,3},{3,2},{4,5},{5,4},{6,7},{7,6},{8,9},{9,8},{10,11... | collective-permute-start | bytes 393224 | tf_op jit(solution)/shard_map/ppermute | solution.py:470
  10.7 22.7 %copy-start.18 = (bf16[128,512]{1,0:T(8,128)(2,1)}, bf16[128,512]{1,0:T(8,128)(2,1)S(1)}, u32[]{:S(2)}) copy-start(bf16[128,512]{1,0:T(8,128)(2,1)S(1)} %collective-permute-done.3.refs_5_) | copy-start | bytes 393220
  10.7 18.0 %collective-permute-start.5 = (bf16[128,512]{1,0:T(8,128)(2,1)S(1)}, bf16[128,512]{1,0:T(8,128)(2,1)S(1)}, u32[]{:S(2)}, u32[]{:S(2)}) collective-permute-start(bf16[128,512]{1,0:T(8,128)(2,1)S(1)} %collective-permute-done.3.refs_5_), channel_id=1, source_target_pairs={{0,2},{1,3},{2,0},{3,1},{4,6},{5,7},{6,4},{7,5},{8,10},{9,11},{10,... | collective-permute-start | bytes 393224 | tf_op jit(solution)/shard_map/ppermute | solution.py:470
  28.1 5.3 %collective-permute-start.4 = (bf16[128,512]{1,0:T(8,128)(2,1)S(1)}, bf16[128,512]{1,0:T(8,128)(2,1)S(1)}, u32[]{:S(2)}, u32[]{:S(2)}) collective-permute-start(bf16[128,512]{1,0:T(8,128)(2,1)S(1)} %collective-permute-done.3.refs_5_), channel_id=1, source_target_pairs={{0,1},{1,0},{2,3},{3,2},{4,5},{5,4},{6,7},{7,6},{8,9},{9,8},{10,11... | collective-permute-start | bytes 393224 | tf_op jit(solution)/shard_map/ppermute | solution.py:470
  28.5 4.9 %collective-permute-start.2 = (bf16[128,512]{1,0:T(8,128)(2,1)S(1)}, bf16[128,512]{1,0:T(8,128)(2,1)S(1)}, u32[]{:S(2)}, u32[]{:S(2)}) collective-permute-start(bf16[128,512]{1,0:T(8,128)(2,1)S(1)} %collective-permute-done.1.refs_3_), channel_id=1, source_target_pairs={{0,1},{1,0},{2,3},{3,2},{4,5},{5,4},{6,7},{7,6},{8,9},{9,8},{10,11... | collective-permute-start | bytes 393224 | tf_op jit(solution)/shard_map/ppermute | solution.py:470
  28.6 4.8 %collective-permute-start.6 = (bf16[128,512]{1,0:T(8,128)(2,1)S(1)}, bf16[128,512]{1,0:T(8,128)(2,1)S(1)}, u32[]{:S(2)}, u32[]{:S(2)}) collective-permute-start(bf16[128,512]{1,0:T(8,128)(2,1)S(1)} %collective-permute-done.5.refs_7_), channel_id=1, source_target_pairs={{0,1},{1,0},{2,3},{3,2},{4,5},{5,4},{6,7},{7,6},{8,9},{9,8},{10,11... | collective-permute-start | bytes 393224 | tf_op jit(solution)/shard_map/ppermute | solution.py:470
  43.9 21.6 %collective-permute-start.27 = (bf16[2,384,256]{2,1,0:T(8,128)(2,1)}, bf16[2,384,256]{2,1,0:T(8,128)(2,1)S(1)}, u32[]{:S(2)}, u32[]{:S(2)}) collective-permute-start(bf16[2,384,256]{2,1,0:T(8,128)(2,1)} %get-tuple-element.49), channel_id=1, source_target_pairs={{0,8},{8,0},{16,24},{24,16},{1,9},{9,1},{17,25},{25,17},{2,10},{10... | collective-permute-start | bytes 1179656 | tf_op jit(solution)/shard_map/ppermute | solution.py:470
  45.5 21.6 %collective-permute-start.29 = (bf16[2,384,256]{2,1,0:T(8,128)(2,1)}, bf16[2,384,256]{2,1,0:T(8,128)(2,1)S(1)}, u32[]{:S(2)}, u32[]{:S(2)}) collective-permute-start(bf16[2,384,256]{2,1,0:T(8,128)(2,1)} %get-tuple-element.52), channel_id=1, source_target_pairs={{0,16},{8,24},{16,0},{24,8},{1,17},{9,25},{17,1},{25,9},{2,18},{10... | collective-permute-start | bytes 1179656 | tf_op jit(solution)/shard_map/ppermute | solution.py:470
  54.8 12.9 %collective-permute-start.17 = (bf16[2,384,256]{2,1,0:T(8,128)(2,1)}, bf16[2,384,256]{2,1,0:T(8,128)(2,1)S(1)}, u32[]{:S(2)}, u32[]{:S(2)}) collective-permute-start(bf16[2,384,256]{2,1,0:T(8,128)(2,1)} %get-tuple-element.43), channel_id=1, source_target_pairs={{0,8},{8,0},{16,24},{24,16},{1,9},{9,1},{17,25},{25,17},{2,10},{10... | collective-permute-start | bytes 1179656 | tf_op jit(solution)/shard_map/ppermute | solution.py:470
  55.4 14.5 %copy-start.14 = (f32[384,256]{1,0:T(8,128)S(1)}, f32[384,256]{1,0:T(8,128)}, u32[]{:S(2)}) copy-start(f32[384,256]{1,0:T(8,128)} %get-tuple-element.47) | copy-start | bytes 1179652
  55.4 12.9 %collective-permute-start.19 = (bf16[2,384,256]{2,1,0:T(8,128)(2,1)}, bf16[2,384,256]{2,1,0:T(8,128)(2,1)S(1)}, u32[]{:S(2)}, u32[]{:S(2)}) collective-permute-start(bf16[2,384,256]{2,1,0:T(8,128)(2,1)} %get-tuple-element.46), channel_id=1, source_target_pairs={{0,16},{8,24},{16,0},{24,8},{1,17},{9,25},{17,1},{25,9},{2,18},{10... | collective-permute-start | bytes 1179656 | tf_op jit(solution)/shard_map/ppermute | solution.py:470
  63.9 15.5 %copy-start.12 = (f32[384,256]{1,0:T(8,128)S(1)}, f32[384,256]{1,0:T(8,128)}, u32[]{:S(2)}) copy-start(f32[384,256]{1,0:T(8,128)} %get-tuple-element.41) | copy-start | bytes 1179652
  63.9 18.6 %copy-start.10 = (f32[384,256]{1,0:T(8,128)S(1)}, f32[384,256]{1,0:T(8,128)}, u32[]{:S(2)}) copy-start(f32[384,256]{1,0:T(8,128)} %get-tuple-element.48) | copy-start | bytes 1179652
  63.9 18.6 %copy-start.11 = (f32[384,256]{1,0:T(8,128)S(1)}, f32[384,256]{1,0:T(8,128)}, u32[]{:S(2)}) copy-start(f32[384,256]{1,0:T(8,128)} %get-tuple-element.51) | copy-start | bytes 1179652
  63.9 12.3 %collective-permute-start.7 = (bf16[2,384,256]{2,1,0:T(8,128)(2,1)}, bf16[2,384,256]{2,1,0:T(8,128)(2,1)S(1)}, u32[]{:S(2)}, u32[]{:S(2)}) collective-permute-start(bf16[2,384,256]{2,1,0:T(8,128)(2,1)} %get-tuple-element.37), channel_id=1, source_target_pairs={{0,8},{8,0},{16,24},{24,16},{1,9},{9,1},{17,25},{25,17},{2,10},{10... | collective-permute-start | bytes 1179656 | tf_op jit(solution)/shard_map/ppermute | solution.py:470
  65.5 12.3 %collective-permute-start.9 = (bf16[2,384,256]{2,1,0:T(8,128)(2,1)}, bf16[2,384,256]{2,1,0:T(8,128)(2,1)S(1)}, u32[]{:S(2)}, u32[]{:S(2)}) collective-permute-start(bf16[2,384,256]{2,1,0:T(8,128)(2,1)} %get-tuple-element.40), channel_id=1, source_target_pairs={{0,16},{8,24},{16,0},{24,8},{1,17},{9,25},{17,1},{25,9},{2,18},{10... | collective-permute-start | bytes 1179656 | tf_op jit(solution)/shard_map/ppermute | solution.py:470
  67.0 21.2 %copy-start.8 = (f32[384,256]{1,0:T(8,128)S(1)}, f32[384,256]{1,0:T(8,128)}, u32[]{:S(2)}) copy-start(f32[384,256]{1,0:T(8,128)} %get-tuple-element.42) | copy-start | bytes 1179652
  67.0 21.2 %copy-start.9 = (f32[384,256]{1,0:T(8,128)S(1)}, f32[384,256]{1,0:T(8,128)}, u32[]{:S(2)}) copy-start(f32[384,256]{1,0:T(8,128)} %get-tuple-element.45) | copy-start | bytes 1179652
  67.1 14.9 %collective-permute-start.28 = (bf16[384,256]{1,0:T(8,128)(2,1)S(1)}, bf16[384,256]{1,0:T(8,128)(2,1)S(1)}, u32[]{:S(2)}, u32[]{:S(2)}) collective-permute-start(bf16[384,256]{1,0:T(8,128)(2,1)S(1)} %fusion.4), channel_id=1, source_target_pairs={{0,16},{8,24},{16,0},{24,8},{1,17},{9,25},{17,1},{25,9},{2,18},{10... | collective-permute-start | bytes 589832 | tf_op jit(solution)/shard_map/ppermute | solution.py:470
  67.7 14.8 %collective-permute-start.30 = (bf16[384,256]{1,0:T(8,128)(2,1)S(1)}, bf16[384,256]{1,0:T(8,128)(2,1)S(1)}, u32[]{:S(2)}, u32[]{:S(2)}) collective-permute-start(bf16[384,256]{1,0:T(8,128)(2,1)S(1)} %fusion), channel_id=1, source_target_pairs={{0,8},{8,0},{16,24},{24,16},{1,9},{9,1},{17,25},{25,17},{2,10},{10... | collective-permute-start | bytes 589832 | tf_op jit(solution)/shard_map/ppermute | solution.py:470
  68.3 24.1 %copy-start.6 = (f32[384,256]{1,0:T(8,128)S(1)}, f32[384,256]{1,0:T(8,128)}, u32[]{:S(2)}) copy-start(f32[384,256]{1,0:T(8,128)} %get-tuple-element.36) | copy-start | bytes 1179652
  68.4 24.1 %copy-start.7 = (f32[384,256]{1,0:T(8,128)S(1)}, f32[384,256]{1,0:T(8,128)}, u32[]{:S(2)}) copy-start(f32[384,256]{1,0:T(8,128)} %get-tuple-element.39) | copy-start | bytes 1179652
  68.4 17.8 %collective-permute-start.18 = (bf16[384,256]{1,0:T(8,128)(2,1)S(1)}, bf16[384,256]{1,0:T(8,128)(2,1)S(1)}, u32[]{:S(2)}, u32[]{:S(2)}) collective-permute-start(bf16[384,256]{1,0:T(8,128)(2,1)S(1)} %fusion.10), channel_id=1, source_target_pairs={{0,16},{8,24},{16,0},{24,8},{1,17},{9,25},{17,1},{25,9},{2,18},{10... | collective-permute-start | bytes 589832 | tf_op jit(solution)/shard_map/ppermute | solution.py:470
  76.2 10.5 %collective-permute-start.20 = (bf16[384,256]{1,0:T(8,128)(2,1)S(1)}, bf16[384,256]{1,0:T(8,128)(2,1)S(1)}, u32[]{:S(2)}, u32[]{:S(2)}) collective-permute-start(bf16[384,256]{1,0:T(8,128)(2,1)S(1)} %fusion.6), channel_id=1, source_target_pairs={{0,8},{8,0},{16,24},{24,16},{1,9},{9,1},{17,25},{25,17},{2,10},{10... | collective-permute-start | bytes 589832 | tf_op jit(solution)/shard_map/ppermute | solution.py:470
  77.8 12.6 %collective-permute-start.8 = (bf16[384,256]{1,0:T(8,128)(2,1)S(1)}, bf16[384,256]{1,0:T(8,128)(2,1)S(1)}, u32[]{:S(2)}, u32[]{:S(2)}) collective-permute-start(bf16[384,256]{1,0:T(8,128)(2,1)S(1)} %fusion.16), channel_id=1, source_target_pairs={{0,16},{8,24},{16,0},{24,8},{1,17},{9,25},{17,1},{25,9},{2,18},{10... | collective-permute-start | bytes 589832 | tf_op jit(solution)/shard_map/ppermute | solution.py:470
  82.0 9.0 %collective-permute-start.10 = (bf16[384,256]{1,0:T(8,128)(2,1)S(1)}, bf16[384,256]{1,0:T(8,128)(2,1)S(1)}, u32[]{:S(2)}, u32[]{:S(2)}) collective-permute-start(bf16[384,256]{1,0:T(8,128)(2,1)S(1)} %fusion.12), channel_id=1, source_target_pairs={{0,8},{8,0},{16,24},{24,16},{1,9},{9,1},{17,25},{25,17},{2,10},{10... | collective-permute-start | bytes 589832 | tf_op jit(solution)/shard_map/ppermute | solution.py:470
  82.7 32.5 %copy-start = (bf16[384,128]{1,0:T(8,128)(2,1)}, bf16[384,128]{1,0:T(8,128)(2,1)S(1)}, u32[]{:S(2)}) copy-start(bf16[384,128]{1,0:T(8,128)(2,1)S(1)} %get-tuple-element.61.refs_1_) | copy-start | bytes 294916
  82.7 32.5 %copy-start.1 = (bf16[384,128]{1,0:T(8,128)(2,1)}, bf16[384,128]{1,0:T(8,128)(2,1)S(1)}, u32[]{:S(2)}) copy-start(bf16[384,128]{1,0:T(8,128)(2,1)S(1)} %get-tuple-element.62.refs_0_) | copy-start | bytes 294916
  82.8 9.9 %collective-permute-start.34 = (bf16[384,128]{1,0:T(8,128)(2,1)S(1)}, bf16[384,128]{1,0:T(8,128)(2,1)S(1)}, u32[]{:S(2)}, u32[]{:S(2)}) collective-permute-start(bf16[384,128]{1,0:T(8,128)(2,1)S(1)} %get-tuple-element.61.refs_1_), channel_id=1, source_target_pairs={{0,16},{8,24},{16,0},{24,8},{1,17},{9,25},{17,1},{25,9},{2,18},{10... | collective-permute-start | bytes 294920 | tf_op jit(solution)/shard_map/ppermute | solution.py:470
  86.2 8.1 %collective-permute-start.32 = (bf16[384,128]{1,0:T(8,128)(2,1)S(1)}, bf16[384,128]{1,0:T(8,128)(2,1)S(1)}, u32[]{:S(2)}, u32[]{:S(2)}) collective-permute-start(bf16[384,128]{1,0:T(8,128)(2,1)S(1)} %get-tuple-element.61.refs_1_), channel_id=1, source_target_pairs={{0,8},{8,0},{16,24},{24,16},{1,9},{9,1},{17,25},{25,17},{2,10},{10... | collective-permute-start | bytes 294920 | tf_op jit(solution)/shard_map/ppermute | solution.py:470
  86.7 8.1 %collective-permute-start.33 = (bf16[384,128]{1,0:T(8,128)(2,1)S(1)}, bf16[384,128]{1,0:T(8,128)(2,1)S(1)}, u32[]{:S(2)}, u32[]{:S(2)}) collective-permute-start(bf16[384,128]{1,0:T(8,128)(2,1)S(1)} %get-tuple-element.62.refs_0_), channel_id=1, source_target_pairs={{0,16},{8,24},{16,0},{24,8},{1,17},{9,25},{17,1},{25,9},{2,18},{10... | collective-permute-start | bytes 294920 | tf_op jit(solution)/shard_map/ppermute | solution.py:470
  88.5 26.8 %copy-start.2 = (bf16[384,128]{1,0:T(8,128)(2,1)}, bf16[384,128]{1,0:T(8,128)(2,1)S(1)}, u32[]{:S(2)}) copy-start(bf16[384,128]{1,0:T(8,128)(2,1)S(1)} %get-tuple-element.63.refs_1_) | copy-start | bytes 294916
  88.5 26.8 %copy-start.3 = (bf16[384,128]{1,0:T(8,128)(2,1)}, bf16[384,128]{1,0:T(8,128)(2,1)S(1)}, u32[]{:S(2)}) copy-start(bf16[384,128]{1,0:T(8,128)(2,1)S(1)} %get-tuple-element.64.refs_0_) | copy-start | bytes 294916
  90.4 5.7 %collective-permute-start.31 = (bf16[384,128]{1,0:T(8,128)(2,1)S(1)}, bf16[384,128]{1,0:T(8,128)(2,1)S(1)}, u32[]{:S(2)}, u32[]{:S(2)}) collective-permute-start(bf16[384,128]{1,0:T(8,128)(2,1)S(1)} %get-tuple-element.62.refs_0_), channel_id=1, source_target_pairs={{0,8},{8,0},{16,24},{24,16},{1,9},{9,1},{17,25},{25,17},{2,10},{10... | collective-permute-start | bytes 294920 | tf_op jit(solution)/shard_map/ppermute | solution.py:470
  90.9 5.9 %collective-permute-start.24 = (bf16[384,128]{1,0:T(8,128)(2,1)S(1)}, bf16[384,128]{1,0:T(8,128)(2,1)S(1)}, u32[]{:S(2)}, u32[]{:S(2)}) collective-permute-start(bf16[384,128]{1,0:T(8,128)(2,1)S(1)} %get-tuple-element.63.refs_1_), channel_id=1, source_target_pairs={{0,16},{8,24},{16,0},{24,8},{1,17},{9,25},{17,1},{25,9},{2,18},{10... | collective-permute-start | bytes 294920 | tf_op jit(solution)/shard_map/ppermute | solution.py:470
  92.7 22.7 %copy-start.4 = (bf16[384,128]{1,0:T(8,128)(2,1)}, bf16[384,128]{1,0:T(8,128)(2,1)S(1)}, u32[]{:S(2)}) copy-start(bf16[384,128]{1,0:T(8,128)(2,1)S(1)} %get-tuple-element.65.refs_1_) | copy-start | bytes 294916
  92.7 24.1 %copy-start.5 = (bf16[384,128]{1,0:T(8,128)(2,1)}, bf16[384,128]{1,0:T(8,128)(2,1)S(1)}, u32[]{:S(2)}) copy-start(bf16[384,128]{1,0:T(8,128)(2,1)S(1)} %get-tuple-element.66.refs_0_) | copy-start | bytes 294916
  92.7 22.5 %copy-start.25 = (bf16[384,128]{1,0:T(8,128)(2,1)}, bf16[384,128]{1,0:T(8,128)(2,1)S(1)}, u32[]{:S(2)}) copy-start(bf16[384,128]{1,0:T(8,128)(2,1)S(1)} %collective-permute-done.34.refs_5_) | copy-start | bytes 294916
  92.7 5.7 %collective-permute-start.22 = (bf16[384,128]{1,0:T(8,128)(2,1)S(1)}, bf16[384,128]{1,0:T(8,128)(2,1)S(1)}, u32[]{:S(2)}, u32[]{:S(2)}) collective-permute-start(bf16[384,128]{1,0:T(8,128)(2,1)S(1)} %get-tuple-element.63.refs_1_), channel_id=1, source_target_pairs={{0,8},{8,0},{16,24},{24,16},{1,9},{9,1},{17,25},{25,17},{2,10},{10... | collective-permute-start | bytes 294920 | tf_op jit(solution)/shard_map/ppermute | solution.py:470
  94.3 21.0 %copy-start.26 = (bf16[384,128]{1,0:T(8,128)(2,1)}, bf16[384,128]{1,0:T(8,128)(2,1)S(1)}, u32[]{:S(2)}) copy-start(bf16[384,128]{1,0:T(8,128)(2,1)S(1)} %collective-permute-done.32.refs_3_) | copy-start | bytes 294916
  94.3 5.1 %collective-permute-start.23 = (bf16[384,128]{1,0:T(8,128)(2,1)S(1)}, bf16[384,128]{1,0:T(8,128)(2,1)S(1)}, u32[]{:S(2)}, u32[]{:S(2)}) collective-permute-start(bf16[384,128]{1,0:T(8,128)(2,1)S(1)} %get-tuple-element.64.refs_0_), channel_id=1, source_target_pairs={{0,16},{8,24},{16,0},{24,8},{1,17},{9,25},{17,1},{25,9},{2,18},{10... | collective-permute-start | bytes 294920 | tf_op jit(solution)/shard_map/ppermute | solution.py:470
  94.8 20.5 %copy-start.27 = (bf16[384,128]{1,0:T(8,128)(2,1)}, bf16[384,128]{1,0:T(8,128)(2,1)S(1)}, u32[]{:S(2)}) copy-start(bf16[384,128]{1,0:T(8,128)(2,1)S(1)} %collective-permute-done.33.refs_4_) | copy-start | bytes 294916
  94.8 5.7 %collective-permute-start.21 = (bf16[384,128]{1,0:T(8,128)(2,1)S(1)}, bf16[384,128]{1,0:T(8,128)(2,1)S(1)}, u32[]{:S(2)}, u32[]{:S(2)}) collective-permute-start(bf16[384,128]{1,0:T(8,128)(2,1)S(1)} %get-tuple-element.64.refs_0_), channel_id=1, source_target_pairs={{0,8},{8,0},{16,24},{24,16},{1,9},{9,1},{17,25},{25,17},{2,10},{10... | collective-permute-start | bytes 294920 | tf_op jit(solution)/shard_map/ppermute | solution.py:470
  96.1 19.2 %copy-start.29 = (bf16[384,128]{1,0:T(8,128)(2,1)}, bf16[384,128]{1,0:T(8,128)(2,1)S(1)}, u32[]{:S(2)}) copy-start(bf16[384,128]{1,0:T(8,128)(2,1)S(1)} %collective-permute-done.31.refs_2_) | copy-start | bytes 294916
  96.1 5.7 %collective-permute-start.14 = (bf16[384,128]{1,0:T(8,128)(2,1)S(1)}, bf16[384,128]{1,0:T(8,128)(2,1)S(1)}, u32[]{:S(2)}, u32[]{:S(2)}) collective-permute-start(bf16[384,128]{1,0:T(8,128)(2,1)S(1)} %get-tuple-element.65.refs_1_), channel_id=1, source_target_pairs={{0,16},{8,24},{16,0},{24,8},{1,17},{9,25},{17,1},{25,9},{2,18},{10... | collective-permute-start | bytes 294920 | tf_op jit(solution)/shard_map/ppermute | solution.py:470
  96.9 18.4 %copy-start.28 = (bf16[384,128]{1,0:T(8,128)(2,1)}, bf16[384,128]{1,0:T(8,128)(2,1)S(1)}, u32[]{:S(2)}) copy-start(bf16[384,128]{1,0:T(8,128)(2,1)S(1)} %collective-permute-done.24.refs_5_) | copy-start | bytes 294916
  96.9 18.5 %collective-permute-start.11 = (bf16[384,128]{1,0:T(8,128)(2,1)S(1)}, bf16[384,128]{1,0:T(8,128)(2,1)S(1)}, u32[]{:S(2)}, u32[]{:S(2)}) collective-permute-start(bf16[384,128]{1,0:T(8,128)(2,1)S(1)} %get-tuple-element.66.refs_0_), channel_id=1, source_target_pairs={{0,8},{8,0},{16,24},{24,16},{1,9},{9,1},{17,25},{25,17},{2,10},{10... | collective-permute-start | bytes 294920 | tf_op jit(solution)/shard_map/ppermute | solution.py:470
  98.4 16.9 %copy-start.31 = (bf16[384,128]{1,0:T(8,128)(2,1)}, bf16[384,128]{1,0:T(8,128)(2,1)S(1)}, u32[]{:S(2)}) copy-start(bf16[384,128]{1,0:T(8,128)(2,1)S(1)} %collective-permute-done.22.refs_3_) | copy-start | bytes 294916
  98.4 18.4 %collective-permute-start.36 = (bf16[384,128]{1,0:T(8,128)(2,1)S(1)}, bf16[384,128]{1,0:T(8,128)(2,1)S(1)}, u32[]{:S(2)}, u32[]{:S(2)}) collective-permute-start(bf16[384,128]{1,0:T(8,128)(2,1)S(1)} %collective-permute-done.34.refs_5_), channel_id=1, source_target_pairs={{0,8},{8,0},{16,24},{24,16},{1,9},{9,1},{17,25},{25,17},{2,10},{10... | collective-permute-start | bytes 294920 | tf_op jit(solution)/shard_map/ppermute | solution.py:470
  99.4 15.9 %copy-start.33 = (bf16[384,128]{1,0:T(8,128)(2,1)}, bf16[384,128]{1,0:T(8,128)(2,1)S(1)}, u32[]{:S(2)}) copy-start(bf16[384,128]{1,0:T(8,128)(2,1)S(1)} %collective-permute-done.23.refs_4_) | copy-start | bytes 294916
  99.4 18.1 %collective-permute-start.35 = (bf16[384,128]{1,0:T(8,128)(2,1)S(1)}, bf16[384,128]{1,0:T(8,128)(2,1)S(1)}, u32[]{:S(2)}, u32[]{:S(2)}) collective-permute-start(bf16[384,128]{1,0:T(8,128)(2,1)S(1)} %collective-permute-done.31.refs_2_), channel_id=1, source_target_pairs={{0,16},{8,24},{16,0},{24,8},{1,17},{9,25},{17,1},{25,9},{2,18},{10... | collective-permute-start | bytes 294920 | tf_op jit(solution)/shard_map/ppermute | solution.py:470
  100.5 14.8 %copy-start.34 = (bf16[384,128]{1,0:T(8,128)(2,1)}, bf16[384,128]{1,0:T(8,128)(2,1)S(1)}, u32[]{:S(2)}) copy-start(bf16[384,128]{1,0:T(8,128)(2,1)S(1)} %collective-permute-done.21.refs_2_) | copy-start | bytes 294916
  100.5 18.4 %collective-permute-start.26 = (bf16[384,128]{1,0:T(8,128)(2,1)S(1)}, bf16[384,128]{1,0:T(8,128)(2,1)S(1)}, u32[]{:S(2)}, u32[]{:S(2)}) collective-permute-start(bf16[384,128]{1,0:T(8,128)(2,1)S(1)} %collective-permute-done.24.refs_5_), channel_id=1, source_target_pairs={{0,8},{8,0},{16,24},{24,16},{1,9},{9,1},{17,25},{25,17},{2,10},{10... | collective-permute-start | bytes 294920 | tf_op jit(solution)/shard_map/ppermute | solution.py:470
  101.7 15.8 %copy-start.30 = (bf16[384,128]{1,0:T(8,128)(2,1)}, bf16[384,128]{1,0:T(8,128)(2,1)S(1)}, u32[]{:S(2)}) copy-start(bf16[384,128]{1,0:T(8,128)(2,1)S(1)} %collective-permute-done.14.refs_5_) | copy-start | bytes 294916
  101.8 23.4 %collective-permute-start.25 = (bf16[384,128]{1,0:T(8,128)(2,1)S(1)}, bf16[384,128]{1,0:T(8,128)(2,1)S(1)}, u32[]{:S(2)}, u32[]{:S(2)}) collective-permute-start(bf16[384,128]{1,0:T(8,128)(2,1)S(1)} %collective-permute-done.21.refs_2_), channel_id=1, source_target_pairs={{0,16},{8,24},{16,0},{24,8},{1,17},{9,25},{17,1},{25,9},{2,18},{10... | collective-permute-start | bytes 294920 | tf_op jit(solution)/shard_map/ppermute | solution.py:470
  115.3 17.1 %collective-permute-start.12 = (bf16[384,128]{1,0:T(8,128)(2,1)S(1)}, bf16[384,128]{1,0:T(8,128)(2,1)S(1)}, u32[]{:S(2)}, u32[]{:S(2)}) collective-permute-start(bf16[384,128]{1,0:T(8,128)(2,1)S(1)} %get-tuple-element.65.refs_1_), channel_id=1, source_target_pairs={{0,8},{8,0},{16,24},{24,16},{1,9},{9,1},{17,25},{25,17},{2,10},{10... | collective-permute-start | bytes 294920 | tf_op jit(solution)/shard_map/ppermute | solution.py:470
  116.8 15.7 %collective-permute-start.13 = (bf16[384,128]{1,0:T(8,128)(2,1)S(1)}, bf16[384,128]{1,0:T(8,128)(2,1)S(1)}, u32[]{:S(2)}, u32[]{:S(2)}) collective-permute-start(bf16[384,128]{1,0:T(8,128)(2,1)S(1)} %get-tuple-element.66.refs_0_), channel_id=1, source_target_pairs={{0,16},{8,24},{16,0},{24,8},{1,17},{9,25},{17,1},{25,9},{2,18},{10... | collective-permute-start | bytes 294920 | tf_op jit(solution)/shard_map/ppermute | solution.py:470
  117.5 15.0 %collective-permute-start.16 = (bf16[384,128]{1,0:T(8,128)(2,1)S(1)}, bf16[384,128]{1,0:T(8,128)(2,1)S(1)}, u32[]{:S(2)}, u32[]{:S(2)}) collective-permute-start(bf16[384,128]{1,0:T(8,128)(2,1)S(1)} %collective-permute-done.14.refs_5_), channel_id=1, source_target_pairs={{0,8},{8,0},{16,24},{24,16},{1,9},{9,1},{17,25},{25,17},{2,10},{10... | collective-permute-start | bytes 294920 | tf_op jit(solution)/shard_map/ppermute | solution.py:470
  118.9 13.7 %collective-permute-start.15 = (bf16[384,128]{1,0:T(8,128)(2,1)S(1)}, bf16[384,128]{1,0:T(8,128)(2,1)S(1)}, u32[]{:S(2)}, u32[]{:S(2)}) collective-permute-start(bf16[384,128]{1,0:T(8,128)(2,1)S(1)} %collective-permute-done.11.refs_2_), channel_id=1, source_target_pairs={{0,16},{8,24},{16,0},{24,8},{1,17},{9,25},{17,1},{25,9},{2,18},{10... | collective-permute-start | bytes 294920 | tf_op jit(solution)/shard_map/ppermute | solution.py:470
  142.1 2.2 %collective-permute-start.37 = (bf16[4,128,512]{2,1,0:T(8,128)(2,1)}, bf16[4,128,512]{2,1,0:T(8,128)(2,1)S(1)}, u32[]{:S(2)}, u32[]{:S(2)}) collective-permute-start(bf16[4,128,512]{2,1,0:T(8,128)(2,1)} %get-tuple-element.60), channel_id=1, source_target_pairs={{0,1},{1,0},{2,3},{3,2},{4,5},{5,4},{6,7},{7,6},{8,9},{9,8},{10,11... | collective-permute-start | bytes 1572872 | tf_op jit(solution)/shard_map/ppermute | solution.py:470
  145.6 8.4 %collective-permute-start.38 = (bf16[2,128,512]{2,1,0:T(8,128)(2,1)S(1)}, bf16[2,128,512]{2,1,0:T(8,128)(2,1)S(1)}, u32[]{:S(2)}, u32[]{:S(2)}) collective-permute-start(bf16[2,128,512]{2,1,0:T(8,128)(2,1)S(1)} %slice.156), channel_id=1, source_target_pairs={{0,2},{1,3},{2,0},{3,1},{4,6},{5,7},{6,4},{7,5},{8,10},{9,11},{10,... | collective-permute-start | bytes 786440 | tf_op jit(solution)/shard_map/ppermute | solution.py:470
  154.1 8.5 %collective-permute-start.39 = (bf16[1,128,512]{2,1,0:T(8,128)(2,1)S(1)}, bf16[1,128,512]{2,1,0:T(8,128)(2,1)S(1)}, u32[]{:S(2)}, u32[]{:S(2)}) collective-permute-start(bf16[1,128,512]{2,1,0:T(8,128)(2,1)S(1)} %slice.157), channel_id=1, source_target_pairs={{0,4},{1,5},{2,6},{3,7},{4,0},{5,1},{6,2},{7,3},{8,12},{9,13},{10,... | collective-permute-start | bytes 393224 | tf_op jit(solution)/shard_map/ppermute | solution.py:470
  (19 other events, 87.2 us)

commit v3 on v2

--- a/solution.py
+++ b/solution.py
@@ -1,4 +1,5 @@
 import functools
+import math
 
 import jax
 import jax.numpy as jnp
@@ -11,6 +12,7 @@
 F32 = jnp.float32
 BF16 = jnp.bfloat16
 VMEM_LIMIT = 56 * 2**20
+VMEM_SPARE = 10 * 2**20
 ALIGN = 16
 META = 16
 
@@ -31,38 +33,44 @@
     return pl.BlockSpec(memory_space=pl.ANY)
 
 
-def params():
-    return pltpu.CompilerParams(vmem_limit_bytes=VMEM_LIMIT)
+def params(*shapes):
+    need = sum(math.prod(s.shape) * jnp.dtype(s.dtype).itemsize for s in shapes if hasattr(s, "dtype"))
+    return pltpu.CompilerParams(vmem_limit_bytes=min(VMEM_LIMIT, need + need // 4 + VMEM_SPARE))
+
+
+def held(*arrays):
+    return [jax.ShapeDtypeStruct(a.shape, a.dtype) for a in arrays]
 
 
 def cost(flops, moved):
     return pl.CostEstimate(flops=int(flops), bytes_accessed=int(moved), transcendentals=0)
 
 
-def prepare_kernel(dims, ids, weights, meta):
+def pack_kernel(dims, tokens, ids, weights, packed):
     rows, top = dims["rows"], dims["top"]
     chance = weights[...]
-    chance = (chance / jnp.sum(chance, axis=1, keepdims=True)).T
+    chance = chance / jnp.sum(chance, axis=0, keepdims=True)
     high = chance.astype(BF16)
     rest = chance - high.astype(F32)
     middle = rest.astype(BF16)
     low = (rest - middle.astype(F32)).astype(BF16)
-    meta[...] = jnp.zeros_like(meta)
-    parts = (ids[...].astype(F32).T, high.astype(F32), middle.astype(F32), low.astype(F32))
+    packed[:rows, :] = tokens[...]
+    packed[rows:, :] = jnp.zeros((META, packed.shape[1]), BF16)
+    parts = (ids[...].astype(F32), high.astype(F32), middle.astype(F32), low.astype(F32))
     for i, part in enumerate(parts):
         block = jnp.concatenate([part, jnp.zeros((META - top, rows), F32)], axis=0)
-        meta[:, i * rows : (i + 1) * rows] = block.astype(BF16)
-
-
-def prepare(dims, ids, weights):
+        packed[rows:, i * rows : (i + 1) * rows] = block.astype(BF16)
+
+
+def pack(dims, tokens, ids, weights):
     return pl.pallas_call(
-        functools.partial(prepare_kernel, dims),
-        out_shape=jax.ShapeDtypeStruct((META, 4 * dims["rows"]), BF16),
-        in_specs=[vmem(), vmem()],
+        functools.partial(pack_kernel, dims),
+        out_shape=jax.ShapeDtypeStruct((dims["rows"] + META, tokens.shape[1]), BF16),
+        in_specs=[vmem()] * 3,
         out_specs=vmem(),
         compiler_params=params(),
-        name="prepare",
-    )(ids, weights)
+        name="pack",
+    )(tokens, ids.T, weights.T)
 
 
 def loop(count, body, carry):
@@ -73,7 +81,7 @@
     return carry
 
 
-def route(dims, base, meta, rowid, probs, rowk):
+def route(dims, base, meta_of, rowid, probs, rowk):
     blocks, rows, top, experts = dims["blocks"], dims["rows"], dims["top"], dims["experts"]
     expert_at = lax.broadcasted_iota(jnp.int32, (experts, rows), 0) + base
     upper = (
@@ -82,10 +90,10 @@
     ).astype(BF16)
 
     def chosen_ids(block):
-        return meta[block, :, :rows].astype(F32)[:top].astype(jnp.int32)
+        return meta_of(block)[:, :rows].astype(F32)[:top].astype(jnp.int32)
 
     def count(block, seen):
-        held = meta[block].astype(F32)[:top]
+        held = meta_of(block).astype(F32)[:top]
         ids = held[:, :rows].astype(jnp.int32)
         chance = held[:, rows : 2 * rows] + held[:, 2 * rows : 3 * rows]
         chance = chance + held[:, 3 * rows : 4 * rows]
@@ -152,20 +160,17 @@
     return starts
 
 
-def route_kernel(dims, me_ref, meta, rowid, probs, rowk, select, offs):
-    start, total = route(dims, me_ref[1] * dims["experts"], meta, rowid, probs, rowk)
-    fill_select(dims, rowid, publish(dims, offs, start, total), select, 0)
-
-
-def dispatch_kernel(dims, me_ref, meta, gathered, rowid, probs, rowk, x, offs, select, total):
+def dispatch_kernel(dims, me_ref, gathered, rowid, probs, rowk, x, offs, select, total):
     blocks, rows, group, tile = dims["blocks"], dims["rows"], dims["group"], dims["tile"]
-    start, count = route(dims, me_ref[1] * dims["experts"], meta, rowid, probs, rowk)
+    start, count = route(
+        dims, me_ref[1] * dims["experts"], lambda block: gathered[block, rows:, :], rowid, probs, rowk
+    )
     starts = publish(dims, offs, start, count)
     total[...] = jnp.zeros_like(total)
 
     def body(step, carry):
         fill_select(dims, rowid, starts, select, step)
-        part = gathered[pl.ds(step * group, group)].reshape(group * rows, x.shape[1])
+        part = gathered[pl.ds(step * group, group), :rows, :].reshape(group * rows, x.shape[1])
         for r in range(0, x.shape[0], tile):
             size = min(tile, x.shape[0] - r)
             got = jnp.dot(select[r : r + size, :], part, preferred_element_type=F32)
@@ -186,35 +191,21 @@
     ), jax.ShapeDtypeStruct((2, experts), jnp.int32)
 
 
-def route_rows(dims, me, meta):
-    shapes, offs = route_shapes(dims)
-    select = jax.ShapeDtypeStruct((dims["padded"], dims["blocks"] * dims["rows"]), BF16)
-    return pl.pallas_call(
-        functools.partial(route_kernel, dims),
-        out_shape=shapes + (select, offs),
-        in_specs=[smem(), vmem()],
-        out_specs=(vmem(),) * 4 + (smem(),),
-        compiler_params=params(),
-        cost_estimate=cost(4e9, 4e6),
-        name="route",
-    )(me, meta)
-
-
-def dispatch(dims, me, meta, gathered):
+def dispatch(dims, me, gathered):
     shapes, offs = route_shapes(dims)
     width, padded = gathered.shape[2], dims["padded"]
     return pl.pallas_call(
         functools.partial(dispatch_kernel, dims),
         out_shape=shapes + (jax.ShapeDtypeStruct((padded, width), BF16), offs),
-        in_specs=[smem(), vmem(), vmem()],
+        in_specs=[smem(), vmem()],
         out_specs=(vmem(),) * 4 + (smem(),),
         scratch_shapes=[
             pltpu.VMEM((padded, dims["group"] * dims["rows"]), BF16),
             pltpu.VMEM((padded, width), F32),
         ],
-        compiler_params=params(),
+        compiler_params=pltpu.CompilerParams(vmem_limit_bytes=VMEM_LIMIT),
         name="dispatch",
-    )(me, meta, gathered)
+    )(me, gathered)
 
 
 def choose(dims, rowk, block):
@@ -226,15 +217,38 @@
     return hit.astype(F32).astype(BF16)
 
 
-def weigh_kernel(dims, offs, rowid, probs, rowk, scale, chosen):
-    if dims["small"]:
-        def pick(block, carry):
-            chosen[block] = choose(dims, rowk, block)
-            return carry
-
-        lax.fori_loop(0, dims["blocks"], pick, 0)
-    else:
-        chosen[...] = jnp.zeros_like(chosen)
+def weigh_small_kernel(dims, offs, select, probs, scale, chosen, table):
+    rows, experts, total, blocks = dims["rows"], dims["experts"], dims["total"], dims["blocks"]
+    same = lax.broadcasted_iota(jnp.int32, (rows, rows), 0) == lax.broadcasted_iota(
+        jnp.int32, (rows, rows), 1
+    )
+    eye = same.astype(F32).astype(BF16)
+    contract = (((1,), (1,)), ((), ()))
+    for b in range(blocks):
+        cols = slice(b * rows, (b + 1) * rows)
+        picked = lax.dot_general(eye, select[:total, cols], contract, preferred_element_type=F32)
+        chosen[b] = picked.astype(BF16)
+        exact = probs[b]
+        high = exact.astype(BF16)
+        rest = exact - high.astype(F32)
+        middle = rest.astype(BF16)
+        low = (rest - middle.astype(F32)).astype(BF16)
+        table[:, cols] = jnp.concatenate([high, middle, low], axis=0)
+    wide = lax.dot_general(select[...], table[...], contract, preferred_element_type=F32)
+    scale[:, : 3 * experts] = wide
+    lane = lax.broadcasted_iota(jnp.int32, (dims["window"], scale.shape[1]), 1)
+    for e in range(experts):
+        first = aligned(offs[0, e])
+        at = pl.ds(first, dims["window"])
+        old = scale[at, :]
+        mine = (lane == e) | (lane == e + experts) | (lane == e + 2 * experts)
+        found = jnp.sum(jnp.where(mine, old, 0.0), axis=1, keepdims=True)
+        mask = row_mask(dims, first, offs, e)
+        scale[at, :] = jnp.where(mask, jnp.broadcast_to(found, old.shape), old)
+
+
+def weigh_large_kernel(dims, offs, rowid, probs, scale, chosen):
+    chosen[...] = jnp.zeros_like(chosen)
     for e in range(dims["experts"]):
         first = aligned(offs[0, e])
         at = pl.ds(first, dims["window"])
@@ -249,20 +263,24 @@
         scale[at, :] = jnp.where(row_mask(dims, first, offs, e), wide, scale[at, :])
 
 
-def weigh(dims, offs, rowid, probs, rowk):
-    picked = (dims["blocks"], dims["rows"], dims["total"]) if dims["small"] else (1, ALIGN, 128)
+def weigh(dims, offs, rows_of, probs):
+    small = dims["small"]
+    picked = (dims["blocks"], dims["rows"], dims["total"]) if small else (1, ALIGN, 128)
+    outs = (
+        jax.ShapeDtypeStruct((dims["padded"], 128), F32),
+        jax.ShapeDtypeStruct(picked, BF16),
+    )
+    table = pltpu.VMEM((3 * dims["experts"], dims["blocks"] * dims["rows"]), BF16)
     return pl.pallas_call(
-        functools.partial(weigh_kernel, dims),
-        out_shape=(
-            jax.ShapeDtypeStruct((dims["padded"], 128), F32),
-            jax.ShapeDtypeStruct(picked, BF16),
-        ),
-        in_specs=[smem(), vmem(), vmem(), vmem()],
+        functools.partial(weigh_small_kernel if small else weigh_large_kernel, dims),
+        out_shape=outs,
+        in_specs=[smem(), vmem(), vmem()],
         out_specs=(vmem(), vmem()),
-        compiler_params=params(),
+        scratch_shapes=[table] if small else [],
+        compiler_params=params(*outs, *held(rows_of, probs)),
         cost_estimate=cost(6e9, 8e6),
         name="weigh",
-    )(offs, rowid, probs, rowk)
+    )(offs, rows_of, probs)
 
 
 def row_mask(dims, first, offs, e):
@@ -275,14 +293,15 @@
     return [range(b, min(b + 4, experts)) for b in range(0, experts, 4)]
 
 
-def gate_up_kernel(dims, c, first_part, me_ref, offs, *refs):
+def gate_up_kernel(dims, c, first_part, me_ref, *refs):
     experts, window, part, quarter = dims["experts"], dims["window"], dims["part"], dims["quarter"]
     if first_part:
         blocks, rows = dims["blocks"], dims["rows"]
-        select, tokens, refs = refs[0], refs[1 : 1 + blocks], refs[1 + blocks :]
-        w_gate, w_up, x, gx, uy, g2, u1, g0, u0, gate_w, up_w, gate, up, sems, table = refs
+        packed, refs = refs[:blocks], refs[blocks:]
+        w_gate, w_up, rowid, probs, rowk, x, select, offs_out, refs = *refs[:8], refs[8:]
+        gx, uy, g2, u1, g0, u0, gate_w, up_w, gate, up, sems, table, meta = refs
     else:
-        x, w_gate, w_up, gx, uy, g2, u1, g0, u0, gate_w, up_w, gate, up, sems = refs
+        offs, x, w_gate, w_up, gx, uy, g2, u1, g0, u0, gate_w, up_w, gate, up, sems = refs
     units = pl.ds(c * part, part)
 
     def copies(e):
@@ -295,8 +314,15 @@
         for copy in copies(e):
             copy.start()
     if first_part:
-        for j, held in enumerate(tokens):
-            table[pl.ds(pl.multiple_of((me_ref[1] ^ j) * rows, rows), rows), :] = held[...]
+        for j, block in enumerate(packed):
+            at = me_ref[1] ^ j
+            table[pl.ds(pl.multiple_of(at * rows, rows), rows), :] = block[:rows, :]
+            meta[at] = block[rows:, :]
+        start, count = route(
+            dims, me_ref[1] * experts, lambda block: meta[block], rowid, probs, rowk
+        )
+        offs = offs_out
+        fill_select(dims, rowid, publish(dims, offs, start, count), select, 0)
         for r in range(0, x.shape[0], dims["tile"]):
             size = min(dims["tile"], x.shape[0] - r)
             got = jnp.dot(select[r : r + size, :], table[...], preferred_element_type=F32)
@@ -330,12 +356,12 @@
     u0[...] = piece(up, 0)
 
 
-def gate_up(dims, c, me, offs, rows_of, w_gate, w_up):
+def gate_up(dims, c, me, sources, w_gate, w_up):
     experts, part, quarter, padded = dims["experts"], dims["part"], dims["quarter"], dims["padded"]
     width = w_gate.shape[2]
     half = jax.ShapeDtypeStruct((2, quarter, part), BF16)
     own = jax.ShapeDtypeStruct((quarter, part), F32)
-    first_part = len(rows_of) > 1
+    first_part = len(sources) > 2
     outs = (half, half, own, own, own, own)
     scratch = [
         pltpu.VMEM((experts, part, width), BF16),
@@ -344,32 +370,40 @@
         pltpu.VMEM((padded, part), F32),
         pltpu.SemaphoreType.DMA((2, experts)),
     ]
+    into = (vmem(),) * len(outs)
     if first_part:
-        outs = (jax.ShapeDtypeStruct((padded, width), BF16),) + outs
-        scratch.append(pltpu.VMEM((dims["blocks"] * dims["rows"], width), BF16))
+        blocks, rows = dims["blocks"], dims["rows"]
+        shapes, offs = route_shapes(dims)
+        x = jax.ShapeDtypeStruct((padded, width), BF16)
+        select = jax.ShapeDtypeStruct((padded, blocks * rows), BF16)
+        outs = shapes + (x, select, offs) + outs
+        into = (vmem(),) * 5 + (smem(),) + into
+        scratch.append(pltpu.VMEM((blocks * rows, width), BF16))
+        scratch.append(pltpu.VMEM((blocks, META, width), BF16))
+        specs = [vmem()] * blocks
+    else:
+        specs = [smem(), vmem()]
     return pl.pallas_call(
         functools.partial(gate_up_kernel, dims, c, first_part),
         out_shape=outs,
-        in_specs=[smem(), smem()] + [vmem()] * len(rows_of) + [hbm(), hbm()],
-        out_specs=(vmem(),) * len(outs),
+        in_specs=[smem()] + specs + [hbm(), hbm()],
+        out_specs=into,
         scratch_shapes=scratch,
-        compiler_params=params(),
+        compiler_params=params(*outs, *held(*sources), *[b for b in scratch if "dma" not in str(b)]),
         cost_estimate=cost(4 * padded * width * part, 4 * experts * part * width + 2 * padded * width),
         name="gate_up",
-    )(me, offs, *rows_of, w_gate, w_up)
+    )(me, *sources, w_gate, w_up)
 
 
 def gather_hidden(dims, me, pieces, hidden):
-    quarter, half = dims["quarter"], dims["part"] // 2
-    for j in range(4):
-        at = pl.ds(pl.multiple_of((me ^ j) * quarter, ALIGN), quarter)
-        for side in range(2):
-            hidden[at, side * half : (side + 1) * half] = pieces[2 * j + side][...]
+    quarter = dims["quarter"]
+    for j, piece in zip((0, 3, 1, 2), pieces):
+        hidden[pl.ds(pl.multiple_of((me ^ j) * quarter, ALIGN), quarter), :] = piece[...]
 
 
 def down_kernel(dims, c, last, me_ref, offs, w_down, *refs):
     experts, window, part = dims["experts"], dims["window"], dims["part"]
-    pieces, refs = refs[:8], refs[8:]
+    pieces, refs = refs[:4], refs[4:]
     y_in = None
     if c > 0:
         y_in, refs = refs[0], refs[1:]
@@ -410,10 +444,9 @@
     rows, total, width = dims["rows"], dims["total"], w_down.shape[2]
     blocks, many = dims["blocks"], min(4, dims["blocks"])
     if dims["small"]:
-        order = halving_order(blocks)
         for side, into in enumerate((stay, away)):
             for p in range(0, blocks // 2, many):
-                at = [me_ref[1] ^ order[side * (blocks // 2) + p + i] for i in range(many)]
+                at = [me_ref[1] ^ (2 * (p + i) + side) for i in range(many)]
                 picked = jnp.concatenate([chosen[i] for i in at], axis=0)
                 summed = jnp.dot(picked, y_out[:total, :], preferred_element_type=F32)
                 into[p : p + many] = summed.astype(BF16).reshape(many, rows, width)
@@ -428,11 +461,6 @@
         return carry
 
     lax.fori_loop(0, blocks // many, combine, 0)
-
-
-def halving_order(blocks):
-    bits = blocks.bit_length() - 1
-    return [sum(((i >> b) & 1) << (bits - 1 - b) for b in range(bits)) for i in range(blocks)]
 
 
 def down(dims, c, last, me, offs, w_down, pieces, y, extra):
@@ -459,7 +487,7 @@
         in_specs=[smem(), smem(), hbm()] + [vmem()] * len(operands),
         out_specs=(vmem(),) * len(outs),
         scratch_shapes=scratch,
-        compiler_params=params(),
+        compiler_params=params(*outs, *held(*operands), *[b for b in scratch if "dma" not in str(b)]),
         cost_estimate=cost(4 * padded * width * part, 2 * experts * part * width + 8 * padded * width),
         name="down",
     )(me, offs, w_down, *operands)
@@ -478,16 +506,11 @@
     up_rest = swap((u1 + from_y[1].astype(F32)).astype(BF16), "rep", 1)
     gate = g0 + from_x[0].astype(F32) + gate_rest.astype(F32)
     up = u0 + from_y[0].astype(F32) + up_rest.astype(F32)
-    hidden = (jax.nn.silu(gate) * up).astype(BF16)
-    half = hidden.shape[1] // 2
-    return hidden[:, :half], hidden[:, half:]
-
-
-def spread_chunk(left, right):
-    x = (swap(left, "rep", 1), swap(right, "rep", 1))
-    y = (swap(left, "rep", 2), swap(right, "rep", 2))
-    corner = (swap(x[0], "rep", 2), swap(y[1], "rep", 1))
-    return [left, right, *x, *y, *corner]
+    return (jax.nn.silu(gate) * up).astype(BF16)
+
+
+def spread_chunk(hidden):
+    return [hidden] + [swap(hidden, "rep", bit) for bit in (3, 1, 2)]
 
 
 def gather_tokens(tokens):
@@ -501,15 +524,11 @@
 
 
 def sum_over_exp(stay, away):
-    bit = 1
-    while True:
-        came = swap(away, "exp", bit)
-        total = stay.astype(F32) + came.astype(F32)
-        count = total.shape[0] // 2
-        if count == 0:
-            return total[0].astype(BF16)
-        stay, away = total[:count], total[count:].astype(BF16)
-        bit *= 2
+    total = stay.astype(F32) + swap(away, "exp", 1).astype(F32)
+    came = [
+        swap(total[i].astype(BF16), "exp", 2 * i) for i in range(total.shape[0] - 1, 0, -1)
+    ]
+    return (total[0] + sum(part.astype(F32) for part in came)).astype(BF16)
 
 
 def local(tokens, expert_ids, route_weights, w_gate, w_up, w_down):
@@ -521,7 +540,7 @@
     cap = replicas * max(1, rows * top * 3 // (8 * EXPERTS))
     total = ceil_to(experts * blocks * cap, replicas * 128)
     window = ceil_to(blocks * cap, ALIGN) + ALIGN
-    part = 256
+    part = units // 2
     small = blocks * rows * total <= 4 * 2**20
     dims = dict(
         blocks=blocks,
@@ -538,23 +557,22 @@
         small=small,
     )
     me = jnp.stack([lax.axis_index("rep"), lax.axis_index("exp")]).astype(jnp.int32)
-    meta = lax.all_gather(prepare(dims, expert_ids, route_weights), "exp", axis=0)
+    packed = pack(dims, tokens, expert_ids, route_weights)
     if small:
-        held = gather_tokens(tokens)
-        rowid, probs, rowk, select, offs = route_rows(dims, me, meta)
-        sources = [select, *held]
+        sources = gather_tokens(packed)
     else:
-        gathered = lax.all_gather(tokens, "exp", axis=0)
-        rowid, probs, rowk, x, offs = dispatch(dims, me, meta, gathered)
-        sources = [x]
-    scale, chosen = weigh(dims, offs, rowid, probs, rowk)
+        gathered = lax.all_gather(packed, "exp", axis=0)
+        rowid, probs, rowk, x, offs = dispatch(dims, me, gathered)
+        rows_of, sources = rowid, [offs, x]
 
     pieces = []
     for c in range(units // part):
-        parts = gate_up(dims, c, me, offs, sources, w_gate, w_up)
-        if len(sources) > 1:
-            sources, parts = [parts[0]], parts[1:]
-        pieces.append(spread_chunk(*reduce_chunk(parts)))
+        parts = gate_up(dims, c, me, sources, w_gate, w_up)
+        if len(sources) > 2:
+            rowid, probs, rowk, x, rows_of, offs = parts[:6]
+            sources, parts = [offs, x], parts[6:]
+        pieces.append(spread_chunk(reduce_chunk(parts)))
+    scale, chosen = weigh(dims, offs, rows_of, probs)
     y = None
     last = len(pieces) - 1
     for c in range(last):

time: 164 us -> 128 us (0.78)
  Pallas kernels: 65.2 us -> 34.8 us
  waiting for transfers between devices: 31.5 us -> 54.8 us
  blocking collectives: 16.1 us -> 0 us
  starting transfers between devices: 41.2 us -> 29.3 us
  local copies, waits for them, and re-layouts: 5.1 us -> 6.9 us
    ppermute x40 -> x25, waiting for transfers between devices: 31.5 us -> 54.8 us  [swap(): return lax.ppermute(value, axis, [(i, i ^ bit) for i in range(count)])]
    all_gather x1 -> x0, blocking collectives: 16.1 us -> none  [local(): lax.all_gather(prepare(dims, expert_ids, route_weights), 'exp', axis=0)]
    pallas_call x3 -> x2, Pallas kernels: 18.7 us -> 4.16 us  [the longest x1 4.13 us: weigh(): pl.pallas_call(functools.partial(weigh_small_kernel if small else weigh_l...]
    ppermute x40 -> x25, starting transfers between devices: 41.2 us -> 29.3 us  [swap(): return lax.ppermute(value, axis, [(i, i ^ bit) for i in range(count)])]
    pallas_call x3 -> x2, Pallas kernels: 25.4 us -> 17.5 us  [gate_up(): pl.pallas_call(functools.partial(gate_up_kernel, dims, c, first_part), ou...]
    pallas_call x3 -> x2, Pallas kernels: 21.1 us -> 13.2 us  [down(): pl.pallas_call(functools.partial(down_kernel, dims, c, last), out_shape=o...]
    unnamed x88 -> x18, local copies, waits for them, and re-layouts: 5 us -> 6.87 us
  transfers between devices with their start and end apart: 40 -> 25, of which waited for: 9 -> 13; matrix products, arithmetic and copies ran while one was open for 3% -> 1% of each run, Pallas kernels for 29% -> 13%
where the time goes in v3:
time: 128 us
  waiting for transfers between devices  54.8 us (43%)
  Pallas kernels  34.8 us (27%)
  starting transfers between devices  29.3 us (23%)
  local copies, waits for them, and re-layouts  6.9 us (5%)
  other arithmetic  1.86 us (1%)
    ppermute x25, waiting for transfers between devices, swap(): return lax.ppermute(value, axis, [(i, i ^ bit) for i in range(count)])  54.8 us
    ppermute x25, starting transfers between devices, swap(): return lax.ppermute(value, axis, [(i, i ^ bit) for i in range(count)])  29.3 us
    pallas_call x2, Pallas kernels, gate_up(): pl.pallas_call(functools.partial(gate_up_kernel, dims, c, first_part), ou...  17.5 us
    pallas_call x2, Pallas kernels, down(): pl.pallas_call(functools.partial(down_kernel, dims, c, last), out_shape=o...  13.2 us
    unnamed x18, local copies, waits for them, and re-layouts  6.87 us
    pallas_call x1, Pallas kernels, weigh(): pl.pallas_call(functools.partial(weigh_small_kernel if small else weigh_l...  4.13 us
  transfers between devices with their start and end apart: 25, of which 13 were waited for; matrix products, arithmetic and copies ran while one was open for 1% of the time, Pallas kernels for 13%

profile of v3, /device:TPU:0, one launch (start us, length us, event | category | flops | bytes accessed | tf_op | source)
XLA Modules:
  0.0 127.9 jit_solution(10532308282506839755)
XLA Ops:
  0.0 0.9 copy-done.1
  0.9 0.7 copy-done.2
  1.6 0.7 copy-done.3
  2.3 4.1 %collective-permute-start.3 = (bf16[144,512]{1,0:T(8,128)(2,1)S(1)}, bf16[144,512]{1,0:T(8,128)(2,1)S(1)}, u32[]{:S(2)}, u32[]{:S(2)}) collective-permute-start(bf16[144,512]{1,0:T(8,128)(2,1)S(1)} %pack.1.refs_0_), channel_id=1, source_target_pairs={{0,4},{1,5},{2,6},{3,7},{4,0},{5,1},{6,2},{7,3},{8,12},{9,13},{10,... | collective-permute-start | bytes 442376 | tf_op jit(solution)/shard_map/ppermute | solution.py:498
  6.4 1.6 %collective-permute-start.1 = (bf16[144,512]{1,0:T(8,128)(2,1)S(1)}, bf16[144,512]{1,0:T(8,128)(2,1)S(1)}, u32[]{:S(2)}, u32[]{:S(2)}) collective-permute-start(bf16[144,512]{1,0:T(8,128)(2,1)S(1)} %pack.1.refs_0_), channel_id=1, source_target_pairs={{0,2},{1,3},{2,0},{3,1},{4,6},{5,7},{6,4},{7,5},{8,10},{9,11},{10,... | collective-permute-start | bytes 442376 | tf_op jit(solution)/shard_map/ppermute | solution.py:498
  8.0 5.5 %collective-permute-done.3.refs_4_ = bf16[144,512]{1,0:T(8,128)(2,1)S(1)} collective-permute-done((bf16[144,512]{1,0:T(8,128)(2,1)S(1)}, bf16[144,512]{1,0:T(8,128)(2,1)S(1)}, u32[]{:S(2)}, u32[]{:S(2)}) %collective-permute-start.3) | collective-permute-done | bytes 147488 | tf_op jit(solution)/shard_map/ppermute | solution.py:498
  13.5 0.6 collective-permute-start.5
  14.1 0.5 collective-permute-start.4
  14.6 0.0 collective-permute-start.2
  14.7 4.0 %collective-permute-done.5.refs_6_ = bf16[144,512]{1,0:T(8,128)(2,1)S(1)} collective-permute-done((bf16[144,512]{1,0:T(8,128)(2,1)S(1)}, bf16[144,512]{1,0:T(8,128)(2,1)S(1)}, u32[]{:S(2)}, u32[]{:S(2)}) %collective-permute-start.5) | collective-permute-done | bytes 147488 | tf_op jit(solution)/shard_map/ppermute | solution.py:498
  18.7 0.0 collective-permute-start.6
  18.7 0.1 pad_add_fusion.me_ref
  18.7 0.0 collective-permute-done.refs_1_
  18.7 0.0 collective-permute-done.4.refs_5_
  18.7 0.0 collective-permute-done.2.refs_3_
  18.8 1.3 %collective-permute-done.6.refs_7_ = bf16[144,512]{1,0:T(8,128)(2,1)S(1)} collective-permute-done((bf16[144,512]{1,0:T(8,128)(2,1)S(1)}, bf16[144,512]{1,0:T(8,128)(2,1)S(1)}, u32[]{:S(2)}, u32[]{:S(2)}) %collective-permute-start.6) | collective-permute-done | bytes 147488 | tf_op jit(solution)/shard_map/ppermute | solution.py:498
  20.0 10.4 %gate_up.2 = (s32[8,16,128]{2,1,0:T(8,128)}, f32[8,16,128]{2,1,0:T(8,128)S(1)}, s32[8,8,128]{2,1,0:T(8,128)S(1)}, bf16[1648,512]{1,0:T(8,128)(2,1)S(1)}, bf16[16...) custom-call(s32[2]{0:T(128)S(1)} %pad_add_fusion.me_ref, ...), custom_call_target="tpu_custom_call" | custom-call | flops 1296039936 | bytes 14270464 | tf_op jit(solution)/shard_map/gate_up/pallas_call | solution.py:386
  30.4 1.6 %collective-permute-start.14 = (bf16[2,384,384]{2,1,0:T(8,128)(2,1)S(1)}, bf16[2,384,384]{2,1,0:T(8,128)(2,1)S(1)}, u32[]{:S(2)}, u32[]{:S(2)}) collective-permute-start(bf16[2,384,384]{2,1,0:T(8,128)(2,1)S(1)} %get-tuple-element.35), channel_id=1, source_target_pairs={{0,8},{8,0},{16,24},{24,16},{1,9},{9,1},{17,25},{25,17},{2,10},{10... | collective-permute-start | bytes 1769480 | tf_op jit(solution)/shard_map/ppermute | solution.py:498
  32.0 1.5 %collective-permute-start.16 = (bf16[2,384,384]{2,1,0:T(8,128)(2,1)S(1)}, bf16[2,384,384]{2,1,0:T(8,128)(2,1)S(1)}, u32[]{:S(2)}, u32[]{:S(2)}) collective-permute-start(bf16[2,384,384]{2,1,0:T(8,128)(2,1)S(1)} %get-tuple-element.38), channel_id=1, source_target_pairs={{0,16},{8,24},{16,0},{24,8},{1,17},{9,25},{17,1},{25,9},{2,18},{10... | collective-permute-start | bytes 1769480 | tf_op jit(solution)/shard_map/ppermute | solution.py:498
  33.5 7.1 %gate_up.3 = (bf16[2,384,384]{2,1,0:T(8,128)(2,1)S(1)}, bf16[2,384,384]{2,1,0:T(8,128)(2,1)S(1)}, f32[384,384]{1,0:T(8,128)S(1)}, f32[384,384]{1,0:T(8,128)S(1)}...) custom-call(s32[2]{0:T(128)S(1)} %pad_add_fusion.me_ref, s32[2,16]{1,0:T(2,128)S(1)} %get-tuple-element.26.refs_0_.offs, ...), custom_call_target="tpu_custom_call" | custom-call | flops 1296039936 | bytes 14270464 | tf_op jit(solution)/shard_map/gate_up/pallas_call | solution.py:386
  40.7 0.6 collective-permute-start.7
  41.3 0.5 collective-permute-start.9
  41.8 4.9 %collective-permute-done.14 = bf16[2,384,384]{2,1,0:T(8,128)(2,1)S(1)} collective-permute-done((bf16[2,384,384]{2,1,0:T(8,128)(2,1)S(1)}, bf16[2,384,384]{2,1,0:T(8,128)(2,1)S(1)}, u32[]{:S(2)}, u32[]{:S(2)}) %collective-permute-start.14) | collective-permute-done | bytes 589856 | tf_op jit(solution)/shard_map/ppermute | solution.py:498
  46.7 0.1 fusion.4
  46.7 1.6 %collective-permute-start.15 = (bf16[384,384]{1,0:T(8,128)(2,1)S(1)}, bf16[384,384]{1,0:T(8,128)(2,1)S(1)}, u32[]{:S(2)}, u32[]{:S(2)}) collective-permute-start(bf16[384,384]{1,0:T(8,128)(2,1)S(1)} %fusion.4), channel_id=1, source_target_pairs={{0,16},{8,24},{16,0},{24,8},{1,17},{9,25},{17,1},{25,9},{2,18},{10... | collective-permute-start | bytes 884744 | tf_op jit(solution)/shard_map/ppermute | solution.py:498
  48.4 0.0 collective-permute-done.16
  48.4 0.1 fusion
  48.4 1.6 %collective-permute-start.17 = (bf16[384,384]{1,0:T(8,128)(2,1)S(1)}, bf16[384,384]{1,0:T(8,128)(2,1)S(1)}, u32[]{:S(2)}, u32[]{:S(2)}) collective-permute-start(bf16[384,384]{1,0:T(8,128)(2,1)S(1)} %fusion), channel_id=1, source_target_pairs={{0,8},{8,0},{16,24},{24,16},{1,9},{9,1},{17,25},{25,17},{2,10},{10... | collective-permute-start | bytes 884744 | tf_op jit(solution)/shard_map/ppermute | solution.py:498
  50.0 9.3 %collective-permute-done.7 = bf16[2,384,384]{2,1,0:T(8,128)(2,1)S(1)} collective-permute-done((bf16[2,384,384]{2,1,0:T(8,128)(2,1)S(1)}, bf16[2,384,384]{2,1,0:T(8,128)(2,1)S(1)}, u32[]{:S(2)}, u32[]{:S(2)}) %collective-permute-start.7) | collective-permute-done | bytes 589856 | tf_op jit(solution)/shard_map/ppermute | solution.py:498
  59.3 0.1 fusion.10
  59.4 1.6 %collective-permute-start.8 = (bf16[384,384]{1,0:T(8,128)(2,1)S(1)}, bf16[384,384]{1,0:T(8,128)(2,1)S(1)}, u32[]{:S(2)}, u32[]{:S(2)}) collective-permute-start(bf16[384,384]{1,0:T(8,128)(2,1)S(1)} %fusion.10), channel_id=1, source_target_pairs={{0,16},{8,24},{16,0},{24,8},{1,17},{9,25},{17,1},{25,9},{2,18},{10... | collective-permute-start | bytes 884744 | tf_op jit(solution)/shard_map/ppermute | solution.py:498
  61.0 0.1 fusion.6
  61.1 1.6 %collective-permute-start.10 = (bf16[384,384]{1,0:T(8,128)(2,1)S(1)}, bf16[384,384]{1,0:T(8,128)(2,1)S(1)}, u32[]{:S(2)}, u32[]{:S(2)}) collective-permute-start(bf16[384,384]{1,0:T(8,128)(2,1)S(1)} %fusion.6), channel_id=1, source_target_pairs={{0,8},{8,0},{16,24},{24,16},{1,9},{9,1},{17,25},{25,17},{2,10},{10... | collective-permute-start | bytes 884744 | tf_op jit(solution)/shard_map/ppermute | solution.py:498
  62.6 4.6 %collective-permute-done.15 = bf16[384,384]{1,0:T(8,128)(2,1)S(1)} collective-permute-done((bf16[384,384]{1,0:T(8,128)(2,1)S(1)}, bf16[384,384]{1,0:T(8,128)(2,1)S(1)}, u32[]{:S(2)}, u32[]{:S(2)}) %collective-permute-start.15) | collective-permute-done | bytes 294944 | tf_op jit(solution)/shard_map/ppermute | solution.py:498
  67.2 0.0 collective-permute-done.17
  67.2 0.3 fusion.3.refs_0_
  67.5 1.6 %collective-permute-start.20 = (bf16[384,384]{1,0:T(8,128)(2,1)S(1)}, bf16[384,384]{1,0:T(8,128)(2,1)S(1)}, u32[]{:S(2)}, u32[]{:S(2)}) collective-permute-start(bf16[384,384]{1,0:T(8,128)(2,1)S(1)} %fusion.3.refs_0_), channel_id=1, source_target_pairs={{0,16},{8,24},{16,0},{24,8},{1,17},{9,25},{17,1},{25,9},{2,18},{10... | collective-permute-start | bytes 884744 | tf_op jit(solution)/shard_map/ppermute | solution.py:498
  69.1 0.5 collective-permute-start.19
  69.6 1.4 %collective-permute-start.18 = (bf16[384,384]{1,0:T(8,128)(2,1)S(1)}, bf16[384,384]{1,0:T(8,128)(2,1)S(1)}, u32[]{:S(2)}, u32[]{:S(2)}) collective-permute-start(bf16[384,384]{1,0:T(8,128)(2,1)S(1)} %fusion.3.refs_0_), channel_id=1, source_target_pairs={{0,24},{8,16},{16,8},{24,0},{1,25},{9,17},{17,9},{25,1},{2,26},{10... | collective-permute-start | bytes 884744 | tf_op jit(solution)/shard_map/ppermute | solution.py:498
  71.1 2.5 %collective-permute-done.8 = bf16[384,384]{1,0:T(8,128)(2,1)S(1)} collective-permute-done((bf16[384,384]{1,0:T(8,128)(2,1)S(1)}, bf16[384,384]{1,0:T(8,128)(2,1)S(1)}, u32[]{:S(2)}, u32[]{:S(2)}) %collective-permute-start.8) | collective-permute-done | bytes 294944 | tf_op jit(solution)/shard_map/ppermute | solution.py:498
  73.5 0.0 collective-permute-done.10
  73.5 0.3 fusion.9.refs_0_
  73.8 1.6 %collective-permute-start.13 = (bf16[384,384]{1,0:T(8,128)(2,1)S(1)}, bf16[384,384]{1,0:T(8,128)(2,1)S(1)}, u32[]{:S(2)}, u32[]{:S(2)}) collective-permute-start(bf16[384,384]{1,0:T(8,128)(2,1)S(1)} %fusion.9.refs_0_), channel_id=1, source_target_pairs={{0,16},{8,24},{16,0},{24,8},{1,17},{9,25},{17,1},{25,9},{2,18},{10... | collective-permute-start | bytes 884744 | tf_op jit(solution)/shard_map/ppermute | solution.py:498
  75.4 0.5 collective-permute-start.12
  76.0 10.2 %collective-permute-done.20.refs_3_ = bf16[384,384]{1,0:T(8,128)(2,1)S(1)} collective-permute-done((bf16[384,384]{1,0:T(8,128)(2,1)S(1)}, bf16[384,384]{1,0:T(8,128)(2,1)S(1)}, u32[]{:S(2)}, u32[]{:S(2)}) %collective-permute-start.20) | collective-permute-done | bytes 294944 | tf_op jit(solution)/shard_map/ppermute | solution.py:498
  86.2 1.5 %collective-permute-start.11 = (bf16[384,384]{1,0:T(8,128)(2,1)S(1)}, bf16[384,384]{1,0:T(8,128)(2,1)S(1)}, u32[]{:S(2)}, u32[]{:S(2)}) collective-permute-start(bf16[384,384]{1,0:T(8,128)(2,1)S(1)} %fusion.9.refs_0_), channel_id=1, source_target_pairs={{0,24},{8,16},{16,8},{24,0},{1,25},{9,17},{17,9},{25,1},{2,26},{10... | collective-permute-start | bytes 884744 | tf_op jit(solution)/shard_map/ppermute | solution.py:498
  87.7 4.1 %weigh.1 = (f32[1648,128]{1,0:T(8,128)S(1)}, bf16[8,128,1536]{2,1,0:T(8,128)(2,1)S(1)}) custom-call(s32[2,16]{1,0:T(2,128)S(1)} %get-tuple-element.26.refs_0_.offs, bf16[1648,1024]{1,0:T(8,128)(2,1)S(1)} %copy-done.5, f32[8,16,128]{2,1,0:T(8,128)S(1)} %get-tuple-element.41.probs), custom_call_target="tpu_custom_call" | custom-call | flops 6000000000 | bytes 8000000 | tf_op jit(solution)/shard_map/weigh/pallas_call | solution.py:274
  91.8 0.0 collective-permute-done.19.refs_2_
  91.9 5.6 %down.2.refs_4_ = f32[1648,512]{1,0:T(8,128)S(1)} custom-call(s32[2]{0:T(128)S(1)} %pad_add_fusion.me_ref, s32[2,16]{1,0:T(2,128)S(1)} %get-tuple-element.26.refs_0_.offs, bf16[16,768,512]{2,1,0:T(8,128)(2,1)S(1)} %bitcast.57, bf16[384,384]{1,0:T(8,128)(2,1)S(1)} %fusion.3.refs_0_, bf16[384,384]{1,0:T(8,128)(2,1)S(1)} %collective-permute-done.18.refs_1_, ...), custom_call_target="tpu_custom_call" | custom-call | flops 1296039936 | bytes 13041664 | tf_op jit(solution)/shard_map/down/pallas_call | solution.py:484
  97.4 0.3 collective-permute-done.13.refs_3_
  97.7 0.0 collective-permute-done.12.refs_2_
  97.7 0.0 collective-permute-done.11.refs_1_
  97.7 4.6 %copy-done = bf16[16,768,512]{2,1,0:T(8,128)(2,1)S(1)} copy-done((bf16[16,768,512]{2,1,0:T(8,128)(2,1)S(1)}, bf16[16,768,512]{2,1,0:T(8,128)(2,1)}, u32[]{:S(2)}) %copy-start) | copy-done | bytes 12582936
  102.3 7.6 %down.3 = (bf16[4,128,512]{2,1,0:T(8,128)(2,1)S(1)}, bf16[4,128,512]{2,1,0:T(8,128)(2,1)S(1)}) custom-call(s32[2]{0:T(128)S(1)} %pad_add_fusion.me_ref, s32[2,16]{1,0:T(2,128)S(1)} %get-tuple-element.26.refs_0_.offs, bf16[16,768,512]{2,1,0:T(8,128)(2,1)S(1)} %copy-done, bf16[384,384]{1,0:T(8,128)(2,1)S(1)} %fusion.9.refs_0_, ...), custom_call_target="tpu_custom_call" | custom-call | flops 1296039936 | bytes 13041664 | tf_op jit(solution)/shard_map/down/pallas_call | solution.py:484
  109.9 0.1 collective-permute-start.21
  110.0 1.9 %collective-permute-done.21 = bf16[4,128,512]{2,1,0:T(8,128)(2,1)S(1)} collective-permute-done((bf16[4,128,512]{2,1,0:T(8,128)(2,1)S(1)}, bf16[4,128,512]{2,1,0:T(8,128)(2,1)S(1)}, u32[]{:S(2)}, u32[]{:S(2)}) %collective-permute-start.21) | collective-permute-done | bytes 524320 | tf_op jit(solution)/shard_map/ppermute | solution.py:498
  111.9 0.2 fusion.14
  112.1 4.1 %collective-permute-start.22 = (bf16[128,512]{1,0:T(8,128)(2,1)S(1)}, bf16[128,512]{1,0:T(8,128)(2,1)S(1)}, u32[]{:S(2)}, u32[]{:S(2)}) collective-permute-start(bf16[128,512]{1,0:T(8,128)(2,1)S(1)} %get-tuple-element.49), channel_id=1, source_target_pairs={{0,6},{1,7},{2,4},{3,5},{4,2},{5,3},{6,0},{7,1},{8,14},{9,15},{10,... | collective-permute-start | bytes 393224 | tf_op jit(solution)/shard_map/ppermute | solution.py:498
  116.2 0.0 collective-permute-start.24
  116.2 0.6 collective-permute-start.23
  116.8 3.7 %collective-permute-done.22 = bf16[128,512]{1,0:T(8,128)(2,1)S(1)} collective-permute-done((bf16[128,512]{1,0:T(8,128)(2,1)S(1)}, bf16[128,512]{1,0:T(8,128)(2,1)S(1)}, u32[]{:S(2)}, u32[]{:S(2)}) %collective-permute-start.22) | collective-permute-done | bytes 131104 | tf_op jit(solution)/shard_map/ppermute | solution.py:498
  120.5 3.7 %collective-permute-done.24 = bf16[128,512]{1,0:T(8,128)(2,1)S(1)} collective-permute-done((bf16[128,512]{1,0:T(8,128)(2,1)S(1)}, bf16[128,512]{1,0:T(8,128)(2,1)S(1)}, u32[]{:S(2)}, u32[]{:S(2)}) %collective-permute-start.24) | collective-permute-done | bytes 131104 | tf_op jit(solution)/shard_map/ppermute | solution.py:498
  124.2 3.0 %collective-permute-done.23 = bf16[128,512]{1,0:T(8,128)(2,1)S(1)} collective-permute-done((bf16[128,512]{1,0:T(8,128)(2,1)S(1)}, bf16[128,512]{1,0:T(8,128)(2,1)S(1)}, u32[]{:S(2)}, u32[]{:S(2)}) %collective-permute-start.23) | collective-permute-done | bytes 131104 | tf_op jit(solution)/shard_map/ppermute | solution.py:498
  127.2 0.7 fusion.13
  (21 shorter events, 0.1 us)
Async XLA Ops:
  0.0 0.9 copy-start.1
  0.9 0.7 copy-start.2
  1.6 0.7 copy-start.3
  2.3 11.2 %collective-permute-start.3 = (bf16[144,512]{1,0:T(8,128)(2,1)S(1)}, bf16[144,512]{1,0:T(8,128)(2,1)S(1)}, u32[]{:S(2)}, u32[]{:S(2)}) collective-permute-start(bf16[144,512]{1,0:T(8,128)(2,1)S(1)} %pack.1.refs_0_), channel_id=1, source_target_pairs={{0,4},{1,5},{2,6},{3,7},{4,0},{5,1},{6,2},{7,3},{8,12},{9,13},{10,... | collective-permute-start | bytes 442376 | tf_op jit(solution)/shard_map/ppermute | solution.py:498
  6.4 8.2 %collective-permute-start.1 = (bf16[144,512]{1,0:T(8,128)(2,1)S(1)}, bf16[144,512]{1,0:T(8,128)(2,1)S(1)}, u32[]{:S(2)}, u32[]{:S(2)}) collective-permute-start(bf16[144,512]{1,0:T(8,128)(2,1)S(1)} %pack.1.refs_0_), channel_id=1, source_target_pairs={{0,2},{1,3},{2,0},{3,1},{4,6},{5,7},{6,4},{7,5},{8,10},{9,11},{10,... | collective-permute-start | bytes 442376 | tf_op jit(solution)/shard_map/ppermute | solution.py:498
  13.5 5.1 %collective-permute-start.5 = (bf16[144,512]{1,0:T(8,128)(2,1)S(1)}, bf16[144,512]{1,0:T(8,128)(2,1)S(1)}, u32[]{:S(2)}, u32[]{:S(2)}) collective-permute-start(bf16[144,512]{1,0:T(8,128)(2,1)S(1)} %collective-permute-done.3.refs_4_), channel_id=1, source_target_pairs={{0,2},{1,3},{2,0},{3,1},{4,6},{5,7},{6,4},{7,5},{8,10},{9,11},{10,... | collective-permute-start | bytes 442376 | tf_op jit(solution)/shard_map/ppermute | solution.py:498
  14.1 4.6 %collective-permute-start = (bf16[144,512]{1,0:T(8,128)(2,1)S(1)}, bf16[144,512]{1,0:T(8,128)(2,1)S(1)}, u32[]{:S(2)}, u32[]{:S(2)}) collective-permute-start(bf16[144,512]{1,0:T(8,128)(2,1)S(1)} %pack.1.refs_0_), channel_id=1, source_target_pairs={{0,1},{1,0},{2,3},{3,2},{4,5},{5,4},{6,7},{7,6},{8,9},{9,8},{10,11... | collective-permute-start | bytes 442376 | tf_op jit(solution)/shard_map/ppermute | solution.py:498
  14.1 4.6 %collective-permute-start.4 = (bf16[144,512]{1,0:T(8,128)(2,1)S(1)}, bf16[144,512]{1,0:T(8,128)(2,1)S(1)}, u32[]{:S(2)}, u32[]{:S(2)}) collective-permute-start(bf16[144,512]{1,0:T(8,128)(2,1)S(1)} %collective-permute-done.3.refs_4_), channel_id=1, source_target_pairs={{0,1},{1,0},{2,3},{3,2},{4,5},{5,4},{6,7},{7,6},{8,9},{9,8},{10,11... | collective-permute-start | bytes 442376 | tf_op jit(solution)/shard_map/ppermute | solution.py:498
  14.6 4.1 %collective-permute-start.2 = (bf16[144,512]{1,0:T(8,128)(2,1)S(1)}, bf16[144,512]{1,0:T(8,128)(2,1)S(1)}, u32[]{:S(2)}, u32[]{:S(2)}) collective-permute-start(bf16[144,512]{1,0:T(8,128)(2,1)S(1)} %collective-permute-done.1.refs_2_), channel_id=1, source_target_pairs={{0,1},{1,0},{2,3},{3,2},{4,5},{5,4},{6,7},{7,6},{8,9},{9,8},{10,11... | collective-permute-start | bytes 442376 | tf_op jit(solution)/shard_map/ppermute | solution.py:498
  18.7 1.4 %collective-permute-start.6 = (bf16[144,512]{1,0:T(8,128)(2,1)S(1)}, bf16[144,512]{1,0:T(8,128)(2,1)S(1)}, u32[]{:S(2)}, u32[]{:S(2)}) collective-permute-start(bf16[144,512]{1,0:T(8,128)(2,1)S(1)} %collective-permute-done.5.refs_6_), channel_id=1, source_target_pairs={{0,1},{1,0},{2,3},{3,2},{4,5},{5,4},{6,7},{7,6},{8,9},{9,8},{10,11... | collective-permute-start | bytes 442376 | tf_op jit(solution)/shard_map/ppermute | solution.py:498
  30.4 10.3 %copy-start.4 = (bf16[1648,1024]{1,0:T(8,128)(2,1)}, bf16[1648,1024]{1,0:T(8,128)(2,1)S(1)}, u32[]{:S(2)}) copy-start(bf16[1648,1024]{1,0:T(8,128)(2,1)S(1)} %get-tuple-element.40.select) | copy-start | bytes 10125316
  30.4 16.2 %collective-permute-start.14 = (bf16[2,384,384]{2,1,0:T(8,128)(2,1)S(1)}, bf16[2,384,384]{2,1,0:T(8,128)(2,1)S(1)}, u32[]{:S(2)}, u32[]{:S(2)}) collective-permute-start(bf16[2,384,384]{2,1,0:T(8,128)(2,1)S(1)} %get-tuple-element.35), channel_id=1, source_target_pairs={{0,8},{8,0},{16,24},{24,16},{1,9},{9,1},{17,25},{25,17},{2,10},{10... | collective-permute-start | bytes 1769480 | tf_op jit(solution)/shard_map/ppermute | solution.py:498
  32.0 16.3 %collective-permute-start.16 = (bf16[2,384,384]{2,1,0:T(8,128)(2,1)S(1)}, bf16[2,384,384]{2,1,0:T(8,128)(2,1)S(1)}, u32[]{:S(2)}, u32[]{:S(2)}) collective-permute-start(bf16[2,384,384]{2,1,0:T(8,128)(2,1)S(1)} %get-tuple-element.38), channel_id=1, source_target_pairs={{0,16},{8,24},{16,0},{24,8},{1,17},{9,25},{17,1},{25,9},{2,18},{10... | collective-permute-start | bytes 1769480 | tf_op jit(solution)/shard_map/ppermute | solution.py:498
  40.7 18.6 %collective-permute-start.7 = (bf16[2,384,384]{2,1,0:T(8,128)(2,1)S(1)}, bf16[2,384,384]{2,1,0:T(8,128)(2,1)S(1)}, u32[]{:S(2)}, u32[]{:S(2)}) collective-permute-start(bf16[2,384,384]{2,1,0:T(8,128)(2,1)S(1)} %get-tuple-element.29), channel_id=1, source_target_pairs={{0,8},{8,0},{16,24},{24,16},{1,9},{9,1},{17,25},{25,17},{2,10},{10... | collective-permute-start | bytes 1769480 | tf_op jit(solution)/shard_map/ppermute | solution.py:498
  41.3 19.7 %collective-permute-start.9 = (bf16[2,384,384]{2,1,0:T(8,128)(2,1)S(1)}, bf16[2,384,384]{2,1,0:T(8,128)(2,1)S(1)}, u32[]{:S(2)}, u32[]{:S(2)}) collective-permute-start(bf16[2,384,384]{2,1,0:T(8,128)(2,1)S(1)} %get-tuple-element.32), channel_id=1, source_target_pairs={{0,16},{8,24},{16,0},{24,8},{1,17},{9,25},{17,1},{25,9},{2,18},{10... | collective-permute-start | bytes 1769480 | tf_op jit(solution)/shard_map/ppermute | solution.py:498
  46.7 20.5 %collective-permute-start.15 = (bf16[384,384]{1,0:T(8,128)(2,1)S(1)}, bf16[384,384]{1,0:T(8,128)(2,1)S(1)}, u32[]{:S(2)}, u32[]{:S(2)}) collective-permute-start(bf16[384,384]{1,0:T(8,128)(2,1)S(1)} %fusion.4), channel_id=1, source_target_pairs={{0,16},{8,24},{16,0},{24,8},{1,17},{9,25},{17,1},{25,9},{2,18},{10... | collective-permute-start | bytes 884744 | tf_op jit(solution)/shard_map/ppermute | solution.py:498
  48.4 18.8 %collective-permute-start.17 = (bf16[384,384]{1,0:T(8,128)(2,1)S(1)}, bf16[384,384]{1,0:T(8,128)(2,1)S(1)}, u32[]{:S(2)}, u32[]{:S(2)}) collective-permute-start(bf16[384,384]{1,0:T(8,128)(2,1)S(1)} %fusion), channel_id=1, source_target_pairs={{0,8},{8,0},{16,24},{24,16},{1,9},{9,1},{17,25},{25,17},{2,10},{10... | collective-permute-start | bytes 884744 | tf_op jit(solution)/shard_map/ppermute | solution.py:498
  59.4 28.3 %copy-start.5 = (bf16[1648,1024]{1,0:T(8,128)(2,1)S(1)}, bf16[1648,1024]{1,0:T(8,128)(2,1)}, u32[]{:S(2)}) copy-start(bf16[1648,1024]{1,0:T(8,128)(2,1)} %copy-done.4) | copy-start | bytes 10125316
  59.4 14.1 %collective-permute-start.8 = (bf16[384,384]{1,0:T(8,128)(2,1)S(1)}, bf16[384,384]{1,0:T(8,128)(2,1)S(1)}, u32[]{:S(2)}, u32[]{:S(2)}) collective-permute-start(bf16[384,384]{1,0:T(8,128)(2,1)S(1)} %fusion.10), channel_id=1, source_target_pairs={{0,16},{8,24},{16,0},{24,8},{1,17},{9,25},{17,1},{25,9},{2,18},{10... | collective-permute-start | bytes 884744 | tf_op jit(solution)/shard_map/ppermute | solution.py:498
  61.1 12.4 %collective-permute-start.10 = (bf16[384,384]{1,0:T(8,128)(2,1)S(1)}, bf16[384,384]{1,0:T(8,128)(2,1)S(1)}, u32[]{:S(2)}, u32[]{:S(2)}) collective-permute-start(bf16[384,384]{1,0:T(8,128)(2,1)S(1)} %fusion.6), channel_id=1, source_target_pairs={{0,8},{8,0},{16,24},{24,16},{1,9},{9,1},{17,25},{25,17},{2,10},{10... | collective-permute-start | bytes 884744 | tf_op jit(solution)/shard_map/ppermute | solution.py:498
  67.5 18.6 %collective-permute-start.20 = (bf16[384,384]{1,0:T(8,128)(2,1)S(1)}, bf16[384,384]{1,0:T(8,128)(2,1)S(1)}, u32[]{:S(2)}, u32[]{:S(2)}) collective-permute-start(bf16[384,384]{1,0:T(8,128)(2,1)S(1)} %fusion.3.refs_0_), channel_id=1, source_target_pairs={{0,16},{8,24},{16,0},{24,8},{1,17},{9,25},{17,1},{25,9},{2,18},{10... | collective-permute-start | bytes 884744 | tf_op jit(solution)/shard_map/ppermute | solution.py:498
  69.1 22.7 %collective-permute-start.19 = (bf16[384,384]{1,0:T(8,128)(2,1)S(1)}, bf16[384,384]{1,0:T(8,128)(2,1)S(1)}, u32[]{:S(2)}, u32[]{:S(2)}) collective-permute-start(bf16[384,384]{1,0:T(8,128)(2,1)S(1)} %fusion.3.refs_0_), channel_id=1, source_target_pairs={{0,8},{8,0},{16,24},{24,16},{1,9},{9,1},{17,25},{25,17},{2,10},{10... | collective-permute-start | bytes 884744 | tf_op jit(solution)/shard_map/ppermute | solution.py:498
  69.6 22.2 %collective-permute-start.18 = (bf16[384,384]{1,0:T(8,128)(2,1)S(1)}, bf16[384,384]{1,0:T(8,128)(2,1)S(1)}, u32[]{:S(2)}, u32[]{:S(2)}) collective-permute-start(bf16[384,384]{1,0:T(8,128)(2,1)S(1)} %fusion.3.refs_0_), channel_id=1, source_target_pairs={{0,24},{8,16},{16,8},{24,0},{1,25},{9,17},{17,9},{25,1},{2,26},{10... | collective-permute-start | bytes 884744 | tf_op jit(solution)/shard_map/ppermute | solution.py:498
  73.5 18.3 %slice-start = ((s8[12582912]{0:T(1024)(128)(4,1)}), s8[4194304]{0:T(1024)(128)(4,1)S(1)}, s32[]{:S(2)}) async-start(s8[12582912]{0:T(1024)(128)(4,1)} %bitcast.56), calls=%async_computation | async-start | bytes 8388608
  73.8 23.8 %collective-permute-start.13 = (bf16[384,384]{1,0:T(8,128)(2,1)S(1)}, bf16[384,384]{1,0:T(8,128)(2,1)S(1)}, u32[]{:S(2)}, u32[]{:S(2)}) collective-permute-start(bf16[384,384]{1,0:T(8,128)(2,1)S(1)} %fusion.9.refs_0_), channel_id=1, source_target_pairs={{0,16},{8,24},{16,0},{24,8},{1,17},{9,25},{17,1},{25,9},{2,18},{10... | collective-permute-start | bytes 884744 | tf_op jit(solution)/shard_map/ppermute | solution.py:498
  75.4 22.3 %collective-permute-start.12 = (bf16[384,384]{1,0:T(8,128)(2,1)S(1)}, bf16[384,384]{1,0:T(8,128)(2,1)S(1)}, u32[]{:S(2)}, u32[]{:S(2)}) collective-permute-start(bf16[384,384]{1,0:T(8,128)(2,1)S(1)} %fusion.9.refs_0_), channel_id=1, source_target_pairs={{0,8},{8,0},{16,24},{24,16},{1,9},{9,1},{17,25},{25,17},{2,10},{10... | collective-permute-start | bytes 884744 | tf_op jit(solution)/shard_map/ppermute | solution.py:498
  86.2 11.5 %collective-permute-start.11 = (bf16[384,384]{1,0:T(8,128)(2,1)S(1)}, bf16[384,384]{1,0:T(8,128)(2,1)S(1)}, u32[]{:S(2)}, u32[]{:S(2)}) collective-permute-start(bf16[384,384]{1,0:T(8,128)(2,1)S(1)} %fusion.9.refs_0_), channel_id=1, source_target_pairs={{0,24},{8,16},{16,8},{24,0},{1,25},{9,17},{17,9},{25,1},{2,26},{10... | collective-permute-start | bytes 884744 | tf_op jit(solution)/shard_map/ppermute | solution.py:498
  87.7 4.2 %slice-start.1 = ((s8[12582912]{0:T(1024)(128)(4,1)}), s8[4194304]{0:T(1024)(128)(4,1)S(1)}, s32[]{:S(2)}) async-start(s8[12582912]{0:T(1024)(128)(4,1)} %bitcast.56), calls=%async_computation.1 | async-start | bytes 8388608
  87.7 4.2 %slice-start.2 = ((s8[12582912]{0:T(1024)(128)(4,1)}), s8[4194304]{0:T(1024)(128)(4,1)S(1)}, s32[]{:S(2)}) async-start(s8[12582912]{0:T(1024)(128)(4,1)} %bitcast.56), calls=%async_computation.2 | async-start | bytes 8388608
  97.7 4.6 %copy-start = (bf16[16,768,512]{2,1,0:T(8,128)(2,1)S(1)}, bf16[16,768,512]{2,1,0:T(8,128)(2,1)}, u32[]{:S(2)}) copy-start(bf16[16,768,512]{2,1,0:T(8,128)(2,1)} %w_down.3) | copy-start | bytes 37748740
  109.9 2.0 %collective-permute-start.21 = (bf16[4,128,512]{2,1,0:T(8,128)(2,1)S(1)}, bf16[4,128,512]{2,1,0:T(8,128)(2,1)S(1)}, u32[]{:S(2)}, u32[]{:S(2)}) collective-permute-start(bf16[4,128,512]{2,1,0:T(8,128)(2,1)S(1)} %get-tuple-element.46), channel_id=1, source_target_pairs={{0,1},{1,0},{2,3},{3,2},{4,5},{5,4},{6,7},{7,6},{8,9},{9,8},{10,11... | collective-permute-start | bytes 1572872 | tf_op jit(solution)/shard_map/ppermute | solution.py:498
  112.1 8.4 %collective-permute-start.22 = (bf16[128,512]{1,0:T(8,128)(2,1)S(1)}, bf16[128,512]{1,0:T(8,128)(2,1)S(1)}, u32[]{:S(2)}, u32[]{:S(2)}) collective-permute-start(bf16[128,512]{1,0:T(8,128)(2,1)S(1)} %get-tuple-element.49), channel_id=1, source_target_pairs={{0,6},{1,7},{2,4},{3,5},{4,2},{5,3},{6,0},{7,1},{8,14},{9,15},{10,... | collective-permute-start | bytes 393224 | tf_op jit(solution)/shard_map/ppermute | solution.py:498
  116.2 8.0 %collective-permute-start.24 = (bf16[128,512]{1,0:T(8,128)(2,1)S(1)}, bf16[128,512]{1,0:T(8,128)(2,1)S(1)}, u32[]{:S(2)}, u32[]{:S(2)}) collective-permute-start(bf16[128,512]{1,0:T(8,128)(2,1)S(1)} %get-tuple-element.50), channel_id=1, source_target_pairs={{0,2},{1,3},{2,0},{3,1},{4,6},{5,7},{6,4},{7,5},{8,10},{9,11},{10,... | collective-permute-start | bytes 393224 | tf_op jit(solution)/shard_map/ppermute | solution.py:498
  116.2 11.0 %collective-permute-start.23 = (bf16[128,512]{1,0:T(8,128)(2,1)S(1)}, bf16[128,512]{1,0:T(8,128)(2,1)S(1)}, u32[]{:S(2)}, u32[]{:S(2)}) collective-permute-start(bf16[128,512]{1,0:T(8,128)(2,1)S(1)} %get-tuple-element.51), channel_id=1, source_target_pairs={{0,4},{1,5},{2,6},{3,7},{4,0},{5,1},{6,2},{7,3},{8,12},{9,13},{10,... | collective-permute-start | bytes 393224 | tf_op jit(solution)/shard_map/ppermute | solution.py:498

commit v4 on v3

--- a/solution.py
+++ b/solution.py
@@ -30,7 +30,7 @@
 
 
 def hbm():
-    return pl.BlockSpec(memory_space=pl.ANY)
+    return pl.BlockSpec(memory_space=pltpu.HBM)
 
 
 def params(*shapes):
@@ -46,7 +46,7 @@
     return pl.CostEstimate(flops=int(flops), bytes_accessed=int(moved), transcendentals=0)
 
 
-def pack_kernel(dims, tokens, ids, weights, packed):
+def pack_kernel(dims, ids, weights, meta):
     rows, top = dims["rows"], dims["top"]
     chance = weights[...]
     chance = chance / jnp.sum(chance, axis=0, keepdims=True)
@@ -54,23 +54,22 @@
     rest = chance - high.astype(F32)
     middle = rest.astype(BF16)
     low = (rest - middle.astype(F32)).astype(BF16)
-    packed[:rows, :] = tokens[...]
-    packed[rows:, :] = jnp.zeros((META, packed.shape[1]), BF16)
+    meta[...] = jnp.zeros_like(meta)
     parts = (ids[...].astype(F32), high.astype(F32), middle.astype(F32), low.astype(F32))
     for i, part in enumerate(parts):
         block = jnp.concatenate([part, jnp.zeros((META - top, rows), F32)], axis=0)
-        packed[rows:, i * rows : (i + 1) * rows] = block.astype(BF16)
-
-
-def pack(dims, tokens, ids, weights):
+        meta[:, i * rows : (i + 1) * rows] = block.astype(BF16)
+
+
+def pack(dims, ids, weights, width):
     return pl.pallas_call(
         functools.partial(pack_kernel, dims),
-        out_shape=jax.ShapeDtypeStruct((dims["rows"] + META, tokens.shape[1]), BF16),
-        in_specs=[vmem()] * 3,
+        out_shape=jax.ShapeDtypeStruct((META, width), BF16),
+        in_specs=[vmem()] * 2,
         out_specs=vmem(),
         compiler_params=params(),
         name="pack",
-    )(tokens, ids.T, weights.T)
+    )(ids.T, weights.T)
 
 
 def loop(count, body, carry):
@@ -136,15 +135,15 @@
     return rowid[block, e : e + 1, :] == at
 
 
-def aligned(value):
-    return pl.multiple_of(value // ALIGN * ALIGN, ALIGN)
+def aligned(dims, value):
+    return pl.multiple_of(jnp.minimum(value // ALIGN * ALIGN, dims["total"]), ALIGN)
 
 
 def fill_select(dims, rowid, starts, select, step):
     rows = dims["rows"]
     select[...] = jnp.zeros_like(select)
     for e in range(dims["experts"]):
-        first = aligned(starts[e])
+        first = aligned(dims, starts[e])
         at = pl.ds(first, dims["window"])
         for inner in range(dims["group"]):
             cols = slice(inner * rows, (inner + 1) * rows)
@@ -160,17 +159,56 @@
     return starts
 
 
-def dispatch_kernel(dims, me_ref, gathered, rowid, probs, rowk, x, offs, select, total):
+def fullest(dims, meta):
+    blocks, rows, top, experts = dims["blocks"], dims["rows"], dims["top"], dims["experts"]
+    ids = [meta[b][:, :rows].astype(F32)[:top].astype(jnp.int32) for b in range(blocks)]
+    counts = []
+    for group in range(blocks):
+        mine = jnp.zeros((top, rows), F32)
+        for held_ids in ids:
+            inside = (held_ids >= group * experts) & (held_ids < (group + 1) * experts)
+            mine = mine + inside.astype(F32)
+        counts.append(jnp.sum(mine, axis=0, keepdims=True))
+    return jnp.max(jnp.sum(jnp.concatenate(counts, axis=0), axis=1, keepdims=True)).astype(jnp.int32)
+
+
+def route_kernel(dims, order, me_ref, packed, rowid, probs, rowk, select, offs, peak, meta):
+    for p, j in enumerate(order):
+        meta[me_ref[1] ^ j] = packed[p]
+    start, count = route(dims, me_ref[1] * dims["experts"], lambda b: meta[b], rowid, probs, rowk)
+    starts = publish(dims, offs, start, count)
+    peak[0] = fullest(dims, meta)
+    fill_select(dims, rowid, starts, select, 0)
+
+
+def route_rows(dims, order, me, packed):
+    shapes, offs = route_shapes(dims)
+    select = jax.ShapeDtypeStruct((dims["padded"], dims["blocks"] * dims["rows"]), BF16)
+    outs = shapes + (select, offs, jax.ShapeDtypeStruct((1,), jnp.int32))
+    scratch = pltpu.VMEM(packed.shape, BF16)
+    return pl.pallas_call(
+        functools.partial(route_kernel, dims, order),
+        out_shape=outs,
+        in_specs=[smem(), vmem()],
+        out_specs=(vmem(),) * 4 + (smem(),) * 2,
+        scratch_shapes=[scratch],
+        compiler_params=params(*outs, *held(packed), scratch),
+        cost_estimate=cost(4e9, 4e6),
+        name="route",
+    )(me, packed)
+
+
+def dispatch_kernel(dims, me_ref, packed, gathered, rowid, probs, rowk, x, offs, select, total):
     blocks, rows, group, tile = dims["blocks"], dims["rows"], dims["group"], dims["tile"]
     start, count = route(
-        dims, me_ref[1] * dims["experts"], lambda block: gathered[block, rows:, :], rowid, probs, rowk
+        dims, me_ref[1] * dims["experts"], lambda block: packed[block], rowid, probs, rowk
     )
     starts = publish(dims, offs, start, count)
     total[...] = jnp.zeros_like(total)
 
     def body(step, carry):
         fill_select(dims, rowid, starts, select, step)
-        part = gathered[pl.ds(step * group, group), :rows, :].reshape(group * rows, x.shape[1])
+        part = gathered[pl.ds(step * group, group)].reshape(group * rows, x.shape[1])
         for r in range(0, x.shape[0], tile):
             size = min(tile, x.shape[0] - r)
             got = jnp.dot(select[r : r + size, :], part, preferred_element_type=F32)
@@ -191,13 +229,13 @@
     ), jax.ShapeDtypeStruct((2, experts), jnp.int32)
 
 
-def dispatch(dims, me, gathered):
+def dispatch(dims, me, packed, gathered):
     shapes, offs = route_shapes(dims)
     width, padded = gathered.shape[2], dims["padded"]
     return pl.pallas_call(
         functools.partial(dispatch_kernel, dims),
         out_shape=shapes + (jax.ShapeDtypeStruct((padded, width), BF16), offs),
-        in_specs=[smem(), vmem()],
+        in_specs=[smem(), vmem(), vmem()],
         out_specs=(vmem(),) * 4 + (smem(),),
         scratch_shapes=[
             pltpu.VMEM((padded, dims["group"] * dims["rows"]), BF16),
@@ -205,7 +243,7 @@
         ],
         compiler_params=pltpu.CompilerParams(vmem_limit_bytes=VMEM_LIMIT),
         name="dispatch",
-    )(me, gathered)
+    )(me, packed, gathered)
 
 
 def choose(dims, rowk, block):
@@ -234,11 +272,13 @@
         middle = rest.astype(BF16)
         low = (rest - middle.astype(F32)).astype(BF16)
         table[:, cols] = jnp.concatenate([high, middle, low], axis=0)
-    wide = lax.dot_general(select[...], table[...], contract, preferred_element_type=F32)
+    wide = lax.dot_general(
+        select[: scale.shape[0], :], table[...], contract, preferred_element_type=F32
+    )
     scale[:, : 3 * experts] = wide
     lane = lax.broadcasted_iota(jnp.int32, (dims["window"], scale.shape[1]), 1)
     for e in range(experts):
-        first = aligned(offs[0, e])
+        first = aligned(dims, offs[0, e])
         at = pl.ds(first, dims["window"])
         old = scale[at, :]
         mine = (lane == e) | (lane == e + experts) | (lane == e + 2 * experts)
@@ -250,7 +290,7 @@
 def weigh_large_kernel(dims, offs, rowid, probs, scale, chosen):
     chosen[...] = jnp.zeros_like(chosen)
     for e in range(dims["experts"]):
-        first = aligned(offs[0, e])
+        first = aligned(dims, offs[0, e])
         at = pl.ds(first, dims["window"])
 
         def share(block, carry):
@@ -297,9 +337,8 @@
     experts, window, part, quarter = dims["experts"], dims["window"], dims["part"], dims["quarter"]
     if first_part:
         blocks, rows = dims["blocks"], dims["rows"]
-        packed, refs = refs[:blocks], refs[blocks:]
-        w_gate, w_up, rowid, probs, rowk, x, select, offs_out, refs = *refs[:8], refs[8:]
-        gx, uy, g2, u1, g0, u0, gate_w, up_w, gate, up, sems, table, meta = refs
+        offs, select, tokens, refs = refs[0], refs[1], refs[2 : 2 + blocks], refs[2 + blocks :]
+        w_gate, w_up, x, gx, uy, g2, u1, g0, u0, gate_w, up_w, gate, up, sems, table = refs
     else:
         offs, x, w_gate, w_up, gx, uy, g2, u1, g0, u0, gate_w, up_w, gate, up, sems = refs
     units = pl.ds(c * part, part)
@@ -314,15 +353,9 @@
         for copy in copies(e):
             copy.start()
     if first_part:
-        for j, block in enumerate(packed):
-            at = me_ref[1] ^ j
-            table[pl.ds(pl.multiple_of(at * rows, rows), rows), :] = block[:rows, :]
-            meta[at] = block[rows:, :]
-        start, count = route(
-            dims, me_ref[1] * experts, lambda block: meta[block], rowid, probs, rowk
-        )
-        offs = offs_out
-        fill_select(dims, rowid, publish(dims, offs, start, count), select, 0)
+        for j, block in enumerate(tokens):
+            at = pl.multiple_of((me_ref[1] ^ j) * rows, rows)
+            table[pl.ds(at, rows), :] = block[...]
         for r in range(0, x.shape[0], dims["tile"]):
             size = min(dims["tile"], x.shape[0] - r)
             got = jnp.dot(select[r : r + size, :], table[...], preferred_element_type=F32)
@@ -333,7 +366,7 @@
             for copy in copies(e):
                 copy.wait()
         for e in batch:
-            first = aligned(offs[0, e])
+            first = aligned(dims, offs[0, e])
             rows_in = x[pl.ds(first, window), :]
             keep = (lax.broadcasted_iota(jnp.int32, (ALIGN, 1), 0) + first) >= offs[0, e]
             edge, rest = pl.ds(first, ALIGN), pl.ds(first + ALIGN, window - ALIGN)
@@ -370,24 +403,14 @@
         pltpu.VMEM((padded, part), F32),
         pltpu.SemaphoreType.DMA((2, experts)),
     ]
-    into = (vmem(),) * len(outs)
     if first_part:
-        blocks, rows = dims["blocks"], dims["rows"]
-        shapes, offs = route_shapes(dims)
-        x = jax.ShapeDtypeStruct((padded, width), BF16)
-        select = jax.ShapeDtypeStruct((padded, blocks * rows), BF16)
-        outs = shapes + (x, select, offs) + outs
-        into = (vmem(),) * 5 + (smem(),) + into
-        scratch.append(pltpu.VMEM((blocks * rows, width), BF16))
-        scratch.append(pltpu.VMEM((blocks, META, width), BF16))
-        specs = [vmem()] * blocks
-    else:
-        specs = [smem(), vmem()]
+        outs = (jax.ShapeDtypeStruct((padded, width), BF16),) + outs
+        scratch.append(pltpu.VMEM((dims["blocks"] * dims["rows"], width), BF16))
     return pl.pallas_call(
         functools.partial(gate_up_kernel, dims, c, first_part),
         out_shape=outs,
-        in_specs=[smem()] + specs + [hbm(), hbm()],
-        out_specs=into,
+        in_specs=[smem(), smem()] + [vmem()] * (len(sources) - 1) + [hbm(), hbm()],
+        out_specs=(vmem(),) * len(outs),
         scratch_shapes=scratch,
         compiler_params=params(*outs, *held(*sources), *[b for b in scratch if "dma" not in str(b)]),
         cost_estimate=cost(4 * padded * width * part, 4 * experts * part * width + 2 * padded * width),
@@ -428,7 +451,7 @@
         for e in batch:
             copy(e).wait()
         for e in batch:
-            first = aligned(offs[0, e])
+            first = aligned(dims, offs[0, e])
             at = pl.ds(first, window)
             got = jnp.dot(hidden[at, :], held[e], preferred_element_type=F32)
             if y_in is not None:
@@ -514,13 +537,22 @@
 
 
 def gather_tokens(tokens):
-    held = {0: tokens}
+    blocks = {0: tokens}
     bit = lax.axis_size("exp") // 2
     while bit:
-        for known in list(held):
-            held[known | bit] = swap(held[known], "exp", bit)
+        for known in list(blocks):
+            blocks[known | bit] = swap(blocks[known], "exp", bit)
         bit //= 2
-    return [held[j] for j in range(len(held))]
+    return [blocks[j] for j in range(len(blocks))]
+
+
+def gather_meta(meta):
+    order, packed, bit = [0], meta[None], 1
+    while bit < lax.axis_size("exp"):
+        packed = jnp.concatenate([packed, swap(packed, "exp", bit)], axis=0)
+        order = order + [j | bit for j in order]
+        bit *= 2
+    return order, packed
 
 
 def sum_over_exp(stay, away):
@@ -542,43 +574,60 @@
     window = ceil_to(blocks * cap, ALIGN) + ALIGN
     part = units // 2
     small = blocks * rows * total <= 4 * 2**20
-    dims = dict(
-        blocks=blocks,
-        rows=rows,
-        top=top,
-        experts=experts,
-        window=window,
-        total=total,
-        quarter=total // replicas,
-        padded=total + window,
-        part=part,
-        group=min(blocks, 8),
-        tile=512,
-        small=small,
+
+    def sizes(total):
+        return dict(
+            blocks=blocks,
+            rows=rows,
+            top=top,
+            experts=experts,
+            window=window,
+            total=total,
+            quarter=total // replicas,
+            padded=total + window,
+            part=part,
+            group=min(blocks, 8),
+            tile=512,
+            small=small,
+        )
+
+    full = sizes(total)
+    me = jnp.stack([lax.axis_index("rep"), lax.axis_index("exp")]).astype(jnp.int32)
+    meta = pack(full, expert_ids, route_weights, width)
+    if not small:
+        packed = lax.all_gather(meta, "exp", axis=0)
+        gathered = lax.all_gather(tokens, "exp", axis=0)
+        rowid, probs, rowk, x, offs = dispatch(full, me, packed, gathered)
+        return one_pass(full, me, [offs, x], rowid, probs, rowk, w_gate, w_up, w_down)
+    blocks_of = gather_tokens(tokens)
+    order, packed = gather_meta(meta)
+    rowid, probs, rowk, select, offs, peak = route_rows(full, order, me, packed)
+    sources = [offs, select, *blocks_of]
+    usual = min(total, ceil_to(rows * top * 5 // 4, replicas * 64))
+    mixed = one_pass(sizes(usual), me, sources, select, probs, rowk, w_gate, w_up, w_down)
+    if usual == total:
+        return mixed
+    return lax.cond(
+        peak[0] > usual,
+        lambda: one_pass(full, me, sources, select, probs, rowk, w_gate, w_up, w_down),
+        lambda: mixed,
     )
-    me = jnp.stack([lax.axis_index("rep"), lax.axis_index("exp")]).astype(jnp.int32)
-    packed = pack(dims, tokens, expert_ids, route_weights)
-    if small:
-        sources = gather_tokens(packed)
-    else:
-        gathered = lax.all_gather(packed, "exp", axis=0)
-        rowid, probs, rowk, x, offs = dispatch(dims, me, gathered)
-        rows_of, sources = rowid, [offs, x]
-
-    pieces = []
-    for c in range(units // part):
+
+
+def one_pass(dims, me, sources, rows_of, probs, rowk, w_gate, w_up, w_down):
+    pieces, offs = [], sources[0]
+    scale, chosen = weigh(dims, offs, rows_of, probs)
+    for c in range(w_gate.shape[1] // dims["part"]):
         parts = gate_up(dims, c, me, sources, w_gate, w_up)
         if len(sources) > 2:
-            rowid, probs, rowk, x, rows_of, offs = parts[:6]
-            sources, parts = [offs, x], parts[6:]
+            sources, parts = [offs, parts[0]], parts[1:]
         pieces.append(spread_chunk(reduce_chunk(parts)))
-    scale, chosen = weigh(dims, offs, rows_of, probs)
     y = None
     last = len(pieces) - 1
     for c in range(last):
         y = down(dims, c, False, me, offs, w_down, pieces[c], y, ())[0]
     mixed = down(dims, last, True, me, offs, w_down, pieces[last], y, (scale, chosen, rowk))
-    if small:
+    if dims["small"]:
         return sum_over_exp(*mixed)
     return lax.psum_scatter(mixed[0], "exp", scatter_dimension=0, tiled=False)
 

time: 128 us -> 137 us (1.070)
  Pallas kernels: 34.8 us -> 42.6 us
  local copies, waits for them, and re-layouts: 6.9 us -> 3.51 us
  waiting for transfers between devices: 54.8 us -> 57.6 us
  starting transfers between devices: 29.3 us -> 30.9 us
    pallas_call x0 -> x1, Pallas kernels: none -> 4.32 us  [route_rows(): pl.pallas_call(functools.partial(route_kernel, dims, order), out_shape=ou...]
    unnamed x18 -> x16, local copies, waits for them, and re-layouts: 6.87 us -> 3.48 us
    ppermute x25 -> x28, waiting for transfers between devices: 54.8 us -> 57.6 us  [swap(): return lax.ppermute(value, axis, [(i, i ^ bit) for i in range(count)])]
    pallas_call x2, Pallas kernels: 17.5 us -> 20 us  [gate_up(): pl.pallas_call(functools.partial(gate_up_kernel, dims, c, first_part), ou...]
    ppermute x25 -> x28, starting transfers between devices: 29.3 us -> 30.9 us  [swap(): return lax.ppermute(value, axis, [(i, i ^ bit) for i in range(count)])]
  transfers between devices with their start and end apart: 25 -> 28, of which waited for: 13 -> 14; matrix products, arithmetic and copies ran while one was open for 1% -> 1% of each run, Pallas kernels for 13% -> 11%
where the time goes in v4:
time: 137 us
  waiting for transfers between devices  57.6 us (42%)
  Pallas kernels  42.6 us (31%)
  starting transfers between devices  30.9 us (23%)
  local copies, waits for them, and re-layouts  3.51 us (3%)
    ppermute x28, waiting for transfers between devices, swap(): return lax.ppermute(value, axis, [(i, i ^ bit) for i in range(count)])  57.6 us
    ppermute x28, starting transfers between devices, swap(): return lax.ppermute(value, axis, [(i, i ^ bit) for i in range(count)])  30.9 us
    pallas_call x2, Pallas kernels, gate_up(): pl.pallas_call(functools.partial(gate_up_kernel, dims, c, first_part), ou...  20 us
    pallas_call x2, Pallas kernels, down(): pl.pallas_call(functools.partial(down_kernel, dims, c, last), out_shape=o...  13.1 us
    pallas_call x1, Pallas kernels, weigh(): pl.pallas_call(functools.partial(weigh_small_kernel if small else weigh_l...  5.22 us
    pallas_call x1, Pallas kernels, route_rows(): pl.pallas_call(functools.partial(route_kernel, dims, order), out_shape=ou...  4.32 us
    unnamed x16, local copies, waits for them, and re-layouts  3.48 us
  transfers between devices with their start and end apart: 28, of which 14 were waited for; matrix products, arithmetic and copies ran while one was open for 1% of the time, Pallas kernels for 11%

profile of v4, /device:TPU:0, one launch (start us, length us, event | category | flops | bytes accessed | tf_op | source)
XLA Modules:
  0.0 136.9 jit_solution(12803180323130995546)
XLA Ops:
  0.0 0.7 copy-done
  0.7 0.7 copy-done.1
  1.4 0.5 collective-permute-start.18
  1.9 0.8 collective-permute-done.18
  2.8 2.9 %collective-permute-start.19 = (bf16[2,16,512]{2,1,0:T(8,128)(2,1)S(1)}, bf16[2,16,512]{2,1,0:T(8,128)(2,1)S(1)}, u32[]{:S(2)}, u32[]{:S(2)}) collective-permute-start(bf16[2,16,512]{2,1,0:T(8,128)(2,1)S(1)} %pad_maximum_fusion.2), channel_id=1, source_target_pairs={{0,2},{1,3},{2,0},{3,1},{4,6},{5,7},{6,4},{7,5},{8,10},{9,11},{10,... | collective-permute-start | bytes 98312 | tf_op jit(solution)/shard_map/ppermute | solution.py:521
  5.7 2.6 %collective-permute-start.24 = (bf16[128,512]{1,0:T(8,128)(2,1)}, bf16[128,512]{1,0:T(8,128)(2,1)S(1)}, u32[]{:S(2)}, u32[]{:S(2)}) collective-permute-start(bf16[128,512]{1,0:T(8,128)(2,1)} %refs_2_.2), channel_id=1, source_target_pairs={{0,4},{1,5},{2,6},{3,7},{4,0},{5,1},{6,2},{7,3},{8,12},{9,13},{10,... | collective-permute-start | bytes 393224 | tf_op jit(solution)/shard_map/ppermute | solution.py:521
  8.3 0.4 collective-permute-start.22
  8.7 0.0 collective-permute-done.19
  8.7 2.3 %collective-permute-start.20 = (bf16[4,16,512]{2,1,0:T(8,128)(2,1)S(1)}, bf16[4,16,512]{2,1,0:T(8,128)(2,1)S(1)}, u32[]{:S(2)}, u32[]{:S(2)}) collective-permute-start(bf16[4,16,512]{2,1,0:T(8,128)(2,1)S(1)} %pad_maximum_fusion.1), channel_id=1, source_target_pairs={{0,4},{1,5},{2,6},{3,7},{4,0},{5,1},{6,2},{7,3},{8,12},{9,13},{10,... | collective-permute-start | bytes 196616 | tf_op jit(solution)/shard_map/ppermute | solution.py:521
  11.0 5.0 %collective-permute-done.24.refs_6_ = bf16[128,512]{1,0:T(8,128)(2,1)S(1)} collective-permute-done((bf16[128,512]{1,0:T(8,128)(2,1)}, bf16[128,512]{1,0:T(8,128)(2,1)S(1)}, u32[]{:S(2)}, u32[]{:S(2)}) %collective-permute-start.24) | collective-permute-done | bytes 131104 | tf_op jit(solution)/shard_map/ppermute | solution.py:521
  15.9 0.0 collective-permute-start.26
  16.0 0.1 pad_add_fusion.me_ref
  16.1 1.8 %collective-permute-done.20 = bf16[4,16,512]{2,1,0:T(8,128)(2,1)S(1)} collective-permute-done((bf16[4,16,512]{2,1,0:T(8,128)(2,1)S(1)}, bf16[4,16,512]{2,1,0:T(8,128)(2,1)S(1)}, u32[]{:S(2)}, u32[]{:S(2)}) %collective-permute-start.20) | collective-permute-done | bytes 65568 | tf_op jit(solution)/shard_map/ppermute | solution.py:521
  17.8 0.0 copy-start.3
  17.8 0.1 collective-permute-start.25
  17.9 0.6 collective-permute-done.22.refs_4_
  18.5 0.0 collective-permute-start.23
  18.5 2.6 %collective-permute-done.26.refs_8_ = bf16[128,512]{1,0:T(8,128)(2,1)S(1)} collective-permute-done((bf16[128,512]{1,0:T(8,128)(2,1)S(1)}, bf16[128,512]{1,0:T(8,128)(2,1)S(1)}, u32[]{:S(2)}, u32[]{:S(2)}) %collective-permute-start.26) | collective-permute-done | bytes 131104 | tf_op jit(solution)/shard_map/ppermute | solution.py:521
  21.1 0.0 collective-permute-start.27
  21.1 4.3 %route.1 = (s32[8,16,128]{2,1,0:T(8,128)}, f32[8,16,128]{2,1,0:T(8,128)S(1)}, s32[8,8,128]{2,1,0:T(8,128)S(1)}, bf16[1648,1024]{1,0:T(8,128)(2,1)}, s32[2,16]{1,0:T(2,128)S(1)}, /*index=5*/s32[1]{0:T(128)}) custom-call(s32[2]{0:T(128)S(1)} %pad_add_fusion.me_ref, bf16[8,16,512]{2,1,0:T(8,128)(2,1)S(1)} %pad_maximum_fusion.packed), custom_call_target="tpu_custom_call" | custom-call | flops 4000000000 | bytes 4000000 | tf_op jit(solution)/shard_map/route/pallas_call | solution.py:189
  25.4 1.4 %copy-done.2 = bf16[16,768,512]{2,1,0:T(8,128)(2,1)S(1)} copy-done((bf16[16,768,512]{2,1,0:T(8,128)(2,1)S(1)}, bf16[16,768,512]{2,1,0:T(8,128)(2,1)}, u32[]{:S(2)}) %copy-start.2) | copy-done | bytes 12582936
  26.9 11.6 %gate_up.6 = (bf16[1392,512]{1,0:T(8,128)(2,1)S(1)}, bf16[2,320,384]{2,1,0:T(8,128)(2,1)S(1)}, bf16[2,320,384]{2,1,0:T(8,128)(2,1)S(1)}, f32[320,384]{1,0:T(8,12...) custom-call(s32[2]{0:T(128)S(1)} %pad_add_fusion.me_ref, ...), custom_call_target="tpu_custom_call" | custom-call | flops 1094713344 | bytes 14008320 | tf_op jit(solution)/shard_map/gate_up/pallas_call | solution.py:409
  38.5 8.3 %gate_up.7 = (bf16[2,320,384]{2,1,0:T(8,128)(2,1)S(1)}, bf16[2,320,384]{2,1,0:T(8,128)(2,1)S(1)}, f32[320,384]{1,0:T(8,128)S(1)}, f32[320,384]{1,0:T(8,128)S(1)}...) custom-call(s32[2]{0:T(128)S(1)} %pad_add_fusion.me_ref, s32[2,16]{1,0:T(2,128)S(1)} %get-tuple-element.97.refs_0_.offs, ...), custom_call_target="tpu_custom_call" | custom-call | flops 1094713344 | bytes 14008320 | tf_op jit(solution)/shard_map/gate_up/pallas_call | solution.py:409
  46.8 1.6 %collective-permute-start.30 = (bf16[2,320,384]{2,1,0:T(8,128)(2,1)S(1)}, bf16[2,320,384]{2,1,0:T(8,128)(2,1)S(1)}, u32[]{:S(2)}, u32[]{:S(2)}) collective-permute-start(bf16[2,320,384]{2,1,0:T(8,128)(2,1)S(1)} %get-tuple-element.104), channel_id=1, source_target_pairs={{0,16},{8,24},{16,0},{24,8},{1,17},{9,25},{17,1},{25,9},{2,18},{10... | collective-permute-start | bytes 1474568 | tf_op jit(solution)/shard_map/ppermute | solution.py:521
  48.4 0.5 collective-permute-start.37
  48.9 1.5 %collective-permute-start.28 = (bf16[2,320,384]{2,1,0:T(8,128)(2,1)S(1)}, bf16[2,320,384]{2,1,0:T(8,128)(2,1)S(1)}, u32[]{:S(2)}, u32[]{:S(2)}) collective-permute-start(bf16[2,320,384]{2,1,0:T(8,128)(2,1)S(1)} %get-tuple-element.101), channel_id=1, source_target_pairs={{0,8},{8,0},{16,24},{24,16},{1,9},{9,1},{17,25},{25,17},{2,10},{10... | collective-permute-start | bytes 1474568 | tf_op jit(solution)/shard_map/ppermute | solution.py:521
  50.4 0.5 collective-permute-start.35
  51.0 10.0 %collective-permute-done.30 = bf16[2,320,384]{2,1,0:T(8,128)(2,1)S(1)} collective-permute-done((bf16[2,320,384]{2,1,0:T(8,128)(2,1)S(1)}, bf16[2,320,384]{2,1,0:T(8,128)(2,1)S(1)}, u32[]{:S(2)}, u32[]{:S(2)}) %collective-permute-start.30) | collective-permute-done | bytes 491552 | tf_op jit(solution)/shard_map/ppermute | solution.py:521
  60.9 0.1 fusion.21
  61.0 1.6 %collective-permute-start.31 = (bf16[320,384]{1,0:T(8,128)(2,1)S(1)}, bf16[320,384]{1,0:T(8,128)(2,1)S(1)}, u32[]{:S(2)}, u32[]{:S(2)}) collective-permute-start(bf16[320,384]{1,0:T(8,128)(2,1)S(1)} %fusion.21), channel_id=1, source_target_pairs={{0,8},{8,0},{16,24},{24,16},{1,9},{9,1},{17,25},{25,17},{2,10},{10... | collective-permute-start | bytes 737288 | tf_op jit(solution)/shard_map/ppermute | solution.py:521
  62.5 8.5 %collective-permute-done.37 = bf16[2,320,384]{2,1,0:T(8,128)(2,1)S(1)} collective-permute-done((bf16[2,320,384]{2,1,0:T(8,128)(2,1)S(1)}, bf16[2,320,384]{2,1,0:T(8,128)(2,1)S(1)}, u32[]{:S(2)}, u32[]{:S(2)}) %collective-permute-start.37) | collective-permute-done | bytes 491552 | tf_op jit(solution)/shard_map/ppermute | solution.py:521
  71.1 0.1 fusion.15
  71.1 1.6 %collective-permute-start.38 = (bf16[320,384]{1,0:T(8,128)(2,1)S(1)}, bf16[320,384]{1,0:T(8,128)(2,1)S(1)}, u32[]{:S(2)}, u32[]{:S(2)}) collective-permute-start(bf16[320,384]{1,0:T(8,128)(2,1)S(1)} %fusion.15), channel_id=1, source_target_pairs={{0,8},{8,0},{16,24},{24,16},{1,9},{9,1},{17,25},{25,17},{2,10},{10... | collective-permute-start | bytes 737288 | tf_op jit(solution)/shard_map/ppermute | solution.py:521
  72.7 0.9 collective-permute-done.35
  73.6 0.1 fusion.19
  73.6 1.6 %collective-permute-start.36 = (bf16[320,384]{1,0:T(8,128)(2,1)S(1)}, bf16[320,384]{1,0:T(8,128)(2,1)S(1)}, u32[]{:S(2)}, u32[]{:S(2)}) collective-permute-start(bf16[320,384]{1,0:T(8,128)(2,1)S(1)} %fusion.19), channel_id=1, source_target_pairs={{0,16},{8,24},{16,0},{24,8},{1,17},{9,25},{17,1},{25,9},{2,18},{10... | collective-permute-start | bytes 737288 | tf_op jit(solution)/shard_map/ppermute | solution.py:521
  75.2 0.1 fusion.25
  75.3 0.6 collective-permute-start.29
  75.8 7.2 %collective-permute-done.38 = bf16[320,384]{1,0:T(8,128)(2,1)S(1)} collective-permute-done((bf16[320,384]{1,0:T(8,128)(2,1)S(1)}, bf16[320,384]{1,0:T(8,128)(2,1)S(1)}, u32[]{:S(2)}, u32[]{:S(2)}) %collective-permute-start.38) | collective-permute-done | bytes 245792 | tf_op jit(solution)/shard_map/ppermute | solution.py:521
  83.1 0.3 fusion.18.refs_0_
  83.3 2.5 %collective-permute-start.39 = (bf16[320,384]{1,0:T(8,128)(2,1)S(1)}, bf16[320,384]{1,0:T(8,128)(2,1)S(1)}, u32[]{:S(2)}, u32[]{:S(2)}) collective-permute-start(bf16[320,384]{1,0:T(8,128)(2,1)S(1)} %fusion.18.refs_0_), channel_id=1, source_target_pairs={{0,24},{8,16},{16,8},{24,0},{1,25},{9,17},{17,9},{25,1},{2,26},{10... | collective-permute-start | bytes 737288 | tf_op jit(solution)/shard_map/ppermute | solution.py:521
  85.9 0.3 fusion.24.refs_0_
  86.1 1.5 %collective-permute-start.32 = (bf16[320,384]{1,0:T(8,128)(2,1)S(1)}, bf16[320,384]{1,0:T(8,128)(2,1)S(1)}, u32[]{:S(2)}, u32[]{:S(2)}) collective-permute-start(bf16[320,384]{1,0:T(8,128)(2,1)S(1)} %fusion.24.refs_0_), channel_id=1, source_target_pairs={{0,24},{8,16},{16,8},{24,0},{1,25},{9,17},{17,9},{25,1},{2,26},{10... | collective-permute-start | bytes 737288 | tf_op jit(solution)/shard_map/ppermute | solution.py:521
  87.7 1.0 collective-permute-start.33
  88.7 1.0 collective-permute-start.34
  89.7 0.5 collective-permute-start.40
  90.2 3.1 %collective-permute-done.39.refs_1_ = bf16[320,384]{1,0:T(8,128)(2,1)S(1)} collective-permute-done((bf16[320,384]{1,0:T(8,128)(2,1)S(1)}, bf16[320,384]{1,0:T(8,128)(2,1)S(1)}, u32[]{:S(2)}, u32[]{:S(2)}) %collective-permute-start.39) | collective-permute-done | bytes 245792 | tf_op jit(solution)/shard_map/ppermute | solution.py:521
  93.3 1.5 %collective-permute-start.41 = (bf16[320,384]{1,0:T(8,128)(2,1)S(1)}, bf16[320,384]{1,0:T(8,128)(2,1)S(1)}, u32[]{:S(2)}, u32[]{:S(2)}) collective-permute-start(bf16[320,384]{1,0:T(8,128)(2,1)S(1)} %fusion.18.refs_0_), channel_id=1, source_target_pairs={{0,16},{8,24},{16,0},{24,8},{1,17},{9,25},{17,1},{25,9},{2,18},{10... | collective-permute-start | bytes 737288 | tf_op jit(solution)/shard_map/ppermute | solution.py:521
  94.8 5.2 %weigh.3 = (f32[1392,128]{1,0:T(8,128)S(1)}, bf16[8,128,1280]{2,1,0:T(8,128)(2,1)S(1)}) custom-call(s32[2,16]{1,0:T(2,128)S(1)} %get-tuple-element.97.refs_0_.offs, bf16[1648,1024]{1,0:T(8,128)(2,1)} %get-tuple-element.98.refs_1_.select, f32[8,16,128]{2,1,0:T(8,128)S(1)} %get-tuple-element.112.probs), custom_call_target="tpu_custom_call" | custom-call | flops 6000000000 | bytes 8000000 | tf_op jit(solution)/shard_map/weigh/pallas_call | solution.py:314
  100.1 7.1 %collective-permute-done.40.refs_2_ = bf16[320,384]{1,0:T(8,128)(2,1)S(1)} collective-permute-done((bf16[320,384]{1,0:T(8,128)(2,1)S(1)}, bf16[320,384]{1,0:T(8,128)(2,1)S(1)}, u32[]{:S(2)}, u32[]{:S(2)}) %collective-permute-start.40) | collective-permute-done | bytes 245792 | tf_op jit(solution)/shard_map/ppermute | solution.py:521
  107.2 5.8 %down.6.refs_4_ = f32[1392,512]{1,0:T(8,128)S(1)} custom-call(s32[2]{0:T(128)S(1)} %pad_add_fusion.me_ref, s32[2,16]{1,0:T(2,128)S(1)} %get-tuple-element.97.refs_0_.offs, bf16[16,768,512]{2,1,0:T(8,128)(2,1)S(1)} %bitcast.117, bf16[320,384]{1,0:T(8,128)(2,1)S(1)} %fusion.18.refs_0_, bf16[320,384]{1,0:T(8,128)(2,1)S(1)} %collective-permute-done.39.refs_1_, ...), custom_call_target="tpu_custom_call" | custom-call | flops 1094713344 | bytes 11993088 | tf_op jit(solution)/shard_map/down/pallas_call | solution.py:507
  113.0 7.3 %down.7 = (bf16[4,128,512]{2,1,0:T(8,128)(2,1)S(1)}, bf16[4,128,512]{2,1,0:T(8,128)(2,1)S(1)}) custom-call(s32[2]{0:T(128)S(1)} %pad_add_fusion.me_ref, s32[2,16]{1,0:T(2,128)S(1)} %get-tuple-element.97.refs_0_.offs, bf16[16,768,512]{2,1,0:T(8,128)(2,1)S(1)} %bitcast.117, bf16[320,384]{1,0:T(8,128)(2,1)S(1)} %fusion.24.refs_0_, ...), custom_call_target="tpu_custom_call" | custom-call | flops 1094713344 | bytes 11993088 | tf_op jit(solution)/shard_map/down/pallas_call | solution.py:507
  120.3 0.1 collective-permute-start.42
  120.4 1.9 %collective-permute-done.42 = bf16[4,128,512]{2,1,0:T(8,128)(2,1)S(1)} collective-permute-done((bf16[4,128,512]{2,1,0:T(8,128)(2,1)S(1)}, bf16[4,128,512]{2,1,0:T(8,128)(2,1)S(1)}, u32[]{:S(2)}, u32[]{:S(2)}) %collective-permute-start.42) | collective-permute-done | bytes 524320 | tf_op jit(solution)/shard_map/ppermute | solution.py:521
  122.3 0.2 fusion.29
  122.5 0.1 collective-permute-start.45
  122.6 3.2 %collective-permute-start.44 = (bf16[128,512]{1,0:T(8,128)(2,1)S(1)}, bf16[128,512]{1,0:T(8,128)(2,1)S(1)}, u32[]{:S(2)}, u32[]{:S(2)}) collective-permute-start(bf16[128,512]{1,0:T(8,128)(2,1)S(1)} %get-tuple-element.128), channel_id=1, source_target_pairs={{0,4},{1,5},{2,6},{3,7},{4,0},{5,1},{6,2},{7,3},{8,12},{9,13},{10,... | collective-permute-start | bytes 393224 | tf_op jit(solution)/shard_map/ppermute | solution.py:521
  125.8 1.1 collective-permute-start.43
  127.7 2.8 %collective-permute-done.45 = bf16[128,512]{1,0:T(8,128)(2,1)S(1)} collective-permute-done((bf16[128,512]{1,0:T(8,128)(2,1)S(1)}, bf16[128,512]{1,0:T(8,128)(2,1)S(1)}, u32[]{:S(2)}, u32[]{:S(2)}) %collective-permute-start.45) | collective-permute-done | bytes 131104 | tf_op jit(solution)/shard_map/ppermute | solution.py:521
  130.4 5.4 %collective-permute-done.44 = bf16[128,512]{1,0:T(8,128)(2,1)S(1)} collective-permute-done((bf16[128,512]{1,0:T(8,128)(2,1)S(1)}, bf16[128,512]{1,0:T(8,128)(2,1)S(1)}, u32[]{:S(2)}, u32[]{:S(2)}) %collective-permute-start.44) | collective-permute-done | bytes 131104 | tf_op jit(solution)/shard_map/ppermute | solution.py:521
  135.8 0.1 fusion.28
  135.9 0.3 conditional.1
  136.2 0.0 copy-start.4
  136.2 0.6 copy-done.4
  (30 shorter events, 0.1 us)
Async XLA Ops:
  0.0 0.7 copy-start
  0.7 0.7 copy-start.1
  1.4 1.4 collective-permute-start.18
  2.8 6.0 %collective-permute-start.19 = (bf16[2,16,512]{2,1,0:T(8,128)(2,1)S(1)}, bf16[2,16,512]{2,1,0:T(8,128)(2,1)S(1)}, u32[]{:S(2)}, u32[]{:S(2)}) collective-permute-start(bf16[2,16,512]{2,1,0:T(8,128)(2,1)S(1)} %pad_maximum_fusion.2), channel_id=1, source_target_pairs={{0,2},{1,3},{2,0},{3,1},{4,6},{5,7},{6,4},{7,5},{8,10},{9,11},{10,... | collective-permute-start | bytes 98312 | tf_op jit(solution)/shard_map/ppermute | solution.py:521
  5.7 10.3 %collective-permute-start.24 = (bf16[128,512]{1,0:T(8,128)(2,1)}, bf16[128,512]{1,0:T(8,128)(2,1)S(1)}, u32[]{:S(2)}, u32[]{:S(2)}) collective-permute-start(bf16[128,512]{1,0:T(8,128)(2,1)} %refs_2_.2), channel_id=1, source_target_pairs={{0,4},{1,5},{2,6},{3,7},{4,0},{5,1},{6,2},{7,3},{8,12},{9,13},{10,... | collective-permute-start | bytes 393224 | tf_op jit(solution)/shard_map/ppermute | solution.py:521
  8.3 17.1 %collective-permute-start.21 = (bf16[128,512]{1,0:T(8,128)(2,1)}, bf16[128,512]{1,0:T(8,128)(2,1)S(1)}, u32[]{:S(2)}, u32[]{:S(2)}) collective-permute-start(bf16[128,512]{1,0:T(8,128)(2,1)} %refs_2_.2), channel_id=1, source_target_pairs={{0,1},{1,0},{2,3},{3,2},{4,5},{5,4},{6,7},{7,6},{8,9},{9,8},{10,11... | collective-permute-start | bytes 393224 | tf_op jit(solution)/shard_map/ppermute | solution.py:521
  8.3 10.2 %collective-permute-start.22 = (bf16[128,512]{1,0:T(8,128)(2,1)}, bf16[128,512]{1,0:T(8,128)(2,1)S(1)}, u32[]{:S(2)}, u32[]{:S(2)}) collective-permute-start(bf16[128,512]{1,0:T(8,128)(2,1)} %refs_2_.2), channel_id=1, source_target_pairs={{0,2},{1,3},{2,0},{3,1},{4,6},{5,7},{6,4},{7,5},{8,10},{9,11},{10,... | collective-permute-start | bytes 393224 | tf_op jit(solution)/shard_map/ppermute | solution.py:521
  8.7 9.1 %collective-permute-start.20 = (bf16[4,16,512]{2,1,0:T(8,128)(2,1)S(1)}, bf16[4,16,512]{2,1,0:T(8,128)(2,1)S(1)}, u32[]{:S(2)}, u32[]{:S(2)}) collective-permute-start(bf16[4,16,512]{2,1,0:T(8,128)(2,1)S(1)} %pad_maximum_fusion.1), channel_id=1, source_target_pairs={{0,4},{1,5},{2,6},{3,7},{4,0},{5,1},{6,2},{7,3},{8,12},{9,13},{10,... | collective-permute-start | bytes 196616 | tf_op jit(solution)/shard_map/ppermute | solution.py:521
  15.9 5.1 %collective-permute-start.26 = (bf16[128,512]{1,0:T(8,128)(2,1)S(1)}, bf16[128,512]{1,0:T(8,128)(2,1)S(1)}, u32[]{:S(2)}, u32[]{:S(2)}) collective-permute-start(bf16[128,512]{1,0:T(8,128)(2,1)S(1)} %collective-permute-done.24.refs_6_), channel_id=1, source_target_pairs={{0,2},{1,3},{2,0},{3,1},{4,6},{5,7},{6,4},{7,5},{8,10},{9,11},{10,... | collective-permute-start | bytes 393224 | tf_op jit(solution)/shard_map/ppermute | solution.py:521
  17.8 7.6 %copy-start.3 = (bf16[128,512]{1,0:T(8,128)(2,1)S(1)}, bf16[128,512]{1,0:T(8,128)(2,1)}, u32[]{:S(2)}) copy-start(bf16[128,512]{1,0:T(8,128)(2,1)} %refs_2_.2) | copy-start | bytes 393220
  17.8 7.6 %collective-permute-start.25 = (bf16[128,512]{1,0:T(8,128)(2,1)S(1)}, bf16[128,512]{1,0:T(8,128)(2,1)S(1)}, u32[]{:S(2)}, u32[]{:S(2)}) collective-permute-start(bf16[128,512]{1,0:T(8,128)(2,1)S(1)} %collective-permute-done.24.refs_6_), channel_id=1, source_target_pairs={{0,1},{1,0},{2,3},{3,2},{4,5},{5,4},{6,7},{7,6},{8,9},{9,8},{10,11... | collective-permute-start | bytes 393224 | tf_op jit(solution)/shard_map/ppermute | solution.py:521
  18.5 6.9 %collective-permute-start.23 = (bf16[128,512]{1,0:T(8,128)(2,1)S(1)}, bf16[128,512]{1,0:T(8,128)(2,1)S(1)}, u32[]{:S(2)}, u32[]{:S(2)}) collective-permute-start(bf16[128,512]{1,0:T(8,128)(2,1)S(1)} %collective-permute-done.22.refs_4_), channel_id=1, source_target_pairs={{0,1},{1,0},{2,3},{3,2},{4,5},{5,4},{6,7},{7,6},{8,9},{9,8},{10,11... | collective-permute-start | bytes 393224 | tf_op jit(solution)/shard_map/ppermute | solution.py:521
  21.1 4.4 %collective-permute-start.27 = (bf16[128,512]{1,0:T(8,128)(2,1)S(1)}, bf16[128,512]{1,0:T(8,128)(2,1)S(1)}, u32[]{:S(2)}, u32[]{:S(2)}) collective-permute-start(bf16[128,512]{1,0:T(8,128)(2,1)S(1)} %collective-permute-done.26.refs_8_), channel_id=1, source_target_pairs={{0,1},{1,0},{2,3},{3,2},{4,5},{5,4},{6,7},{7,6},{8,9},{9,8},{10,11... | collective-permute-start | bytes 393224 | tf_op jit(solution)/shard_map/ppermute | solution.py:521
  21.1 5.8 %copy-start.2 = (bf16[16,768,512]{2,1,0:T(8,128)(2,1)S(1)}, bf16[16,768,512]{2,1,0:T(8,128)(2,1)}, u32[]{:S(2)}) copy-start(bf16[16,768,512]{2,1,0:T(8,128)(2,1)} %refs_2_.3) | copy-start | bytes 37748740
  46.8 14.1 %collective-permute-start.30 = (bf16[2,320,384]{2,1,0:T(8,128)(2,1)S(1)}, bf16[2,320,384]{2,1,0:T(8,128)(2,1)S(1)}, u32[]{:S(2)}, u32[]{:S(2)}) collective-permute-start(bf16[2,320,384]{2,1,0:T(8,128)(2,1)S(1)} %get-tuple-element.104), channel_id=1, source_target_pairs={{0,16},{8,24},{16,0},{24,8},{1,17},{9,25},{17,1},{25,9},{2,18},{10... | collective-permute-start | bytes 1474568 | tf_op jit(solution)/shard_map/ppermute | solution.py:521
  48.4 22.7 %collective-permute-start.37 = (bf16[2,320,384]{2,1,0:T(8,128)(2,1)S(1)}, bf16[2,320,384]{2,1,0:T(8,128)(2,1)S(1)}, u32[]{:S(2)}, u32[]{:S(2)}) collective-permute-start(bf16[2,320,384]{2,1,0:T(8,128)(2,1)S(1)} %get-tuple-element.110), channel_id=1, source_target_pairs={{0,16},{8,24},{16,0},{24,8},{1,17},{9,25},{17,1},{25,9},{2,18},{10... | collective-permute-start | bytes 1474568 | tf_op jit(solution)/shard_map/ppermute | solution.py:521
  48.9 26.3 %collective-permute-start.28 = (bf16[2,320,384]{2,1,0:T(8,128)(2,1)S(1)}, bf16[2,320,384]{2,1,0:T(8,128)(2,1)S(1)}, u32[]{:S(2)}, u32[]{:S(2)}) collective-permute-start(bf16[2,320,384]{2,1,0:T(8,128)(2,1)S(1)} %get-tuple-element.101), channel_id=1, source_target_pairs={{0,8},{8,0},{16,24},{24,16},{1,9},{9,1},{17,25},{25,17},{2,10},{10... | collective-permute-start | bytes 1474568 | tf_op jit(solution)/shard_map/ppermute | solution.py:521
  50.4 23.1 %collective-permute-start.35 = (bf16[2,320,384]{2,1,0:T(8,128)(2,1)S(1)}, bf16[2,320,384]{2,1,0:T(8,128)(2,1)S(1)}, u32[]{:S(2)}, u32[]{:S(2)}) collective-permute-start(bf16[2,320,384]{2,1,0:T(8,128)(2,1)S(1)} %get-tuple-element.107), channel_id=1, source_target_pairs={{0,8},{8,0},{16,24},{24,16},{1,9},{9,1},{17,25},{25,17},{2,10},{10... | collective-permute-start | bytes 1474568 | tf_op jit(solution)/shard_map/ppermute | solution.py:521
  61.0 24.9 %collective-permute-start.31 = (bf16[320,384]{1,0:T(8,128)(2,1)S(1)}, bf16[320,384]{1,0:T(8,128)(2,1)S(1)}, u32[]{:S(2)}, u32[]{:S(2)}) collective-permute-start(bf16[320,384]{1,0:T(8,128)(2,1)S(1)} %fusion.21), channel_id=1, source_target_pairs={{0,8},{8,0},{16,24},{24,16},{1,9},{9,1},{17,25},{25,17},{2,10},{10... | collective-permute-start | bytes 737288 | tf_op jit(solution)/shard_map/ppermute | solution.py:521
  71.1 11.9 %collective-permute-start.38 = (bf16[320,384]{1,0:T(8,128)(2,1)S(1)}, bf16[320,384]{1,0:T(8,128)(2,1)S(1)}, u32[]{:S(2)}, u32[]{:S(2)}) collective-permute-start(bf16[320,384]{1,0:T(8,128)(2,1)S(1)} %fusion.15), channel_id=1, source_target_pairs={{0,8},{8,0},{16,24},{24,16},{1,9},{9,1},{17,25},{25,17},{2,10},{10... | collective-permute-start | bytes 737288 | tf_op jit(solution)/shard_map/ppermute | solution.py:521
  73.6 9.5 %collective-permute-start.36 = (bf16[320,384]{1,0:T(8,128)(2,1)S(1)}, bf16[320,384]{1,0:T(8,128)(2,1)S(1)}, u32[]{:S(2)}, u32[]{:S(2)}) collective-permute-start(bf16[320,384]{1,0:T(8,128)(2,1)S(1)} %fusion.19), channel_id=1, source_target_pairs={{0,16},{8,24},{16,0},{24,8},{1,17},{9,25},{17,1},{25,9},{2,18},{10... | collective-permute-start | bytes 737288 | tf_op jit(solution)/shard_map/ppermute | solution.py:521
  75.3 10.6 %collective-permute-start.29 = (bf16[320,384]{1,0:T(8,128)(2,1)S(1)}, bf16[320,384]{1,0:T(8,128)(2,1)S(1)}, u32[]{:S(2)}, u32[]{:S(2)}) collective-permute-start(bf16[320,384]{1,0:T(8,128)(2,1)S(1)} %fusion.25), channel_id=1, source_target_pairs={{0,16},{8,24},{16,0},{24,8},{1,17},{9,25},{17,1},{25,9},{2,18},{10... | collective-permute-start | bytes 737288 | tf_op jit(solution)/shard_map/ppermute | solution.py:521
  83.3 10.0 %collective-permute-start.39 = (bf16[320,384]{1,0:T(8,128)(2,1)S(1)}, bf16[320,384]{1,0:T(8,128)(2,1)S(1)}, u32[]{:S(2)}, u32[]{:S(2)}) collective-permute-start(bf16[320,384]{1,0:T(8,128)(2,1)S(1)} %fusion.18.refs_0_), channel_id=1, source_target_pairs={{0,24},{8,16},{16,8},{24,0},{1,25},{9,17},{17,9},{25,1},{2,26},{10... | collective-permute-start | bytes 737288 | tf_op jit(solution)/shard_map/ppermute | solution.py:521
  85.9 21.3 %slice-start = ((s8[12582912]{0:T(1024)(128)(4,1)}), s8[4194304]{0:T(1024)(128)(4,1)S(1)}, s32[]{:S(2)}) async-start(s8[12582912]{0:T(1024)(128)(4,1)} %bitcast.116), calls=%async_computation | async-start | bytes 8388608
  86.1 26.9 %collective-permute-start.32 = (bf16[320,384]{1,0:T(8,128)(2,1)S(1)}, bf16[320,384]{1,0:T(8,128)(2,1)S(1)}, u32[]{:S(2)}, u32[]{:S(2)}) collective-permute-start(bf16[320,384]{1,0:T(8,128)(2,1)S(1)} %fusion.24.refs_0_), channel_id=1, source_target_pairs={{0,24},{8,16},{16,8},{24,0},{1,25},{9,17},{17,9},{25,1},{2,26},{10... | collective-permute-start | bytes 737288 | tf_op jit(solution)/shard_map/ppermute | solution.py:521
  87.7 25.3 %collective-permute-start.33 = (bf16[320,384]{1,0:T(8,128)(2,1)S(1)}, bf16[320,384]{1,0:T(8,128)(2,1)S(1)}, u32[]{:S(2)}, u32[]{:S(2)}) collective-permute-start(bf16[320,384]{1,0:T(8,128)(2,1)S(1)} %fusion.24.refs_0_), channel_id=1, source_target_pairs={{0,8},{8,0},{16,24},{24,16},{1,9},{9,1},{17,25},{25,17},{2,10},{10... | collective-permute-start | bytes 737288 | tf_op jit(solution)/shard_map/ppermute | solution.py:521
  88.7 24.3 %collective-permute-start.34 = (bf16[320,384]{1,0:T(8,128)(2,1)S(1)}, bf16[320,384]{1,0:T(8,128)(2,1)S(1)}, u32[]{:S(2)}, u32[]{:S(2)}) collective-permute-start(bf16[320,384]{1,0:T(8,128)(2,1)S(1)} %fusion.24.refs_0_), channel_id=1, source_target_pairs={{0,16},{8,24},{16,0},{24,8},{1,17},{9,25},{17,1},{25,9},{2,18},{10... | collective-permute-start | bytes 737288 | tf_op jit(solution)/shard_map/ppermute | solution.py:521
  89.7 17.5 %collective-permute-start.40 = (bf16[320,384]{1,0:T(8,128)(2,1)S(1)}, bf16[320,384]{1,0:T(8,128)(2,1)S(1)}, u32[]{:S(2)}, u32[]{:S(2)}) collective-permute-start(bf16[320,384]{1,0:T(8,128)(2,1)S(1)} %fusion.18.refs_0_), channel_id=1, source_target_pairs={{0,8},{8,0},{16,24},{24,16},{1,9},{9,1},{17,25},{25,17},{2,10},{10... | collective-permute-start | bytes 737288 | tf_op jit(solution)/shard_map/ppermute | solution.py:521
  93.3 13.9 %collective-permute-start.41 = (bf16[320,384]{1,0:T(8,128)(2,1)S(1)}, bf16[320,384]{1,0:T(8,128)(2,1)S(1)}, u32[]{:S(2)}, u32[]{:S(2)}) collective-permute-start(bf16[320,384]{1,0:T(8,128)(2,1)S(1)} %fusion.18.refs_0_), channel_id=1, source_target_pairs={{0,16},{8,24},{16,0},{24,8},{1,17},{9,25},{17,1},{25,9},{2,18},{10... | collective-permute-start | bytes 737288 | tf_op jit(solution)/shard_map/ppermute | solution.py:521
  94.8 12.4 %slice-start.1 = ((s8[12582912]{0:T(1024)(128)(4,1)}), s8[4194304]{0:T(1024)(128)(4,1)S(1)}, s32[]{:S(2)}) async-start(s8[12582912]{0:T(1024)(128)(4,1)} %bitcast.116), calls=%async_computation.1 | async-start | bytes 8388608
  94.8 12.4 %slice-start.2 = ((s8[12582912]{0:T(1024)(128)(4,1)}), s8[4194304]{0:T(1024)(128)(4,1)S(1)}, s32[]{:S(2)}) async-start(s8[12582912]{0:T(1024)(128)(4,1)} %bitcast.116), calls=%async_computation.2 | async-start | bytes 8388608
  120.3 2.0 %collective-permute-start.42 = (bf16[4,128,512]{2,1,0:T(8,128)(2,1)S(1)}, bf16[4,128,512]{2,1,0:T(8,128)(2,1)S(1)}, u32[]{:S(2)}, u32[]{:S(2)}) collective-permute-start(bf16[4,128,512]{2,1,0:T(8,128)(2,1)S(1)} %get-tuple-element.117), channel_id=1, source_target_pairs={{0,1},{1,0},{2,3},{3,2},{4,5},{5,4},{6,7},{7,6},{8,9},{9,8},{10,11... | collective-permute-start | bytes 1572872 | tf_op jit(solution)/shard_map/ppermute | solution.py:521
  122.5 7.9 %collective-permute-start.45 = (bf16[128,512]{1,0:T(8,128)(2,1)S(1)}, bf16[128,512]{1,0:T(8,128)(2,1)S(1)}, u32[]{:S(2)}, u32[]{:S(2)}) collective-permute-start(bf16[128,512]{1,0:T(8,128)(2,1)S(1)} %get-tuple-element.127), channel_id=1, source_target_pairs={{0,2},{1,3},{2,0},{3,1},{4,6},{5,7},{6,4},{7,5},{8,10},{9,11},{10,... | collective-permute-start | bytes 393224 | tf_op jit(solution)/shard_map/ppermute | solution.py:521
  122.6 13.2 %collective-permute-start.44 = (bf16[128,512]{1,0:T(8,128)(2,1)S(1)}, bf16[128,512]{1,0:T(8,128)(2,1)S(1)}, u32[]{:S(2)}, u32[]{:S(2)}) collective-permute-start(bf16[128,512]{1,0:T(8,128)(2,1)S(1)} %get-tuple-element.128), channel_id=1, source_target_pairs={{0,4},{1,5},{2,6},{3,7},{4,0},{5,1},{6,2},{7,3},{8,12},{9,13},{10,... | collective-permute-start | bytes 393224 | tf_op jit(solution)/shard_map/ppermute | solution.py:521
  125.8 10.0 %collective-permute-start.43 = (bf16[128,512]{1,0:T(8,128)(2,1)S(1)}, bf16[128,512]{1,0:T(8,128)(2,1)S(1)}, u32[]{:S(2)}, u32[]{:S(2)}) collective-permute-start(bf16[128,512]{1,0:T(8,128)(2,1)S(1)} %get-tuple-element.126), channel_id=1, source_target_pairs={{0,6},{1,7},{2,4},{3,5},{4,2},{5,3},{6,0},{7,1},{8,14},{9,15},{10,... | collective-permute-start | bytes 393224 | tf_op jit(solution)/shard_map/ppermute | solution.py:521
  136.2 0.7 copy-start.4

commit v5 on v3

--- a/solution.py
+++ b/solution.py
@@ -30,7 +30,7 @@
 
 
 def hbm():
-    return pl.BlockSpec(memory_space=pl.ANY)
+    return pl.BlockSpec(memory_space=pltpu.HBM)
 
 
 def params(*shapes):
@@ -136,15 +136,15 @@
     return rowid[block, e : e + 1, :] == at
 
 
-def aligned(value):
-    return pl.multiple_of(value // ALIGN * ALIGN, ALIGN)
+def aligned(dims, value):
+    return pl.multiple_of(jnp.minimum(value // ALIGN * ALIGN, dims["total"]), ALIGN)
 
 
 def fill_select(dims, rowid, starts, select, step):
     rows = dims["rows"]
     select[...] = jnp.zeros_like(select)
     for e in range(dims["experts"]):
-        first = aligned(starts[e])
+        first = aligned(dims, starts[e])
         at = pl.ds(first, dims["window"])
         for inner in range(dims["group"]):
             cols = slice(inner * rows, (inner + 1) * rows)
@@ -158,6 +158,19 @@
         offs[0, e] = starts[e]
         offs[1, e] = total[e, 0]
     return starts
+
+
+def fullest(dims, meta):
+    blocks, rows, top, experts = dims["blocks"], dims["rows"], dims["top"], dims["experts"]
+    ids = [meta[b][:, :rows].astype(F32)[:top].astype(jnp.int32) for b in range(blocks)]
+    counts = []
+    for group in range(blocks):
+        mine = jnp.zeros((top, rows), F32)
+        for block_ids in ids:
+            inside = (block_ids >= group * experts) & (block_ids < (group + 1) * experts)
+            mine = mine + inside.astype(F32)
+        counts.append(jnp.sum(mine, axis=0, keepdims=True))
+    return jnp.max(jnp.sum(jnp.concatenate(counts, axis=0), axis=1, keepdims=True)).astype(jnp.int32)
 
 
 def dispatch_kernel(dims, me_ref, gathered, rowid, probs, rowk, x, offs, select, total):
@@ -238,7 +251,7 @@
     scale[:, : 3 * experts] = wide
     lane = lax.broadcasted_iota(jnp.int32, (dims["window"], scale.shape[1]), 1)
     for e in range(experts):
-        first = aligned(offs[0, e])
+        first = aligned(dims, offs[0, e])
         at = pl.ds(first, dims["window"])
         old = scale[at, :]
         mine = (lane == e) | (lane == e + experts) | (lane == e + 2 * experts)
@@ -250,7 +263,7 @@
 def weigh_large_kernel(dims, offs, rowid, probs, scale, chosen):
     chosen[...] = jnp.zeros_like(chosen)
     for e in range(dims["experts"]):
-        first = aligned(offs[0, e])
+        first = aligned(dims, offs[0, e])
         at = pl.ds(first, dims["window"])
 
         def share(block, carry):
@@ -298,7 +311,7 @@
     if first_part:
         blocks, rows = dims["blocks"], dims["rows"]
         packed, refs = refs[:blocks], refs[blocks:]
-        w_gate, w_up, rowid, probs, rowk, x, select, offs_out, refs = *refs[:8], refs[8:]
+        w_gate, w_up, rowid, probs, rowk, x, select, offs_out, peak, refs = *refs[:9], refs[9:]
         gx, uy, g2, u1, g0, u0, gate_w, up_w, gate, up, sems, table, meta = refs
     else:
         offs, x, w_gate, w_up, gx, uy, g2, u1, g0, u0, gate_w, up_w, gate, up, sems = refs
@@ -322,6 +335,7 @@
             dims, me_ref[1] * experts, lambda block: meta[block], rowid, probs, rowk
         )
         offs = offs_out
+        peak[0] = fullest(dims, meta)
         fill_select(dims, rowid, publish(dims, offs, start, count), select, 0)
         for r in range(0, x.shape[0], dims["tile"]):
             size = min(dims["tile"], x.shape[0] - r)
@@ -333,7 +347,7 @@
             for copy in copies(e):
                 copy.wait()
         for e in batch:
-            first = aligned(offs[0, e])
+            first = aligned(dims, offs[0, e])
             rows_in = x[pl.ds(first, window), :]
             keep = (lax.broadcasted_iota(jnp.int32, (ALIGN, 1), 0) + first) >= offs[0, e]
             edge, rest = pl.ds(first, ALIGN), pl.ds(first + ALIGN, window - ALIGN)
@@ -376,8 +390,9 @@
         shapes, offs = route_shapes(dims)
         x = jax.ShapeDtypeStruct((padded, width), BF16)
         select = jax.ShapeDtypeStruct((padded, blocks * rows), BF16)
-        outs = shapes + (x, select, offs) + outs
-        into = (vmem(),) * 5 + (smem(),) + into
+        peak = jax.ShapeDtypeStruct((1,), jnp.int32)
+        outs = shapes + (x, select, offs, peak) + outs
+        into = (vmem(),) * 5 + (smem(),) * 2 + into
         scratch.append(pltpu.VMEM((blocks * rows, width), BF16))
         scratch.append(pltpu.VMEM((blocks, META, width), BF16))
         specs = [vmem()] * blocks
@@ -428,7 +443,7 @@
         for e in batch:
             copy(e).wait()
         for e in batch:
-            first = aligned(offs[0, e])
+            first = aligned(dims, offs[0, e])
             at = pl.ds(first, window)
             got = jnp.dot(hidden[at, :], held[e], preferred_element_type=F32)
             if y_in is not None:
@@ -498,10 +513,9 @@
     return lax.ppermute(value, axis, [(i, i ^ bit) for i in range(count)])
 
 
-def reduce_chunk(parts):
-    gx, uy, g2, u1, g0, u0 = parts
-    from_x = swap(gx, "rep", 1)
-    from_y = swap(uy, "rep", 2)
+def reduce_chunk(came, kept):
+    from_x, from_y = came
+    g2, u1, g0, u0 = kept
     gate_rest = swap((g2 + from_x[1].astype(F32)).astype(BF16), "rep", 2)
     up_rest = swap((u1 + from_y[1].astype(F32)).astype(BF16), "rep", 1)
     gate = g0 + from_x[0].astype(F32) + gate_rest.astype(F32)
@@ -542,45 +556,74 @@
     window = ceil_to(blocks * cap, ALIGN) + ALIGN
     part = units // 2
     small = blocks * rows * total <= 4 * 2**20
-    dims = dict(
-        blocks=blocks,
-        rows=rows,
-        top=top,
-        experts=experts,
-        window=window,
-        total=total,
-        quarter=total // replicas,
-        padded=total + window,
-        part=part,
-        group=min(blocks, 8),
-        tile=512,
-        small=small,
+
+    def sizes(total):
+        return dict(
+            blocks=blocks,
+            rows=rows,
+            top=top,
+            experts=experts,
+            window=window,
+            total=total,
+            quarter=total // replicas,
+            padded=total + window,
+            part=part,
+            group=min(blocks, 8),
+            tile=512,
+            small=small,
+        )
+
+    full = sizes(total)
+    me = jnp.stack([lax.axis_index("rep"), lax.axis_index("exp")]).astype(jnp.int32)
+    packed = pack(full, tokens, expert_ids, route_weights)
+    weights = (w_gate, w_up, w_down)
+    if not small:
+        gathered = lax.all_gather(packed, "exp", axis=0)
+        return one_pass(full, me, gathered, *weights)[0]
+    sources = gather_tokens(packed)
+    usual = min(total, ceil_to(rows * top * 5 // 4, replicas * 64))
+    mixed, peak = one_pass(sizes(usual), me, sources, *weights)
+    if usual == total:
+        return mixed
+    return lax.cond(
+        peak[0] > usual, lambda: one_pass(full, me, sources, *weights)[0], lambda: mixed
     )
-    me = jnp.stack([lax.axis_index("rep"), lax.axis_index("exp")]).astype(jnp.int32)
-    packed = pack(dims, tokens, expert_ids, route_weights)
-    if small:
-        sources = gather_tokens(packed)
-    else:
-        gathered = lax.all_gather(packed, "exp", axis=0)
-        rowid, probs, rowk, x, offs = dispatch(dims, me, gathered)
+
+
+def one_pass(dims, me, sources, w_gate, w_up, w_down):
+    peak = None
+    if not dims["small"]:
+        rowid, probs, rowk, x, offs = dispatch(dims, me, sources)
         rows_of, sources = rowid, [offs, x]
-
+    parts = []
+    for c in range(w_gate.shape[1] // dims["part"]):
+        parts.append(gate_up(dims, c, me, sources, w_gate, w_up))
+        if len(sources) > 2:
+            rowid, probs, rowk, x, rows_of, offs, peak = parts[0][:7]
+            sources, parts[0] = [offs, x], parts[0][7:]
+
+    came = []
+    for c, (gx, uy, *kept) in enumerate(parts):
+        if c > 0:
+            came[-1], gx, uy = lax.optimization_barrier((came[-1], gx, uy))
+        came.append((swap(gx, "rep", 1), swap(uy, "rep", 2)))
+        parts[c] = kept
+    rows_of, _ = lax.optimization_barrier((rows_of, parts[-1]))
+    scale, chosen = weigh(dims, offs, rows_of, probs)
     pieces = []
-    for c in range(units // part):
-        parts = gate_up(dims, c, me, sources, w_gate, w_up)
-        if len(sources) > 2:
-            rowid, probs, rowk, x, rows_of, offs = parts[:6]
-            sources, parts = [offs, x], parts[6:]
-        pieces.append(spread_chunk(reduce_chunk(parts)))
-    scale, chosen = weigh(dims, offs, rows_of, probs)
+    for c, kept in enumerate(parts):
+        hidden = reduce_chunk(came[c], kept)
+        if c == 0:
+            hidden, scale, chosen = lax.optimization_barrier((hidden, scale, chosen))
+        pieces.append(spread_chunk(hidden))
     y = None
     last = len(pieces) - 1
     for c in range(last):
         y = down(dims, c, False, me, offs, w_down, pieces[c], y, ())[0]
     mixed = down(dims, last, True, me, offs, w_down, pieces[last], y, (scale, chosen, rowk))
-    if small:
-        return sum_over_exp(*mixed)
-    return lax.psum_scatter(mixed[0], "exp", scatter_dimension=0, tiled=False)
+    if dims["small"]:
+        return sum_over_exp(*mixed), peak
+    return lax.psum_scatter(mixed[0], "exp", scatter_dimension=0, tiled=False), peak
 
 
 def solution(mesh):

time: 128 us -> 118 us (0.922)
  waiting for transfers between devices: 54.8 us -> 46.2 us
  local copies, waits for them, and re-layouts: 6.9 us -> 2.97 us
  starting transfers between devices: 29.3 us -> 31.5 us
    ppermute x25, waiting for transfers between devices: 54.8 us -> 46.2 us  [swap(): return lax.ppermute(value, axis, [(i, i ^ bit) for i in range(count)])]
    unnamed x18 -> x14, local copies, waits for them, and re-layouts: 6.87 us -> 2.94 us
    ppermute x25, starting transfers between devices: 29.3 us -> 31.5 us  [swap(): return lax.ppermute(value, axis, [(i, i ^ bit) for i in range(count)])]
  transfers between devices with their start and end apart: 25 -> 25, of which waited for: 13 -> 14; matrix products, arithmetic and copies ran while one was open for 1% -> 1% of each run, Pallas kernels for 13% -> 14%
where the time goes in v5:
time: 118 us
  waiting for transfers between devices  46.2 us (39%)
  Pallas kernels  34.8 us (29%)
  starting transfers between devices  31.5 us (27%)
  local copies, waits for them, and re-layouts  2.97 us (3%)
    ppermute x25, waiting for transfers between devices, swap(): return lax.ppermute(value, axis, [(i, i ^ bit) for i in range(count)])  46.2 us
    ppermute x25, starting transfers between devices, swap(): return lax.ppermute(value, axis, [(i, i ^ bit) for i in range(count)])  31.5 us
    pallas_call x2, Pallas kernels, gate_up(): pl.pallas_call(functools.partial(gate_up_kernel, dims, c, first_part), ou...  18.3 us
    pallas_call x2, Pallas kernels, down(): pl.pallas_call(functools.partial(down_kernel, dims, c, last), out_shape=o...  12.8 us
    pallas_call x1, Pallas kernels, weigh(): pl.pallas_call(functools.partial(weigh_small_kernel if small else weigh_l...  3.66 us
    unnamed x14, local copies, waits for them, and re-layouts  2.94 us
  transfers between devices with their start and end apart: 25, of which 14 were waited for; matrix products, arithmetic and copies ran while one was open for 1% of the time, Pallas kernels for 14%

profile of v5, /device:TPU:0, one launch (start us, length us, event | category | flops | bytes accessed | tf_op | source)
XLA Modules:
  0.0 117.6 jit_solution(7111373319044508976)
XLA Ops:
  0.0 0.9 copy-done
  0.9 0.7 copy-done.1
  1.6 0.7 copy-done.2
  2.3 4.1 %collective-permute-start.21 = (bf16[144,512]{1,0:T(8,128)(2,1)S(1)}, bf16[144,512]{1,0:T(8,128)(2,1)S(1)}, u32[]{:S(2)}, u32[]{:S(2)}) collective-permute-start(bf16[144,512]{1,0:T(8,128)(2,1)S(1)} %pack.1.refs_0_), channel_id=1, source_target_pairs={{0,4},{1,5},{2,6},{3,7},{4,0},{5,1},{6,2},{7,3},{8,12},{9,13},{10,... | collective-permute-start | bytes 442376 | tf_op jit(solution)/shard_map/ppermute | solution.py:513
  6.4 1.6 %collective-permute-start.19 = (bf16[144,512]{1,0:T(8,128)(2,1)S(1)}, bf16[144,512]{1,0:T(8,128)(2,1)S(1)}, u32[]{:S(2)}, u32[]{:S(2)}) collective-permute-start(bf16[144,512]{1,0:T(8,128)(2,1)S(1)} %pack.1.refs_0_), channel_id=1, source_target_pairs={{0,2},{1,3},{2,0},{3,1},{4,6},{5,7},{6,4},{7,5},{8,10},{9,11},{10,... | collective-permute-start | bytes 442376 | tf_op jit(solution)/shard_map/ppermute | solution.py:513
  8.0 5.5 %collective-permute-done.21.refs_4_ = bf16[144,512]{1,0:T(8,128)(2,1)S(1)} collective-permute-done((bf16[144,512]{1,0:T(8,128)(2,1)S(1)}, bf16[144,512]{1,0:T(8,128)(2,1)S(1)}, u32[]{:S(2)}, u32[]{:S(2)}) %collective-permute-start.21) | collective-permute-done | bytes 147488 | tf_op jit(solution)/shard_map/ppermute | solution.py:513
  13.5 0.6 collective-permute-start.23
  14.1 0.0 collective-permute-start.18
  14.1 0.5 collective-permute-start.22
  14.6 0.0 collective-permute-start.20
  14.7 4.0 %collective-permute-done.23.refs_6_ = bf16[144,512]{1,0:T(8,128)(2,1)S(1)} collective-permute-done((bf16[144,512]{1,0:T(8,128)(2,1)S(1)}, bf16[144,512]{1,0:T(8,128)(2,1)S(1)}, u32[]{:S(2)}, u32[]{:S(2)}) %collective-permute-start.23) | collective-permute-done | bytes 147488 | tf_op jit(solution)/shard_map/ppermute | solution.py:513
  18.7 0.0 collective-permute-start.24
  18.7 0.1 pad_add_fusion.me_ref
  18.7 0.0 collective-permute-done.22.refs_5_
  18.7 0.0 collective-permute-done.20.refs_3_
  18.8 1.3 %collective-permute-done.24.refs_7_ = bf16[144,512]{1,0:T(8,128)(2,1)S(1)} collective-permute-done((bf16[144,512]{1,0:T(8,128)(2,1)S(1)}, bf16[144,512]{1,0:T(8,128)(2,1)S(1)}, u32[]{:S(2)}, u32[]{:S(2)}) %collective-permute-start.24) | collective-permute-done | bytes 147488 | tf_op jit(solution)/shard_map/ppermute | solution.py:513
  20.0 11.2 %gate_up.6 = (s32[8,16,128]{2,1,0:T(8,128)}, f32[8,16,128]{2,1,0:T(8,128)S(1)}, s32[8,8,128]{2,1,0:T(8,128)S(1)}, bf16[1392,512]{1,0:T(8,128)(2,1)S(1)}, bf16[13...) custom-call(s32[2]{0:T(128)S(1)} %pad_add_fusion.me_ref, ...), custom_call_target="tpu_custom_call" | custom-call | flops 1094713344 | bytes 14008320 | tf_op jit(solution)/shard_map/gate_up/pallas_call | solution.py:401
  31.3 1.6 %collective-permute-start.25 = (bf16[2,320,384]{2,1,0:T(8,128)(2,1)S(1)}, bf16[2,320,384]{2,1,0:T(8,128)(2,1)S(1)}, u32[]{:S(2)}, u32[]{:S(2)}) collective-permute-start(bf16[2,320,384]{2,1,0:T(8,128)(2,1)S(1)} %get-tuple-element.108), channel_id=1, source_target_pairs={{0,8},{8,0},{16,24},{24,16},{1,9},{9,1},{17,25},{25,17},{2,10},{10... | collective-permute-start | bytes 1474568 | tf_op jit(solution)/shard_map/ppermute | solution.py:513
  32.9 1.5 %collective-permute-start.26 = (bf16[2,320,384]{2,1,0:T(8,128)(2,1)S(1)}, bf16[2,320,384]{2,1,0:T(8,128)(2,1)S(1)}, u32[]{:S(2)}, u32[]{:S(2)}) collective-permute-start(bf16[2,320,384]{2,1,0:T(8,128)(2,1)S(1)} %get-tuple-element.109), channel_id=1, source_target_pairs={{0,16},{8,24},{16,0},{24,8},{1,17},{9,25},{17,1},{25,9},{2,18},{10... | collective-permute-start | bytes 1474568 | tf_op jit(solution)/shard_map/ppermute | solution.py:513
  34.4 7.1 %gate_up.7 = (bf16[2,320,384]{2,1,0:T(8,128)(2,1)S(1)}, bf16[2,320,384]{2,1,0:T(8,128)(2,1)S(1)}, f32[320,384]{1,0:T(8,128)S(1)}, f32[320,384]{1,0:T(8,128)S(1)}...) custom-call(s32[2]{0:T(128)S(1)} %pad_add_fusion.me_ref, s32[2,16]{1,0:T(2,128)S(1)} %get-tuple-element.105.refs_0_.offs, ...), custom_call_target="tpu_custom_call" | custom-call | flops 1094713344 | bytes 14008320 | tf_op jit(solution)/shard_map/gate_up/pallas_call | solution.py:401
  41.5 0.0 slice-start
  41.5 0.0 slice-start.1
  41.5 0.0 slice-start.2
  41.5 3.7 %weigh.3 = (f32[1392,128]{1,0:T(8,128)S(1)}, bf16[8,128,1280]{2,1,0:T(8,128)(2,1)S(1)}) custom-call(s32[2,16]{1,0:T(2,128)S(1)} %get-tuple-element.105.refs_0_.offs, bf16[1392,1024]{1,0:T(8,128)(2,1)S(1)} %get-tuple-element.124.select, f32[8,16,128]{2,1,0:T(8,128)S(1)} %get-tuple-element.125.probs), custom_call_target="tpu_custom_call" | custom-call | flops 6000000000 | bytes 8000000 | tf_op jit(solution)/shard_map/weigh/pallas_call | solution.py:287
  45.2 0.0 collective-permute-done.25
  45.2 0.7 collective-permute-done.26
  45.9 0.5 collective-permute-start.27
  46.3 0.1 fusion.19
  46.4 1.6 %collective-permute-start.34 = (bf16[320,384]{1,0:T(8,128)(2,1)S(1)}, bf16[320,384]{1,0:T(8,128)(2,1)S(1)}, u32[]{:S(2)}, u32[]{:S(2)}) collective-permute-start(bf16[320,384]{1,0:T(8,128)(2,1)S(1)} %fusion.19), channel_id=1, source_target_pairs={{0,16},{8,24},{16,0},{24,8},{1,17},{9,25},{17,1},{25,9},{2,18},{10... | collective-permute-start | bytes 737288 | tf_op jit(solution)/shard_map/ppermute | solution.py:513
  48.0 0.5 collective-permute-start.29
  48.5 0.1 fusion.15
  48.5 1.6 %collective-permute-start.35 = (bf16[320,384]{1,0:T(8,128)(2,1)S(1)}, bf16[320,384]{1,0:T(8,128)(2,1)S(1)}, u32[]{:S(2)}, u32[]{:S(2)}) collective-permute-start(bf16[320,384]{1,0:T(8,128)(2,1)S(1)} %fusion.15), channel_id=1, source_target_pairs={{0,8},{8,0},{16,24},{24,16},{1,9},{9,1},{17,25},{25,17},{2,10},{10... | collective-permute-start | bytes 737288 | tf_op jit(solution)/shard_map/ppermute | solution.py:513
  50.1 9.9 %collective-permute-done.27 = bf16[2,320,384]{2,1,0:T(8,128)(2,1)S(1)} collective-permute-done((bf16[2,320,384]{2,1,0:T(8,128)(2,1)S(1)}, bf16[2,320,384]{2,1,0:T(8,128)(2,1)S(1)}, u32[]{:S(2)}, u32[]{:S(2)}) %collective-permute-start.27) | collective-permute-done | bytes 491552 | tf_op jit(solution)/shard_map/ppermute | solution.py:513
  60.0 0.1 fusion.25
  60.1 1.8 %collective-permute-start.28 = (bf16[320,384]{1,0:T(8,128)(2,1)S(1)}, bf16[320,384]{1,0:T(8,128)(2,1)S(1)}, u32[]{:S(2)}, u32[]{:S(2)}) collective-permute-start(bf16[320,384]{1,0:T(8,128)(2,1)S(1)} %fusion.25), channel_id=1, source_target_pairs={{0,16},{8,24},{16,0},{24,8},{1,17},{9,25},{17,1},{25,9},{2,18},{10... | collective-permute-start | bytes 737288 | tf_op jit(solution)/shard_map/ppermute | solution.py:513
  61.8 4.1 %collective-permute-done.29 = bf16[2,320,384]{2,1,0:T(8,128)(2,1)S(1)} collective-permute-done((bf16[2,320,384]{2,1,0:T(8,128)(2,1)S(1)}, bf16[2,320,384]{2,1,0:T(8,128)(2,1)S(1)}, u32[]{:S(2)}, u32[]{:S(2)}) %collective-permute-start.29) | collective-permute-done | bytes 491552 | tf_op jit(solution)/shard_map/ppermute | solution.py:513
  65.9 0.1 fusion.21
  65.9 1.6 %collective-permute-start.30 = (bf16[320,384]{1,0:T(8,128)(2,1)S(1)}, bf16[320,384]{1,0:T(8,128)(2,1)S(1)}, u32[]{:S(2)}, u32[]{:S(2)}) collective-permute-start(bf16[320,384]{1,0:T(8,128)(2,1)S(1)} %fusion.21), channel_id=1, source_target_pairs={{0,8},{8,0},{16,24},{24,16},{1,9},{9,1},{17,25},{25,17},{2,10},{10... | collective-permute-start | bytes 737288 | tf_op jit(solution)/shard_map/ppermute | solution.py:513
  67.6 0.2 fusion.18.refs_0_
  67.8 1.6 %collective-permute-start.38 = (bf16[320,384]{1,0:T(8,128)(2,1)S(1)}, bf16[320,384]{1,0:T(8,128)(2,1)S(1)}, u32[]{:S(2)}, u32[]{:S(2)}) collective-permute-start(bf16[320,384]{1,0:T(8,128)(2,1)S(1)} %fusion.18.refs_0_), channel_id=1, source_target_pairs={{0,16},{8,24},{16,0},{24,8},{1,17},{9,25},{17,1},{25,9},{2,18},{10... | collective-permute-start | bytes 737288 | tf_op jit(solution)/shard_map/ppermute | solution.py:513
  69.4 0.5 collective-permute-start.37
  69.9 1.4 %collective-permute-start.36 = (bf16[320,384]{1,0:T(8,128)(2,1)S(1)}, bf16[320,384]{1,0:T(8,128)(2,1)S(1)}, u32[]{:S(2)}, u32[]{:S(2)}) collective-permute-start(bf16[320,384]{1,0:T(8,128)(2,1)S(1)} %fusion.18.refs_0_), channel_id=1, source_target_pairs={{0,24},{8,16},{16,8},{24,0},{1,25},{9,17},{17,9},{25,1},{2,26},{10... | collective-permute-start | bytes 737288 | tf_op jit(solution)/shard_map/ppermute | solution.py:513
  71.4 0.7 collective-permute-done.28
  72.1 2.8 %collective-permute-done.30 = bf16[320,384]{1,0:T(8,128)(2,1)S(1)} collective-permute-done((bf16[320,384]{1,0:T(8,128)(2,1)S(1)}, bf16[320,384]{1,0:T(8,128)(2,1)S(1)}, u32[]{:S(2)}, u32[]{:S(2)}) %collective-permute-start.30) | collective-permute-done | bytes 245792 | tf_op jit(solution)/shard_map/ppermute | solution.py:513
  74.9 0.2 fusion.24.refs_0_
  75.1 1.6 %collective-permute-start.33 = (bf16[320,384]{1,0:T(8,128)(2,1)S(1)}, bf16[320,384]{1,0:T(8,128)(2,1)S(1)}, u32[]{:S(2)}, u32[]{:S(2)}) collective-permute-start(bf16[320,384]{1,0:T(8,128)(2,1)S(1)} %fusion.24.refs_0_), channel_id=1, source_target_pairs={{0,16},{8,24},{16,0},{24,8},{1,17},{9,25},{17,1},{25,9},{2,18},{10... | collective-permute-start | bytes 737288 | tf_op jit(solution)/shard_map/ppermute | solution.py:513
  76.8 1.5 %collective-permute-start.32 = (bf16[320,384]{1,0:T(8,128)(2,1)S(1)}, bf16[320,384]{1,0:T(8,128)(2,1)S(1)}, u32[]{:S(2)}, u32[]{:S(2)}) collective-permute-start(bf16[320,384]{1,0:T(8,128)(2,1)S(1)} %fusion.24.refs_0_), channel_id=1, source_target_pairs={{0,8},{8,0},{16,24},{24,16},{1,9},{9,1},{17,25},{25,17},{2,10},{10... | collective-permute-start | bytes 737288 | tf_op jit(solution)/shard_map/ppermute | solution.py:513
  78.3 0.8 collective-permute-done.38.refs_3_
  79.0 2.5 %collective-permute-start.31 = (bf16[320,384]{1,0:T(8,128)(2,1)S(1)}, bf16[320,384]{1,0:T(8,128)(2,1)S(1)}, u32[]{:S(2)}, u32[]{:S(2)}) collective-permute-start(bf16[320,384]{1,0:T(8,128)(2,1)S(1)} %fusion.24.refs_0_), channel_id=1, source_target_pairs={{0,24},{8,16},{16,8},{24,0},{1,25},{9,17},{17,9},{25,1},{2,26},{10... | collective-permute-start | bytes 737288 | tf_op jit(solution)/shard_map/ppermute | solution.py:513
  81.5 4.8 %collective-permute-done.36.refs_1_ = bf16[320,384]{1,0:T(8,128)(2,1)S(1)} collective-permute-done((bf16[320,384]{1,0:T(8,128)(2,1)S(1)}, bf16[320,384]{1,0:T(8,128)(2,1)S(1)}, u32[]{:S(2)}, u32[]{:S(2)}) %collective-permute-start.36) | collective-permute-done | bytes 245792 | tf_op jit(solution)/shard_map/ppermute | solution.py:513
  86.4 5.5 %down.6.refs_4_ = f32[1392,512]{1,0:T(8,128)S(1)} custom-call(s32[2]{0:T(128)S(1)} %pad_add_fusion.me_ref, s32[2,16]{1,0:T(2,128)S(1)} %get-tuple-element.105.refs_0_.offs, bf16[16,768,512]{2,1,0:T(8,128)(2,1)S(1)} %bitcast.96, bf16[320,384]{1,0:T(8,128)(2,1)S(1)} %fusion.18.refs_0_, bf16[320,384]{1,0:T(8,128)(2,1)S(1)} %collective-permute-done.36.refs_1_, ...), custom_call_target="tpu_custom_call" | custom-call | flops 1094713344 | bytes 11993088 | tf_op jit(solution)/shard_map/down/pallas_call | solution.py:499
  91.9 7.3 %down.7 = (bf16[4,128,512]{2,1,0:T(8,128)(2,1)S(1)}, bf16[4,128,512]{2,1,0:T(8,128)(2,1)S(1)}) custom-call(s32[2]{0:T(128)S(1)} %pad_add_fusion.me_ref, s32[2,16]{1,0:T(2,128)S(1)} %get-tuple-element.105.refs_0_.offs, bf16[16,768,512]{2,1,0:T(8,128)(2,1)S(1)} %bitcast.96, bf16[320,384]{1,0:T(8,128)(2,1)S(1)} %fusion.24.refs_0_, ...), custom_call_target="tpu_custom_call" | custom-call | flops 1094713344 | bytes 11993088 | tf_op jit(solution)/shard_map/down/pallas_call | solution.py:499
  99.2 0.1 collective-permute-start.39
  99.3 1.9 %collective-permute-done.39 = bf16[4,128,512]{2,1,0:T(8,128)(2,1)S(1)} collective-permute-done((bf16[4,128,512]{2,1,0:T(8,128)(2,1)S(1)}, bf16[4,128,512]{2,1,0:T(8,128)(2,1)S(1)}, u32[]{:S(2)}, u32[]{:S(2)}) %collective-permute-start.39) | collective-permute-done | bytes 524320 | tf_op jit(solution)/shard_map/ppermute | solution.py:513
  101.2 0.2 fusion.29
  101.4 4.2 %collective-permute-start.40 = (bf16[128,512]{1,0:T(8,128)(2,1)S(1)}, bf16[128,512]{1,0:T(8,128)(2,1)S(1)}, u32[]{:S(2)}, u32[]{:S(2)}) collective-permute-start(bf16[128,512]{1,0:T(8,128)(2,1)S(1)} %get-tuple-element.142), channel_id=1, source_target_pairs={{0,6},{1,7},{2,4},{3,5},{4,2},{5,3},{6,0},{7,1},{8,14},{9,15},{10,... | collective-permute-start | bytes 393224 | tf_op jit(solution)/shard_map/ppermute | solution.py:513
  105.6 0.6 collective-permute-start.41
  106.8 3.1 %collective-permute-done.40 = bf16[128,512]{1,0:T(8,128)(2,1)S(1)} collective-permute-done((bf16[128,512]{1,0:T(8,128)(2,1)S(1)}, bf16[128,512]{1,0:T(8,128)(2,1)S(1)}, u32[]{:S(2)}, u32[]{:S(2)}) %collective-permute-start.40) | collective-permute-done | bytes 131104 | tf_op jit(solution)/shard_map/ppermute | solution.py:513
  109.9 3.7 %collective-permute-done.42 = bf16[128,512]{1,0:T(8,128)(2,1)S(1)} collective-permute-done((bf16[128,512]{1,0:T(8,128)(2,1)S(1)}, bf16[128,512]{1,0:T(8,128)(2,1)S(1)}, u32[]{:S(2)}, u32[]{:S(2)}) %collective-permute-start.42) | collective-permute-done | bytes 131104 | tf_op jit(solution)/shard_map/ppermute | solution.py:513
  113.6 3.0 %collective-permute-done.41 = bf16[128,512]{1,0:T(8,128)(2,1)S(1)} collective-permute-done((bf16[128,512]{1,0:T(8,128)(2,1)S(1)}, bf16[128,512]{1,0:T(8,128)(2,1)S(1)}, u32[]{:S(2)}, u32[]{:S(2)}) %collective-permute-start.41) | collective-permute-done | bytes 131104 | tf_op jit(solution)/shard_map/ppermute | solution.py:513
  116.6 0.1 fusion.28
  116.7 0.3 conditional.1
  117.0 0.0 copy-start.4
  117.0 0.6 copy-done.4
  (18 shorter events, 0.1 us)
Async XLA Ops:
  0.0 0.9 copy-start
  0.9 0.7 copy-start.1
  1.6 0.7 copy-start.2
  2.3 11.2 %collective-permute-start.21 = (bf16[144,512]{1,0:T(8,128)(2,1)S(1)}, bf16[144,512]{1,0:T(8,128)(2,1)S(1)}, u32[]{:S(2)}, u32[]{:S(2)}) collective-permute-start(bf16[144,512]{1,0:T(8,128)(2,1)S(1)} %pack.1.refs_0_), channel_id=1, source_target_pairs={{0,4},{1,5},{2,6},{3,7},{4,0},{5,1},{6,2},{7,3},{8,12},{9,13},{10,... | collective-permute-start | bytes 442376 | tf_op jit(solution)/shard_map/ppermute | solution.py:513
  6.4 8.2 %collective-permute-start.19 = (bf16[144,512]{1,0:T(8,128)(2,1)S(1)}, bf16[144,512]{1,0:T(8,128)(2,1)S(1)}, u32[]{:S(2)}, u32[]{:S(2)}) collective-permute-start(bf16[144,512]{1,0:T(8,128)(2,1)S(1)} %pack.1.refs_0_), channel_id=1, source_target_pairs={{0,2},{1,3},{2,0},{3,1},{4,6},{5,7},{6,4},{7,5},{8,10},{9,11},{10,... | collective-permute-start | bytes 442376 | tf_op jit(solution)/shard_map/ppermute | solution.py:513
  13.5 5.1 %collective-permute-start.23 = (bf16[144,512]{1,0:T(8,128)(2,1)S(1)}, bf16[144,512]{1,0:T(8,128)(2,1)S(1)}, u32[]{:S(2)}, u32[]{:S(2)}) collective-permute-start(bf16[144,512]{1,0:T(8,128)(2,1)S(1)} %collective-permute-done.21.refs_4_), channel_id=1, source_target_pairs={{0,2},{1,3},{2,0},{3,1},{4,6},{5,7},{6,4},{7,5},{8,10},{9,11},{10,... | collective-permute-start | bytes 442376 | tf_op jit(solution)/shard_map/ppermute | solution.py:513
  14.1 4.6 %collective-permute-start.18 = (bf16[144,512]{1,0:T(8,128)(2,1)S(1)}, bf16[144,512]{1,0:T(8,128)(2,1)S(1)}, u32[]{:S(2)}, u32[]{:S(2)}) collective-permute-start(bf16[144,512]{1,0:T(8,128)(2,1)S(1)} %pack.1.refs_0_), channel_id=1, source_target_pairs={{0,1},{1,0},{2,3},{3,2},{4,5},{5,4},{6,7},{7,6},{8,9},{9,8},{10,11... | collective-permute-start | bytes 442376 | tf_op jit(solution)/shard_map/ppermute | solution.py:513
  14.1 4.6 %collective-permute-start.22 = (bf16[144,512]{1,0:T(8,128)(2,1)S(1)}, bf16[144,512]{1,0:T(8,128)(2,1)S(1)}, u32[]{:S(2)}, u32[]{:S(2)}) collective-permute-start(bf16[144,512]{1,0:T(8,128)(2,1)S(1)} %collective-permute-done.21.refs_4_), channel_id=1, source_target_pairs={{0,1},{1,0},{2,3},{3,2},{4,5},{5,4},{6,7},{7,6},{8,9},{9,8},{10,11... | collective-permute-start | bytes 442376 | tf_op jit(solution)/shard_map/ppermute | solution.py:513
  14.6 4.1 %collective-permute-start.20 = (bf16[144,512]{1,0:T(8,128)(2,1)S(1)}, bf16[144,512]{1,0:T(8,128)(2,1)S(1)}, u32[]{:S(2)}, u32[]{:S(2)}) collective-permute-start(bf16[144,512]{1,0:T(8,128)(2,1)S(1)} %collective-permute-done.19.refs_2_), channel_id=1, source_target_pairs={{0,1},{1,0},{2,3},{3,2},{4,5},{5,4},{6,7},{7,6},{8,9},{9,8},{10,11... | collective-permute-start | bytes 442376 | tf_op jit(solution)/shard_map/ppermute | solution.py:513
  18.7 1.4 %collective-permute-start.24 = (bf16[144,512]{1,0:T(8,128)(2,1)S(1)}, bf16[144,512]{1,0:T(8,128)(2,1)S(1)}, u32[]{:S(2)}, u32[]{:S(2)}) collective-permute-start(bf16[144,512]{1,0:T(8,128)(2,1)S(1)} %collective-permute-done.23.refs_6_), channel_id=1, source_target_pairs={{0,1},{1,0},{2,3},{3,2},{4,5},{5,4},{6,7},{7,6},{8,9},{9,8},{10,11... | collective-permute-start | bytes 442376 | tf_op jit(solution)/shard_map/ppermute | solution.py:513
  31.3 13.9 %collective-permute-start.25 = (bf16[2,320,384]{2,1,0:T(8,128)(2,1)S(1)}, bf16[2,320,384]{2,1,0:T(8,128)(2,1)S(1)}, u32[]{:S(2)}, u32[]{:S(2)}) collective-permute-start(bf16[2,320,384]{2,1,0:T(8,128)(2,1)S(1)} %get-tuple-element.108), channel_id=1, source_target_pairs={{0,8},{8,0},{16,24},{24,16},{1,9},{9,1},{17,25},{25,17},{2,10},{10... | collective-permute-start | bytes 1474568 | tf_op jit(solution)/shard_map/ppermute | solution.py:513
  32.9 13.0 %collective-permute-start.26 = (bf16[2,320,384]{2,1,0:T(8,128)(2,1)S(1)}, bf16[2,320,384]{2,1,0:T(8,128)(2,1)S(1)}, u32[]{:S(2)}, u32[]{:S(2)}) collective-permute-start(bf16[2,320,384]{2,1,0:T(8,128)(2,1)S(1)} %get-tuple-element.109), channel_id=1, source_target_pairs={{0,16},{8,24},{16,0},{24,8},{1,17},{9,25},{17,1},{25,9},{2,18},{10... | collective-permute-start | bytes 1474568 | tf_op jit(solution)/shard_map/ppermute | solution.py:513
  41.5 44.9 %slice-start = ((s8[12582912]{0:T(1024)(128)(4,1)}), s8[4194304]{0:T(1024)(128)(4,1)S(1)}, s32[]{:S(2)}) async-start(s8[12582912]{0:T(1024)(128)(4,1)} %bitcast.95), calls=%async_computation | async-start | bytes 8388608
  41.5 44.9 %slice-start.1 = ((s8[12582912]{0:T(1024)(128)(4,1)}), s8[4194304]{0:T(1024)(128)(4,1)S(1)}, s32[]{:S(2)}) async-start(s8[12582912]{0:T(1024)(128)(4,1)} %bitcast.95), calls=%async_computation.1 | async-start | bytes 8388608
  41.5 44.9 %slice-start.2 = ((s8[12582912]{0:T(1024)(128)(4,1)}), s8[4194304]{0:T(1024)(128)(4,1)S(1)}, s32[]{:S(2)}) async-start(s8[12582912]{0:T(1024)(128)(4,1)} %bitcast.95), calls=%async_computation.2 | async-start | bytes 8388608
  45.9 14.2 %collective-permute-start.27 = (bf16[2,320,384]{2,1,0:T(8,128)(2,1)S(1)}, bf16[2,320,384]{2,1,0:T(8,128)(2,1)S(1)}, u32[]{:S(2)}, u32[]{:S(2)}) collective-permute-start(bf16[2,320,384]{2,1,0:T(8,128)(2,1)S(1)} %get-tuple-element.112), channel_id=1, source_target_pairs={{0,8},{8,0},{16,24},{24,16},{1,9},{9,1},{17,25},{25,17},{2,10},{10... | collective-permute-start | bytes 1474568 | tf_op jit(solution)/shard_map/ppermute | solution.py:513
  46.4 21.2 %collective-permute-start.34 = (bf16[320,384]{1,0:T(8,128)(2,1)S(1)}, bf16[320,384]{1,0:T(8,128)(2,1)S(1)}, u32[]{:S(2)}, u32[]{:S(2)}) collective-permute-start(bf16[320,384]{1,0:T(8,128)(2,1)S(1)} %fusion.19), channel_id=1, source_target_pairs={{0,16},{8,24},{16,0},{24,8},{1,17},{9,25},{17,1},{25,9},{2,18},{10... | collective-permute-start | bytes 737288 | tf_op jit(solution)/shard_map/ppermute | solution.py:513
  48.0 17.9 %collective-permute-start.29 = (bf16[2,320,384]{2,1,0:T(8,128)(2,1)S(1)}, bf16[2,320,384]{2,1,0:T(8,128)(2,1)S(1)}, u32[]{:S(2)}, u32[]{:S(2)}) collective-permute-start(bf16[2,320,384]{2,1,0:T(8,128)(2,1)S(1)} %get-tuple-element.115), channel_id=1, source_target_pairs={{0,16},{8,24},{16,0},{24,8},{1,17},{9,25},{17,1},{25,9},{2,18},{10... | collective-permute-start | bytes 1474568 | tf_op jit(solution)/shard_map/ppermute | solution.py:513
  48.5 19.0 %collective-permute-start.35 = (bf16[320,384]{1,0:T(8,128)(2,1)S(1)}, bf16[320,384]{1,0:T(8,128)(2,1)S(1)}, u32[]{:S(2)}, u32[]{:S(2)}) collective-permute-start(bf16[320,384]{1,0:T(8,128)(2,1)S(1)} %fusion.15), channel_id=1, source_target_pairs={{0,8},{8,0},{16,24},{24,16},{1,9},{9,1},{17,25},{25,17},{2,10},{10... | collective-permute-start | bytes 737288 | tf_op jit(solution)/shard_map/ppermute | solution.py:513
  60.1 12.0 %collective-permute-start.28 = (bf16[320,384]{1,0:T(8,128)(2,1)S(1)}, bf16[320,384]{1,0:T(8,128)(2,1)S(1)}, u32[]{:S(2)}, u32[]{:S(2)}) collective-permute-start(bf16[320,384]{1,0:T(8,128)(2,1)S(1)} %fusion.25), channel_id=1, source_target_pairs={{0,16},{8,24},{16,0},{24,8},{1,17},{9,25},{17,1},{25,9},{2,18},{10... | collective-permute-start | bytes 737288 | tf_op jit(solution)/shard_map/ppermute | solution.py:513
  65.9 9.0 %collective-permute-start.30 = (bf16[320,384]{1,0:T(8,128)(2,1)S(1)}, bf16[320,384]{1,0:T(8,128)(2,1)S(1)}, u32[]{:S(2)}, u32[]{:S(2)}) collective-permute-start(bf16[320,384]{1,0:T(8,128)(2,1)S(1)} %fusion.21), channel_id=1, source_target_pairs={{0,8},{8,0},{16,24},{24,16},{1,9},{9,1},{17,25},{25,17},{2,10},{10... | collective-permute-start | bytes 737288 | tf_op jit(solution)/shard_map/ppermute | solution.py:513
  67.8 11.2 %collective-permute-start.38 = (bf16[320,384]{1,0:T(8,128)(2,1)S(1)}, bf16[320,384]{1,0:T(8,128)(2,1)S(1)}, u32[]{:S(2)}, u32[]{:S(2)}) collective-permute-start(bf16[320,384]{1,0:T(8,128)(2,1)S(1)} %fusion.18.refs_0_), channel_id=1, source_target_pairs={{0,16},{8,24},{16,0},{24,8},{1,17},{9,25},{17,1},{25,9},{2,18},{10... | collective-permute-start | bytes 737288 | tf_op jit(solution)/shard_map/ppermute | solution.py:513
  69.4 12.2 %collective-permute-start.37 = (bf16[320,384]{1,0:T(8,128)(2,1)S(1)}, bf16[320,384]{1,0:T(8,128)(2,1)S(1)}, u32[]{:S(2)}, u32[]{:S(2)}) collective-permute-start(bf16[320,384]{1,0:T(8,128)(2,1)S(1)} %fusion.18.refs_0_), channel_id=1, source_target_pairs={{0,8},{8,0},{16,24},{24,16},{1,9},{9,1},{17,25},{25,17},{2,10},{10... | collective-permute-start | bytes 737288 | tf_op jit(solution)/shard_map/ppermute | solution.py:513
  69.9 16.4 %collective-permute-start.36 = (bf16[320,384]{1,0:T(8,128)(2,1)S(1)}, bf16[320,384]{1,0:T(8,128)(2,1)S(1)}, u32[]{:S(2)}, u32[]{:S(2)}) collective-permute-start(bf16[320,384]{1,0:T(8,128)(2,1)S(1)} %fusion.18.refs_0_), channel_id=1, source_target_pairs={{0,24},{8,16},{16,8},{24,0},{1,25},{9,17},{17,9},{25,1},{2,26},{10... | collective-permute-start | bytes 737288 | tf_op jit(solution)/shard_map/ppermute | solution.py:513
  75.1 16.8 %collective-permute-start.33 = (bf16[320,384]{1,0:T(8,128)(2,1)S(1)}, bf16[320,384]{1,0:T(8,128)(2,1)S(1)}, u32[]{:S(2)}, u32[]{:S(2)}) collective-permute-start(bf16[320,384]{1,0:T(8,128)(2,1)S(1)} %fusion.24.refs_0_), channel_id=1, source_target_pairs={{0,16},{8,24},{16,0},{24,8},{1,17},{9,25},{17,1},{25,9},{2,18},{10... | collective-permute-start | bytes 737288 | tf_op jit(solution)/shard_map/ppermute | solution.py:513
  76.8 15.1 %collective-permute-start.32 = (bf16[320,384]{1,0:T(8,128)(2,1)S(1)}, bf16[320,384]{1,0:T(8,128)(2,1)S(1)}, u32[]{:S(2)}, u32[]{:S(2)}) collective-permute-start(bf16[320,384]{1,0:T(8,128)(2,1)S(1)} %fusion.24.refs_0_), channel_id=1, source_target_pairs={{0,8},{8,0},{16,24},{24,16},{1,9},{9,1},{17,25},{25,17},{2,10},{10... | collective-permute-start | bytes 737288 | tf_op jit(solution)/shard_map/ppermute | solution.py:513
  79.0 12.9 %collective-permute-start.31 = (bf16[320,384]{1,0:T(8,128)(2,1)S(1)}, bf16[320,384]{1,0:T(8,128)(2,1)S(1)}, u32[]{:S(2)}, u32[]{:S(2)}) collective-permute-start(bf16[320,384]{1,0:T(8,128)(2,1)S(1)} %fusion.24.refs_0_), channel_id=1, source_target_pairs={{0,24},{8,16},{16,8},{24,0},{1,25},{9,17},{17,9},{25,1},{2,26},{10... | collective-permute-start | bytes 737288 | tf_op jit(solution)/shard_map/ppermute | solution.py:513
  99.2 2.0 %collective-permute-start.39 = (bf16[4,128,512]{2,1,0:T(8,128)(2,1)S(1)}, bf16[4,128,512]{2,1,0:T(8,128)(2,1)S(1)}, u32[]{:S(2)}, u32[]{:S(2)}) collective-permute-start(bf16[4,128,512]{2,1,0:T(8,128)(2,1)S(1)} %get-tuple-element.133), channel_id=1, source_target_pairs={{0,1},{1,0},{2,3},{3,2},{4,5},{5,4},{6,7},{7,6},{8,9},{9,8},{10,11... | collective-permute-start | bytes 1572872 | tf_op jit(solution)/shard_map/ppermute | solution.py:513
  101.4 8.5 %collective-permute-start.40 = (bf16[128,512]{1,0:T(8,128)(2,1)S(1)}, bf16[128,512]{1,0:T(8,128)(2,1)S(1)}, u32[]{:S(2)}, u32[]{:S(2)}) collective-permute-start(bf16[128,512]{1,0:T(8,128)(2,1)S(1)} %get-tuple-element.142), channel_id=1, source_target_pairs={{0,6},{1,7},{2,4},{3,5},{4,2},{5,3},{6,0},{7,1},{8,14},{9,15},{10,... | collective-permute-start | bytes 393224 | tf_op jit(solution)/shard_map/ppermute | solution.py:513
  105.6 8.0 %collective-permute-start.42 = (bf16[128,512]{1,0:T(8,128)(2,1)S(1)}, bf16[128,512]{1,0:T(8,128)(2,1)S(1)}, u32[]{:S(2)}, u32[]{:S(2)}) collective-permute-start(bf16[128,512]{1,0:T(8,128)(2,1)S(1)} %get-tuple-element.143), channel_id=1, source_target_pairs={{0,2},{1,3},{2,0},{3,1},{4,6},{5,7},{6,4},{7,5},{8,10},{9,11},{10,... | collective-permute-start | bytes 393224 | tf_op jit(solution)/shard_map/ppermute | solution.py:513
  105.6 11.0 %collective-permute-start.41 = (bf16[128,512]{1,0:T(8,128)(2,1)S(1)}, bf16[128,512]{1,0:T(8,128)(2,1)S(1)}, u32[]{:S(2)}, u32[]{:S(2)}) collective-permute-start(bf16[128,512]{1,0:T(8,128)(2,1)S(1)} %get-tuple-element.144), channel_id=1, source_target_pairs={{0,4},{1,5},{2,6},{3,7},{4,0},{5,1},{6,2},{7,3},{8,12},{9,13},{10,... | collective-permute-start | bytes 393224 | tf_op jit(solution)/shard_map/ppermute | solution.py:513
  117.0 0.7 copy-start.4

commit v6 on v5

--- a/solution.py
+++ b/solution.py
@@ -230,7 +230,8 @@
     return hit.astype(F32).astype(BF16)
 
 
-def weigh_small_kernel(dims, offs, select, probs, scale, chosen, table):
+def weigh_small_kernel(dims, offs, select, probs, meta, scale, chosen, peak, table):
+    peak[0] = fullest(dims, meta)
     rows, experts, total, blocks = dims["rows"], dims["experts"], dims["total"], dims["blocks"]
     same = lax.broadcasted_iota(jnp.int32, (rows, rows), 0) == lax.broadcasted_iota(
         jnp.int32, (rows, rows), 1
@@ -276,7 +277,7 @@
         scale[at, :] = jnp.where(row_mask(dims, first, offs, e), wide, scale[at, :])
 
 
-def weigh(dims, offs, rows_of, probs):
+def weigh(dims, offs, rows_of, probs, meta):
     small = dims["small"]
     picked = (dims["blocks"], dims["rows"], dims["total"]) if small else (1, ALIGN, 128)
     outs = (
@@ -284,16 +285,20 @@
         jax.ShapeDtypeStruct(picked, BF16),
     )
     table = pltpu.VMEM((3 * dims["experts"], dims["blocks"] * dims["rows"]), BF16)
+    operands = (rows_of, probs)
+    if small:
+        operands += (meta,)
+        outs += (jax.ShapeDtypeStruct((1,), jnp.int32),)
     return pl.pallas_call(
         functools.partial(weigh_small_kernel if small else weigh_large_kernel, dims),
         out_shape=outs,
-        in_specs=[smem(), vmem(), vmem()],
-        out_specs=(vmem(), vmem()),
+        in_specs=[smem()] + [vmem()] * len(operands),
+        out_specs=(vmem(), vmem(), smem())[: len(outs)],
         scratch_shapes=[table] if small else [],
-        compiler_params=params(*outs, *held(rows_of, probs)),
+        compiler_params=params(*outs, *held(*operands)),
         cost_estimate=cost(6e9, 8e6),
         name="weigh",
-    )(offs, rows_of, probs)
+    )(offs, *operands)
 
 
 def row_mask(dims, first, offs, e):
@@ -311,8 +316,8 @@
     if first_part:
         blocks, rows = dims["blocks"], dims["rows"]
         packed, refs = refs[:blocks], refs[blocks:]
-        w_gate, w_up, rowid, probs, rowk, x, select, offs_out, peak, refs = *refs[:9], refs[9:]
-        gx, uy, g2, u1, g0, u0, gate_w, up_w, gate, up, sems, table, meta = refs
+        w_gate, w_up, rowid, probs, rowk, x, select, offs_out, meta, refs = *refs[:9], refs[9:]
+        gx, uy, g2, u1, g0, u0, gate_w, up_w, gate, up, sems, table = refs
     else:
         offs, x, w_gate, w_up, gx, uy, g2, u1, g0, u0, gate_w, up_w, gate, up, sems = refs
     units = pl.ds(c * part, part)
@@ -335,7 +340,6 @@
             dims, me_ref[1] * experts, lambda block: meta[block], rowid, probs, rowk
         )
         offs = offs_out
-        peak[0] = fullest(dims, meta)
         fill_select(dims, rowid, publish(dims, offs, start, count), select, 0)
         for r in range(0, x.shape[0], dims["tile"]):
             size = min(dims["tile"], x.shape[0] - r)
@@ -390,11 +394,10 @@
         shapes, offs = route_shapes(dims)
         x = jax.ShapeDtypeStruct((padded, width), BF16)
         select = jax.ShapeDtypeStruct((padded, blocks * rows), BF16)
-        peak = jax.ShapeDtypeStruct((1,), jnp.int32)
-        outs = shapes + (x, select, offs, peak) + outs
-        into = (vmem(),) * 5 + (smem(),) * 2 + into
+        meta = jax.ShapeDtypeStruct((blocks, META, width), BF16)
+        outs = shapes + (x, select, offs, meta) + outs
+        into = (vmem(),) * 5 + (smem(), vmem()) + into
         scratch.append(pltpu.VMEM((blocks * rows, width), BF16))
-        scratch.append(pltpu.VMEM((blocks, META, width), BF16))
         specs = [vmem()] * blocks
     else:
         specs = [smem(), vmem()]
@@ -410,52 +413,23 @@
     )(me, *sources, w_gate, w_up)
 
 
-def gather_hidden(dims, me, pieces, hidden):
-    quarter = dims["quarter"]
-    for j, piece in zip((0, 3, 1, 2), pieces):
-        hidden[pl.ds(pl.multiple_of((me ^ j) * quarter, ALIGN), quarter), :] = piece[...]
-
-
-def down_kernel(dims, c, last, me_ref, offs, w_down, *refs):
-    experts, window, part = dims["experts"], dims["window"], dims["part"]
-    pieces, refs = refs[:4], refs[4:]
-    y_in = None
-    if c > 0:
-        y_in, refs = refs[0], refs[1:]
-    if last:
-        scale, chosen, rowk, refs = refs[0], refs[1], refs[2], refs[3:]
-        if dims["small"]:
-            stay, away, held, hidden, sems, y_out = refs
-        else:
-            out, held, hidden, sems, y_out = refs
-        y_out[...] = jnp.zeros_like(y_out)
+def down_kernel(dims, places, me_ref, offs, w_down, scale, chosen, rowk, *refs):
+    experts, window, part, quarter = dims["experts"], dims["window"], dims["part"], dims["quarter"]
+    pieces, refs = refs[: len(places)], refs[len(places) :]
+    if dims["small"]:
+        stay, away, hidden, scaled = refs
     else:
-        y_out, held, hidden, sems = refs
-    units = pl.ds(c * part, part)
-
-    def copy(e):
-        return pltpu.make_async_copy(w_down.at[e, units, :], held.at[e], sems.at[e])
-
+        out, hidden, scaled = refs
+    scaled[...] = jnp.zeros_like(scaled)
+    for (c, j, skip), piece in zip(places, pieces):
+        first = pl.multiple_of((me_ref[0] ^ j) * quarter + skip, ALIGN)
+        hidden[pl.ds(first, piece.shape[0]), c * part : (c + 1) * part] = piece[...]
     for e in range(experts):
-        copy(e).start()
-    gather_hidden(dims, me_ref[0], pieces, hidden)
-    for batch in batches(experts):
-        for e in batch:
-            copy(e).wait()
-        for e in batch:
-            first = aligned(dims, offs[0, e])
-            at = pl.ds(first, window)
-            got = jnp.dot(hidden[at, :], held[e], preferred_element_type=F32)
-            if y_in is not None:
-                got = got + y_in[at, :]
-            mask = row_mask(dims, first, offs, e)
-            if last:
-                got = got * scale[at, 0:1]
-                y_out[at, :] = jnp.where(mask, got, y_out[at, :].astype(F32)).astype(BF16)
-            else:
-                y_out[at, :] = jnp.where(mask, got, y_out[at, :])
-    if not last:
-        return
+        first = aligned(dims, offs[0, e])
+        at = pl.ds(first, window)
+        got = jnp.dot(hidden[at, :], w_down[e], preferred_element_type=F32) * scale[at, 0:1]
+        mask = row_mask(dims, first, offs, e)
+        scaled[at, :] = jnp.where(mask, got, scaled[at, :].astype(F32)).astype(BF16)
     rows, total, width = dims["rows"], dims["total"], w_down.shape[2]
     blocks, many = dims["blocks"], min(4, dims["blocks"])
     if dims["small"]:
@@ -463,14 +437,14 @@
             for p in range(0, blocks // 2, many):
                 at = [me_ref[1] ^ (2 * (p + i) + side) for i in range(many)]
                 picked = jnp.concatenate([chosen[i] for i in at], axis=0)
-                summed = jnp.dot(picked, y_out[:total, :], preferred_element_type=F32)
+                summed = jnp.dot(picked, scaled[:total, :], preferred_element_type=F32)
                 into[p : p + many] = summed.astype(BF16).reshape(many, rows, width)
         return
 
     def combine(step, carry):
         picked = [choose(dims, rowk, step * many + i) for i in range(many)]
         summed = jnp.dot(
-            jnp.concatenate(picked, axis=0), y_out[:total, :], preferred_element_type=F32
+            jnp.concatenate(picked, axis=0), scaled[:total, :], preferred_element_type=F32
         )
         out[pl.ds(step * many, many)] = summed.astype(BF16).reshape(many, rows, width)
         return carry
@@ -478,34 +452,30 @@
     lax.fori_loop(0, blocks // many, combine, 0)
 
 
-def down(dims, c, last, me, offs, w_down, pieces, y, extra):
-    experts, padded, part = dims["experts"], dims["padded"], dims["part"]
-    width = w_down.shape[2]
-    operands = list(pieces) + ([y] if c > 0 else []) + list(extra)
+def down(dims, me, offs, w_down, scale, chosen, rowk, chunks):
+    padded, width = dims["padded"], w_down.shape[2]
+    places = [(c, j, skip) for c, chunk in enumerate(chunks) for j, skip, _ in chunk]
+    pieces = [piece for chunk in chunks for _, _, piece in chunk]
+    operands = [w_down, scale, chosen, rowk, *pieces]
     blocks, rows = dims["blocks"], dims["rows"]
     scratch = [
-        pltpu.VMEM((experts, part, width), BF16),
-        pltpu.VMEM((padded, part), BF16),
-        pltpu.SemaphoreType.DMA((experts,)),
+        pltpu.VMEM((padded, w_down.shape[1]), BF16),
+        pltpu.VMEM((padded, width), BF16),
     ]
-    if not last:
-        outs = (jax.ShapeDtypeStruct((padded, width), F32),)
+    if dims["small"]:
+        outs = (jax.ShapeDtypeStruct((blocks // 2, rows, width), BF16),) * 2
     else:
-        scratch.append(pltpu.VMEM((padded, width), BF16))
-        if dims["small"]:
-            outs = (jax.ShapeDtypeStruct((blocks // 2, rows, width), BF16),) * 2
-        else:
-            outs = (jax.ShapeDtypeStruct((blocks, rows, width), BF16),)
+        outs = (jax.ShapeDtypeStruct((blocks, rows, width), BF16),)
     return pl.pallas_call(
-        functools.partial(down_kernel, dims, c, last),
+        functools.partial(down_kernel, dims, places),
         out_shape=outs,
-        in_specs=[smem(), smem(), hbm()] + [vmem()] * len(operands),
+        in_specs=[smem(), smem()] + [vmem()] * len(operands),
         out_specs=(vmem(),) * len(outs),
         scratch_shapes=scratch,
-        compiler_params=params(*outs, *held(*operands), *[b for b in scratch if "dma" not in str(b)]),
-        cost_estimate=cost(4 * padded * width * part, 2 * experts * part * width + 8 * padded * width),
+        compiler_params=params(*outs, *held(*operands), *scratch),
+        cost_estimate=cost(2 * padded * width * (w_down.shape[1] + blocks * rows), 2 * w_down.size),
         name="down",
-    )(me, offs, w_down, *operands)
+    )(me, offs, *operands)
 
 
 def swap(value, axis, bit):
@@ -523,8 +493,14 @@
     return (jax.nn.silu(gate) * up).astype(BF16)
 
 
-def spread_chunk(hidden):
-    return [hidden] + [swap(hidden, "rep", bit) for bit in (3, 1, 2)]
+def spread_chunk(hidden, two_steps):
+    x, y = swap(hidden, "rep", 1), swap(hidden, "rep", 2)
+    if two_steps:
+        half = hidden.shape[0] // 2
+        corner = [(3, 0, swap(x[:half], "rep", 2)), (3, half, swap(y[half:], "rep", 1))]
+    else:
+        corner = [(3, 0, swap(hidden, "rep", 3))]
+    return [(0, 0, hidden), (1, 0, x), (2, 0, y)] + corner
 
 
 def gather_tokens(tokens):
@@ -591,7 +567,7 @@
 
 
 def one_pass(dims, me, sources, w_gate, w_up, w_down):
-    peak = None
+    meta = None
     if not dims["small"]:
         rowid, probs, rowk, x, offs = dispatch(dims, me, sources)
         rows_of, sources = rowid, [offs, x]
@@ -599,31 +575,25 @@
     for c in range(w_gate.shape[1] // dims["part"]):
         parts.append(gate_up(dims, c, me, sources, w_gate, w_up))
         if len(sources) > 2:
-            rowid, probs, rowk, x, rows_of, offs, peak = parts[0][:7]
+            rowid, probs, rowk, x, rows_of, offs, meta = parts[0][:7]
             sources, parts[0] = [offs, x], parts[0][7:]
 
     came = []
     for c, (gx, uy, *kept) in enumerate(parts):
-        if c > 0:
-            came[-1], gx, uy = lax.optimization_barrier((came[-1], gx, uy))
         came.append((swap(gx, "rep", 1), swap(uy, "rep", 2)))
         parts[c] = kept
     rows_of, _ = lax.optimization_barrier((rows_of, parts[-1]))
-    scale, chosen = weigh(dims, offs, rows_of, probs)
-    pieces = []
+    scale, chosen, *peak = weigh(dims, offs, rows_of, probs, meta)
+    chunks = []
     for c, kept in enumerate(parts):
         hidden = reduce_chunk(came[c], kept)
         if c == 0:
             hidden, scale, chosen = lax.optimization_barrier((hidden, scale, chosen))
-        pieces.append(spread_chunk(hidden))
-    y = None
-    last = len(pieces) - 1
-    for c in range(last):
-        y = down(dims, c, False, me, offs, w_down, pieces[c], y, ())[0]
-    mixed = down(dims, last, True, me, offs, w_down, pieces[last], y, (scale, chosen, rowk))
+        chunks.append(spread_chunk(hidden, c + 1 < len(parts)))
+    mixed = down(dims, me, offs, w_down, scale, chosen, rowk, chunks)
     if dims["small"]:
-        return sum_over_exp(*mixed), peak
-    return lax.psum_scatter(mixed[0], "exp", scatter_dimension=0, tiled=False), peak
+        return sum_over_exp(*mixed), peak[0]
+    return lax.psum_scatter(mixed[0], "exp", scatter_dimension=0, tiled=False), None
 
 
 def solution(mesh):

time: 118 us -> 112 us (0.949)
  starting transfers between devices: 31.5 us -> 28.7 us
  Pallas kernels: 34.8 us -> 32.2 us
    pallas_call x2 -> x1, Pallas kernels: 12.8 us -> 8.34 us  [down(): pl.pallas_call(functools.partial(down_kernel, dims, places), out_shape=ou...]
    ppermute x25 -> x26, starting transfers between devices: 31.5 us -> 28.7 us  [swap(): return lax.ppermute(value, axis, [(i, i ^ bit) for i in range(count)])]
    pallas_call x2, Pallas kernels: 18.3 us -> 19.7 us  [gate_up(): pl.pallas_call(functools.partial(gate_up_kernel, dims, c, first_part), ou...]
    ppermute x25 -> x26, waiting for transfers between devices: 46.2 us -> 46 us  [swap(): return lax.ppermute(value, axis, [(i, i ^ bit) for i in range(count)])]
  transfers between devices with their start and end apart: 25 -> 26, of which waited for: 14 -> 14; matrix products, arithmetic and copies ran while one was open for 1% -> 1% of each run, Pallas kernels for 14% -> 11%
where the time goes in v6:
time: 112 us
  waiting for transfers between devices  46 us (41%)
  Pallas kernels  32.2 us (29%)
  starting transfers between devices  28.7 us (26%)
  local copies, waits for them, and re-layouts  2.99 us (3%)
    ppermute x26, waiting for transfers between devices, swap(): return lax.ppermute(value, axis, [(i, i ^ bit) for i in range(count)])  46 us
    ppermute x26, starting transfers between devices, swap(): return lax.ppermute(value, axis, [(i, i ^ bit) for i in range(count)])  28.7 us
    pallas_call x2, Pallas kernels, gate_up(): pl.pallas_call(functools.partial(gate_up_kernel, dims, c, first_part), ou...  19.7 us
    pallas_call x1, Pallas kernels, down(): pl.pallas_call(functools.partial(down_kernel, dims, places), out_shape=ou...  8.34 us
    pallas_call x1, Pallas kernels, weigh(): pl.pallas_call(functools.partial(weigh_small_kernel if small else weigh_l...  4.13 us
    unnamed x14, local copies, waits for them, and re-layouts  2.94 us
  transfers between devices with their start and end apart: 26, of which 14 were waited for; matrix products, arithmetic and copies ran while one was open for 1% of the time, Pallas kernels for 11%

profile of v6, /device:TPU:0, one launch (start us, length us, event | category | flops | bytes accessed | tf_op | source)
XLA Modules:
  0.0 112.0 jit_solution(12829645913449825239)
XLA Ops:
  0.0 0.9 copy-done
  0.9 0.7 copy-done.1
  1.6 0.7 copy-done.2
  2.3 4.1 %collective-permute-start.22 = (bf16[144,512]{1,0:T(8,128)(2,1)S(1)}, bf16[144,512]{1,0:T(8,128)(2,1)S(1)}, u32[]{:S(2)}, u32[]{:S(2)}) collective-permute-start(bf16[144,512]{1,0:T(8,128)(2,1)S(1)} %pack.1.refs_0_), channel_id=1, source_target_pairs={{0,4},{1,5},{2,6},{3,7},{4,0},{5,1},{6,2},{7,3},{8,12},{9,13},{10,... | collective-permute-start | bytes 442376 | tf_op jit(solution)/shard_map/ppermute | solution.py:483
  6.4 1.6 %collective-permute-start.20 = (bf16[144,512]{1,0:T(8,128)(2,1)S(1)}, bf16[144,512]{1,0:T(8,128)(2,1)S(1)}, u32[]{:S(2)}, u32[]{:S(2)}) collective-permute-start(bf16[144,512]{1,0:T(8,128)(2,1)S(1)} %pack.1.refs_0_), channel_id=1, source_target_pairs={{0,2},{1,3},{2,0},{3,1},{4,6},{5,7},{6,4},{7,5},{8,10},{9,11},{10,... | collective-permute-start | bytes 442376 | tf_op jit(solution)/shard_map/ppermute | solution.py:483
  8.0 5.5 %collective-permute-done.22.refs_4_ = bf16[144,512]{1,0:T(8,128)(2,1)S(1)} collective-permute-done((bf16[144,512]{1,0:T(8,128)(2,1)S(1)}, bf16[144,512]{1,0:T(8,128)(2,1)S(1)}, u32[]{:S(2)}, u32[]{:S(2)}) %collective-permute-start.22) | collective-permute-done | bytes 147488 | tf_op jit(solution)/shard_map/ppermute | solution.py:483
  13.5 0.6 collective-permute-start.24
  14.1 0.0 collective-permute-start.19
  14.1 0.5 collective-permute-start.23
  14.6 0.0 collective-permute-start.21
  14.7 4.0 %collective-permute-done.24.refs_6_ = bf16[144,512]{1,0:T(8,128)(2,1)S(1)} collective-permute-done((bf16[144,512]{1,0:T(8,128)(2,1)S(1)}, bf16[144,512]{1,0:T(8,128)(2,1)S(1)}, u32[]{:S(2)}, u32[]{:S(2)}) %collective-permute-start.24) | collective-permute-done | bytes 147488 | tf_op jit(solution)/shard_map/ppermute | solution.py:483
  18.7 0.0 collective-permute-start.25
  18.7 0.1 pad_add_fusion.me_ref
  18.7 0.0 collective-permute-done.19.refs_1_
  18.7 0.0 collective-permute-done.23.refs_5_
  18.8 0.0 collective-permute-done.21.refs_3_
  18.8 1.3 %collective-permute-done.25.refs_7_ = bf16[144,512]{1,0:T(8,128)(2,1)S(1)} collective-permute-done((bf16[144,512]{1,0:T(8,128)(2,1)S(1)}, bf16[144,512]{1,0:T(8,128)(2,1)S(1)}, u32[]{:S(2)}, u32[]{:S(2)}) %collective-permute-start.25) | collective-permute-done | bytes 147488 | tf_op jit(solution)/shard_map/ppermute | solution.py:483
  20.0 11.2 %gate_up.6 = (s32[8,16,128]{2,1,0:T(8,128)}, f32[8,16,128]{2,1,0:T(8,128)S(1)}, s32[8,8,128]{2,1,0:T(8,128)S(1)}, bf16[1392,512]{1,0:T(8,128)(2,1)S(1)}, bf16[13...) custom-call(s32[2]{0:T(128)S(1)} %pad_add_fusion.me_ref, ...), custom_call_target="tpu_custom_call" | custom-call | flops 1094713344 | bytes 14008320 | tf_op jit(solution)/shard_map/gate_up/pallas_call | solution.py:404
  31.2 1.6 %collective-permute-start.26 = (bf16[2,320,384]{2,1,0:T(8,128)(2,1)S(1)}, bf16[2,320,384]{2,1,0:T(8,128)(2,1)S(1)}, u32[]{:S(2)}, u32[]{:S(2)}) collective-permute-start(bf16[2,320,384]{2,1,0:T(8,128)(2,1)S(1)} %get-tuple-element.110), channel_id=1, source_target_pairs={{0,8},{8,0},{16,24},{24,16},{1,9},{9,1},{17,25},{25,17},{2,10},{10... | collective-permute-start | bytes 1474568 | tf_op jit(solution)/shard_map/ppermute | solution.py:483
  32.8 1.5 %collective-permute-start.28 = (bf16[2,320,384]{2,1,0:T(8,128)(2,1)S(1)}, bf16[2,320,384]{2,1,0:T(8,128)(2,1)S(1)}, u32[]{:S(2)}, u32[]{:S(2)}) collective-permute-start(bf16[2,320,384]{2,1,0:T(8,128)(2,1)S(1)} %get-tuple-element.113), channel_id=1, source_target_pairs={{0,16},{8,24},{16,0},{24,8},{1,17},{9,25},{17,1},{25,9},{2,18},{10... | collective-permute-start | bytes 1474568 | tf_op jit(solution)/shard_map/ppermute | solution.py:483
  34.4 8.5 %gate_up.7 = (bf16[2,320,384]{2,1,0:T(8,128)(2,1)S(1)}, bf16[2,320,384]{2,1,0:T(8,128)(2,1)S(1)}, f32[320,384]{1,0:T(8,128)S(1)}, f32[320,384]{1,0:T(8,128)S(1)}...) custom-call(s32[2]{0:T(128)S(1)} %pad_add_fusion.me_ref, s32[2,16]{1,0:T(2,128)S(1)} %get-tuple-element.98.refs_0_.offs, ...), custom_call_target="tpu_custom_call" | custom-call | flops 1094713344 | bytes 14008320 | tf_op jit(solution)/shard_map/gate_up/pallas_call | solution.py:404
  42.8 0.6 collective-permute-start.34
  43.4 0.5 collective-permute-start.36
  43.9 4.1 %weigh.3 = (f32[1392,128]{1,0:T(8,128)S(1)}, bf16[8,128,1280]{2,1,0:T(8,128)(2,1)S(1)}, s32[1]{0:T(128)}) custom-call(s32[2,16]{1,0:T(2,128)S(1)} %get-tuple-element.98.refs_0_.offs, bf16[1392,1024]{1,0:T(8,128)(2,1)S(1)} %get-tuple-element.105.select, f32[8,16,128]{2,1,0:T(8,128)S(1)} %get-tuple-element.106.probs, ...), custom_call_target="tpu_custom_call" | custom-call | flops 6000000000 | bytes 8000000 | tf_op jit(solution)/shard_map/weigh/pallas_call | solution.py:292
  48.0 0.0 collective-permute-done.26
  48.0 0.1 fusion.25
  48.1 1.6 %collective-permute-start.27 = (bf16[320,384]{1,0:T(8,128)(2,1)S(1)}, bf16[320,384]{1,0:T(8,128)(2,1)S(1)}, u32[]{:S(2)}, u32[]{:S(2)}) collective-permute-start(bf16[320,384]{1,0:T(8,128)(2,1)S(1)} %fusion.25), channel_id=1, source_target_pairs={{0,16},{8,24},{16,0},{24,8},{1,17},{9,25},{17,1},{25,9},{2,18},{10... | collective-permute-start | bytes 737288 | tf_op jit(solution)/shard_map/ppermute | solution.py:483
  49.7 0.1 fusion.21
  49.8 1.6 %collective-permute-start.29 = (bf16[320,384]{1,0:T(8,128)(2,1)S(1)}, bf16[320,384]{1,0:T(8,128)(2,1)S(1)}, u32[]{:S(2)}, u32[]{:S(2)}) collective-permute-start(bf16[320,384]{1,0:T(8,128)(2,1)S(1)} %fusion.21), channel_id=1, source_target_pairs={{0,8},{8,0},{16,24},{24,16},{1,9},{9,1},{17,25},{25,17},{2,10},{10... | collective-permute-start | bytes 737288 | tf_op jit(solution)/shard_map/ppermute | solution.py:483
  51.4 5.7 %collective-permute-done.34 = bf16[2,320,384]{2,1,0:T(8,128)(2,1)S(1)} collective-permute-done((bf16[2,320,384]{2,1,0:T(8,128)(2,1)S(1)}, bf16[2,320,384]{2,1,0:T(8,128)(2,1)S(1)}, u32[]{:S(2)}, u32[]{:S(2)}) %collective-permute-start.34) | collective-permute-done | bytes 491552 | tf_op jit(solution)/shard_map/ppermute | solution.py:483
  57.1 0.1 fusion.19
  57.1 0.5 collective-permute-start.35
  57.7 0.1 fusion.15
  57.7 1.5 %collective-permute-start.37 = (bf16[320,384]{1,0:T(8,128)(2,1)S(1)}, bf16[320,384]{1,0:T(8,128)(2,1)S(1)}, u32[]{:S(2)}, u32[]{:S(2)}) collective-permute-start(bf16[320,384]{1,0:T(8,128)(2,1)S(1)} %fusion.15), channel_id=1, source_target_pairs={{0,8},{8,0},{16,24},{24,16},{1,9},{9,1},{17,25},{25,17},{2,10},{10... | collective-permute-start | bytes 737288 | tf_op jit(solution)/shard_map/ppermute | solution.py:483
  59.2 3.6 %collective-permute-done.27 = bf16[320,384]{1,0:T(8,128)(2,1)S(1)} collective-permute-done((bf16[320,384]{1,0:T(8,128)(2,1)S(1)}, bf16[320,384]{1,0:T(8,128)(2,1)S(1)}, u32[]{:S(2)}, u32[]{:S(2)}) %collective-permute-start.27) | collective-permute-done | bytes 245792 | tf_op jit(solution)/shard_map/ppermute | solution.py:483
  62.9 0.3 fusion.24.refs_0_
  63.1 1.5 %collective-permute-start.31 = (bf16[320,384]{1,0:T(8,128)(2,1)S(1)}, bf16[320,384]{1,0:T(8,128)(2,1)S(1)}, u32[]{:S(2)}, u32[]{:S(2)}) collective-permute-start(bf16[320,384]{1,0:T(8,128)(2,1)S(1)} %fusion.24.refs_0_), channel_id=1, source_target_pairs={{0,16},{8,24},{16,0},{24,8},{1,17},{9,25},{17,1},{25,9},{2,18},{10... | collective-permute-start | bytes 737288 | tf_op jit(solution)/shard_map/ppermute | solution.py:483
  64.6 0.6 collective-permute-start.30
  65.2 2.9 %collective-permute-done.35 = bf16[320,384]{1,0:T(8,128)(2,1)S(1)} collective-permute-done((bf16[320,384]{1,0:T(8,128)(2,1)S(1)}, bf16[320,384]{1,0:T(8,128)(2,1)S(1)}, u32[]{:S(2)}, u32[]{:S(2)}) %collective-permute-start.35) | collective-permute-done | bytes 245792 | tf_op jit(solution)/shard_map/ppermute | solution.py:483
  68.1 0.3 fusion.18.refs_5_
  68.4 1.5 %collective-permute-start.40 = (bf16[320,384]{1,0:T(8,128)(2,1)S(1)}, bf16[320,384]{1,0:T(8,128)(2,1)S(1)}, u32[]{:S(2)}, u32[]{:S(2)}) collective-permute-start(bf16[320,384]{1,0:T(8,128)(2,1)S(1)} %fusion.18.refs_5_), channel_id=1, source_target_pairs={{0,24},{8,16},{16,8},{24,0},{1,25},{9,17},{17,9},{25,1},{2,26},{10... | collective-permute-start | bytes 737288 | tf_op jit(solution)/shard_map/ppermute | solution.py:483
  69.9 1.5 %collective-permute-start.39 = (bf16[320,384]{1,0:T(8,128)(2,1)S(1)}, bf16[320,384]{1,0:T(8,128)(2,1)S(1)}, u32[]{:S(2)}, u32[]{:S(2)}) collective-permute-start(bf16[320,384]{1,0:T(8,128)(2,1)S(1)} %fusion.18.refs_5_), channel_id=1, source_target_pairs={{0,16},{8,24},{16,0},{24,8},{1,17},{9,25},{17,1},{25,9},{2,18},{10... | collective-permute-start | bytes 737288 | tf_op jit(solution)/shard_map/ppermute | solution.py:483
  71.4 0.5 collective-permute-start.38
  72.0 6.5 %collective-permute-done.31.refs_2_ = bf16[320,384]{1,0:T(8,128)(2,1)S(1)} collective-permute-done((bf16[320,384]{1,0:T(8,128)(2,1)S(1)}, bf16[320,384]{1,0:T(8,128)(2,1)S(1)}, u32[]{:S(2)}, u32[]{:S(2)}) %collective-permute-start.31) | collective-permute-done | bytes 245792 | tf_op jit(solution)/shard_map/ppermute | solution.py:483
  78.5 1.2 %collective-permute-start.33 = (bf16[160,384]{1,0:T(8,128)(2,1)S(1)}, bf16[160,384]{1,0:T(8,128)(2,1)S(1)}, u32[]{:S(2)}, u32[]{:S(2)}) collective-permute-start(bf16[160,384]{1,0:T(8,128)(2,1)S(1)} %slice.123), channel_id=1, source_target_pairs={{0,8},{8,0},{16,24},{24,16},{1,9},{9,1},{17,25},{25,17},{2,10},{10... | collective-permute-start | bytes 368648 | tf_op jit(solution)/shard_map/ppermute | solution.py:483
  79.7 0.9 collective-permute-start.32
  80.6 0.0 collective-permute-done.40.refs_8_
  80.6 3.3 %collective-permute-done.39.refs_7_ = bf16[320,384]{1,0:T(8,128)(2,1)S(1)} collective-permute-done((bf16[320,384]{1,0:T(8,128)(2,1)S(1)}, bf16[320,384]{1,0:T(8,128)(2,1)S(1)}, u32[]{:S(2)}, u32[]{:S(2)}) %collective-permute-start.39) | collective-permute-done | bytes 245792 | tf_op jit(solution)/shard_map/ppermute | solution.py:483
  83.9 0.7 collective-permute-done.33.refs_4_
  84.6 0.7 collective-permute-done.32.refs_3_
  85.3 8.3 %down.3 = (bf16[4,128,512]{2,1,0:T(8,128)(2,1)S(1)}, bf16[4,128,512]{2,1,0:T(8,128)(2,1)S(1)}) custom-call(s32[2]{0:T(128)S(1)} %pad_add_fusion.me_ref, s32[2,16]{1,0:T(2,128)S(1)} %get-tuple-element.98.refs_0_.offs, bf16[16,768,512]{2,1,0:T(8,128)(2,1)} %w_down.1, f32[1392,128]{1,0:T(8,128)S(1)} %get-tuple-element.117.scale, ...), custom_call_target="tpu_custom_call" | custom-call | flops 2554331136 | bytes 12582912 | tf_op jit(solution)/shard_map/down/pallas_call | solution.py:469
  93.7 0.1 collective-permute-start.41
  93.8 1.9 %collective-permute-done.41 = bf16[4,128,512]{2,1,0:T(8,128)(2,1)S(1)} collective-permute-done((bf16[4,128,512]{2,1,0:T(8,128)(2,1)S(1)}, bf16[4,128,512]{2,1,0:T(8,128)(2,1)S(1)}, u32[]{:S(2)}, u32[]{:S(2)}) %collective-permute-start.41) | collective-permute-done | bytes 524320 | tf_op jit(solution)/shard_map/ppermute | solution.py:483
  95.7 0.2 fusion.29
  95.9 4.1 %collective-permute-start.42 = (bf16[128,512]{1,0:T(8,128)(2,1)S(1)}, bf16[128,512]{1,0:T(8,128)(2,1)S(1)}, u32[]{:S(2)}, u32[]{:S(2)}) collective-permute-start(bf16[128,512]{1,0:T(8,128)(2,1)S(1)} %get-tuple-element.133), channel_id=1, source_target_pairs={{0,6},{1,7},{2,4},{3,5},{4,2},{5,3},{6,0},{7,1},{8,14},{9,15},{10,... | collective-permute-start | bytes 393224 | tf_op jit(solution)/shard_map/ppermute | solution.py:483
  100.0 0.0 collective-permute-start.44
  100.0 0.6 collective-permute-start.43
  101.3 3.0 %collective-permute-done.42 = bf16[128,512]{1,0:T(8,128)(2,1)S(1)} collective-permute-done((bf16[128,512]{1,0:T(8,128)(2,1)S(1)}, bf16[128,512]{1,0:T(8,128)(2,1)S(1)}, u32[]{:S(2)}, u32[]{:S(2)}) %collective-permute-start.42) | collective-permute-done | bytes 131104 | tf_op jit(solution)/shard_map/ppermute | solution.py:483
  104.3 3.7 %collective-permute-done.44 = bf16[128,512]{1,0:T(8,128)(2,1)S(1)} collective-permute-done((bf16[128,512]{1,0:T(8,128)(2,1)S(1)}, bf16[128,512]{1,0:T(8,128)(2,1)S(1)}, u32[]{:S(2)}, u32[]{:S(2)}) %collective-permute-start.44) | collective-permute-done | bytes 131104 | tf_op jit(solution)/shard_map/ppermute | solution.py:483
  108.0 3.0 %collective-permute-done.43 = bf16[128,512]{1,0:T(8,128)(2,1)S(1)} collective-permute-done((bf16[128,512]{1,0:T(8,128)(2,1)S(1)}, bf16[128,512]{1,0:T(8,128)(2,1)S(1)}, u32[]{:S(2)}, u32[]{:S(2)}) %collective-permute-start.43) | collective-permute-done | bytes 131104 | tf_op jit(solution)/shard_map/ppermute | solution.py:483
  111.0 0.1 fusion.28
  111.1 0.3 conditional.1
  111.4 0.0 copy-start.4
  111.4 0.6 copy-done.4
  (21 shorter events, 0.1 us)
Async XLA Ops:
  0.0 0.9 copy-start
  0.9 0.7 copy-start.1
  1.6 0.7 copy-start.2
  2.3 11.2 %collective-permute-start.22 = (bf16[144,512]{1,0:T(8,128)(2,1)S(1)}, bf16[144,512]{1,0:T(8,128)(2,1)S(1)}, u32[]{:S(2)}, u32[]{:S(2)}) collective-permute-start(bf16[144,512]{1,0:T(8,128)(2,1)S(1)} %pack.1.refs_0_), channel_id=1, source_target_pairs={{0,4},{1,5},{2,6},{3,7},{4,0},{5,1},{6,2},{7,3},{8,12},{9,13},{10,... | collective-permute-start | bytes 442376 | tf_op jit(solution)/shard_map/ppermute | solution.py:483
  6.4 8.2 %collective-permute-start.20 = (bf16[144,512]{1,0:T(8,128)(2,1)S(1)}, bf16[144,512]{1,0:T(8,128)(2,1)S(1)}, u32[]{:S(2)}, u32[]{:S(2)}) collective-permute-start(bf16[144,512]{1,0:T(8,128)(2,1)S(1)} %pack.1.refs_0_), channel_id=1, source_target_pairs={{0,2},{1,3},{2,0},{3,1},{4,6},{5,7},{6,4},{7,5},{8,10},{9,11},{10,... | collective-permute-start | bytes 442376 | tf_op jit(solution)/shard_map/ppermute | solution.py:483
  13.5 5.1 %collective-permute-start.24 = (bf16[144,512]{1,0:T(8,128)(2,1)S(1)}, bf16[144,512]{1,0:T(8,128)(2,1)S(1)}, u32[]{:S(2)}, u32[]{:S(2)}) collective-permute-start(bf16[144,512]{1,0:T(8,128)(2,1)S(1)} %collective-permute-done.22.refs_4_), channel_id=1, source_target_pairs={{0,2},{1,3},{2,0},{3,1},{4,6},{5,7},{6,4},{7,5},{8,10},{9,11},{10,... | collective-permute-start | bytes 442376 | tf_op jit(solution)/shard_map/ppermute | solution.py:483
  14.1 4.6 %collective-permute-start.19 = (bf16[144,512]{1,0:T(8,128)(2,1)S(1)}, bf16[144,512]{1,0:T(8,128)(2,1)S(1)}, u32[]{:S(2)}, u32[]{:S(2)}) collective-permute-start(bf16[144,512]{1,0:T(8,128)(2,1)S(1)} %pack.1.refs_0_), channel_id=1, source_target_pairs={{0,1},{1,0},{2,3},{3,2},{4,5},{5,4},{6,7},{7,6},{8,9},{9,8},{10,11... | collective-permute-start | bytes 442376 | tf_op jit(solution)/shard_map/ppermute | solution.py:483
  14.1 4.6 %collective-permute-start.23 = (bf16[144,512]{1,0:T(8,128)(2,1)S(1)}, bf16[144,512]{1,0:T(8,128)(2,1)S(1)}, u32[]{:S(2)}, u32[]{:S(2)}) collective-permute-start(bf16[144,512]{1,0:T(8,128)(2,1)S(1)} %collective-permute-done.22.refs_4_), channel_id=1, source_target_pairs={{0,1},{1,0},{2,3},{3,2},{4,5},{5,4},{6,7},{7,6},{8,9},{9,8},{10,11... | collective-permute-start | bytes 442376 | tf_op jit(solution)/shard_map/ppermute | solution.py:483
  14.6 4.1 %collective-permute-start.21 = (bf16[144,512]{1,0:T(8,128)(2,1)S(1)}, bf16[144,512]{1,0:T(8,128)(2,1)S(1)}, u32[]{:S(2)}, u32[]{:S(2)}) collective-permute-start(bf16[144,512]{1,0:T(8,128)(2,1)S(1)} %collective-permute-done.20.refs_2_), channel_id=1, source_target_pairs={{0,1},{1,0},{2,3},{3,2},{4,5},{5,4},{6,7},{7,6},{8,9},{9,8},{10,11... | collective-permute-start | bytes 442376 | tf_op jit(solution)/shard_map/ppermute | solution.py:483
  18.7 1.4 %collective-permute-start.25 = (bf16[144,512]{1,0:T(8,128)(2,1)S(1)}, bf16[144,512]{1,0:T(8,128)(2,1)S(1)}, u32[]{:S(2)}, u32[]{:S(2)}) collective-permute-start(bf16[144,512]{1,0:T(8,128)(2,1)S(1)} %collective-permute-done.24.refs_6_), channel_id=1, source_target_pairs={{0,1},{1,0},{2,3},{3,2},{4,5},{5,4},{6,7},{7,6},{8,9},{9,8},{10,11... | collective-permute-start | bytes 442376 | tf_op jit(solution)/shard_map/ppermute | solution.py:483
  18.7 15.7 %slice-start = ((s8[12582912]{0:T(1024)(128)(4,1)}), s8[4194304]{0:T(1024)(128)(4,1)S(1)}, s32[]{:S(2)}) async-start(s8[12582912]{0:T(1024)(128)(4,1)} %bitcast.111), calls=%async_computation | async-start | bytes 8388608
  18.7 15.6 %slice-start.1 = ((s8[12582912]{0:T(1024)(128)(4,1)}), s8[4194304]{0:T(1024)(128)(4,1)S(1)}, s32[]{:S(2)}) async-start(s8[12582912]{0:T(1024)(128)(4,1)} %bitcast.111), calls=%async_computation.1 | async-start | bytes 8388608
  18.7 15.6 %slice-start.2 = ((s8[12582912]{0:T(1024)(128)(4,1)}), s8[4194304]{0:T(1024)(128)(4,1)S(1)}, s32[]{:S(2)}) async-start(s8[12582912]{0:T(1024)(128)(4,1)} %bitcast.111), calls=%async_computation.2 | async-start | bytes 8388608
  31.2 16.8 %collective-permute-start.26 = (bf16[2,320,384]{2,1,0:T(8,128)(2,1)S(1)}, bf16[2,320,384]{2,1,0:T(8,128)(2,1)S(1)}, u32[]{:S(2)}, u32[]{:S(2)}) collective-permute-start(bf16[2,320,384]{2,1,0:T(8,128)(2,1)S(1)} %get-tuple-element.110), channel_id=1, source_target_pairs={{0,8},{8,0},{16,24},{24,16},{1,9},{9,1},{17,25},{25,17},{2,10},{10... | collective-permute-start | bytes 1474568 | tf_op jit(solution)/shard_map/ppermute | solution.py:483
  32.8 16.9 %collective-permute-start.28 = (bf16[2,320,384]{2,1,0:T(8,128)(2,1)S(1)}, bf16[2,320,384]{2,1,0:T(8,128)(2,1)S(1)}, u32[]{:S(2)}, u32[]{:S(2)}) collective-permute-start(bf16[2,320,384]{2,1,0:T(8,128)(2,1)S(1)} %get-tuple-element.113), channel_id=1, source_target_pairs={{0,16},{8,24},{16,0},{24,8},{1,17},{9,25},{17,1},{25,9},{2,18},{10... | collective-permute-start | bytes 1474568 | tf_op jit(solution)/shard_map/ppermute | solution.py:483
  42.8 14.2 %collective-permute-start.34 = (bf16[2,320,384]{2,1,0:T(8,128)(2,1)S(1)}, bf16[2,320,384]{2,1,0:T(8,128)(2,1)S(1)}, u32[]{:S(2)}, u32[]{:S(2)}) collective-permute-start(bf16[2,320,384]{2,1,0:T(8,128)(2,1)S(1)} %get-tuple-element.121), channel_id=1, source_target_pairs={{0,8},{8,0},{16,24},{24,16},{1,9},{9,1},{17,25},{25,17},{2,10},{10... | collective-permute-start | bytes 1474568 | tf_op jit(solution)/shard_map/ppermute | solution.py:483
  43.4 14.2 %collective-permute-start.36 = (bf16[2,320,384]{2,1,0:T(8,128)(2,1)S(1)}, bf16[2,320,384]{2,1,0:T(8,128)(2,1)S(1)}, u32[]{:S(2)}, u32[]{:S(2)}) collective-permute-start(bf16[2,320,384]{2,1,0:T(8,128)(2,1)S(1)} %get-tuple-element.122), channel_id=1, source_target_pairs={{0,16},{8,24},{16,0},{24,8},{1,17},{9,25},{17,1},{25,9},{2,18},{10... | collective-permute-start | bytes 1474568 | tf_op jit(solution)/shard_map/ppermute | solution.py:483
  48.1 14.8 %collective-permute-start.27 = (bf16[320,384]{1,0:T(8,128)(2,1)S(1)}, bf16[320,384]{1,0:T(8,128)(2,1)S(1)}, u32[]{:S(2)}, u32[]{:S(2)}) collective-permute-start(bf16[320,384]{1,0:T(8,128)(2,1)S(1)} %fusion.25), channel_id=1, source_target_pairs={{0,16},{8,24},{16,0},{24,8},{1,17},{9,25},{17,1},{25,9},{2,18},{10... | collective-permute-start | bytes 737288 | tf_op jit(solution)/shard_map/ppermute | solution.py:483
  49.8 13.1 %collective-permute-start.29 = (bf16[320,384]{1,0:T(8,128)(2,1)S(1)}, bf16[320,384]{1,0:T(8,128)(2,1)S(1)}, u32[]{:S(2)}, u32[]{:S(2)}) collective-permute-start(bf16[320,384]{1,0:T(8,128)(2,1)S(1)} %fusion.21), channel_id=1, source_target_pairs={{0,8},{8,0},{16,24},{24,16},{1,9},{9,1},{17,25},{25,17},{2,10},{10... | collective-permute-start | bytes 737288 | tf_op jit(solution)/shard_map/ppermute | solution.py:483
  57.1 11.0 %collective-permute-start.35 = (bf16[320,384]{1,0:T(8,128)(2,1)S(1)}, bf16[320,384]{1,0:T(8,128)(2,1)S(1)}, u32[]{:S(2)}, u32[]{:S(2)}) collective-permute-start(bf16[320,384]{1,0:T(8,128)(2,1)S(1)} %fusion.19), channel_id=1, source_target_pairs={{0,16},{8,24},{16,0},{24,8},{1,17},{9,25},{17,1},{25,9},{2,18},{10... | collective-permute-start | bytes 737288 | tf_op jit(solution)/shard_map/ppermute | solution.py:483
  57.7 10.4 %collective-permute-start.37 = (bf16[320,384]{1,0:T(8,128)(2,1)S(1)}, bf16[320,384]{1,0:T(8,128)(2,1)S(1)}, u32[]{:S(2)}, u32[]{:S(2)}) collective-permute-start(bf16[320,384]{1,0:T(8,128)(2,1)S(1)} %fusion.15), channel_id=1, source_target_pairs={{0,8},{8,0},{16,24},{24,16},{1,9},{9,1},{17,25},{25,17},{2,10},{10... | collective-permute-start | bytes 737288 | tf_op jit(solution)/shard_map/ppermute | solution.py:483
  63.1 15.3 %collective-permute-start.31 = (bf16[320,384]{1,0:T(8,128)(2,1)S(1)}, bf16[320,384]{1,0:T(8,128)(2,1)S(1)}, u32[]{:S(2)}, u32[]{:S(2)}) collective-permute-start(bf16[320,384]{1,0:T(8,128)(2,1)S(1)} %fusion.24.refs_0_), channel_id=1, source_target_pairs={{0,16},{8,24},{16,0},{24,8},{1,17},{9,25},{17,1},{25,9},{2,18},{10... | collective-permute-start | bytes 737288 | tf_op jit(solution)/shard_map/ppermute | solution.py:483
  64.6 15.1 %collective-permute-start.30 = (bf16[320,384]{1,0:T(8,128)(2,1)S(1)}, bf16[320,384]{1,0:T(8,128)(2,1)S(1)}, u32[]{:S(2)}, u32[]{:S(2)}) collective-permute-start(bf16[320,384]{1,0:T(8,128)(2,1)S(1)} %fusion.24.refs_0_), channel_id=1, source_target_pairs={{0,8},{8,0},{16,24},{24,16},{1,9},{9,1},{17,25},{25,17},{2,10},{10... | collective-permute-start | bytes 737288 | tf_op jit(solution)/shard_map/ppermute | solution.py:483
  68.4 12.2 %collective-permute-start.40 = (bf16[320,384]{1,0:T(8,128)(2,1)S(1)}, bf16[320,384]{1,0:T(8,128)(2,1)S(1)}, u32[]{:S(2)}, u32[]{:S(2)}) collective-permute-start(bf16[320,384]{1,0:T(8,128)(2,1)S(1)} %fusion.18.refs_5_), channel_id=1, source_target_pairs={{0,24},{8,16},{16,8},{24,0},{1,25},{9,17},{17,9},{25,1},{2,26},{10... | collective-permute-start | bytes 737288 | tf_op jit(solution)/shard_map/ppermute | solution.py:483
  69.9 14.0 %collective-permute-start.39 = (bf16[320,384]{1,0:T(8,128)(2,1)S(1)}, bf16[320,384]{1,0:T(8,128)(2,1)S(1)}, u32[]{:S(2)}, u32[]{:S(2)}) collective-permute-start(bf16[320,384]{1,0:T(8,128)(2,1)S(1)} %fusion.18.refs_5_), channel_id=1, source_target_pairs={{0,16},{8,24},{16,0},{24,8},{1,17},{9,25},{17,1},{25,9},{2,18},{10... | collective-permute-start | bytes 737288 | tf_op jit(solution)/shard_map/ppermute | solution.py:483
  71.4 12.5 %collective-permute-start.38 = (bf16[320,384]{1,0:T(8,128)(2,1)S(1)}, bf16[320,384]{1,0:T(8,128)(2,1)S(1)}, u32[]{:S(2)}, u32[]{:S(2)}) collective-permute-start(bf16[320,384]{1,0:T(8,128)(2,1)S(1)} %fusion.18.refs_5_), channel_id=1, source_target_pairs={{0,8},{8,0},{16,24},{24,16},{1,9},{9,1},{17,25},{25,17},{2,10},{10... | collective-permute-start | bytes 737288 | tf_op jit(solution)/shard_map/ppermute | solution.py:483
  78.5 6.2 %collective-permute-start.33 = (bf16[160,384]{1,0:T(8,128)(2,1)S(1)}, bf16[160,384]{1,0:T(8,128)(2,1)S(1)}, u32[]{:S(2)}, u32[]{:S(2)}) collective-permute-start(bf16[160,384]{1,0:T(8,128)(2,1)S(1)} %slice.123), channel_id=1, source_target_pairs={{0,8},{8,0},{16,24},{24,16},{1,9},{9,1},{17,25},{25,17},{2,10},{10... | collective-permute-start | bytes 368648 | tf_op jit(solution)/shard_map/ppermute | solution.py:483
  79.7 5.7 %collective-permute-start.32 = (bf16[160,384]{1,0:T(8,128)(2,1)S(1)}, bf16[160,384]{1,0:T(8,128)(2,1)S(1)}, u32[]{:S(2)}, u32[]{:S(2)}) collective-permute-start(bf16[160,384]{1,0:T(8,128)(2,1)S(1)} %slice.122), channel_id=1, source_target_pairs={{0,16},{8,24},{16,0},{24,8},{1,17},{9,25},{17,1},{25,9},{2,18},{10... | collective-permute-start | bytes 368648 | tf_op jit(solution)/shard_map/ppermute | solution.py:483
  93.7 2.0 %collective-permute-start.41 = (bf16[4,128,512]{2,1,0:T(8,128)(2,1)S(1)}, bf16[4,128,512]{2,1,0:T(8,128)(2,1)S(1)}, u32[]{:S(2)}, u32[]{:S(2)}) collective-permute-start(bf16[4,128,512]{2,1,0:T(8,128)(2,1)S(1)} %get-tuple-element.124), channel_id=1, source_target_pairs={{0,1},{1,0},{2,3},{3,2},{4,5},{5,4},{6,7},{7,6},{8,9},{9,8},{10,11... | collective-permute-start | bytes 1572872 | tf_op jit(solution)/shard_map/ppermute | solution.py:483
  95.9 8.4 %collective-permute-start.42 = (bf16[128,512]{1,0:T(8,128)(2,1)S(1)}, bf16[128,512]{1,0:T(8,128)(2,1)S(1)}, u32[]{:S(2)}, u32[]{:S(2)}) collective-permute-start(bf16[128,512]{1,0:T(8,128)(2,1)S(1)} %get-tuple-element.133), channel_id=1, source_target_pairs={{0,6},{1,7},{2,4},{3,5},{4,2},{5,3},{6,0},{7,1},{8,14},{9,15},{10,... | collective-permute-start | bytes 393224 | tf_op jit(solution)/shard_map/ppermute | solution.py:483
  100.0 8.0 %collective-permute-start.44 = (bf16[128,512]{1,0:T(8,128)(2,1)S(1)}, bf16[128,512]{1,0:T(8,128)(2,1)S(1)}, u32[]{:S(2)}, u32[]{:S(2)}) collective-permute-start(bf16[128,512]{1,0:T(8,128)(2,1)S(1)} %get-tuple-element.134), channel_id=1, source_target_pairs={{0,2},{1,3},{2,0},{3,1},{4,6},{5,7},{6,4},{7,5},{8,10},{9,11},{10,... | collective-permute-start | bytes 393224 | tf_op jit(solution)/shard_map/ppermute | solution.py:483
  100.0 11.0 %collective-permute-start.43 = (bf16[128,512]{1,0:T(8,128)(2,1)S(1)}, bf16[128,512]{1,0:T(8,128)(2,1)S(1)}, u32[]{:S(2)}, u32[]{:S(2)}) collective-permute-start(bf16[128,512]{1,0:T(8,128)(2,1)S(1)} %get-tuple-element.135), channel_id=1, source_target_pairs={{0,4},{1,5},{2,6},{3,7},{4,0},{5,1},{6,2},{7,3},{8,12},{9,13},{10,... | collective-permute-start | bytes 393224 | tf_op jit(solution)/shard_map/ppermute | solution.py:483
  111.4 0.7 copy-start.4

commit v7 on v6

--- a/solution.py
+++ b/solution.py
@@ -46,9 +46,9 @@
     return pl.CostEstimate(flops=int(flops), bytes_accessed=int(moved), transcendentals=0)
 
 
-def pack_kernel(dims, tokens, ids, weights, packed):
+def pack_kernel(dims, tokens, routing, packed):
     rows, top = dims["rows"], dims["top"]
-    chance = weights[...]
+    chance = routing[top:, :]
     chance = chance / jnp.sum(chance, axis=0, keepdims=True)
     high = chance.astype(BF16)
     rest = chance - high.astype(F32)
@@ -56,7 +56,7 @@
     low = (rest - middle.astype(F32)).astype(BF16)
     packed[:rows, :] = tokens[...]
     packed[rows:, :] = jnp.zeros((META, packed.shape[1]), BF16)
-    parts = (ids[...].astype(F32), high.astype(F32), middle.astype(F32), low.astype(F32))
+    parts = (routing[:top, :], high.astype(F32), middle.astype(F32), low.astype(F32))
     for i, part in enumerate(parts):
         block = jnp.concatenate([part, jnp.zeros((META - top, rows), F32)], axis=0)
         packed[rows:, i * rows : (i + 1) * rows] = block.astype(BF16)
@@ -66,11 +66,11 @@
     return pl.pallas_call(
         functools.partial(pack_kernel, dims),
         out_shape=jax.ShapeDtypeStruct((dims["rows"] + META, tokens.shape[1]), BF16),
-        in_specs=[vmem()] * 3,
+        in_specs=[vmem()] * 2,
         out_specs=vmem(),
         compiler_params=params(),
         name="pack",
-    )(tokens, ids.T, weights.T)
+    )(tokens, jnp.concatenate([ids.T.astype(F32), weights.T], axis=0))
 
 
 def loop(count, body, carry):
@@ -114,7 +114,7 @@
         starts.append(before)
         before = before + total[e : e + 1, :]
     start = jnp.concatenate(starts, axis=0) if experts > 1 else starts[0]
-    start, total = start.astype(jnp.int32), total.astype(jnp.int32)
+    start, before = start.astype(jnp.int32), before.astype(jnp.int32)
 
     def place(block, carry):
         ids = chosen_ids(block)
@@ -128,7 +128,7 @@
         return carry
 
     loop(blocks, place, 0)
-    return start, total
+    return start, before
 
 
 def window_hits(dims, rowid, block, e, start):
@@ -152,11 +152,11 @@
             select[at, cols] = select[at, cols] + hit.astype(F32).astype(BF16)
 
 
-def publish(dims, offs, start, total):
+def publish(dims, offs, start, end):
     starts = [start[e, 0] for e in range(dims["experts"])]
     for e in range(dims["experts"]):
         offs[0, e] = starts[e]
-        offs[1, e] = total[e, 0]
+    offs[0, dims["experts"]] = end[0, 0]
     return starts
 
 
@@ -201,7 +201,7 @@
         jax.ShapeDtypeStruct((blocks, experts, rows), jnp.int32),
         jax.ShapeDtypeStruct((blocks, experts, rows), F32),
         jax.ShapeDtypeStruct((blocks, top, rows), jnp.int32),
-    ), jax.ShapeDtypeStruct((2, experts), jnp.int32)
+    ), jax.ShapeDtypeStruct((1, experts + 1), jnp.int32)
 
 
 def dispatch(dims, me, gathered):
@@ -303,8 +303,7 @@
 
 def row_mask(dims, first, offs, e):
     at = lax.broadcasted_iota(jnp.int32, (dims["window"], 1), 0) + first
-    begin = offs[0, e]
-    return (at >= begin) & (at < begin + offs[1, e])
+    return (at >= offs[0, e]) & (at < offs[0, e + 1])
 
 
 def batches(experts):
@@ -317,15 +316,15 @@
         blocks, rows = dims["blocks"], dims["rows"]
         packed, refs = refs[:blocks], refs[blocks:]
         w_gate, w_up, rowid, probs, rowk, x, select, offs_out, meta, refs = *refs[:9], refs[9:]
-        gx, uy, g2, u1, g0, u0, gate_w, up_w, gate, up, sems, table = refs
+        gx, uy, g2, u1, g0, u0, weights, sums, sems, table = refs
     else:
-        offs, x, w_gate, w_up, gx, uy, g2, u1, g0, u0, gate_w, up_w, gate, up, sems = refs
+        offs, x, w_gate, w_up, gx, uy, g2, u1, g0, u0, weights, sums, sems = refs
     units = pl.ds(c * part, part)
 
     def copies(e):
         return (
-            pltpu.make_async_copy(w_gate.at[e, units, :], gate_w.at[e], sems.at[0, e]),
-            pltpu.make_async_copy(w_up.at[e, units, :], up_w.at[e], sems.at[1, e]),
+            pltpu.make_async_copy(w_gate.at[e, units, :], weights.at[e, pl.ds(0, part), :], sems.at[0, e]),
+            pltpu.make_async_copy(w_up.at[e, units, :], weights.at[e, pl.ds(part, part), :], sems.at[1, e]),
         )
 
     for e in range(experts):
@@ -355,14 +354,15 @@
             rows_in = x[pl.ds(first, window), :]
             keep = (lax.broadcasted_iota(jnp.int32, (ALIGN, 1), 0) + first) >= offs[0, e]
             edge, rest = pl.ds(first, ALIGN), pl.ds(first + ALIGN, window - ALIGN)
-            for held, into in ((gate_w, gate), (up_w, up)):
-                got = lax.dot_general(rows_in, held[e], contract, preferred_element_type=F32)
-                into[edge, :] = jnp.where(keep, got[:ALIGN], into[edge, :])
-                into[rest, :] = got[ALIGN:]
+            got = lax.dot_general(rows_in, weights[e], contract, preferred_element_type=F32)
+            sums[edge, :] = jnp.where(keep, got[:ALIGN], sums[edge, :])
+            sums[rest, :] = got[ALIGN:]
     me = me_ref[0]
 
-    def piece(total, j):
-        return total[pl.ds(pl.multiple_of((me ^ j) * quarter, ALIGN), quarter), :]
+    gate, up = slice(0, part), slice(part, 2 * part)
+
+    def piece(cols, j):
+        return sums[pl.ds(pl.multiple_of((me ^ j) * quarter, ALIGN), quarter), cols]
 
     gx[0] = piece(gate, 1).astype(BF16)
     gx[1] = piece(gate, 3).astype(BF16)
@@ -382,10 +382,8 @@
     first_part = len(sources) > 2
     outs = (half, half, own, own, own, own)
     scratch = [
-        pltpu.VMEM((experts, part, width), BF16),
-        pltpu.VMEM((experts, part, width), BF16),
-        pltpu.VMEM((padded, part), F32),
-        pltpu.VMEM((padded, part), F32),
+        pltpu.VMEM((experts, 2 * part, width), BF16),
+        pltpu.VMEM((padded, 2 * part), F32),
         pltpu.SemaphoreType.DMA((2, experts)),
     ]
     into = (vmem(),) * len(outs)

time: 112 us -> 113 us (level)
  local copies, waits for them, and re-layouts: 2.99 us -> 1.62 us
  other arithmetic: 1.09 us -> 2.4 us
    unnamed x14 -> x10, local copies, waits for them, and re-layouts: 2.94 us -> 1.56 us
where the time goes in v7:
time: 113 us; the launch traced here: 112 us
  waiting for transfers between devices  45.8 us (41%)
  Pallas kernels  32.6 us (29%)
  starting transfers between devices  28.8 us (25%)
  other arithmetic  2.4 us (2%)
  local copies, waits for them, and re-layouts  1.62 us (1%)
    ppermute x26, waiting for transfers between devices, swap(): return lax.ppermute(value, axis, [(i, i ^ bit) for i in range(count)])  45.8 us
    ppermute x26, starting transfers between devices, swap(): return lax.ppermute(value, axis, [(i, i ^ bit) for i in range(count)])  28.8 us
    pallas_call x2, Pallas kernels, gate_up(): pl.pallas_call(functools.partial(gate_up_kernel, dims, c, first_part), ou...  20.1 us
    pallas_call x1, Pallas kernels, down(): pl.pallas_call(functools.partial(down_kernel, dims, places), out_shape=ou...  8.35 us
    pallas_call x1, Pallas kernels, weigh(): pl.pallas_call(functools.partial(weigh_small_kernel if small else weigh_l...  4.12 us
  transfers between devices with their start and end apart: 26, of which 14 were waited for; matrix products, arithmetic and copies ran while one was open for 1% of the time, Pallas kernels for 11%

profile of v7, /device:TPU:0, one launch (start us, length us, event | category | flops | bytes accessed | tf_op | source)
XLA Modules:
  0.0 112.3 jit_solution(9500365579230840455)
XLA Ops:
  0.0 0.7 convert_bitcast_fusion
  0.7 0.7 pad_maximum_fusion.routing
  1.4 0.9 copy-done
  2.3 4.1 %collective-permute-start.22 = (bf16[144,512]{1,0:T(8,128)(2,1)S(1)}, bf16[144,512]{1,0:T(8,128)(2,1)S(1)}, u32[]{:S(2)}, u32[]{:S(2)}) collective-permute-start(bf16[144,512]{1,0:T(8,128)(2,1)S(1)} %pack.1.refs_0_), channel_id=1, source_target_pairs={{0,4},{1,5},{2,6},{3,7},{4,0},{5,1},{6,2},{7,3},{8,12},{9,13},{10,... | collective-permute-start | bytes 442376 | tf_op jit(solution)/shard_map/ppermute | solution.py:481
  6.4 1.6 %collective-permute-start.20 = (bf16[144,512]{1,0:T(8,128)(2,1)S(1)}, bf16[144,512]{1,0:T(8,128)(2,1)S(1)}, u32[]{:S(2)}, u32[]{:S(2)}) collective-permute-start(bf16[144,512]{1,0:T(8,128)(2,1)S(1)} %pack.1.refs_0_), channel_id=1, source_target_pairs={{0,2},{1,3},{2,0},{3,1},{4,6},{5,7},{6,4},{7,5},{8,10},{9,11},{10,... | collective-permute-start | bytes 442376 | tf_op jit(solution)/shard_map/ppermute | solution.py:481
  8.0 5.5 %collective-permute-done.22.refs_4_ = bf16[144,512]{1,0:T(8,128)(2,1)S(1)} collective-permute-done((bf16[144,512]{1,0:T(8,128)(2,1)S(1)}, bf16[144,512]{1,0:T(8,128)(2,1)S(1)}, u32[]{:S(2)}, u32[]{:S(2)}) %collective-permute-start.22) | collective-permute-done | bytes 147488 | tf_op jit(solution)/shard_map/ppermute | solution.py:481
  13.5 0.6 collective-permute-start.24
  14.1 0.0 collective-permute-start.19
  14.1 0.5 collective-permute-start.23
  14.7 0.0 collective-permute-start.21
  14.7 4.0 %collective-permute-done.24.refs_6_ = bf16[144,512]{1,0:T(8,128)(2,1)S(1)} collective-permute-done((bf16[144,512]{1,0:T(8,128)(2,1)S(1)}, bf16[144,512]{1,0:T(8,128)(2,1)S(1)}, u32[]{:S(2)}, u32[]{:S(2)}) %collective-permute-start.24) | collective-permute-done | bytes 147488 | tf_op jit(solution)/shard_map/ppermute | solution.py:481
  18.7 0.1 pad_add_fusion.me_ref
  18.7 0.0 collective-permute-done.19.refs_1_
  18.8 0.0 collective-permute-done.23.refs_5_
  18.8 0.0 collective-permute-done.21.refs_3_
  18.8 1.3 %collective-permute-done.25.refs_7_ = bf16[144,512]{1,0:T(8,128)(2,1)S(1)} collective-permute-done((bf16[144,512]{1,0:T(8,128)(2,1)S(1)}, bf16[144,512]{1,0:T(8,128)(2,1)S(1)}, u32[]{:S(2)}, u32[]{:S(2)}) %collective-permute-start.25) | collective-permute-done | bytes 147488 | tf_op jit(solution)/shard_map/ppermute | solution.py:481
  20.0 11.4 %gate_up.6 = (s32[8,16,128]{2,1,0:T(8,128)}, f32[8,16,128]{2,1,0:T(8,128)S(1)}, s32[8,8,128]{2,1,0:T(8,128)S(1)}, bf16[1392,512]{1,0:T(8,128)(2,1)S(1)}, bf16[13...) custom-call(s32[2]{0:T(128)S(1)} %pad_add_fusion.me_ref, ...), custom_call_target="tpu_custom_call" | custom-call | flops 1094713344 | bytes 14008320 | tf_op jit(solution)/shard_map/gate_up/pallas_call | solution.py:402
  31.5 1.6 %collective-permute-start.26 = (bf16[2,320,384]{2,1,0:T(8,128)(2,1)S(1)}, bf16[2,320,384]{2,1,0:T(8,128)(2,1)S(1)}, u32[]{:S(2)}, u32[]{:S(2)}) collective-permute-start(bf16[2,320,384]{2,1,0:T(8,128)(2,1)S(1)} %get-tuple-element.110), channel_id=1, source_target_pairs={{0,8},{8,0},{16,24},{24,16},{1,9},{9,1},{17,25},{25,17},{2,10},{10... | collective-permute-start | bytes 1474568 | tf_op jit(solution)/shard_map/ppermute | solution.py:481
  33.1 1.5 %collective-permute-start.28 = (bf16[2,320,384]{2,1,0:T(8,128)(2,1)S(1)}, bf16[2,320,384]{2,1,0:T(8,128)(2,1)S(1)}, u32[]{:S(2)}, u32[]{:S(2)}) collective-permute-start(bf16[2,320,384]{2,1,0:T(8,128)(2,1)S(1)} %get-tuple-element.113), channel_id=1, source_target_pairs={{0,16},{8,24},{16,0},{24,8},{1,17},{9,25},{17,1},{25,9},{2,18},{10... | collective-permute-start | bytes 1474568 | tf_op jit(solution)/shard_map/ppermute | solution.py:481
  34.6 8.7 %gate_up.7 = (bf16[2,320,384]{2,1,0:T(8,128)(2,1)S(1)}, bf16[2,320,384]{2,1,0:T(8,128)(2,1)S(1)}, f32[320,384]{1,0:T(8,128)S(1)}, f32[320,384]{1,0:T(8,128)S(1)}...) custom-call(s32[2]{0:T(128)S(1)} %pad_add_fusion.me_ref, s32[1,17]{1,0:T(1,128)S(1)} %get-tuple-element.98.refs_0_.offs, ...), custom_call_target="tpu_custom_call" | custom-call | flops 1094713344 | bytes 14008320 | tf_op jit(solution)/shard_map/gate_up/pallas_call | solution.py:402
  43.3 0.6 collective-permute-start.34
  43.9 0.5 collective-permute-start.36
  44.4 4.1 %weigh.3 = (f32[1392,128]{1,0:T(8,128)S(1)}, bf16[8,128,1280]{2,1,0:T(8,128)(2,1)S(1)}, s32[1]{0:T(128)}) custom-call(s32[1,17]{1,0:T(1,128)S(1)} %get-tuple-element.98.refs_0_.offs, bf16[1392,1024]{1,0:T(8,128)(2,1)S(1)} %get-tuple-element.105.select, f32[8,16,128]{2,1,0:T(8,128)S(1)} %get-tuple-element.106.probs, ...), custom_call_target="tpu_custom_call" | custom-call | flops 6000000000 | bytes 8000000 | tf_op jit(solution)/shard_map/weigh/pallas_call | solution.py:292
  48.5 0.1 fusion.25
  48.6 1.6 %collective-permute-start.27 = (bf16[320,384]{1,0:T(8,128)(2,1)S(1)}, bf16[320,384]{1,0:T(8,128)(2,1)S(1)}, u32[]{:S(2)}, u32[]{:S(2)}) collective-permute-start(bf16[320,384]{1,0:T(8,128)(2,1)S(1)} %fusion.25), channel_id=1, source_target_pairs={{0,16},{8,24},{16,0},{24,8},{1,17},{9,25},{17,1},{25,9},{2,18},{10... | collective-permute-start | bytes 737288 | tf_op jit(solution)/shard_map/ppermute | solution.py:481
  50.2 0.0 collective-permute-done.28
  50.2 0.1 fusion.21
  50.3 1.6 %collective-permute-start.29 = (bf16[320,384]{1,0:T(8,128)(2,1)S(1)}, bf16[320,384]{1,0:T(8,128)(2,1)S(1)}, u32[]{:S(2)}, u32[]{:S(2)}) collective-permute-start(bf16[320,384]{1,0:T(8,128)(2,1)S(1)} %fusion.21), channel_id=1, source_target_pairs={{0,8},{8,0},{16,24},{24,16},{1,9},{9,1},{17,25},{25,17},{2,10},{10... | collective-permute-start | bytes 737288 | tf_op jit(solution)/shard_map/ppermute | solution.py:481
  51.8 5.7 %collective-permute-done.34 = bf16[2,320,384]{2,1,0:T(8,128)(2,1)S(1)} collective-permute-done((bf16[2,320,384]{2,1,0:T(8,128)(2,1)S(1)}, bf16[2,320,384]{2,1,0:T(8,128)(2,1)S(1)}, u32[]{:S(2)}, u32[]{:S(2)}) %collective-permute-start.34) | collective-permute-done | bytes 491552 | tf_op jit(solution)/shard_map/ppermute | solution.py:481
  57.5 0.1 fusion.19
  57.6 0.6 collective-permute-start.35
  58.2 0.0 collective-permute-done.36
  58.2 0.1 fusion.15
  58.2 1.5 %collective-permute-start.37 = (bf16[320,384]{1,0:T(8,128)(2,1)S(1)}, bf16[320,384]{1,0:T(8,128)(2,1)S(1)}, u32[]{:S(2)}, u32[]{:S(2)}) collective-permute-start(bf16[320,384]{1,0:T(8,128)(2,1)S(1)} %fusion.15), channel_id=1, source_target_pairs={{0,8},{8,0},{16,24},{24,16},{1,9},{9,1},{17,25},{25,17},{2,10},{10... | collective-permute-start | bytes 737288 | tf_op jit(solution)/shard_map/ppermute | solution.py:481
  59.7 3.7 %collective-permute-done.27 = bf16[320,384]{1,0:T(8,128)(2,1)S(1)} collective-permute-done((bf16[320,384]{1,0:T(8,128)(2,1)S(1)}, bf16[320,384]{1,0:T(8,128)(2,1)S(1)}, u32[]{:S(2)}, u32[]{:S(2)}) %collective-permute-start.27) | collective-permute-done | bytes 245792 | tf_op jit(solution)/shard_map/ppermute | solution.py:481
  63.4 0.2 fusion.24.refs_0_
  63.6 1.2 %collective-permute-start.31 = (bf16[320,384]{1,0:T(8,128)(2,1)S(1)}, bf16[320,384]{1,0:T(8,128)(2,1)S(1)}, u32[]{:S(2)}, u32[]{:S(2)}) collective-permute-start(bf16[320,384]{1,0:T(8,128)(2,1)S(1)} %fusion.24.refs_0_), channel_id=1, source_target_pairs={{0,16},{8,24},{16,0},{24,8},{1,17},{9,25},{17,1},{25,9},{2,18},{10... | collective-permute-start | bytes 737288 | tf_op jit(solution)/shard_map/ppermute | solution.py:481
  64.8 0.8 collective-permute-start.30
  65.7 3.0 %collective-permute-done.35 = bf16[320,384]{1,0:T(8,128)(2,1)S(1)} collective-permute-done((bf16[320,384]{1,0:T(8,128)(2,1)S(1)}, bf16[320,384]{1,0:T(8,128)(2,1)S(1)}, u32[]{:S(2)}, u32[]{:S(2)}) %collective-permute-start.35) | collective-permute-done | bytes 245792 | tf_op jit(solution)/shard_map/ppermute | solution.py:481
  68.6 0.0 collective-permute-done.37
  68.6 0.2 fusion.18.refs_5_
  68.9 1.5 %collective-permute-start.40 = (bf16[320,384]{1,0:T(8,128)(2,1)S(1)}, bf16[320,384]{1,0:T(8,128)(2,1)S(1)}, u32[]{:S(2)}, u32[]{:S(2)}) collective-permute-start(bf16[320,384]{1,0:T(8,128)(2,1)S(1)} %fusion.18.refs_5_), channel_id=1, source_target_pairs={{0,24},{8,16},{16,8},{24,0},{1,25},{9,17},{17,9},{25,1},{2,26},{10... | collective-permute-start | bytes 737288 | tf_op jit(solution)/shard_map/ppermute | solution.py:481
  70.4 1.5 %collective-permute-start.39 = (bf16[320,384]{1,0:T(8,128)(2,1)S(1)}, bf16[320,384]{1,0:T(8,128)(2,1)S(1)}, u32[]{:S(2)}, u32[]{:S(2)}) collective-permute-start(bf16[320,384]{1,0:T(8,128)(2,1)S(1)} %fusion.18.refs_5_), channel_id=1, source_target_pairs={{0,16},{8,24},{16,0},{24,8},{1,17},{9,25},{17,1},{25,9},{2,18},{10... | collective-permute-start | bytes 737288 | tf_op jit(solution)/shard_map/ppermute | solution.py:481
  71.9 0.5 collective-permute-start.38
  72.4 6.5 %collective-permute-done.31.refs_2_ = bf16[320,384]{1,0:T(8,128)(2,1)S(1)} collective-permute-done((bf16[320,384]{1,0:T(8,128)(2,1)S(1)}, bf16[320,384]{1,0:T(8,128)(2,1)S(1)}, u32[]{:S(2)}, u32[]{:S(2)}) %collective-permute-start.31) | collective-permute-done | bytes 245792 | tf_op jit(solution)/shard_map/ppermute | solution.py:481
  79.0 1.6 %collective-permute-start.33 = (bf16[160,384]{1,0:T(8,128)(2,1)S(1)}, bf16[160,384]{1,0:T(8,128)(2,1)S(1)}, u32[]{:S(2)}, u32[]{:S(2)}) collective-permute-start(bf16[160,384]{1,0:T(8,128)(2,1)S(1)} %slice.123), channel_id=1, source_target_pairs={{0,8},{8,0},{16,24},{24,16},{1,9},{9,1},{17,25},{25,17},{2,10},{10... | collective-permute-start | bytes 368648 | tf_op jit(solution)/shard_map/ppermute | solution.py:481
  80.5 0.0 collective-permute-done.30.refs_1_
  80.6 0.6 collective-permute-start.32
  81.1 3.1 %collective-permute-done.39.refs_7_ = bf16[320,384]{1,0:T(8,128)(2,1)S(1)} collective-permute-done((bf16[320,384]{1,0:T(8,128)(2,1)S(1)}, bf16[320,384]{1,0:T(8,128)(2,1)S(1)}, u32[]{:S(2)}, u32[]{:S(2)}) %collective-permute-start.39) | collective-permute-done | bytes 245792 | tf_op jit(solution)/shard_map/ppermute | solution.py:481
  84.3 0.9 collective-permute-done.33.refs_4_
  85.1 0.5 collective-permute-done.32.refs_3_
  85.6 8.4 %down.3 = (bf16[4,128,512]{2,1,0:T(8,128)(2,1)S(1)}, bf16[4,128,512]{2,1,0:T(8,128)(2,1)S(1)}) custom-call(s32[2]{0:T(128)S(1)} %pad_add_fusion.me_ref, s32[1,17]{1,0:T(1,128)S(1)} %get-tuple-element.98.refs_0_.offs, bf16[16,768,512]{2,1,0:T(8,128)(2,1)} %w_down.1, f32[1392,128]{1,0:T(8,128)S(1)} %get-tuple-element.117.scale, ...), custom_call_target="tpu_custom_call" | custom-call | flops 2554331136 | bytes 12582912 | tf_op jit(solution)/shard_map/down/pallas_call | solution.py:467
  93.9 0.1 collective-permute-start.41
  94.0 1.9 %collective-permute-done.41 = bf16[4,128,512]{2,1,0:T(8,128)(2,1)S(1)} collective-permute-done((bf16[4,128,512]{2,1,0:T(8,128)(2,1)S(1)}, bf16[4,128,512]{2,1,0:T(8,128)(2,1)S(1)}, u32[]{:S(2)}, u32[]{:S(2)}) %collective-permute-start.41) | collective-permute-done | bytes 524320 | tf_op jit(solution)/shard_map/ppermute | solution.py:481
  95.9 0.2 fusion.29
  96.2 4.1 %collective-permute-start.42 = (bf16[128,512]{1,0:T(8,128)(2,1)S(1)}, bf16[128,512]{1,0:T(8,128)(2,1)S(1)}, u32[]{:S(2)}, u32[]{:S(2)}) collective-permute-start(bf16[128,512]{1,0:T(8,128)(2,1)S(1)} %get-tuple-element.133), channel_id=1, source_target_pairs={{0,6},{1,7},{2,4},{3,5},{4,2},{5,3},{6,0},{7,1},{8,14},{9,15},{10,... | collective-permute-start | bytes 393224 | tf_op jit(solution)/shard_map/ppermute | solution.py:481
  100.2 0.6 collective-permute-start.43
  101.5 3.0 %collective-permute-done.42 = bf16[128,512]{1,0:T(8,128)(2,1)S(1)} collective-permute-done((bf16[128,512]{1,0:T(8,128)(2,1)S(1)}, bf16[128,512]{1,0:T(8,128)(2,1)S(1)}, u32[]{:S(2)}, u32[]{:S(2)}) %collective-permute-start.42) | collective-permute-done | bytes 131104 | tf_op jit(solution)/shard_map/ppermute | solution.py:481
  104.6 3.7 %collective-permute-done.44 = bf16[128,512]{1,0:T(8,128)(2,1)S(1)} collective-permute-done((bf16[128,512]{1,0:T(8,128)(2,1)S(1)}, bf16[128,512]{1,0:T(8,128)(2,1)S(1)}, u32[]{:S(2)}, u32[]{:S(2)}) %collective-permute-start.44) | collective-permute-done | bytes 131104 | tf_op jit(solution)/shard_map/ppermute | solution.py:481
  108.2 3.0 %collective-permute-done.43 = bf16[128,512]{1,0:T(8,128)(2,1)S(1)} collective-permute-done((bf16[128,512]{1,0:T(8,128)(2,1)S(1)}, bf16[128,512]{1,0:T(8,128)(2,1)S(1)}, u32[]{:S(2)}, u32[]{:S(2)}) %collective-permute-start.43) | collective-permute-done | bytes 131104 | tf_op jit(solution)/shard_map/ppermute | solution.py:481
  111.3 0.1 fusion.28
  111.3 0.3 conditional.1
  111.6 0.0 copy-start.2
  111.6 0.6 copy-done.2
  (19 shorter events, 0.1 us)
Async XLA Ops:
  1.4 0.9 copy-start
  2.3 11.2 %collective-permute-start.22 = (bf16[144,512]{1,0:T(8,128)(2,1)S(1)}, bf16[144,512]{1,0:T(8,128)(2,1)S(1)}, u32[]{:S(2)}, u32[]{:S(2)}) collective-permute-start(bf16[144,512]{1,0:T(8,128)(2,1)S(1)} %pack.1.refs_0_), channel_id=1, source_target_pairs={{0,4},{1,5},{2,6},{3,7},{4,0},{5,1},{6,2},{7,3},{8,12},{9,13},{10,... | collective-permute-start | bytes 442376 | tf_op jit(solution)/shard_map/ppermute | solution.py:481
  6.4 8.2 %collective-permute-start.20 = (bf16[144,512]{1,0:T(8,128)(2,1)S(1)}, bf16[144,512]{1,0:T(8,128)(2,1)S(1)}, u32[]{:S(2)}, u32[]{:S(2)}) collective-permute-start(bf16[144,512]{1,0:T(8,128)(2,1)S(1)} %pack.1.refs_0_), channel_id=1, source_target_pairs={{0,2},{1,3},{2,0},{3,1},{4,6},{5,7},{6,4},{7,5},{8,10},{9,11},{10,... | collective-permute-start | bytes 442376 | tf_op jit(solution)/shard_map/ppermute | solution.py:481
  13.5 5.1 %collective-permute-start.24 = (bf16[144,512]{1,0:T(8,128)(2,1)S(1)}, bf16[144,512]{1,0:T(8,128)(2,1)S(1)}, u32[]{:S(2)}, u32[]{:S(2)}) collective-permute-start(bf16[144,512]{1,0:T(8,128)(2,1)S(1)} %collective-permute-done.22.refs_4_), channel_id=1, source_target_pairs={{0,2},{1,3},{2,0},{3,1},{4,6},{5,7},{6,4},{7,5},{8,10},{9,11},{10,... | collective-permute-start | bytes 442376 | tf_op jit(solution)/shard_map/ppermute | solution.py:481
  14.1 4.6 %collective-permute-start.19 = (bf16[144,512]{1,0:T(8,128)(2,1)S(1)}, bf16[144,512]{1,0:T(8,128)(2,1)S(1)}, u32[]{:S(2)}, u32[]{:S(2)}) collective-permute-start(bf16[144,512]{1,0:T(8,128)(2,1)S(1)} %pack.1.refs_0_), channel_id=1, source_target_pairs={{0,1},{1,0},{2,3},{3,2},{4,5},{5,4},{6,7},{7,6},{8,9},{9,8},{10,11... | collective-permute-start | bytes 442376 | tf_op jit(solution)/shard_map/ppermute | solution.py:481
  14.1 4.6 %collective-permute-start.23 = (bf16[144,512]{1,0:T(8,128)(2,1)S(1)}, bf16[144,512]{1,0:T(8,128)(2,1)S(1)}, u32[]{:S(2)}, u32[]{:S(2)}) collective-permute-start(bf16[144,512]{1,0:T(8,128)(2,1)S(1)} %collective-permute-done.22.refs_4_), channel_id=1, source_target_pairs={{0,1},{1,0},{2,3},{3,2},{4,5},{5,4},{6,7},{7,6},{8,9},{9,8},{10,11... | collective-permute-start | bytes 442376 | tf_op jit(solution)/shard_map/ppermute | solution.py:481
  14.7 4.1 %collective-permute-start.21 = (bf16[144,512]{1,0:T(8,128)(2,1)S(1)}, bf16[144,512]{1,0:T(8,128)(2,1)S(1)}, u32[]{:S(2)}, u32[]{:S(2)}) collective-permute-start(bf16[144,512]{1,0:T(8,128)(2,1)S(1)} %collective-permute-done.20.refs_2_), channel_id=1, source_target_pairs={{0,1},{1,0},{2,3},{3,2},{4,5},{5,4},{6,7},{7,6},{8,9},{9,8},{10,11... | collective-permute-start | bytes 442376 | tf_op jit(solution)/shard_map/ppermute | solution.py:481
  18.7 1.4 %collective-permute-start.25 = (bf16[144,512]{1,0:T(8,128)(2,1)S(1)}, bf16[144,512]{1,0:T(8,128)(2,1)S(1)}, u32[]{:S(2)}, u32[]{:S(2)}) collective-permute-start(bf16[144,512]{1,0:T(8,128)(2,1)S(1)} %collective-permute-done.24.refs_6_), channel_id=1, source_target_pairs={{0,1},{1,0},{2,3},{3,2},{4,5},{5,4},{6,7},{7,6},{8,9},{9,8},{10,11... | collective-permute-start | bytes 442376 | tf_op jit(solution)/shard_map/ppermute | solution.py:481
  18.7 16.0 %slice-start = ((s8[12582912]{0:T(1024)(128)(4,1)}), s8[4194304]{0:T(1024)(128)(4,1)S(1)}, s32[]{:S(2)}) async-start(s8[12582912]{0:T(1024)(128)(4,1)} %bitcast.110), calls=%async_computation | async-start | bytes 8388608
  18.7 15.9 %slice-start.1 = ((s8[12582912]{0:T(1024)(128)(4,1)}), s8[4194304]{0:T(1024)(128)(4,1)S(1)}, s32[]{:S(2)}) async-start(s8[12582912]{0:T(1024)(128)(4,1)} %bitcast.110), calls=%async_computation.1 | async-start | bytes 8388608
  18.7 15.9 %slice-start.2 = ((s8[12582912]{0:T(1024)(128)(4,1)}), s8[4194304]{0:T(1024)(128)(4,1)S(1)}, s32[]{:S(2)}) async-start(s8[12582912]{0:T(1024)(128)(4,1)} %bitcast.110), calls=%async_computation.2 | async-start | bytes 8388608
  31.5 17.0 %collective-permute-start.26 = (bf16[2,320,384]{2,1,0:T(8,128)(2,1)S(1)}, bf16[2,320,384]{2,1,0:T(8,128)(2,1)S(1)}, u32[]{:S(2)}, u32[]{:S(2)}) collective-permute-start(bf16[2,320,384]{2,1,0:T(8,128)(2,1)S(1)} %get-tuple-element.110), channel_id=1, source_target_pairs={{0,8},{8,0},{16,24},{24,16},{1,9},{9,1},{17,25},{25,17},{2,10},{10... | collective-permute-start | bytes 1474568 | tf_op jit(solution)/shard_map/ppermute | solution.py:481
  33.1 17.1 %collective-permute-start.28 = (bf16[2,320,384]{2,1,0:T(8,128)(2,1)S(1)}, bf16[2,320,384]{2,1,0:T(8,128)(2,1)S(1)}, u32[]{:S(2)}, u32[]{:S(2)}) collective-permute-start(bf16[2,320,384]{2,1,0:T(8,128)(2,1)S(1)} %get-tuple-element.113), channel_id=1, source_target_pairs={{0,16},{8,24},{16,0},{24,8},{1,17},{9,25},{17,1},{25,9},{2,18},{10... | collective-permute-start | bytes 1474568 | tf_op jit(solution)/shard_map/ppermute | solution.py:481
  43.3 14.2 %collective-permute-start.34 = (bf16[2,320,384]{2,1,0:T(8,128)(2,1)S(1)}, bf16[2,320,384]{2,1,0:T(8,128)(2,1)S(1)}, u32[]{:S(2)}, u32[]{:S(2)}) collective-permute-start(bf16[2,320,384]{2,1,0:T(8,128)(2,1)S(1)} %get-tuple-element.121), channel_id=1, source_target_pairs={{0,8},{8,0},{16,24},{24,16},{1,9},{9,1},{17,25},{25,17},{2,10},{10... | collective-permute-start | bytes 1474568 | tf_op jit(solution)/shard_map/ppermute | solution.py:481
  43.9 14.2 %collective-permute-start.36 = (bf16[2,320,384]{2,1,0:T(8,128)(2,1)S(1)}, bf16[2,320,384]{2,1,0:T(8,128)(2,1)S(1)}, u32[]{:S(2)}, u32[]{:S(2)}) collective-permute-start(bf16[2,320,384]{2,1,0:T(8,128)(2,1)S(1)} %get-tuple-element.122), channel_id=1, source_target_pairs={{0,16},{8,24},{16,0},{24,8},{1,17},{9,25},{17,1},{25,9},{2,18},{10... | collective-permute-start | bytes 1474568 | tf_op jit(solution)/shard_map/ppermute | solution.py:481
  48.6 14.8 %collective-permute-start.27 = (bf16[320,384]{1,0:T(8,128)(2,1)S(1)}, bf16[320,384]{1,0:T(8,128)(2,1)S(1)}, u32[]{:S(2)}, u32[]{:S(2)}) collective-permute-start(bf16[320,384]{1,0:T(8,128)(2,1)S(1)} %fusion.25), channel_id=1, source_target_pairs={{0,16},{8,24},{16,0},{24,8},{1,17},{9,25},{17,1},{25,9},{2,18},{10... | collective-permute-start | bytes 737288 | tf_op jit(solution)/shard_map/ppermute | solution.py:481
  50.3 13.1 %collective-permute-start.29 = (bf16[320,384]{1,0:T(8,128)(2,1)S(1)}, bf16[320,384]{1,0:T(8,128)(2,1)S(1)}, u32[]{:S(2)}, u32[]{:S(2)}) collective-permute-start(bf16[320,384]{1,0:T(8,128)(2,1)S(1)} %fusion.21), channel_id=1, source_target_pairs={{0,8},{8,0},{16,24},{24,16},{1,9},{9,1},{17,25},{25,17},{2,10},{10... | collective-permute-start | bytes 737288 | tf_op jit(solution)/shard_map/ppermute | solution.py:481
  57.6 11.0 %collective-permute-start.35 = (bf16[320,384]{1,0:T(8,128)(2,1)S(1)}, bf16[320,384]{1,0:T(8,128)(2,1)S(1)}, u32[]{:S(2)}, u32[]{:S(2)}) collective-permute-start(bf16[320,384]{1,0:T(8,128)(2,1)S(1)} %fusion.19), channel_id=1, source_target_pairs={{0,16},{8,24},{16,0},{24,8},{1,17},{9,25},{17,1},{25,9},{2,18},{10... | collective-permute-start | bytes 737288 | tf_op jit(solution)/shard_map/ppermute | solution.py:481
  58.2 10.4 %collective-permute-start.37 = (bf16[320,384]{1,0:T(8,128)(2,1)S(1)}, bf16[320,384]{1,0:T(8,128)(2,1)S(1)}, u32[]{:S(2)}, u32[]{:S(2)}) collective-permute-start(bf16[320,384]{1,0:T(8,128)(2,1)S(1)} %fusion.15), channel_id=1, source_target_pairs={{0,8},{8,0},{16,24},{24,16},{1,9},{9,1},{17,25},{25,17},{2,10},{10... | collective-permute-start | bytes 737288 | tf_op jit(solution)/shard_map/ppermute | solution.py:481
  63.6 15.3 %collective-permute-start.31 = (bf16[320,384]{1,0:T(8,128)(2,1)S(1)}, bf16[320,384]{1,0:T(8,128)(2,1)S(1)}, u32[]{:S(2)}, u32[]{:S(2)}) collective-permute-start(bf16[320,384]{1,0:T(8,128)(2,1)S(1)} %fusion.24.refs_0_), channel_id=1, source_target_pairs={{0,16},{8,24},{16,0},{24,8},{1,17},{9,25},{17,1},{25,9},{2,18},{10... | collective-permute-start | bytes 737288 | tf_op jit(solution)/shard_map/ppermute | solution.py:481
  64.8 15.7 %collective-permute-start.30 = (bf16[320,384]{1,0:T(8,128)(2,1)S(1)}, bf16[320,384]{1,0:T(8,128)(2,1)S(1)}, u32[]{:S(2)}, u32[]{:S(2)}) collective-permute-start(bf16[320,384]{1,0:T(8,128)(2,1)S(1)} %fusion.24.refs_0_), channel_id=1, source_target_pairs={{0,8},{8,0},{16,24},{24,16},{1,9},{9,1},{17,25},{25,17},{2,10},{10... | collective-permute-start | bytes 737288 | tf_op jit(solution)/shard_map/ppermute | solution.py:481
  68.9 12.3 %collective-permute-start.40 = (bf16[320,384]{1,0:T(8,128)(2,1)S(1)}, bf16[320,384]{1,0:T(8,128)(2,1)S(1)}, u32[]{:S(2)}, u32[]{:S(2)}) collective-permute-start(bf16[320,384]{1,0:T(8,128)(2,1)S(1)} %fusion.18.refs_5_), channel_id=1, source_target_pairs={{0,24},{8,16},{16,8},{24,0},{1,25},{9,17},{17,9},{25,1},{2,26},{10... | collective-permute-start | bytes 737288 | tf_op jit(solution)/shard_map/ppermute | solution.py:481
  70.4 13.9 %collective-permute-start.39 = (bf16[320,384]{1,0:T(8,128)(2,1)S(1)}, bf16[320,384]{1,0:T(8,128)(2,1)S(1)}, u32[]{:S(2)}, u32[]{:S(2)}) collective-permute-start(bf16[320,384]{1,0:T(8,128)(2,1)S(1)} %fusion.18.refs_5_), channel_id=1, source_target_pairs={{0,16},{8,24},{16,0},{24,8},{1,17},{9,25},{17,1},{25,9},{2,18},{10... | collective-permute-start | bytes 737288 | tf_op jit(solution)/shard_map/ppermute | solution.py:481
  71.9 12.4 %collective-permute-start.38 = (bf16[320,384]{1,0:T(8,128)(2,1)S(1)}, bf16[320,384]{1,0:T(8,128)(2,1)S(1)}, u32[]{:S(2)}, u32[]{:S(2)}) collective-permute-start(bf16[320,384]{1,0:T(8,128)(2,1)S(1)} %fusion.18.refs_5_), channel_id=1, source_target_pairs={{0,8},{8,0},{16,24},{24,16},{1,9},{9,1},{17,25},{25,17},{2,10},{10... | collective-permute-start | bytes 737288 | tf_op jit(solution)/shard_map/ppermute | solution.py:481
  79.0 6.1 %collective-permute-start.33 = (bf16[160,384]{1,0:T(8,128)(2,1)S(1)}, bf16[160,384]{1,0:T(8,128)(2,1)S(1)}, u32[]{:S(2)}, u32[]{:S(2)}) collective-permute-start(bf16[160,384]{1,0:T(8,128)(2,1)S(1)} %slice.123), channel_id=1, source_target_pairs={{0,8},{8,0},{16,24},{24,16},{1,9},{9,1},{17,25},{25,17},{2,10},{10... | collective-permute-start | bytes 368648 | tf_op jit(solution)/shard_map/ppermute | solution.py:481
  80.6 5.0 %collective-permute-start.32 = (bf16[160,384]{1,0:T(8,128)(2,1)S(1)}, bf16[160,384]{1,0:T(8,128)(2,1)S(1)}, u32[]{:S(2)}, u32[]{:S(2)}) collective-permute-start(bf16[160,384]{1,0:T(8,128)(2,1)S(1)} %slice.122), channel_id=1, source_target_pairs={{0,16},{8,24},{16,0},{24,8},{1,17},{9,25},{17,1},{25,9},{2,18},{10... | collective-permute-start | bytes 368648 | tf_op jit(solution)/shard_map/ppermute | solution.py:481
  93.9 2.0 %collective-permute-start.41 = (bf16[4,128,512]{2,1,0:T(8,128)(2,1)S(1)}, bf16[4,128,512]{2,1,0:T(8,128)(2,1)S(1)}, u32[]{:S(2)}, u32[]{:S(2)}) collective-permute-start(bf16[4,128,512]{2,1,0:T(8,128)(2,1)S(1)} %get-tuple-element.124), channel_id=1, source_target_pairs={{0,1},{1,0},{2,3},{3,2},{4,5},{5,4},{6,7},{7,6},{8,9},{9,8},{10,11... | collective-permute-start | bytes 1572872 | tf_op jit(solution)/shard_map/ppermute | solution.py:481
  96.2 8.4 %collective-permute-start.42 = (bf16[128,512]{1,0:T(8,128)(2,1)S(1)}, bf16[128,512]{1,0:T(8,128)(2,1)S(1)}, u32[]{:S(2)}, u32[]{:S(2)}) collective-permute-start(bf16[128,512]{1,0:T(8,128)(2,1)S(1)} %get-tuple-element.133), channel_id=1, source_target_pairs={{0,6},{1,7},{2,4},{3,5},{4,2},{5,3},{6,0},{7,1},{8,14},{9,15},{10,... | collective-permute-start | bytes 393224 | tf_op jit(solution)/shard_map/ppermute | solution.py:481
  100.2 8.0 %collective-permute-start.44 = (bf16[128,512]{1,0:T(8,128)(2,1)S(1)}, bf16[128,512]{1,0:T(8,128)(2,1)S(1)}, u32[]{:S(2)}, u32[]{:S(2)}) collective-permute-start(bf16[128,512]{1,0:T(8,128)(2,1)S(1)} %get-tuple-element.134), channel_id=1, source_target_pairs={{0,2},{1,3},{2,0},{3,1},{4,6},{5,7},{6,4},{7,5},{8,10},{9,11},{10,... | collective-permute-start | bytes 393224 | tf_op jit(solution)/shard_map/ppermute | solution.py:481
  100.2 11.1 %collective-permute-start.43 = (bf16[128,512]{1,0:T(8,128)(2,1)S(1)}, bf16[128,512]{1,0:T(8,128)(2,1)S(1)}, u32[]{:S(2)}, u32[]{:S(2)}) collective-permute-start(bf16[128,512]{1,0:T(8,128)(2,1)S(1)} %get-tuple-element.135), channel_id=1, source_target_pairs={{0,4},{1,5},{2,6},{3,7},{4,0},{5,1},{6,2},{7,3},{8,12},{9,13},{10,... | collective-permute-start | bytes 393224 | tf_op jit(solution)/shard_map/ppermute | solution.py:481
  111.6 0.7 copy-start.2

commit v8 on v6

--- a/solution.py
+++ b/solution.py
@@ -13,6 +13,7 @@
 BF16 = jnp.bfloat16
 VMEM_LIMIT = 56 * 2**20
 VMEM_SPARE = 10 * 2**20
+PACK_VMEM = 64 * 2**20
 ALIGN = 16
 META = 16
 
@@ -46,29 +47,43 @@
     return pl.CostEstimate(flops=int(flops), bytes_accessed=int(moved), transcendentals=0)
 
 
-def pack_kernel(dims, tokens, ids, weights, packed):
+def pack_kernel(dims, tokens, ids_in, weights_in, packed, ids, weights, sems):
     rows, top = dims["rows"], dims["top"]
+    copies = [
+        pltpu.make_async_copy(ids_in, ids, sems.at[0]),
+        pltpu.make_async_copy(weights_in, weights, sems.at[1]),
+        pltpu.make_async_copy(tokens, packed.at[pl.ds(0, rows), :], sems.at[2]),
+    ]
+    for copy in copies:
+        copy.start()
+    for copy in copies[:2]:
+        copy.wait()
     chance = weights[...]
     chance = chance / jnp.sum(chance, axis=0, keepdims=True)
     high = chance.astype(BF16)
     rest = chance - high.astype(F32)
     middle = rest.astype(BF16)
     low = (rest - middle.astype(F32)).astype(BF16)
-    packed[:rows, :] = tokens[...]
     packed[rows:, :] = jnp.zeros((META, packed.shape[1]), BF16)
     parts = (ids[...].astype(F32), high.astype(F32), middle.astype(F32), low.astype(F32))
     for i, part in enumerate(parts):
         block = jnp.concatenate([part, jnp.zeros((META - top, rows), F32)], axis=0)
         packed[rows:, i * rows : (i + 1) * rows] = block.astype(BF16)
+    copies[2].wait()
 
 
 def pack(dims, tokens, ids, weights):
     return pl.pallas_call(
         functools.partial(pack_kernel, dims),
         out_shape=jax.ShapeDtypeStruct((dims["rows"] + META, tokens.shape[1]), BF16),
-        in_specs=[vmem()] * 3,
+        in_specs=[hbm()] * 3,
         out_specs=vmem(),
-        compiler_params=params(),
+        scratch_shapes=[
+            pltpu.VMEM(ids.T.shape, jnp.int32),
+            pltpu.VMEM(weights.T.shape, F32),
+            pltpu.SemaphoreType.DMA((3,)),
+        ],
+        compiler_params=pltpu.CompilerParams(vmem_limit_bytes=PACK_VMEM),
         name="pack",
     )(tokens, ids.T, weights.T)
 
@@ -493,13 +508,10 @@
     return (jax.nn.silu(gate) * up).astype(BF16)
 
 
-def spread_chunk(hidden, two_steps):
+def spread_chunk(hidden):
     x, y = swap(hidden, "rep", 1), swap(hidden, "rep", 2)
-    if two_steps:
-        half = hidden.shape[0] // 2
-        corner = [(3, 0, swap(x[:half], "rep", 2)), (3, half, swap(y[half:], "rep", 1))]
-    else:
-        corner = [(3, 0, swap(hidden, "rep", 3))]
+    half = hidden.shape[0] // 2
+    corner = [(3, 0, swap(x[:half], "rep", 2)), (3, half, swap(y[half:], "rep", 1))]
     return [(0, 0, hidden), (1, 0, x), (2, 0, y)] + corner
 
 
@@ -589,7 +601,7 @@
         hidden = reduce_chunk(came[c], kept)
         if c == 0:
             hidden, scale, chosen = lax.optimization_barrier((hidden, scale, chosen))
-        chunks.append(spread_chunk(hidden, c + 1 < len(parts)))
+        chunks.append(spread_chunk(hidden))
     mixed = down(dims, me, offs, w_down, scale, chosen, rowk, chunks)
     if dims["small"]:
         return sum_over_exp(*mixed), peak[0]

time: 112 us -> 112 us (level)
  Pallas kernels: 32.2 us -> 34.7 us
  local copies, waits for them, and re-layouts: 2.99 us -> 0.75 us
  waiting for transfers between devices: 46 us -> 44.6 us
    unnamed x14 -> x10, local copies, waits for them, and re-layouts: 2.94 us -> 0.67 us
    pallas_call x1, Pallas kernels: 0.03 us -> 1.61 us  [pack(): pl.pallas_call(functools.partial(pack_kernel, dims), out_shape=jax.ShapeD...]
    ppermute x26 -> x27, waiting for transfers between devices: 46 us -> 44.6 us  [swap(): return lax.ppermute(value, axis, [(i, i ^ bit) for i in range(count)])]
    ppermute x26 -> x27, starting transfers between devices: 28.7 us -> 29.6 us  [swap(): return lax.ppermute(value, axis, [(i, i ^ bit) for i in range(count)])]
  transfers between devices with their start and end apart: 26 -> 27, of which waited for: 14 -> 15; matrix products, arithmetic and copies ran while one was open for 1% -> 1% of each run, Pallas kernels for 11% -> 11%
where the time goes in v8:
time: 112 us
  waiting for transfers between devices  44.6 us (40%)
  Pallas kernels  34.7 us (31%)
  starting transfers between devices  29.6 us (26%)
    ppermute x27, waiting for transfers between devices, swap(): return lax.ppermute(value, axis, [(i, i ^ bit) for i in range(count)])  44.6 us
    ppermute x27, starting transfers between devices, swap(): return lax.ppermute(value, axis, [(i, i ^ bit) for i in range(count)])  29.6 us
    pallas_call x2, Pallas kernels, gate_up(): pl.pallas_call(functools.partial(gate_up_kernel, dims, c, first_part), ou...  20.7 us
    pallas_call x1, Pallas kernels, down(): pl.pallas_call(functools.partial(down_kernel, dims, places), out_shape=ou...  8.34 us
    pallas_call x1, Pallas kernels, weigh(): pl.pallas_call(functools.partial(weigh_small_kernel if small else weigh_l...  4.13 us
  transfers between devices with their start and end apart: 27, of which 15 were waited for; matrix products, arithmetic and copies ran while one was open for 1% of the time, Pallas kernels for 11%

profile of v8, /device:TPU:0, one launch (start us, length us, event | category | flops | bytes accessed | tf_op | source)
XLA Modules:
  0.0 111.9 jit_solution(16107835185566773113)
XLA Ops:
  0.0 1.6 %pack.1.refs_0_ = bf16[144,512]{1,0:T(8,128)(2,1)} custom-call(bf16[128,512]{1,0:T(8,128)(2,1)} %tokens.1, s32[8,128]{1,0:T(8,128)} %bitcast.113, f32[8,128]{1,0:T(8,128)} %bitcast.114), custom_call_target="tpu_custom_call" | custom-call | tf_op jit(solution)/shard_map/pack/pallas_call | solution.py:76
  1.6 4.1 %collective-permute-start.23 = (bf16[144,512]{1,0:T(8,128)(2,1)}, bf16[144,512]{1,0:T(8,128)(2,1)S(1)}, u32[]{:S(2)}, u32[]{:S(2)}) collective-permute-start(bf16[144,512]{1,0:T(8,128)(2,1)} %pack.1.refs_0_), channel_id=1, source_target_pairs={{0,4},{1,5},{2,6},{3,7},{4,0},{5,1},{6,2},{7,3},{8,12},{9,13},{10,... | collective-permute-start | bytes 442376 | tf_op jit(solution)/shard_map/ppermute | solution.py:498
  5.7 1.6 %collective-permute-start.21 = (bf16[144,512]{1,0:T(8,128)(2,1)}, bf16[144,512]{1,0:T(8,128)(2,1)S(1)}, u32[]{:S(2)}, u32[]{:S(2)}) collective-permute-start(bf16[144,512]{1,0:T(8,128)(2,1)} %pack.1.refs_0_), channel_id=1, source_target_pairs={{0,2},{1,3},{2,0},{3,1},{4,6},{5,7},{6,4},{7,5},{8,10},{9,11},{10,... | collective-permute-start | bytes 442376 | tf_op jit(solution)/shard_map/ppermute | solution.py:498
  7.3 5.7 %collective-permute-done.23.refs_4_ = bf16[144,512]{1,0:T(8,128)(2,1)S(1)} collective-permute-done((bf16[144,512]{1,0:T(8,128)(2,1)}, bf16[144,512]{1,0:T(8,128)(2,1)S(1)}, u32[]{:S(2)}, u32[]{:S(2)}) %collective-permute-start.23) | collective-permute-done | bytes 147488 | tf_op jit(solution)/shard_map/ppermute | solution.py:498
  13.0 0.7 collective-permute-start.25
  13.8 0.0 collective-permute-start.20
  13.8 0.5 collective-permute-start.24
  14.3 0.0 collective-permute-done.21.refs_2_
  14.3 0.0 collective-permute-start.22
  14.3 3.9 %collective-permute-done.25.refs_6_ = bf16[144,512]{1,0:T(8,128)(2,1)S(1)} collective-permute-done((bf16[144,512]{1,0:T(8,128)(2,1)S(1)}, bf16[144,512]{1,0:T(8,128)(2,1)S(1)}, u32[]{:S(2)}, u32[]{:S(2)}) %collective-permute-start.25) | collective-permute-done | bytes 147488 | tf_op jit(solution)/shard_map/ppermute | solution.py:498
  18.2 0.0 collective-permute-start.26
  18.2 0.1 pad_add_fusion.me_ref
  18.3 0.0 collective-permute-done.20.refs_1_
  18.3 1.3 %collective-permute-done.26.refs_7_ = bf16[144,512]{1,0:T(8,128)(2,1)S(1)} collective-permute-done((bf16[144,512]{1,0:T(8,128)(2,1)S(1)}, bf16[144,512]{1,0:T(8,128)(2,1)S(1)}, u32[]{:S(2)}, u32[]{:S(2)}) %collective-permute-start.26) | collective-permute-done | bytes 147488 | tf_op jit(solution)/shard_map/ppermute | solution.py:498
  19.6 12.2 %gate_up.6 = (s32[8,16,128]{2,1,0:T(8,128)}, f32[8,16,128]{2,1,0:T(8,128)S(1)}, s32[8,8,128]{2,1,0:T(8,128)S(1)}, bf16[1392,512]{1,0:T(8,128)(2,1)S(1)}, bf16[13...) custom-call(s32[2]{0:T(128)S(1)} %pad_add_fusion.me_ref, ...), custom_call_target="tpu_custom_call" | custom-call | flops 1094713344 | bytes 14008320 | tf_op jit(solution)/shard_map/gate_up/pallas_call | solution.py:419
  31.8 1.6 %collective-permute-start.27 = (bf16[2,320,384]{2,1,0:T(8,128)(2,1)S(1)}, bf16[2,320,384]{2,1,0:T(8,128)(2,1)S(1)}, u32[]{:S(2)}, u32[]{:S(2)}) collective-permute-start(bf16[2,320,384]{2,1,0:T(8,128)(2,1)S(1)} %get-tuple-element.110), channel_id=1, source_target_pairs={{0,8},{8,0},{16,24},{24,16},{1,9},{9,1},{17,25},{25,17},{2,10},{10... | collective-permute-start | bytes 1474568 | tf_op jit(solution)/shard_map/ppermute | solution.py:498
  33.4 1.5 %collective-permute-start.29 = (bf16[2,320,384]{2,1,0:T(8,128)(2,1)S(1)}, bf16[2,320,384]{2,1,0:T(8,128)(2,1)S(1)}, u32[]{:S(2)}, u32[]{:S(2)}) collective-permute-start(bf16[2,320,384]{2,1,0:T(8,128)(2,1)S(1)} %get-tuple-element.113), channel_id=1, source_target_pairs={{0,16},{8,24},{16,0},{24,8},{1,17},{9,25},{17,1},{25,9},{2,18},{10... | collective-permute-start | bytes 1474568 | tf_op jit(solution)/shard_map/ppermute | solution.py:498
  34.9 8.5 %gate_up.7 = (bf16[2,320,384]{2,1,0:T(8,128)(2,1)S(1)}, bf16[2,320,384]{2,1,0:T(8,128)(2,1)S(1)}, f32[320,384]{1,0:T(8,128)S(1)}, f32[320,384]{1,0:T(8,128)S(1)}...) custom-call(s32[2]{0:T(128)S(1)} %pad_add_fusion.me_ref, s32[2,16]{1,0:T(2,128)S(1)} %get-tuple-element.98.refs_0_.offs, ...), custom_call_target="tpu_custom_call" | custom-call | flops 1094713344 | bytes 14008320 | tf_op jit(solution)/shard_map/gate_up/pallas_call | solution.py:419
  43.4 0.6 collective-permute-start.35
  44.0 0.4 collective-permute-start.37
  44.4 4.1 %weigh.3 = (f32[1392,128]{1,0:T(8,128)S(1)}, bf16[8,128,1280]{2,1,0:T(8,128)(2,1)S(1)}, s32[1]{0:T(128)}) custom-call(s32[2,16]{1,0:T(2,128)S(1)} %get-tuple-element.98.refs_0_.offs, bf16[1392,1024]{1,0:T(8,128)(2,1)S(1)} %get-tuple-element.105.select, f32[8,16,128]{2,1,0:T(8,128)S(1)} %get-tuple-element.106.probs, ...), custom_call_target="tpu_custom_call" | custom-call | flops 6000000000 | bytes 8000000 | tf_op jit(solution)/shard_map/weigh/pallas_call | solution.py:307
  48.6 0.0 collective-permute-done.27
  48.6 0.1 fusion.25
  48.6 1.6 %collective-permute-start.28 = (bf16[320,384]{1,0:T(8,128)(2,1)S(1)}, bf16[320,384]{1,0:T(8,128)(2,1)S(1)}, u32[]{:S(2)}, u32[]{:S(2)}) collective-permute-start(bf16[320,384]{1,0:T(8,128)(2,1)S(1)} %fusion.25), channel_id=1, source_target_pairs={{0,16},{8,24},{16,0},{24,8},{1,17},{9,25},{17,1},{25,9},{2,18},{10... | collective-permute-start | bytes 737288 | tf_op jit(solution)/shard_map/ppermute | solution.py:498
  50.3 0.0 collective-permute-done.29
  50.3 0.1 fusion.21
  50.3 1.6 %collective-permute-start.30 = (bf16[320,384]{1,0:T(8,128)(2,1)S(1)}, bf16[320,384]{1,0:T(8,128)(2,1)S(1)}, u32[]{:S(2)}, u32[]{:S(2)}) collective-permute-start(bf16[320,384]{1,0:T(8,128)(2,1)S(1)} %fusion.21), channel_id=1, source_target_pairs={{0,8},{8,0},{16,24},{24,16},{1,9},{9,1},{17,25},{25,17},{2,10},{10... | collective-permute-start | bytes 737288 | tf_op jit(solution)/shard_map/ppermute | solution.py:498
  51.9 5.7 %collective-permute-done.35 = bf16[2,320,384]{2,1,0:T(8,128)(2,1)S(1)} collective-permute-done((bf16[2,320,384]{2,1,0:T(8,128)(2,1)S(1)}, bf16[2,320,384]{2,1,0:T(8,128)(2,1)S(1)}, u32[]{:S(2)}, u32[]{:S(2)}) %collective-permute-start.35) | collective-permute-done | bytes 491552 | tf_op jit(solution)/shard_map/ppermute | solution.py:498
  57.6 0.1 fusion.19
  57.7 0.6 collective-permute-start.36
  58.2 0.1 fusion.15
  58.3 1.5 %collective-permute-start.38 = (bf16[320,384]{1,0:T(8,128)(2,1)S(1)}, bf16[320,384]{1,0:T(8,128)(2,1)S(1)}, u32[]{:S(2)}, u32[]{:S(2)}) collective-permute-start(bf16[320,384]{1,0:T(8,128)(2,1)S(1)} %fusion.15), channel_id=1, source_target_pairs={{0,8},{8,0},{16,24},{24,16},{1,9},{9,1},{17,25},{25,17},{2,10},{10... | collective-permute-start | bytes 737288 | tf_op jit(solution)/shard_map/ppermute | solution.py:498
  59.8 3.6 %collective-permute-done.28 = bf16[320,384]{1,0:T(8,128)(2,1)S(1)} collective-permute-done((bf16[320,384]{1,0:T(8,128)(2,1)S(1)}, bf16[320,384]{1,0:T(8,128)(2,1)S(1)}, u32[]{:S(2)}, u32[]{:S(2)}) %collective-permute-start.28) | collective-permute-done | bytes 245792 | tf_op jit(solution)/shard_map/ppermute | solution.py:498
  63.4 0.3 fusion.24.refs_0_
  63.7 1.5 %collective-permute-start.32 = (bf16[320,384]{1,0:T(8,128)(2,1)S(1)}, bf16[320,384]{1,0:T(8,128)(2,1)S(1)}, u32[]{:S(2)}, u32[]{:S(2)}) collective-permute-start(bf16[320,384]{1,0:T(8,128)(2,1)S(1)} %fusion.24.refs_0_), channel_id=1, source_target_pairs={{0,16},{8,24},{16,0},{24,8},{1,17},{9,25},{17,1},{25,9},{2,18},{10... | collective-permute-start | bytes 737288 | tf_op jit(solution)/shard_map/ppermute | solution.py:498
  65.2 0.6 collective-permute-start.31
  65.7 2.9 %collective-permute-done.36 = bf16[320,384]{1,0:T(8,128)(2,1)S(1)} collective-permute-done((bf16[320,384]{1,0:T(8,128)(2,1)S(1)}, bf16[320,384]{1,0:T(8,128)(2,1)S(1)}, u32[]{:S(2)}, u32[]{:S(2)}) %collective-permute-start.36) | collective-permute-done | bytes 245792 | tf_op jit(solution)/shard_map/ppermute | solution.py:498
  68.7 0.3 fusion.18.refs_5_
  69.0 1.5 %collective-permute-start.40 = (bf16[320,384]{1,0:T(8,128)(2,1)S(1)}, bf16[320,384]{1,0:T(8,128)(2,1)S(1)}, u32[]{:S(2)}, u32[]{:S(2)}) collective-permute-start(bf16[320,384]{1,0:T(8,128)(2,1)S(1)} %fusion.18.refs_5_), channel_id=1, source_target_pairs={{0,16},{8,24},{16,0},{24,8},{1,17},{9,25},{17,1},{25,9},{2,18},{10... | collective-permute-start | bytes 737288 | tf_op jit(solution)/shard_map/ppermute | solution.py:498
  70.4 0.6 collective-permute-start.39
  71.0 2.9 %collective-permute-done.32.refs_2_ = bf16[320,384]{1,0:T(8,128)(2,1)S(1)} collective-permute-done((bf16[320,384]{1,0:T(8,128)(2,1)S(1)}, bf16[320,384]{1,0:T(8,128)(2,1)S(1)}, u32[]{:S(2)}, u32[]{:S(2)}) %collective-permute-start.32) | collective-permute-done | bytes 245792 | tf_op jit(solution)/shard_map/ppermute | solution.py:498
  74.0 1.6 %collective-permute-start.34 = (bf16[160,384]{1,0:T(8,128)(2,1)S(1)}, bf16[160,384]{1,0:T(8,128)(2,1)S(1)}, u32[]{:S(2)}, u32[]{:S(2)}) collective-permute-start(bf16[160,384]{1,0:T(8,128)(2,1)S(1)} %slice.139), channel_id=1, source_target_pairs={{0,8},{8,0},{16,24},{24,16},{1,9},{9,1},{17,25},{25,17},{2,10},{10... | collective-permute-start | bytes 368648 | tf_op jit(solution)/shard_map/ppermute | solution.py:498
  75.5 0.6 collective-permute-start.33
  76.1 3.0 %collective-permute-done.40.refs_7_ = bf16[320,384]{1,0:T(8,128)(2,1)S(1)} collective-permute-done((bf16[320,384]{1,0:T(8,128)(2,1)S(1)}, bf16[320,384]{1,0:T(8,128)(2,1)S(1)}, u32[]{:S(2)}, u32[]{:S(2)}) %collective-permute-start.40) | collective-permute-done | bytes 245792 | tf_op jit(solution)/shard_map/ppermute | solution.py:498
  79.2 1.1 collective-permute-start.42
  80.2 0.0 collective-permute-done.39.refs_6_
  80.2 1.1 %collective-permute-start.41 = (bf16[160,384]{1,0:T(8,128)(2,1)S(1)}, bf16[160,384]{1,0:T(8,128)(2,1)S(1)}, u32[]{:S(2)}, u32[]{:S(2)}) collective-permute-start(bf16[160,384]{1,0:T(8,128)(2,1)S(1)} %slice.144), channel_id=1, source_target_pairs={{0,16},{8,24},{16,0},{24,8},{1,17},{9,25},{17,1},{25,9},{2,18},{10... | collective-permute-start | bytes 368648 | tf_op jit(solution)/shard_map/ppermute | solution.py:498
  81.4 0.2 collective-permute-done.33.refs_3_
  81.5 2.6 %collective-permute-done.42.refs_9_ = bf16[160,384]{1,0:T(8,128)(2,1)S(1)} collective-permute-done((bf16[160,384]{1,0:T(8,128)(2,1)S(1)}, bf16[160,384]{1,0:T(8,128)(2,1)S(1)}, u32[]{:S(2)}, u32[]{:S(2)}) %collective-permute-start.42) | collective-permute-done | bytes 122912 | tf_op jit(solution)/shard_map/ppermute | solution.py:498
  84.1 1.1 collective-permute-done.41.refs_8_
  85.2 8.3 %down.3 = (bf16[4,128,512]{2,1,0:T(8,128)(2,1)S(1)}, bf16[4,128,512]{2,1,0:T(8,128)(2,1)S(1)}) custom-call(s32[2]{0:T(128)S(1)} %pad_add_fusion.me_ref, s32[2,16]{1,0:T(2,128)S(1)} %get-tuple-element.98.refs_0_.offs, bf16[16,768,512]{2,1,0:T(8,128)(2,1)} %w_down.1, f32[1392,128]{1,0:T(8,128)S(1)} %get-tuple-element.117.scale, ...), custom_call_target="tpu_custom_call" | custom-call | flops 2554331136 | bytes 12582912 | tf_op jit(solution)/shard_map/down/pallas_call | solution.py:484
  93.5 0.1 collective-permute-start.43
  93.6 1.9 %collective-permute-done.43 = bf16[4,128,512]{2,1,0:T(8,128)(2,1)S(1)} collective-permute-done((bf16[4,128,512]{2,1,0:T(8,128)(2,1)S(1)}, bf16[4,128,512]{2,1,0:T(8,128)(2,1)S(1)}, u32[]{:S(2)}, u32[]{:S(2)}) %collective-permute-start.43) | collective-permute-done | bytes 524320 | tf_op jit(solution)/shard_map/ppermute | solution.py:498
  95.5 0.2 fusion.29
  95.7 4.1 %collective-permute-start.44 = (bf16[128,512]{1,0:T(8,128)(2,1)S(1)}, bf16[128,512]{1,0:T(8,128)(2,1)S(1)}, u32[]{:S(2)}, u32[]{:S(2)}) collective-permute-start(bf16[128,512]{1,0:T(8,128)(2,1)S(1)} %get-tuple-element.133), channel_id=1, source_target_pairs={{0,6},{1,7},{2,4},{3,5},{4,2},{5,3},{6,0},{7,1},{8,14},{9,15},{10,... | collective-permute-start | bytes 393224 | tf_op jit(solution)/shard_map/ppermute | solution.py:498
  99.8 0.0 collective-permute-start.46
  99.8 0.6 collective-permute-start.45
  101.1 3.0 %collective-permute-done.44 = bf16[128,512]{1,0:T(8,128)(2,1)S(1)} collective-permute-done((bf16[128,512]{1,0:T(8,128)(2,1)S(1)}, bf16[128,512]{1,0:T(8,128)(2,1)S(1)}, u32[]{:S(2)}, u32[]{:S(2)}) %collective-permute-start.44) | collective-permute-done | bytes 131104 | tf_op jit(solution)/shard_map/ppermute | solution.py:498
  104.1 3.7 %collective-permute-done.46 = bf16[128,512]{1,0:T(8,128)(2,1)S(1)} collective-permute-done((bf16[128,512]{1,0:T(8,128)(2,1)S(1)}, bf16[128,512]{1,0:T(8,128)(2,1)S(1)}, u32[]{:S(2)}, u32[]{:S(2)}) %collective-permute-start.46) | collective-permute-done | bytes 131104 | tf_op jit(solution)/shard_map/ppermute | solution.py:498
  107.9 3.0 %collective-permute-done.45 = bf16[128,512]{1,0:T(8,128)(2,1)S(1)} collective-permute-done((bf16[128,512]{1,0:T(8,128)(2,1)S(1)}, bf16[128,512]{1,0:T(8,128)(2,1)S(1)}, u32[]{:S(2)}, u32[]{:S(2)}) %collective-permute-start.45) | collective-permute-done | bytes 131104 | tf_op jit(solution)/shard_map/ppermute | solution.py:498
  110.8 0.1 fusion.28
  110.9 0.3 conditional.1
  111.2 0.0 copy-start.2
  111.2 0.6 copy-done.2
  (21 shorter events, 0.1 us)
Async XLA Ops:
  1.6 11.4 %collective-permute-start.23 = (bf16[144,512]{1,0:T(8,128)(2,1)}, bf16[144,512]{1,0:T(8,128)(2,1)S(1)}, u32[]{:S(2)}, u32[]{:S(2)}) collective-permute-start(bf16[144,512]{1,0:T(8,128)(2,1)} %pack.1.refs_0_), channel_id=1, source_target_pairs={{0,4},{1,5},{2,6},{3,7},{4,0},{5,1},{6,2},{7,3},{8,12},{9,13},{10,... | collective-permute-start | bytes 442376 | tf_op jit(solution)/shard_map/ppermute | solution.py:498
  5.7 8.6 %collective-permute-start.21 = (bf16[144,512]{1,0:T(8,128)(2,1)}, bf16[144,512]{1,0:T(8,128)(2,1)S(1)}, u32[]{:S(2)}, u32[]{:S(2)}) collective-permute-start(bf16[144,512]{1,0:T(8,128)(2,1)} %pack.1.refs_0_), channel_id=1, source_target_pairs={{0,2},{1,3},{2,0},{3,1},{4,6},{5,7},{6,4},{7,5},{8,10},{9,11},{10,... | collective-permute-start | bytes 442376 | tf_op jit(solution)/shard_map/ppermute | solution.py:498
  13.0 5.1 %collective-permute-start.25 = (bf16[144,512]{1,0:T(8,128)(2,1)S(1)}, bf16[144,512]{1,0:T(8,128)(2,1)S(1)}, u32[]{:S(2)}, u32[]{:S(2)}) collective-permute-start(bf16[144,512]{1,0:T(8,128)(2,1)S(1)} %collective-permute-done.23.refs_4_), channel_id=1, source_target_pairs={{0,2},{1,3},{2,0},{3,1},{4,6},{5,7},{6,4},{7,5},{8,10},{9,11},{10,... | collective-permute-start | bytes 442376 | tf_op jit(solution)/shard_map/ppermute | solution.py:498
  13.8 4.5 %collective-permute-start.20 = (bf16[144,512]{1,0:T(8,128)(2,1)}, bf16[144,512]{1,0:T(8,128)(2,1)S(1)}, u32[]{:S(2)}, u32[]{:S(2)}) collective-permute-start(bf16[144,512]{1,0:T(8,128)(2,1)} %pack.1.refs_0_), channel_id=1, source_target_pairs={{0,1},{1,0},{2,3},{3,2},{4,5},{5,4},{6,7},{7,6},{8,9},{9,8},{10,11... | collective-permute-start | bytes 442376 | tf_op jit(solution)/shard_map/ppermute | solution.py:498
  13.8 4.5 %collective-permute-start.24 = (bf16[144,512]{1,0:T(8,128)(2,1)S(1)}, bf16[144,512]{1,0:T(8,128)(2,1)S(1)}, u32[]{:S(2)}, u32[]{:S(2)}) collective-permute-start(bf16[144,512]{1,0:T(8,128)(2,1)S(1)} %collective-permute-done.23.refs_4_), channel_id=1, source_target_pairs={{0,1},{1,0},{2,3},{3,2},{4,5},{5,4},{6,7},{7,6},{8,9},{9,8},{10,11... | collective-permute-start | bytes 442376 | tf_op jit(solution)/shard_map/ppermute | solution.py:498
  14.3 4.0 %collective-permute-start.22 = (bf16[144,512]{1,0:T(8,128)(2,1)S(1)}, bf16[144,512]{1,0:T(8,128)(2,1)S(1)}, u32[]{:S(2)}, u32[]{:S(2)}) collective-permute-start(bf16[144,512]{1,0:T(8,128)(2,1)S(1)} %collective-permute-done.21.refs_2_), channel_id=1, source_target_pairs={{0,1},{1,0},{2,3},{3,2},{4,5},{5,4},{6,7},{7,6},{8,9},{9,8},{10,11... | collective-permute-start | bytes 442376 | tf_op jit(solution)/shard_map/ppermute | solution.py:498
  18.2 1.4 %collective-permute-start.26 = (bf16[144,512]{1,0:T(8,128)(2,1)S(1)}, bf16[144,512]{1,0:T(8,128)(2,1)S(1)}, u32[]{:S(2)}, u32[]{:S(2)}) collective-permute-start(bf16[144,512]{1,0:T(8,128)(2,1)S(1)} %collective-permute-done.25.refs_6_), channel_id=1, source_target_pairs={{0,1},{1,0},{2,3},{3,2},{4,5},{5,4},{6,7},{7,6},{8,9},{9,8},{10,11... | collective-permute-start | bytes 442376 | tf_op jit(solution)/shard_map/ppermute | solution.py:498
  18.2 16.7 %slice-start = ((s8[12582912]{0:T(1024)(128)(4,1)}), s8[4194304]{0:T(1024)(128)(4,1)S(1)}, s32[]{:S(2)}) async-start(s8[12582912]{0:T(1024)(128)(4,1)} %bitcast.109), calls=%async_computation | async-start | bytes 8388608
  18.3 16.6 %slice-start.1 = ((s8[12582912]{0:T(1024)(128)(4,1)}), s8[4194304]{0:T(1024)(128)(4,1)S(1)}, s32[]{:S(2)}) async-start(s8[12582912]{0:T(1024)(128)(4,1)} %bitcast.109), calls=%async_computation.1 | async-start | bytes 8388608
  18.3 16.6 %slice-start.2 = ((s8[12582912]{0:T(1024)(128)(4,1)}), s8[4194304]{0:T(1024)(128)(4,1)S(1)}, s32[]{:S(2)}) async-start(s8[12582912]{0:T(1024)(128)(4,1)} %bitcast.109), calls=%async_computation.2 | async-start | bytes 8388608
  31.8 16.8 %collective-permute-start.27 = (bf16[2,320,384]{2,1,0:T(8,128)(2,1)S(1)}, bf16[2,320,384]{2,1,0:T(8,128)(2,1)S(1)}, u32[]{:S(2)}, u32[]{:S(2)}) collective-permute-start(bf16[2,320,384]{2,1,0:T(8,128)(2,1)S(1)} %get-tuple-element.110), channel_id=1, source_target_pairs={{0,8},{8,0},{16,24},{24,16},{1,9},{9,1},{17,25},{25,17},{2,10},{10... | collective-permute-start | bytes 1474568 | tf_op jit(solution)/shard_map/ppermute | solution.py:498
  33.4 16.9 %collective-permute-start.29 = (bf16[2,320,384]{2,1,0:T(8,128)(2,1)S(1)}, bf16[2,320,384]{2,1,0:T(8,128)(2,1)S(1)}, u32[]{:S(2)}, u32[]{:S(2)}) collective-permute-start(bf16[2,320,384]{2,1,0:T(8,128)(2,1)S(1)} %get-tuple-element.113), channel_id=1, source_target_pairs={{0,16},{8,24},{16,0},{24,8},{1,17},{9,25},{17,1},{25,9},{2,18},{10... | collective-permute-start | bytes 1474568 | tf_op jit(solution)/shard_map/ppermute | solution.py:498
  43.4 14.2 %collective-permute-start.35 = (bf16[2,320,384]{2,1,0:T(8,128)(2,1)S(1)}, bf16[2,320,384]{2,1,0:T(8,128)(2,1)S(1)}, u32[]{:S(2)}, u32[]{:S(2)}) collective-permute-start(bf16[2,320,384]{2,1,0:T(8,128)(2,1)S(1)} %get-tuple-element.121), channel_id=1, source_target_pairs={{0,8},{8,0},{16,24},{24,16},{1,9},{9,1},{17,25},{25,17},{2,10},{10... | collective-permute-start | bytes 1474568 | tf_op jit(solution)/shard_map/ppermute | solution.py:498
  44.0 14.3 %collective-permute-start.37 = (bf16[2,320,384]{2,1,0:T(8,128)(2,1)S(1)}, bf16[2,320,384]{2,1,0:T(8,128)(2,1)S(1)}, u32[]{:S(2)}, u32[]{:S(2)}) collective-permute-start(bf16[2,320,384]{2,1,0:T(8,128)(2,1)S(1)} %get-tuple-element.122), channel_id=1, source_target_pairs={{0,16},{8,24},{16,0},{24,8},{1,17},{9,25},{17,1},{25,9},{2,18},{10... | collective-permute-start | bytes 1474568 | tf_op jit(solution)/shard_map/ppermute | solution.py:498
  48.6 14.8 %collective-permute-start.28 = (bf16[320,384]{1,0:T(8,128)(2,1)S(1)}, bf16[320,384]{1,0:T(8,128)(2,1)S(1)}, u32[]{:S(2)}, u32[]{:S(2)}) collective-permute-start(bf16[320,384]{1,0:T(8,128)(2,1)S(1)} %fusion.25), channel_id=1, source_target_pairs={{0,16},{8,24},{16,0},{24,8},{1,17},{9,25},{17,1},{25,9},{2,18},{10... | collective-permute-start | bytes 737288 | tf_op jit(solution)/shard_map/ppermute | solution.py:498
  50.3 13.1 %collective-permute-start.30 = (bf16[320,384]{1,0:T(8,128)(2,1)S(1)}, bf16[320,384]{1,0:T(8,128)(2,1)S(1)}, u32[]{:S(2)}, u32[]{:S(2)}) collective-permute-start(bf16[320,384]{1,0:T(8,128)(2,1)S(1)} %fusion.21), channel_id=1, source_target_pairs={{0,8},{8,0},{16,24},{24,16},{1,9},{9,1},{17,25},{25,17},{2,10},{10... | collective-permute-start | bytes 737288 | tf_op jit(solution)/shard_map/ppermute | solution.py:498
  57.7 11.0 %collective-permute-start.36 = (bf16[320,384]{1,0:T(8,128)(2,1)S(1)}, bf16[320,384]{1,0:T(8,128)(2,1)S(1)}, u32[]{:S(2)}, u32[]{:S(2)}) collective-permute-start(bf16[320,384]{1,0:T(8,128)(2,1)S(1)} %fusion.19), channel_id=1, source_target_pairs={{0,16},{8,24},{16,0},{24,8},{1,17},{9,25},{17,1},{25,9},{2,18},{10... | collective-permute-start | bytes 737288 | tf_op jit(solution)/shard_map/ppermute | solution.py:498
  58.3 10.4 %collective-permute-start.38 = (bf16[320,384]{1,0:T(8,128)(2,1)S(1)}, bf16[320,384]{1,0:T(8,128)(2,1)S(1)}, u32[]{:S(2)}, u32[]{:S(2)}) collective-permute-start(bf16[320,384]{1,0:T(8,128)(2,1)S(1)} %fusion.15), channel_id=1, source_target_pairs={{0,8},{8,0},{16,24},{24,16},{1,9},{9,1},{17,25},{25,17},{2,10},{10... | collective-permute-start | bytes 737288 | tf_op jit(solution)/shard_map/ppermute | solution.py:498
  63.7 10.3 %collective-permute-start.32 = (bf16[320,384]{1,0:T(8,128)(2,1)S(1)}, bf16[320,384]{1,0:T(8,128)(2,1)S(1)}, u32[]{:S(2)}, u32[]{:S(2)}) collective-permute-start(bf16[320,384]{1,0:T(8,128)(2,1)S(1)} %fusion.24.refs_0_), channel_id=1, source_target_pairs={{0,16},{8,24},{16,0},{24,8},{1,17},{9,25},{17,1},{25,9},{2,18},{10... | collective-permute-start | bytes 737288 | tf_op jit(solution)/shard_map/ppermute | solution.py:498
  65.2 10.4 %collective-permute-start.31 = (bf16[320,384]{1,0:T(8,128)(2,1)S(1)}, bf16[320,384]{1,0:T(8,128)(2,1)S(1)}, u32[]{:S(2)}, u32[]{:S(2)}) collective-permute-start(bf16[320,384]{1,0:T(8,128)(2,1)S(1)} %fusion.24.refs_0_), channel_id=1, source_target_pairs={{0,8},{8,0},{16,24},{24,16},{1,9},{9,1},{17,25},{25,17},{2,10},{10... | collective-permute-start | bytes 737288 | tf_op jit(solution)/shard_map/ppermute | solution.py:498
  69.0 10.2 %collective-permute-start.40 = (bf16[320,384]{1,0:T(8,128)(2,1)S(1)}, bf16[320,384]{1,0:T(8,128)(2,1)S(1)}, u32[]{:S(2)}, u32[]{:S(2)}) collective-permute-start(bf16[320,384]{1,0:T(8,128)(2,1)S(1)} %fusion.18.refs_5_), channel_id=1, source_target_pairs={{0,16},{8,24},{16,0},{24,8},{1,17},{9,25},{17,1},{25,9},{2,18},{10... | collective-permute-start | bytes 737288 | tf_op jit(solution)/shard_map/ppermute | solution.py:498
  70.4 9.8 %collective-permute-start.39 = (bf16[320,384]{1,0:T(8,128)(2,1)S(1)}, bf16[320,384]{1,0:T(8,128)(2,1)S(1)}, u32[]{:S(2)}, u32[]{:S(2)}) collective-permute-start(bf16[320,384]{1,0:T(8,128)(2,1)S(1)} %fusion.18.refs_5_), channel_id=1, source_target_pairs={{0,8},{8,0},{16,24},{24,16},{1,9},{9,1},{17,25},{25,17},{2,10},{10... | collective-permute-start | bytes 737288 | tf_op jit(solution)/shard_map/ppermute | solution.py:498
  74.0 7.4 %collective-permute-start.34 = (bf16[160,384]{1,0:T(8,128)(2,1)S(1)}, bf16[160,384]{1,0:T(8,128)(2,1)S(1)}, u32[]{:S(2)}, u32[]{:S(2)}) collective-permute-start(bf16[160,384]{1,0:T(8,128)(2,1)S(1)} %slice.139), channel_id=1, source_target_pairs={{0,8},{8,0},{16,24},{24,16},{1,9},{9,1},{17,25},{25,17},{2,10},{10... | collective-permute-start | bytes 368648 | tf_op jit(solution)/shard_map/ppermute | solution.py:498
  75.5 6.0 %collective-permute-start.33 = (bf16[160,384]{1,0:T(8,128)(2,1)S(1)}, bf16[160,384]{1,0:T(8,128)(2,1)S(1)}, u32[]{:S(2)}, u32[]{:S(2)}) collective-permute-start(bf16[160,384]{1,0:T(8,128)(2,1)S(1)} %slice.138), channel_id=1, source_target_pairs={{0,16},{8,24},{16,0},{24,8},{1,17},{9,25},{17,1},{25,9},{2,18},{10... | collective-permute-start | bytes 368648 | tf_op jit(solution)/shard_map/ppermute | solution.py:498
  79.2 4.9 %collective-permute-start.42 = (bf16[160,384]{1,0:T(8,128)(2,1)S(1)}, bf16[160,384]{1,0:T(8,128)(2,1)S(1)}, u32[]{:S(2)}, u32[]{:S(2)}) collective-permute-start(bf16[160,384]{1,0:T(8,128)(2,1)S(1)} %slice.145), channel_id=1, source_target_pairs={{0,8},{8,0},{16,24},{24,16},{1,9},{9,1},{17,25},{25,17},{2,10},{10... | collective-permute-start | bytes 368648 | tf_op jit(solution)/shard_map/ppermute | solution.py:498
  80.2 4.9 %collective-permute-start.41 = (bf16[160,384]{1,0:T(8,128)(2,1)S(1)}, bf16[160,384]{1,0:T(8,128)(2,1)S(1)}, u32[]{:S(2)}, u32[]{:S(2)}) collective-permute-start(bf16[160,384]{1,0:T(8,128)(2,1)S(1)} %slice.144), channel_id=1, source_target_pairs={{0,16},{8,24},{16,0},{24,8},{1,17},{9,25},{17,1},{25,9},{2,18},{10... | collective-permute-start | bytes 368648 | tf_op jit(solution)/shard_map/ppermute | solution.py:498
  93.5 17.4 %copy-start.1 = (bf16[144,512]{1,0:T(8,128)(2,1)S(1)}, bf16[144,512]{1,0:T(8,128)(2,1)}, u32[]{:S(2)}) copy-start(bf16[144,512]{1,0:T(8,128)(2,1)} %pack.1.refs_0_) | copy-start | bytes 442372
  93.5 2.0 %collective-permute-start.43 = (bf16[4,128,512]{2,1,0:T(8,128)(2,1)S(1)}, bf16[4,128,512]{2,1,0:T(8,128)(2,1)S(1)}, u32[]{:S(2)}, u32[]{:S(2)}) collective-permute-start(bf16[4,128,512]{2,1,0:T(8,128)(2,1)S(1)} %get-tuple-element.124), channel_id=1, source_target_pairs={{0,1},{1,0},{2,3},{3,2},{4,5},{5,4},{6,7},{7,6},{8,9},{9,8},{10,11... | collective-permute-start | bytes 1572872 | tf_op jit(solution)/shard_map/ppermute | solution.py:498
  95.7 8.4 %collective-permute-start.44 = (bf16[128,512]{1,0:T(8,128)(2,1)S(1)}, bf16[128,512]{1,0:T(8,128)(2,1)S(1)}, u32[]{:S(2)}, u32[]{:S(2)}) collective-permute-start(bf16[128,512]{1,0:T(8,128)(2,1)S(1)} %get-tuple-element.133), channel_id=1, source_target_pairs={{0,6},{1,7},{2,4},{3,5},{4,2},{5,3},{6,0},{7,1},{8,14},{9,15},{10,... | collective-permute-start | bytes 393224 | tf_op jit(solution)/shard_map/ppermute | solution.py:498
  99.8 8.0 %collective-permute-start.46 = (bf16[128,512]{1,0:T(8,128)(2,1)S(1)}, bf16[128,512]{1,0:T(8,128)(2,1)S(1)}, u32[]{:S(2)}, u32[]{:S(2)}) collective-permute-start(bf16[128,512]{1,0:T(8,128)(2,1)S(1)} %get-tuple-element.134), channel_id=1, source_target_pairs={{0,2},{1,3},{2,0},{3,1},{4,6},{5,7},{6,4},{7,5},{8,10},{9,11},{10,... | collective-permute-start | bytes 393224 | tf_op jit(solution)/shard_map/ppermute | solution.py:498
  99.8 11.0 %collective-permute-start.45 = (bf16[128,512]{1,0:T(8,128)(2,1)S(1)}, bf16[128,512]{1,0:T(8,128)(2,1)S(1)}, u32[]{:S(2)}, u32[]{:S(2)}) collective-permute-start(bf16[128,512]{1,0:T(8,128)(2,1)S(1)} %get-tuple-element.135), channel_id=1, source_target_pairs={{0,4},{1,5},{2,6},{3,7},{4,0},{5,1},{6,2},{7,3},{8,12},{9,13},{10,... | collective-permute-start | bytes 393224 | tf_op jit(solution)/shard_map/ppermute | solution.py:498
  111.2 0.7 copy-start.2

commit v9 on v6

--- a/solution.py
+++ b/solution.py
@@ -263,6 +263,7 @@
 
 def weigh_large_kernel(dims, offs, rowid, probs, scale, chosen):
     chosen[...] = jnp.zeros_like(chosen)
+    scale[...] = jnp.zeros_like(scale)
     for e in range(dims["experts"]):
         first = aligned(dims, offs[0, e])
         at = pl.ds(first, dims["window"])
@@ -428,8 +429,11 @@
         first = aligned(dims, offs[0, e])
         at = pl.ds(first, window)
         got = jnp.dot(hidden[at, :], w_down[e], preferred_element_type=F32) * scale[at, 0:1]
-        mask = row_mask(dims, first, offs, e)
-        scaled[at, :] = jnp.where(mask, got, scaled[at, :].astype(F32)).astype(BF16)
+        keep = (lax.broadcasted_iota(jnp.int32, (ALIGN, 1), 0) + first) >= offs[0, e]
+        edge = pl.ds(first, ALIGN)
+        old = scaled[edge, :].astype(F32)
+        scaled[edge, :] = jnp.where(keep, got[:ALIGN], old).astype(BF16)
+        scaled[pl.ds(first + ALIGN, window - ALIGN), :] = got[ALIGN:].astype(BF16)
     rows, total, width = dims["rows"], dims["total"], w_down.shape[2]
     blocks, many = dims["blocks"], min(4, dims["blocks"])
     if dims["small"]:
@@ -493,13 +497,10 @@
     return (jax.nn.silu(gate) * up).astype(BF16)
 
 
-def spread_chunk(hidden, two_steps):
+def spread_chunk(hidden):
     x, y = swap(hidden, "rep", 1), swap(hidden, "rep", 2)
-    if two_steps:
-        half = hidden.shape[0] // 2
-        corner = [(3, 0, swap(x[:half], "rep", 2)), (3, half, swap(y[half:], "rep", 1))]
-    else:
-        corner = [(3, 0, swap(hidden, "rep", 3))]
+    half = hidden.shape[0] // 2
+    corner = [(3, 0, swap(x[:half], "rep", 2)), (3, half, swap(y[half:], "rep", 1))]
     return [(0, 0, hidden), (1, 0, x), (2, 0, y)] + corner
 
 
@@ -582,14 +583,14 @@
     for c, (gx, uy, *kept) in enumerate(parts):
         came.append((swap(gx, "rep", 1), swap(uy, "rep", 2)))
         parts[c] = kept
-    rows_of, _ = lax.optimization_barrier((rows_of, parts[-1]))
+    rows_of, came[0] = lax.optimization_barrier((rows_of, came[0]))
     scale, chosen, *peak = weigh(dims, offs, rows_of, probs, meta)
     chunks = []
     for c, kept in enumerate(parts):
         hidden = reduce_chunk(came[c], kept)
         if c == 0:
             hidden, scale, chosen = lax.optimization_barrier((hidden, scale, chosen))
-        chunks.append(spread_chunk(hidden, c + 1 < len(parts)))
+        chunks.append(spread_chunk(hidden))
     mixed = down(dims, me, offs, w_down, scale, chosen, rowk, chunks)
     if dims["small"]:
         return sum_over_exp(*mixed), peak[0]

time: 112 us -> 111 us (level)
    ppermute x26 -> x27, waiting for transfers between devices: 46 us -> 45.5 us  [swap(): return lax.ppermute(value, axis, [(i, i ^ bit) for i in range(count)])]
    ppermute x26 -> x27, starting transfers between devices: 28.7 us -> 28.7 us  [swap(): return lax.ppermute(value, axis, [(i, i ^ bit) for i in range(count)])]
  transfers between devices with their start and end apart: 26 -> 27, of which waited for: 14 -> 15; matrix products, arithmetic and copies ran while one was open for 1% -> 1% of each run, Pallas kernels for 11% -> 11%
where the time goes in v9:
time: 111 us
  waiting for transfers between devices  45.5 us (41%)
  Pallas kernels  31.9 us (29%)
  starting transfers between devices  28.7 us (26%)
  local copies, waits for them, and re-layouts  3.02 us (3%)
    ppermute x27, waiting for transfers between devices, swap(): return lax.ppermute(value, axis, [(i, i ^ bit) for i in range(count)])  45.5 us
    ppermute x27, starting transfers between devices, swap(): return lax.ppermute(value, axis, [(i, i ^ bit) for i in range(count)])  28.7 us
    pallas_call x2, Pallas kernels, gate_up(): pl.pallas_call(functools.partial(gate_up_kernel, dims, c, first_part), ou...  19.7 us
    pallas_call x1, Pallas kernels, down(): pl.pallas_call(functools.partial(down_kernel, dims, places), out_shape=ou...  8.14 us
    pallas_call x1, Pallas kernels, weigh(): pl.pallas_call(functools.partial(weigh_small_kernel if small else weigh_l...  4.12 us
    unnamed x14, local copies, waits for them, and re-layouts  2.94 us
  transfers between devices with their start and end apart: 27, of which 15 were waited for; matrix products, arithmetic and copies ran while one was open for 1% of the time, Pallas kernels for 11%

profile of v9, /device:TPU:0, one launch (start us, length us, event | category | flops | bytes accessed | tf_op | source)
XLA Modules:
  0.0 111.3 jit_solution(1875040356531266141)
XLA Ops:
  0.0 0.9 copy-done
  0.9 0.7 copy-done.1
  1.6 0.7 copy-done.2
  2.3 4.1 %collective-permute-start.23 = (bf16[144,512]{1,0:T(8,128)(2,1)S(1)}, bf16[144,512]{1,0:T(8,128)(2,1)S(1)}, u32[]{:S(2)}, u32[]{:S(2)}) collective-permute-start(bf16[144,512]{1,0:T(8,128)(2,1)S(1)} %pack.1.refs_0_), channel_id=1, source_target_pairs={{0,4},{1,5},{2,6},{3,7},{4,0},{5,1},{6,2},{7,3},{8,12},{9,13},{10,... | collective-permute-start | bytes 442376 | tf_op jit(solution)/shard_map/ppermute | solution.py:487
  6.4 1.6 %collective-permute-start.21 = (bf16[144,512]{1,0:T(8,128)(2,1)S(1)}, bf16[144,512]{1,0:T(8,128)(2,1)S(1)}, u32[]{:S(2)}, u32[]{:S(2)}) collective-permute-start(bf16[144,512]{1,0:T(8,128)(2,1)S(1)} %pack.1.refs_0_), channel_id=1, source_target_pairs={{0,2},{1,3},{2,0},{3,1},{4,6},{5,7},{6,4},{7,5},{8,10},{9,11},{10,... | collective-permute-start | bytes 442376 | tf_op jit(solution)/shard_map/ppermute | solution.py:487
  8.0 5.5 %collective-permute-done.23.refs_4_ = bf16[144,512]{1,0:T(8,128)(2,1)S(1)} collective-permute-done((bf16[144,512]{1,0:T(8,128)(2,1)S(1)}, bf16[144,512]{1,0:T(8,128)(2,1)S(1)}, u32[]{:S(2)}, u32[]{:S(2)}) %collective-permute-start.23) | collective-permute-done | bytes 147488 | tf_op jit(solution)/shard_map/ppermute | solution.py:487
  13.5 0.6 collective-permute-start.25
  14.1 0.5 collective-permute-start.24
  14.6 0.0 collective-permute-start.22
  14.7 4.0 %collective-permute-done.25.refs_6_ = bf16[144,512]{1,0:T(8,128)(2,1)S(1)} collective-permute-done((bf16[144,512]{1,0:T(8,128)(2,1)S(1)}, bf16[144,512]{1,0:T(8,128)(2,1)S(1)}, u32[]{:S(2)}, u32[]{:S(2)}) %collective-permute-start.25) | collective-permute-done | bytes 147488 | tf_op jit(solution)/shard_map/ppermute | solution.py:487
  18.7 0.0 collective-permute-start.26
  18.7 0.1 pad_add_fusion.me_ref
  18.7 0.0 collective-permute-done.20.refs_1_
  18.7 0.0 collective-permute-done.24.refs_5_
  18.8 0.0 collective-permute-done.22.refs_3_
  18.8 1.3 %collective-permute-done.26.refs_7_ = bf16[144,512]{1,0:T(8,128)(2,1)S(1)} collective-permute-done((bf16[144,512]{1,0:T(8,128)(2,1)S(1)}, bf16[144,512]{1,0:T(8,128)(2,1)S(1)}, u32[]{:S(2)}, u32[]{:S(2)}) %collective-permute-start.26) | collective-permute-done | bytes 147488 | tf_op jit(solution)/shard_map/ppermute | solution.py:487
  20.0 11.2 %gate_up.6 = (s32[8,16,128]{2,1,0:T(8,128)}, f32[8,16,128]{2,1,0:T(8,128)S(1)}, s32[8,8,128]{2,1,0:T(8,128)S(1)}, bf16[1392,512]{1,0:T(8,128)(2,1)S(1)}, bf16[13...) custom-call(s32[2]{0:T(128)S(1)} %pad_add_fusion.me_ref, ...), custom_call_target="tpu_custom_call" | custom-call | flops 1094713344 | bytes 14008320 | tf_op jit(solution)/shard_map/gate_up/pallas_call | solution.py:405
  31.2 1.6 %collective-permute-start.27 = (bf16[2,320,384]{2,1,0:T(8,128)(2,1)S(1)}, bf16[2,320,384]{2,1,0:T(8,128)(2,1)S(1)}, u32[]{:S(2)}, u32[]{:S(2)}) collective-permute-start(bf16[2,320,384]{2,1,0:T(8,128)(2,1)S(1)} %get-tuple-element.104), channel_id=1, source_target_pairs={{0,8},{8,0},{16,24},{24,16},{1,9},{9,1},{17,25},{25,17},{2,10},{10... | collective-permute-start | bytes 1474568 | tf_op jit(solution)/shard_map/ppermute | solution.py:487
  32.8 1.5 %collective-permute-start.28 = (bf16[2,320,384]{2,1,0:T(8,128)(2,1)S(1)}, bf16[2,320,384]{2,1,0:T(8,128)(2,1)S(1)}, u32[]{:S(2)}, u32[]{:S(2)}) collective-permute-start(bf16[2,320,384]{2,1,0:T(8,128)(2,1)S(1)} %get-tuple-element.105), channel_id=1, source_target_pairs={{0,16},{8,24},{16,0},{24,8},{1,17},{9,25},{17,1},{25,9},{2,18},{10... | collective-permute-start | bytes 1474568 | tf_op jit(solution)/shard_map/ppermute | solution.py:487
  34.4 8.5 %gate_up.7 = (bf16[2,320,384]{2,1,0:T(8,128)(2,1)S(1)}, bf16[2,320,384]{2,1,0:T(8,128)(2,1)S(1)}, f32[320,384]{1,0:T(8,128)S(1)}, f32[320,384]{1,0:T(8,128)S(1)}...) custom-call(s32[2]{0:T(128)S(1)} %pad_add_fusion.me_ref, s32[2,16]{1,0:T(2,128)S(1)} %get-tuple-element.102.offs.refs_0_, ...), custom_call_target="tpu_custom_call" | custom-call | flops 1094713344 | bytes 14008320 | tf_op jit(solution)/shard_map/gate_up/pallas_call | solution.py:405
  42.8 0.6 collective-permute-start.35
  43.4 0.5 collective-permute-start.37
  43.9 0.7 collective-permute-done.27
  44.6 1.7 %collective-permute-done.28 = bf16[2,320,384]{2,1,0:T(8,128)(2,1)S(1)} collective-permute-done((bf16[2,320,384]{2,1,0:T(8,128)(2,1)S(1)}, bf16[2,320,384]{2,1,0:T(8,128)(2,1)S(1)}, u32[]{:S(2)}, u32[]{:S(2)}) %collective-permute-start.28) | collective-permute-done | bytes 491552 | tf_op jit(solution)/shard_map/ppermute | solution.py:487
  46.3 0.1 fusion.25
  46.3 2.3 %collective-permute-start.29 = (bf16[320,384]{1,0:T(8,128)(2,1)S(1)}, bf16[320,384]{1,0:T(8,128)(2,1)S(1)}, u32[]{:S(2)}, u32[]{:S(2)}) collective-permute-start(bf16[320,384]{1,0:T(8,128)(2,1)S(1)} %fusion.25), channel_id=1, source_target_pairs={{0,16},{8,24},{16,0},{24,8},{1,17},{9,25},{17,1},{25,9},{2,18},{10... | collective-permute-start | bytes 737288 | tf_op jit(solution)/shard_map/ppermute | solution.py:487
  48.6 0.1 fusion.21
  48.7 0.1 collective-permute-start.30
  48.7 8.3 %collective-permute-done.35 = bf16[2,320,384]{2,1,0:T(8,128)(2,1)S(1)} collective-permute-done((bf16[2,320,384]{2,1,0:T(8,128)(2,1)S(1)}, bf16[2,320,384]{2,1,0:T(8,128)(2,1)S(1)}, u32[]{:S(2)}, u32[]{:S(2)}) %collective-permute-start.35) | collective-permute-done | bytes 491552 | tf_op jit(solution)/shard_map/ppermute | solution.py:487
  57.0 0.1 fusion.19
  57.1 0.6 collective-permute-start.36
  57.7 0.0 collective-permute-done.37
  57.7 0.1 fusion.15
  57.8 1.5 %collective-permute-start.38 = (bf16[320,384]{1,0:T(8,128)(2,1)S(1)}, bf16[320,384]{1,0:T(8,128)(2,1)S(1)}, u32[]{:S(2)}, u32[]{:S(2)}) collective-permute-start(bf16[320,384]{1,0:T(8,128)(2,1)S(1)} %fusion.15), channel_id=1, source_target_pairs={{0,8},{8,0},{16,24},{24,16},{1,9},{9,1},{17,25},{25,17},{2,10},{10... | collective-permute-start | bytes 737288 | tf_op jit(solution)/shard_map/ppermute | solution.py:487
  59.2 4.1 %weigh.3 = (f32[1392,128]{1,0:T(8,128)S(1)}, bf16[8,128,1280]{2,1,0:T(8,128)(2,1)S(1)}, s32[1]{0:T(128)}) custom-call(s32[2,16]{1,0:T(2,128)S(1)} %get-tuple-element.102.offs.refs_0_, bf16[1392,1024]{1,0:T(8,128)(2,1)S(1)} %get-tuple-element.106.select, f32[8,16,128]{2,1,0:T(8,128)S(1)} %get-tuple-element.107.probs, ...), custom_call_target="tpu_custom_call" | custom-call | flops 6000000000 | bytes 8000000 | tf_op jit(solution)/shard_map/weigh/pallas_call | solution.py:293
  63.3 0.0 collective-permute-done.29
  63.4 0.3 fusion.24.refs_0_
  63.6 1.0 collective-permute-start.32
  64.6 1.2 %collective-permute-start.31 = (bf16[320,384]{1,0:T(8,128)(2,1)S(1)}, bf16[320,384]{1,0:T(8,128)(2,1)S(1)}, u32[]{:S(2)}, u32[]{:S(2)}) collective-permute-start(bf16[320,384]{1,0:T(8,128)(2,1)S(1)} %fusion.24.refs_0_), channel_id=1, source_target_pairs={{0,8},{8,0},{16,24},{24,16},{1,9},{9,1},{17,25},{25,17},{2,10},{10... | collective-permute-start | bytes 737288 | tf_op jit(solution)/shard_map/ppermute | solution.py:487
  65.8 2.3 %collective-permute-done.36 = bf16[320,384]{1,0:T(8,128)(2,1)S(1)} collective-permute-done((bf16[320,384]{1,0:T(8,128)(2,1)S(1)}, bf16[320,384]{1,0:T(8,128)(2,1)S(1)}, u32[]{:S(2)}, u32[]{:S(2)}) %collective-permute-start.36) | collective-permute-done | bytes 245792 | tf_op jit(solution)/shard_map/ppermute | solution.py:487
  68.1 0.3 fusion.18.refs_5_
  68.4 1.5 %collective-permute-start.40 = (bf16[320,384]{1,0:T(8,128)(2,1)S(1)}, bf16[320,384]{1,0:T(8,128)(2,1)S(1)}, u32[]{:S(2)}, u32[]{:S(2)}) collective-permute-start(bf16[320,384]{1,0:T(8,128)(2,1)S(1)} %fusion.18.refs_5_), channel_id=1, source_target_pairs={{0,16},{8,24},{16,0},{24,8},{1,17},{9,25},{17,1},{25,9},{2,18},{10... | collective-permute-start | bytes 737288 | tf_op jit(solution)/shard_map/ppermute | solution.py:487
  69.9 0.6 collective-permute-start.39
  70.5 2.9 %collective-permute-done.32.refs_2_ = bf16[320,384]{1,0:T(8,128)(2,1)S(1)} collective-permute-done((bf16[320,384]{1,0:T(8,128)(2,1)S(1)}, bf16[320,384]{1,0:T(8,128)(2,1)S(1)}, u32[]{:S(2)}, u32[]{:S(2)}) %collective-permute-start.32) | collective-permute-done | bytes 245792 | tf_op jit(solution)/shard_map/ppermute | solution.py:487
  73.4 1.6 %collective-permute-start.34 = (bf16[160,384]{1,0:T(8,128)(2,1)S(1)}, bf16[160,384]{1,0:T(8,128)(2,1)S(1)}, u32[]{:S(2)}, u32[]{:S(2)}) collective-permute-start(bf16[160,384]{1,0:T(8,128)(2,1)S(1)} %slice.131), channel_id=1, source_target_pairs={{0,8},{8,0},{16,24},{24,16},{1,9},{9,1},{17,25},{25,17},{2,10},{10... | collective-permute-start | bytes 368648 | tf_op jit(solution)/shard_map/ppermute | solution.py:487
  75.0 0.6 collective-permute-start.33
  75.6 3.1 %collective-permute-done.40.refs_7_ = bf16[320,384]{1,0:T(8,128)(2,1)S(1)} collective-permute-done((bf16[320,384]{1,0:T(8,128)(2,1)S(1)}, bf16[320,384]{1,0:T(8,128)(2,1)S(1)}, u32[]{:S(2)}, u32[]{:S(2)}) %collective-permute-start.40) | collective-permute-done | bytes 245792 | tf_op jit(solution)/shard_map/ppermute | solution.py:487
  78.7 1.1 %collective-permute-start.42 = (bf16[160,384]{1,0:T(8,128)(2,1)S(1)}, bf16[160,384]{1,0:T(8,128)(2,1)S(1)}, u32[]{:S(2)}, u32[]{:S(2)}) collective-permute-start(bf16[160,384]{1,0:T(8,128)(2,1)S(1)} %slice.137), channel_id=1, source_target_pairs={{0,8},{8,0},{16,24},{24,16},{1,9},{9,1},{17,25},{25,17},{2,10},{10... | collective-permute-start | bytes 368648 | tf_op jit(solution)/shard_map/ppermute | solution.py:487
  79.8 1.0 collective-permute-start.41
  80.8 2.8 %collective-permute-done.42.refs_9_ = bf16[160,384]{1,0:T(8,128)(2,1)S(1)} collective-permute-done((bf16[160,384]{1,0:T(8,128)(2,1)S(1)}, bf16[160,384]{1,0:T(8,128)(2,1)S(1)}, u32[]{:S(2)}, u32[]{:S(2)}) %collective-permute-start.42) | collective-permute-done | bytes 122912 | tf_op jit(solution)/shard_map/ppermute | solution.py:487
  83.6 1.2 %collective-permute-done.41.refs_8_ = bf16[160,384]{1,0:T(8,128)(2,1)S(1)} collective-permute-done((bf16[160,384]{1,0:T(8,128)(2,1)S(1)}, bf16[160,384]{1,0:T(8,128)(2,1)S(1)}, u32[]{:S(2)}, u32[]{:S(2)}) %collective-permute-start.41) | collective-permute-done | bytes 122912 | tf_op jit(solution)/shard_map/ppermute | solution.py:487
  84.8 8.1 %down.3 = (bf16[4,128,512]{2,1,0:T(8,128)(2,1)S(1)}, bf16[4,128,512]{2,1,0:T(8,128)(2,1)S(1)}) custom-call(s32[2]{0:T(128)S(1)} %pad_add_fusion.me_ref, s32[2,16]{1,0:T(2,128)S(1)} %get-tuple-element.102.offs.refs_0_, bf16[16,768,512]{2,1,0:T(8,128)(2,1)} %w_down.1, f32[1392,128]{1,0:T(8,128)S(1)} %get-tuple-element.118.scale, ...), custom_call_target="tpu_custom_call" | custom-call | flops 2554331136 | bytes 12582912 | tf_op jit(solution)/shard_map/down/pallas_call | solution.py:473
  92.9 0.1 collective-permute-start.43
  93.0 1.9 %collective-permute-done.43 = bf16[4,128,512]{2,1,0:T(8,128)(2,1)S(1)} collective-permute-done((bf16[4,128,512]{2,1,0:T(8,128)(2,1)S(1)}, bf16[4,128,512]{2,1,0:T(8,128)(2,1)S(1)}, u32[]{:S(2)}, u32[]{:S(2)}) %collective-permute-start.43) | collective-permute-done | bytes 524320 | tf_op jit(solution)/shard_map/ppermute | solution.py:487
  94.9 0.2 fusion.29
  95.1 4.1 %collective-permute-start.44 = (bf16[128,512]{1,0:T(8,128)(2,1)S(1)}, bf16[128,512]{1,0:T(8,128)(2,1)S(1)}, u32[]{:S(2)}, u32[]{:S(2)}) collective-permute-start(bf16[128,512]{1,0:T(8,128)(2,1)S(1)} %get-tuple-element.139), channel_id=1, source_target_pairs={{0,6},{1,7},{2,4},{3,5},{4,2},{5,3},{6,0},{7,1},{8,14},{9,15},{10,... | collective-permute-start | bytes 393224 | tf_op jit(solution)/shard_map/ppermute | solution.py:487
  99.2 0.6 collective-permute-start.45
  100.5 3.0 %collective-permute-done.44 = bf16[128,512]{1,0:T(8,128)(2,1)S(1)} collective-permute-done((bf16[128,512]{1,0:T(8,128)(2,1)S(1)}, bf16[128,512]{1,0:T(8,128)(2,1)S(1)}, u32[]{:S(2)}, u32[]{:S(2)}) %collective-permute-start.44) | collective-permute-done | bytes 131104 | tf_op jit(solution)/shard_map/ppermute | solution.py:487
  103.5 3.7 %collective-permute-done.46 = bf16[128,512]{1,0:T(8,128)(2,1)S(1)} collective-permute-done((bf16[128,512]{1,0:T(8,128)(2,1)S(1)}, bf16[128,512]{1,0:T(8,128)(2,1)S(1)}, u32[]{:S(2)}, u32[]{:S(2)}) %collective-permute-start.46) | collective-permute-done | bytes 131104 | tf_op jit(solution)/shard_map/ppermute | solution.py:487
  107.2 3.0 %collective-permute-done.45 = bf16[128,512]{1,0:T(8,128)(2,1)S(1)} collective-permute-done((bf16[128,512]{1,0:T(8,128)(2,1)S(1)}, bf16[128,512]{1,0:T(8,128)(2,1)S(1)}, u32[]{:S(2)}, u32[]{:S(2)}) %collective-permute-start.45) | collective-permute-done | bytes 131104 | tf_op jit(solution)/shard_map/ppermute | solution.py:487
  110.3 0.1 fusion.28
  110.3 0.3 conditional.1
  110.6 0.0 copy-start.4
  110.6 0.6 copy-done.4
  (25 shorter events, 0.1 us)
Async XLA Ops:
  0.0 0.9 copy-start
  0.9 0.7 copy-start.1
  1.6 0.7 copy-start.2
  2.3 11.2 %collective-permute-start.23 = (bf16[144,512]{1,0:T(8,128)(2,1)S(1)}, bf16[144,512]{1,0:T(8,128)(2,1)S(1)}, u32[]{:S(2)}, u32[]{:S(2)}) collective-permute-start(bf16[144,512]{1,0:T(8,128)(2,1)S(1)} %pack.1.refs_0_), channel_id=1, source_target_pairs={{0,4},{1,5},{2,6},{3,7},{4,0},{5,1},{6,2},{7,3},{8,12},{9,13},{10,... | collective-permute-start | bytes 442376 | tf_op jit(solution)/shard_map/ppermute | solution.py:487
  6.4 8.2 %collective-permute-start.21 = (bf16[144,512]{1,0:T(8,128)(2,1)S(1)}, bf16[144,512]{1,0:T(8,128)(2,1)S(1)}, u32[]{:S(2)}, u32[]{:S(2)}) collective-permute-start(bf16[144,512]{1,0:T(8,128)(2,1)S(1)} %pack.1.refs_0_), channel_id=1, source_target_pairs={{0,2},{1,3},{2,0},{3,1},{4,6},{5,7},{6,4},{7,5},{8,10},{9,11},{10,... | collective-permute-start | bytes 442376 | tf_op jit(solution)/shard_map/ppermute | solution.py:487
  13.5 5.1 %collective-permute-start.25 = (bf16[144,512]{1,0:T(8,128)(2,1)S(1)}, bf16[144,512]{1,0:T(8,128)(2,1)S(1)}, u32[]{:S(2)}, u32[]{:S(2)}) collective-permute-start(bf16[144,512]{1,0:T(8,128)(2,1)S(1)} %collective-permute-done.23.refs_4_), channel_id=1, source_target_pairs={{0,2},{1,3},{2,0},{3,1},{4,6},{5,7},{6,4},{7,5},{8,10},{9,11},{10,... | collective-permute-start | bytes 442376 | tf_op jit(solution)/shard_map/ppermute | solution.py:487
  14.1 4.6 %collective-permute-start.20 = (bf16[144,512]{1,0:T(8,128)(2,1)S(1)}, bf16[144,512]{1,0:T(8,128)(2,1)S(1)}, u32[]{:S(2)}, u32[]{:S(2)}) collective-permute-start(bf16[144,512]{1,0:T(8,128)(2,1)S(1)} %pack.1.refs_0_), channel_id=1, source_target_pairs={{0,1},{1,0},{2,3},{3,2},{4,5},{5,4},{6,7},{7,6},{8,9},{9,8},{10,11... | collective-permute-start | bytes 442376 | tf_op jit(solution)/shard_map/ppermute | solution.py:487
  14.1 4.6 %collective-permute-start.24 = (bf16[144,512]{1,0:T(8,128)(2,1)S(1)}, bf16[144,512]{1,0:T(8,128)(2,1)S(1)}, u32[]{:S(2)}, u32[]{:S(2)}) collective-permute-start(bf16[144,512]{1,0:T(8,128)(2,1)S(1)} %collective-permute-done.23.refs_4_), channel_id=1, source_target_pairs={{0,1},{1,0},{2,3},{3,2},{4,5},{5,4},{6,7},{7,6},{8,9},{9,8},{10,11... | collective-permute-start | bytes 442376 | tf_op jit(solution)/shard_map/ppermute | solution.py:487
  14.6 4.1 %collective-permute-start.22 = (bf16[144,512]{1,0:T(8,128)(2,1)S(1)}, bf16[144,512]{1,0:T(8,128)(2,1)S(1)}, u32[]{:S(2)}, u32[]{:S(2)}) collective-permute-start(bf16[144,512]{1,0:T(8,128)(2,1)S(1)} %collective-permute-done.21.refs_2_), channel_id=1, source_target_pairs={{0,1},{1,0},{2,3},{3,2},{4,5},{5,4},{6,7},{7,6},{8,9},{9,8},{10,11... | collective-permute-start | bytes 442376 | tf_op jit(solution)/shard_map/ppermute | solution.py:487
  18.7 1.4 %collective-permute-start.26 = (bf16[144,512]{1,0:T(8,128)(2,1)S(1)}, bf16[144,512]{1,0:T(8,128)(2,1)S(1)}, u32[]{:S(2)}, u32[]{:S(2)}) collective-permute-start(bf16[144,512]{1,0:T(8,128)(2,1)S(1)} %collective-permute-done.25.refs_6_), channel_id=1, source_target_pairs={{0,1},{1,0},{2,3},{3,2},{4,5},{5,4},{6,7},{7,6},{8,9},{9,8},{10,11... | collective-permute-start | bytes 442376 | tf_op jit(solution)/shard_map/ppermute | solution.py:487
  18.7 15.7 %slice-start = ((s8[12582912]{0:T(1024)(128)(4,1)}), s8[4194304]{0:T(1024)(128)(4,1)S(1)}, s32[]{:S(2)}) async-start(s8[12582912]{0:T(1024)(128)(4,1)} %bitcast.95), calls=%async_computation | async-start | bytes 8388608
  18.7 15.6 %slice-start.1 = ((s8[12582912]{0:T(1024)(128)(4,1)}), s8[4194304]{0:T(1024)(128)(4,1)S(1)}, s32[]{:S(2)}) async-start(s8[12582912]{0:T(1024)(128)(4,1)} %bitcast.95), calls=%async_computation.1 | async-start | bytes 8388608
  18.7 15.6 %slice-start.2 = ((s8[12582912]{0:T(1024)(128)(4,1)}), s8[4194304]{0:T(1024)(128)(4,1)S(1)}, s32[]{:S(2)}) async-start(s8[12582912]{0:T(1024)(128)(4,1)} %bitcast.95), calls=%async_computation.2 | async-start | bytes 8388608
  31.2 13.3 %collective-permute-start.27 = (bf16[2,320,384]{2,1,0:T(8,128)(2,1)S(1)}, bf16[2,320,384]{2,1,0:T(8,128)(2,1)S(1)}, u32[]{:S(2)}, u32[]{:S(2)}) collective-permute-start(bf16[2,320,384]{2,1,0:T(8,128)(2,1)S(1)} %get-tuple-element.104), channel_id=1, source_target_pairs={{0,8},{8,0},{16,24},{24,16},{1,9},{9,1},{17,25},{25,17},{2,10},{10... | collective-permute-start | bytes 1474568 | tf_op jit(solution)/shard_map/ppermute | solution.py:487
  32.8 13.4 %collective-permute-start.28 = (bf16[2,320,384]{2,1,0:T(8,128)(2,1)S(1)}, bf16[2,320,384]{2,1,0:T(8,128)(2,1)S(1)}, u32[]{:S(2)}, u32[]{:S(2)}) collective-permute-start(bf16[2,320,384]{2,1,0:T(8,128)(2,1)S(1)} %get-tuple-element.105), channel_id=1, source_target_pairs={{0,16},{8,24},{16,0},{24,8},{1,17},{9,25},{17,1},{25,9},{2,18},{10... | collective-permute-start | bytes 1474568 | tf_op jit(solution)/shard_map/ppermute | solution.py:487
  42.8 14.2 %collective-permute-start.35 = (bf16[2,320,384]{2,1,0:T(8,128)(2,1)S(1)}, bf16[2,320,384]{2,1,0:T(8,128)(2,1)S(1)}, u32[]{:S(2)}, u32[]{:S(2)}) collective-permute-start(bf16[2,320,384]{2,1,0:T(8,128)(2,1)S(1)} %get-tuple-element.124), channel_id=1, source_target_pairs={{0,8},{8,0},{16,24},{24,16},{1,9},{9,1},{17,25},{25,17},{2,10},{10... | collective-permute-start | bytes 1474568 | tf_op jit(solution)/shard_map/ppermute | solution.py:487
  43.4 14.2 %collective-permute-start.37 = (bf16[2,320,384]{2,1,0:T(8,128)(2,1)S(1)}, bf16[2,320,384]{2,1,0:T(8,128)(2,1)S(1)}, u32[]{:S(2)}, u32[]{:S(2)}) collective-permute-start(bf16[2,320,384]{2,1,0:T(8,128)(2,1)S(1)} %get-tuple-element.127), channel_id=1, source_target_pairs={{0,16},{8,24},{16,0},{24,8},{1,17},{9,25},{17,1},{25,9},{2,18},{10... | collective-permute-start | bytes 1474568 | tf_op jit(solution)/shard_map/ppermute | solution.py:487
  46.3 17.0 %collective-permute-start.29 = (bf16[320,384]{1,0:T(8,128)(2,1)S(1)}, bf16[320,384]{1,0:T(8,128)(2,1)S(1)}, u32[]{:S(2)}, u32[]{:S(2)}) collective-permute-start(bf16[320,384]{1,0:T(8,128)(2,1)S(1)} %fusion.25), channel_id=1, source_target_pairs={{0,16},{8,24},{16,0},{24,8},{1,17},{9,25},{17,1},{25,9},{2,18},{10... | collective-permute-start | bytes 737288 | tf_op jit(solution)/shard_map/ppermute | solution.py:487
  48.7 14.7 %collective-permute-start.30 = (bf16[320,384]{1,0:T(8,128)(2,1)S(1)}, bf16[320,384]{1,0:T(8,128)(2,1)S(1)}, u32[]{:S(2)}, u32[]{:S(2)}) collective-permute-start(bf16[320,384]{1,0:T(8,128)(2,1)S(1)} %fusion.21), channel_id=1, source_target_pairs={{0,8},{8,0},{16,24},{24,16},{1,9},{9,1},{17,25},{25,17},{2,10},{10... | collective-permute-start | bytes 737288 | tf_op jit(solution)/shard_map/ppermute | solution.py:487
  57.1 11.0 %collective-permute-start.36 = (bf16[320,384]{1,0:T(8,128)(2,1)S(1)}, bf16[320,384]{1,0:T(8,128)(2,1)S(1)}, u32[]{:S(2)}, u32[]{:S(2)}) collective-permute-start(bf16[320,384]{1,0:T(8,128)(2,1)S(1)} %fusion.19), channel_id=1, source_target_pairs={{0,16},{8,24},{16,0},{24,8},{1,17},{9,25},{17,1},{25,9},{2,18},{10... | collective-permute-start | bytes 737288 | tf_op jit(solution)/shard_map/ppermute | solution.py:487
  57.8 10.4 %collective-permute-start.38 = (bf16[320,384]{1,0:T(8,128)(2,1)S(1)}, bf16[320,384]{1,0:T(8,128)(2,1)S(1)}, u32[]{:S(2)}, u32[]{:S(2)}) collective-permute-start(bf16[320,384]{1,0:T(8,128)(2,1)S(1)} %fusion.15), channel_id=1, source_target_pairs={{0,8},{8,0},{16,24},{24,16},{1,9},{9,1},{17,25},{25,17},{2,10},{10... | collective-permute-start | bytes 737288 | tf_op jit(solution)/shard_map/ppermute | solution.py:487
  63.6 9.8 %collective-permute-start.32 = (bf16[320,384]{1,0:T(8,128)(2,1)S(1)}, bf16[320,384]{1,0:T(8,128)(2,1)S(1)}, u32[]{:S(2)}, u32[]{:S(2)}) collective-permute-start(bf16[320,384]{1,0:T(8,128)(2,1)S(1)} %fusion.24.refs_0_), channel_id=1, source_target_pairs={{0,16},{8,24},{16,0},{24,8},{1,17},{9,25},{17,1},{25,9},{2,18},{10... | collective-permute-start | bytes 737288 | tf_op jit(solution)/shard_map/ppermute | solution.py:487
  64.6 10.4 %collective-permute-start.31 = (bf16[320,384]{1,0:T(8,128)(2,1)S(1)}, bf16[320,384]{1,0:T(8,128)(2,1)S(1)}, u32[]{:S(2)}, u32[]{:S(2)}) collective-permute-start(bf16[320,384]{1,0:T(8,128)(2,1)S(1)} %fusion.24.refs_0_), channel_id=1, source_target_pairs={{0,8},{8,0},{16,24},{24,16},{1,9},{9,1},{17,25},{25,17},{2,10},{10... | collective-permute-start | bytes 737288 | tf_op jit(solution)/shard_map/ppermute | solution.py:487
  68.4 10.3 %collective-permute-start.40 = (bf16[320,384]{1,0:T(8,128)(2,1)S(1)}, bf16[320,384]{1,0:T(8,128)(2,1)S(1)}, u32[]{:S(2)}, u32[]{:S(2)}) collective-permute-start(bf16[320,384]{1,0:T(8,128)(2,1)S(1)} %fusion.18.refs_5_), channel_id=1, source_target_pairs={{0,16},{8,24},{16,0},{24,8},{1,17},{9,25},{17,1},{25,9},{2,18},{10... | collective-permute-start | bytes 737288 | tf_op jit(solution)/shard_map/ppermute | solution.py:487
  69.9 10.0 %collective-permute-start.39 = (bf16[320,384]{1,0:T(8,128)(2,1)S(1)}, bf16[320,384]{1,0:T(8,128)(2,1)S(1)}, u32[]{:S(2)}, u32[]{:S(2)}) collective-permute-start(bf16[320,384]{1,0:T(8,128)(2,1)S(1)} %fusion.18.refs_5_), channel_id=1, source_target_pairs={{0,8},{8,0},{16,24},{24,16},{1,9},{9,1},{17,25},{25,17},{2,10},{10... | collective-permute-start | bytes 737288 | tf_op jit(solution)/shard_map/ppermute | solution.py:487
  73.4 7.4 %collective-permute-start.34 = (bf16[160,384]{1,0:T(8,128)(2,1)S(1)}, bf16[160,384]{1,0:T(8,128)(2,1)S(1)}, u32[]{:S(2)}, u32[]{:S(2)}) collective-permute-start(bf16[160,384]{1,0:T(8,128)(2,1)S(1)} %slice.131), channel_id=1, source_target_pairs={{0,8},{8,0},{16,24},{24,16},{1,9},{9,1},{17,25},{25,17},{2,10},{10... | collective-permute-start | bytes 368648 | tf_op jit(solution)/shard_map/ppermute | solution.py:487
  75.0 5.8 %collective-permute-start.33 = (bf16[160,384]{1,0:T(8,128)(2,1)S(1)}, bf16[160,384]{1,0:T(8,128)(2,1)S(1)}, u32[]{:S(2)}, u32[]{:S(2)}) collective-permute-start(bf16[160,384]{1,0:T(8,128)(2,1)S(1)} %slice.130), channel_id=1, source_target_pairs={{0,16},{8,24},{16,0},{24,8},{1,17},{9,25},{17,1},{25,9},{2,18},{10... | collective-permute-start | bytes 368648 | tf_op jit(solution)/shard_map/ppermute | solution.py:487
  78.7 4.9 %collective-permute-start.42 = (bf16[160,384]{1,0:T(8,128)(2,1)S(1)}, bf16[160,384]{1,0:T(8,128)(2,1)S(1)}, u32[]{:S(2)}, u32[]{:S(2)}) collective-permute-start(bf16[160,384]{1,0:T(8,128)(2,1)S(1)} %slice.137), channel_id=1, source_target_pairs={{0,8},{8,0},{16,24},{24,16},{1,9},{9,1},{17,25},{25,17},{2,10},{10... | collective-permute-start | bytes 368648 | tf_op jit(solution)/shard_map/ppermute | solution.py:487
  79.8 4.9 %collective-permute-start.41 = (bf16[160,384]{1,0:T(8,128)(2,1)S(1)}, bf16[160,384]{1,0:T(8,128)(2,1)S(1)}, u32[]{:S(2)}, u32[]{:S(2)}) collective-permute-start(bf16[160,384]{1,0:T(8,128)(2,1)S(1)} %slice.136), channel_id=1, source_target_pairs={{0,16},{8,24},{16,0},{24,8},{1,17},{9,25},{17,1},{25,9},{2,18},{10... | collective-permute-start | bytes 368648 | tf_op jit(solution)/shard_map/ppermute | solution.py:487
  92.9 2.0 %collective-permute-start.43 = (bf16[4,128,512]{2,1,0:T(8,128)(2,1)S(1)}, bf16[4,128,512]{2,1,0:T(8,128)(2,1)S(1)}, u32[]{:S(2)}, u32[]{:S(2)}) collective-permute-start(bf16[4,128,512]{2,1,0:T(8,128)(2,1)S(1)} %get-tuple-element.130), channel_id=1, source_target_pairs={{0,1},{1,0},{2,3},{3,2},{4,5},{5,4},{6,7},{7,6},{8,9},{9,8},{10,11... | collective-permute-start | bytes 1572872 | tf_op jit(solution)/shard_map/ppermute | solution.py:487
  95.1 8.4 %collective-permute-start.44 = (bf16[128,512]{1,0:T(8,128)(2,1)S(1)}, bf16[128,512]{1,0:T(8,128)(2,1)S(1)}, u32[]{:S(2)}, u32[]{:S(2)}) collective-permute-start(bf16[128,512]{1,0:T(8,128)(2,1)S(1)} %get-tuple-element.139), channel_id=1, source_target_pairs={{0,6},{1,7},{2,4},{3,5},{4,2},{5,3},{6,0},{7,1},{8,14},{9,15},{10,... | collective-permute-start | bytes 393224 | tf_op jit(solution)/shard_map/ppermute | solution.py:487
  99.2 8.0 %collective-permute-start.46 = (bf16[128,512]{1,0:T(8,128)(2,1)S(1)}, bf16[128,512]{1,0:T(8,128)(2,1)S(1)}, u32[]{:S(2)}, u32[]{:S(2)}) collective-permute-start(bf16[128,512]{1,0:T(8,128)(2,1)S(1)} %get-tuple-element.140), channel_id=1, source_target_pairs={{0,2},{1,3},{2,0},{3,1},{4,6},{5,7},{6,4},{7,5},{8,10},{9,11},{10,... | collective-permute-start | bytes 393224 | tf_op jit(solution)/shard_map/ppermute | solution.py:487
  99.2 11.0 %collective-permute-start.45 = (bf16[128,512]{1,0:T(8,128)(2,1)S(1)}, bf16[128,512]{1,0:T(8,128)(2,1)S(1)}, u32[]{:S(2)}, u32[]{:S(2)}) collective-permute-start(bf16[128,512]{1,0:T(8,128)(2,1)S(1)} %get-tuple-element.141), channel_id=1, source_target_pairs={{0,4},{1,5},{2,6},{3,7},{4,0},{5,1},{6,2},{7,3},{8,12},{9,13},{10,... | collective-permute-start | bytes 393224 | tf_op jit(solution)/shard_map/ppermute | solution.py:487
  110.6 0.7 copy-start.4

commit v10 on v9

--- a/solution.py
+++ b/solution.py
@@ -505,13 +505,13 @@
 
 
 def gather_tokens(tokens):
-    held = {0: tokens}
-    bit = lax.axis_size("exp") // 2
-    while bit:
-        for known in list(held):
-            held[known | bit] = swap(held[known], "exp", bit)
-        bit //= 2
-    return [held[j] for j in range(len(held))]
+    count = lax.axis_size("exp")
+    blocks = {0: tokens}
+    for j in range(count - 2, 0, -2):
+        blocks[j] = swap(tokens, "exp", j)
+    for j in range(0, count, 2):
+        blocks[j + 1] = swap(blocks[j], "exp", 1)
+    return [blocks[j] for j in range(count)]
 
 
 def sum_over_exp(stay, away):

time: 111 us -> 111 us (level)
  transfers between devices with their start and end apart: 27 -> 27, of which waited for: 15 -> 16; matrix products, arithmetic and copies ran while one was open for 1% -> 1% of each run, Pallas kernels for 11% -> 11%
where the time goes in v10:
time: 111 us
  waiting for transfers between devices  46 us (41%)
  Pallas kernels  31.9 us (29%)
  starting transfers between devices  27.8 us (25%)
  local copies, waits for them, and re-layouts  3.02 us (3%)
    ppermute x27, waiting for transfers between devices, swap(): return lax.ppermute(value, axis, [(i, i ^ bit) for i in range(count)])  46 us
    ppermute x27, starting transfers between devices, swap(): return lax.ppermute(value, axis, [(i, i ^ bit) for i in range(count)])  27.8 us
    pallas_call x2, Pallas kernels, gate_up(): pl.pallas_call(functools.partial(gate_up_kernel, dims, c, first_part), ou...  19.6 us
    pallas_call x1, Pallas kernels, down(): pl.pallas_call(functools.partial(down_kernel, dims, places), out_shape=ou...  8.13 us
    pallas_call x1, Pallas kernels, weigh(): pl.pallas_call(functools.partial(weigh_small_kernel if small else weigh_l...  4.11 us
    unnamed x14, local copies, waits for them, and re-layouts  2.94 us
  transfers between devices with their start and end apart: 27, of which 16 were waited for; matrix products, arithmetic and copies ran while one was open for 1% of the time, Pallas kernels for 11%

profile of v10, /device:TPU:0, one launch (start us, length us, event | category | flops | bytes accessed | tf_op | source)
XLA Modules:
  0.0 110.9 jit_solution(17562189178328101227)
XLA Ops:
  0.0 0.9 copy-done
  0.9 0.7 copy-done.1
  1.6 0.7 copy-done.2
  2.3 5.1 %collective-permute-start.25 = (bf16[144,512]{1,0:T(8,128)(2,1)S(1)}, bf16[144,512]{1,0:T(8,128)(2,1)S(1)}, u32[]{:S(2)}, u32[]{:S(2)}) collective-permute-start(bf16[144,512]{1,0:T(8,128)(2,1)S(1)} %pack.1.refs_0_), channel_id=1, source_target_pairs={{0,6},{1,7},{2,4},{3,5},{4,2},{5,3},{6,0},{7,1},{8,14},{9,15},{10,... | collective-permute-start | bytes 442376 | tf_op jit(solution)/shard_map/ppermute | solution.py:487
  7.4 0.0 collective-permute-start.23
  7.4 0.6 collective-permute-start.21
  8.1 0.0 collective-permute-start.20
  8.1 4.1 %collective-permute-done.25.refs_6_ = bf16[144,512]{1,0:T(8,128)(2,1)S(1)} collective-permute-done((bf16[144,512]{1,0:T(8,128)(2,1)S(1)}, bf16[144,512]{1,0:T(8,128)(2,1)S(1)}, u32[]{:S(2)}, u32[]{:S(2)}) %collective-permute-start.25) | collective-permute-done | bytes 147488 | tf_op jit(solution)/shard_map/ppermute | solution.py:487
  12.2 0.0 collective-permute-start.26
  12.2 7.7 %collective-permute-done.23.refs_4_ = bf16[144,512]{1,0:T(8,128)(2,1)S(1)} collective-permute-done((bf16[144,512]{1,0:T(8,128)(2,1)S(1)}, bf16[144,512]{1,0:T(8,128)(2,1)S(1)}, u32[]{:S(2)}, u32[]{:S(2)}) %collective-permute-start.23) | collective-permute-done | bytes 147488 | tf_op jit(solution)/shard_map/ppermute | solution.py:487
  19.9 0.0 collective-permute-start.24
  19.9 0.0 collective-permute-done.21.refs_2_
  19.9 0.5 collective-permute-start.22
  20.4 0.1 pad_add_fusion.me_ref
  20.5 0.0 collective-permute-done.20.refs_1_
  20.5 0.0 collective-permute-done.26.refs_7_
  20.5 0.8 collective-permute-done.24.refs_5_
  21.3 0.2 collective-permute-done.22.refs_3_
  21.5 11.2 %gate_up.6 = (s32[8,16,128]{2,1,0:T(8,128)}, f32[8,16,128]{2,1,0:T(8,128)S(1)}, s32[8,8,128]{2,1,0:T(8,128)S(1)}, bf16[1392,512]{1,0:T(8,128)(2,1)S(1)}, bf16[13...) custom-call(s32[2]{0:T(128)S(1)} %pad_add_fusion.me_ref, ...), custom_call_target="tpu_custom_call" | custom-call | flops 1094713344 | bytes 14008320 | tf_op jit(solution)/shard_map/gate_up/pallas_call | solution.py:405
  32.7 1.6 %collective-permute-start.27 = (bf16[2,320,384]{2,1,0:T(8,128)(2,1)S(1)}, bf16[2,320,384]{2,1,0:T(8,128)(2,1)S(1)}, u32[]{:S(2)}, u32[]{:S(2)}) collective-permute-start(bf16[2,320,384]{2,1,0:T(8,128)(2,1)S(1)} %get-tuple-element.104), channel_id=1, source_target_pairs={{0,8},{8,0},{16,24},{24,16},{1,9},{9,1},{17,25},{25,17},{2,10},{10... | collective-permute-start | bytes 1474568 | tf_op jit(solution)/shard_map/ppermute | solution.py:487
  34.2 1.5 %collective-permute-start.28 = (bf16[2,320,384]{2,1,0:T(8,128)(2,1)S(1)}, bf16[2,320,384]{2,1,0:T(8,128)(2,1)S(1)}, u32[]{:S(2)}, u32[]{:S(2)}) collective-permute-start(bf16[2,320,384]{2,1,0:T(8,128)(2,1)S(1)} %get-tuple-element.105), channel_id=1, source_target_pairs={{0,16},{8,24},{16,0},{24,8},{1,17},{9,25},{17,1},{25,9},{2,18},{10... | collective-permute-start | bytes 1474568 | tf_op jit(solution)/shard_map/ppermute | solution.py:487
  35.8 8.5 %gate_up.7 = (bf16[2,320,384]{2,1,0:T(8,128)(2,1)S(1)}, bf16[2,320,384]{2,1,0:T(8,128)(2,1)S(1)}, f32[320,384]{1,0:T(8,128)S(1)}, f32[320,384]{1,0:T(8,128)S(1)}...) custom-call(s32[2]{0:T(128)S(1)} %pad_add_fusion.me_ref, s32[2,16]{1,0:T(2,128)S(1)} %get-tuple-element.102.offs.refs_0_, ...), custom_call_target="tpu_custom_call" | custom-call | flops 1094713344 | bytes 14008320 | tf_op jit(solution)/shard_map/gate_up/pallas_call | solution.py:405
  44.2 0.6 collective-permute-start.35
  44.8 0.5 collective-permute-start.37
  45.3 0.8 collective-permute-done.27
  46.2 1.6 %collective-permute-done.28 = bf16[2,320,384]{2,1,0:T(8,128)(2,1)S(1)} collective-permute-done((bf16[2,320,384]{2,1,0:T(8,128)(2,1)S(1)}, bf16[2,320,384]{2,1,0:T(8,128)(2,1)S(1)}, u32[]{:S(2)}, u32[]{:S(2)}) %collective-permute-start.28) | collective-permute-done | bytes 491552 | tf_op jit(solution)/shard_map/ppermute | solution.py:487
  47.8 0.1 fusion.25
  47.9 2.1 %collective-permute-start.29 = (bf16[320,384]{1,0:T(8,128)(2,1)S(1)}, bf16[320,384]{1,0:T(8,128)(2,1)S(1)}, u32[]{:S(2)}, u32[]{:S(2)}) collective-permute-start(bf16[320,384]{1,0:T(8,128)(2,1)S(1)} %fusion.25), channel_id=1, source_target_pairs={{0,16},{8,24},{16,0},{24,8},{1,17},{9,25},{17,1},{25,9},{2,18},{10... | collective-permute-start | bytes 737288 | tf_op jit(solution)/shard_map/ppermute | solution.py:487
  50.0 0.1 fusion.21
  50.0 0.2 collective-permute-start.30
  50.2 8.2 %collective-permute-done.35 = bf16[2,320,384]{2,1,0:T(8,128)(2,1)S(1)} collective-permute-done((bf16[2,320,384]{2,1,0:T(8,128)(2,1)S(1)}, bf16[2,320,384]{2,1,0:T(8,128)(2,1)S(1)}, u32[]{:S(2)}, u32[]{:S(2)}) %collective-permute-start.35) | collective-permute-done | bytes 491552 | tf_op jit(solution)/shard_map/ppermute | solution.py:487
  58.4 0.1 fusion.19
  58.5 0.6 collective-permute-start.36
  59.1 0.1 fusion.15
  59.1 1.5 %collective-permute-start.38 = (bf16[320,384]{1,0:T(8,128)(2,1)S(1)}, bf16[320,384]{1,0:T(8,128)(2,1)S(1)}, u32[]{:S(2)}, u32[]{:S(2)}) collective-permute-start(bf16[320,384]{1,0:T(8,128)(2,1)S(1)} %fusion.15), channel_id=1, source_target_pairs={{0,8},{8,0},{16,24},{24,16},{1,9},{9,1},{17,25},{25,17},{2,10},{10... | collective-permute-start | bytes 737288 | tf_op jit(solution)/shard_map/ppermute | solution.py:487
  60.6 4.1 %weigh.3 = (f32[1392,128]{1,0:T(8,128)S(1)}, bf16[8,128,1280]{2,1,0:T(8,128)(2,1)S(1)}, s32[1]{0:T(128)}) custom-call(s32[2,16]{1,0:T(2,128)S(1)} %get-tuple-element.102.offs.refs_0_, bf16[1392,1024]{1,0:T(8,128)(2,1)S(1)} %get-tuple-element.106.select, f32[8,16,128]{2,1,0:T(8,128)S(1)} %get-tuple-element.107.probs, ...), custom_call_target="tpu_custom_call" | custom-call | flops 6000000000 | bytes 8000000 | tf_op jit(solution)/shard_map/weigh/pallas_call | solution.py:293
  64.8 0.3 fusion.24.refs_0_
  65.0 0.9 collective-permute-start.32
  66.0 1.2 %collective-permute-start.31 = (bf16[320,384]{1,0:T(8,128)(2,1)S(1)}, bf16[320,384]{1,0:T(8,128)(2,1)S(1)}, u32[]{:S(2)}, u32[]{:S(2)}) collective-permute-start(bf16[320,384]{1,0:T(8,128)(2,1)S(1)} %fusion.24.refs_0_), channel_id=1, source_target_pairs={{0,8},{8,0},{16,24},{24,16},{1,9},{9,1},{17,25},{25,17},{2,10},{10... | collective-permute-start | bytes 737288 | tf_op jit(solution)/shard_map/ppermute | solution.py:487
  67.2 2.3 %collective-permute-done.36 = bf16[320,384]{1,0:T(8,128)(2,1)S(1)} collective-permute-done((bf16[320,384]{1,0:T(8,128)(2,1)S(1)}, bf16[320,384]{1,0:T(8,128)(2,1)S(1)}, u32[]{:S(2)}, u32[]{:S(2)}) %collective-permute-start.36) | collective-permute-done | bytes 245792 | tf_op jit(solution)/shard_map/ppermute | solution.py:487
  69.5 0.3 fusion.18.refs_5_
  69.8 1.4 %collective-permute-start.40 = (bf16[320,384]{1,0:T(8,128)(2,1)S(1)}, bf16[320,384]{1,0:T(8,128)(2,1)S(1)}, u32[]{:S(2)}, u32[]{:S(2)}) collective-permute-start(bf16[320,384]{1,0:T(8,128)(2,1)S(1)} %fusion.18.refs_5_), channel_id=1, source_target_pairs={{0,16},{8,24},{16,0},{24,8},{1,17},{9,25},{17,1},{25,9},{2,18},{10... | collective-permute-start | bytes 737288 | tf_op jit(solution)/shard_map/ppermute | solution.py:487
  71.2 0.6 collective-permute-start.39
  71.9 2.9 %collective-permute-done.32.refs_2_ = bf16[320,384]{1,0:T(8,128)(2,1)S(1)} collective-permute-done((bf16[320,384]{1,0:T(8,128)(2,1)S(1)}, bf16[320,384]{1,0:T(8,128)(2,1)S(1)}, u32[]{:S(2)}, u32[]{:S(2)}) %collective-permute-start.32) | collective-permute-done | bytes 245792 | tf_op jit(solution)/shard_map/ppermute | solution.py:487
  74.8 1.5 %collective-permute-start.34 = (bf16[160,384]{1,0:T(8,128)(2,1)S(1)}, bf16[160,384]{1,0:T(8,128)(2,1)S(1)}, u32[]{:S(2)}, u32[]{:S(2)}) collective-permute-start(bf16[160,384]{1,0:T(8,128)(2,1)S(1)} %slice.131), channel_id=1, source_target_pairs={{0,8},{8,0},{16,24},{24,16},{1,9},{9,1},{17,25},{25,17},{2,10},{10... | collective-permute-start | bytes 368648 | tf_op jit(solution)/shard_map/ppermute | solution.py:487
  76.4 0.6 collective-permute-start.33
  77.0 3.1 %collective-permute-done.40.refs_7_ = bf16[320,384]{1,0:T(8,128)(2,1)S(1)} collective-permute-done((bf16[320,384]{1,0:T(8,128)(2,1)S(1)}, bf16[320,384]{1,0:T(8,128)(2,1)S(1)}, u32[]{:S(2)}, u32[]{:S(2)}) %collective-permute-start.40) | collective-permute-done | bytes 245792 | tf_op jit(solution)/shard_map/ppermute | solution.py:487
  80.1 1.3 %collective-permute-start.42 = (bf16[160,384]{1,0:T(8,128)(2,1)S(1)}, bf16[160,384]{1,0:T(8,128)(2,1)S(1)}, u32[]{:S(2)}, u32[]{:S(2)}) collective-permute-start(bf16[160,384]{1,0:T(8,128)(2,1)S(1)} %slice.137), channel_id=1, source_target_pairs={{0,8},{8,0},{16,24},{24,16},{1,9},{9,1},{17,25},{25,17},{2,10},{10... | collective-permute-start | bytes 368648 | tf_op jit(solution)/shard_map/ppermute | solution.py:487
  81.4 0.8 collective-permute-start.41
  82.2 2.8 %collective-permute-done.42.refs_9_ = bf16[160,384]{1,0:T(8,128)(2,1)S(1)} collective-permute-done((bf16[160,384]{1,0:T(8,128)(2,1)S(1)}, bf16[160,384]{1,0:T(8,128)(2,1)S(1)}, u32[]{:S(2)}, u32[]{:S(2)}) %collective-permute-start.42) | collective-permute-done | bytes 122912 | tf_op jit(solution)/shard_map/ppermute | solution.py:487
  85.0 1.3 %collective-permute-done.41.refs_8_ = bf16[160,384]{1,0:T(8,128)(2,1)S(1)} collective-permute-done((bf16[160,384]{1,0:T(8,128)(2,1)S(1)}, bf16[160,384]{1,0:T(8,128)(2,1)S(1)}, u32[]{:S(2)}, u32[]{:S(2)}) %collective-permute-start.41) | collective-permute-done | bytes 122912 | tf_op jit(solution)/shard_map/ppermute | solution.py:487
  86.3 8.1 %down.3 = (bf16[4,128,512]{2,1,0:T(8,128)(2,1)S(1)}, bf16[4,128,512]{2,1,0:T(8,128)(2,1)S(1)}) custom-call(s32[2]{0:T(128)S(1)} %pad_add_fusion.me_ref, s32[2,16]{1,0:T(2,128)S(1)} %get-tuple-element.102.offs.refs_0_, bf16[16,768,512]{2,1,0:T(8,128)(2,1)} %w_down.1, f32[1392,128]{1,0:T(8,128)S(1)} %get-tuple-element.118.scale, ...), custom_call_target="tpu_custom_call" | custom-call | flops 2554331136 | bytes 12582912 | tf_op jit(solution)/shard_map/down/pallas_call | solution.py:473
  94.5 0.1 collective-permute-start.43
  94.6 1.9 %collective-permute-done.43 = bf16[4,128,512]{2,1,0:T(8,128)(2,1)S(1)} collective-permute-done((bf16[4,128,512]{2,1,0:T(8,128)(2,1)S(1)}, bf16[4,128,512]{2,1,0:T(8,128)(2,1)S(1)}, u32[]{:S(2)}, u32[]{:S(2)}) %collective-permute-start.43) | collective-permute-done | bytes 524320 | tf_op jit(solution)/shard_map/ppermute | solution.py:487
  96.5 0.2 fusion.29
  96.7 2.6 %collective-permute-start.44 = (bf16[128,512]{1,0:T(8,128)(2,1)S(1)}, bf16[128,512]{1,0:T(8,128)(2,1)S(1)}, u32[]{:S(2)}, u32[]{:S(2)}) collective-permute-start(bf16[128,512]{1,0:T(8,128)(2,1)S(1)} %get-tuple-element.139), channel_id=1, source_target_pairs={{0,6},{1,7},{2,4},{3,5},{4,2},{5,3},{6,0},{7,1},{8,14},{9,15},{10,... | collective-permute-start | bytes 393224 | tf_op jit(solution)/shard_map/ppermute | solution.py:487
  99.3 1.9 %collective-permute-start.45 = (bf16[128,512]{1,0:T(8,128)(2,1)S(1)}, bf16[128,512]{1,0:T(8,128)(2,1)S(1)}, u32[]{:S(2)}, u32[]{:S(2)}) collective-permute-start(bf16[128,512]{1,0:T(8,128)(2,1)S(1)} %get-tuple-element.141), channel_id=1, source_target_pairs={{0,4},{1,5},{2,6},{3,7},{4,0},{5,1},{6,2},{7,3},{8,12},{9,13},{10,... | collective-permute-start | bytes 393224 | tf_op jit(solution)/shard_map/ppermute | solution.py:487
  101.8 3.2 %collective-permute-done.44 = bf16[128,512]{1,0:T(8,128)(2,1)S(1)} collective-permute-done((bf16[128,512]{1,0:T(8,128)(2,1)S(1)}, bf16[128,512]{1,0:T(8,128)(2,1)S(1)}, u32[]{:S(2)}, u32[]{:S(2)}) %collective-permute-start.44) | collective-permute-done | bytes 131104 | tf_op jit(solution)/shard_map/ppermute | solution.py:487
  105.0 4.8 %collective-permute-done.46 = bf16[128,512]{1,0:T(8,128)(2,1)S(1)} collective-permute-done((bf16[128,512]{1,0:T(8,128)(2,1)S(1)}, bf16[128,512]{1,0:T(8,128)(2,1)S(1)}, u32[]{:S(2)}, u32[]{:S(2)}) %collective-permute-start.46) | collective-permute-done | bytes 131104 | tf_op jit(solution)/shard_map/ppermute | solution.py:487
  109.8 0.1 collective-permute-done.45
  109.9 0.1 fusion.28
  109.9 0.3 conditional.1
  110.2 0.0 copy-start.4
  110.2 0.6 copy-done.4
  (25 shorter events, 0.1 us)
Async XLA Ops:
  0.0 0.9 copy-start
  0.9 0.7 copy-start.1
  1.6 0.7 copy-start.2
  2.3 9.9 %collective-permute-start.25 = (bf16[144,512]{1,0:T(8,128)(2,1)S(1)}, bf16[144,512]{1,0:T(8,128)(2,1)S(1)}, u32[]{:S(2)}, u32[]{:S(2)}) collective-permute-start(bf16[144,512]{1,0:T(8,128)(2,1)S(1)} %pack.1.refs_0_), channel_id=1, source_target_pairs={{0,6},{1,7},{2,4},{3,5},{4,2},{5,3},{6,0},{7,1},{8,14},{9,15},{10,... | collective-permute-start | bytes 442376 | tf_op jit(solution)/shard_map/ppermute | solution.py:487
  7.4 12.5 %collective-permute-start.23 = (bf16[144,512]{1,0:T(8,128)(2,1)S(1)}, bf16[144,512]{1,0:T(8,128)(2,1)S(1)}, u32[]{:S(2)}, u32[]{:S(2)}) collective-permute-start(bf16[144,512]{1,0:T(8,128)(2,1)S(1)} %pack.1.refs_0_), channel_id=1, source_target_pairs={{0,4},{1,5},{2,6},{3,7},{4,0},{5,1},{6,2},{7,3},{8,12},{9,13},{10,... | collective-permute-start | bytes 442376 | tf_op jit(solution)/shard_map/ppermute | solution.py:487
  7.4 12.5 %collective-permute-start.21 = (bf16[144,512]{1,0:T(8,128)(2,1)S(1)}, bf16[144,512]{1,0:T(8,128)(2,1)S(1)}, u32[]{:S(2)}, u32[]{:S(2)}) collective-permute-start(bf16[144,512]{1,0:T(8,128)(2,1)S(1)} %pack.1.refs_0_), channel_id=1, source_target_pairs={{0,2},{1,3},{2,0},{3,1},{4,6},{5,7},{6,4},{7,5},{8,10},{9,11},{10,... | collective-permute-start | bytes 442376 | tf_op jit(solution)/shard_map/ppermute | solution.py:487
  8.1 12.4 %collective-permute-start.20 = (bf16[144,512]{1,0:T(8,128)(2,1)S(1)}, bf16[144,512]{1,0:T(8,128)(2,1)S(1)}, u32[]{:S(2)}, u32[]{:S(2)}) collective-permute-start(bf16[144,512]{1,0:T(8,128)(2,1)S(1)} %pack.1.refs_0_), channel_id=1, source_target_pairs={{0,1},{1,0},{2,3},{3,2},{4,5},{5,4},{6,7},{7,6},{8,9},{9,8},{10,11... | collective-permute-start | bytes 442376 | tf_op jit(solution)/shard_map/ppermute | solution.py:487
  12.2 8.3 %collective-permute-start.26 = (bf16[144,512]{1,0:T(8,128)(2,1)S(1)}, bf16[144,512]{1,0:T(8,128)(2,1)S(1)}, u32[]{:S(2)}, u32[]{:S(2)}) collective-permute-start(bf16[144,512]{1,0:T(8,128)(2,1)S(1)} %collective-permute-done.25.refs_6_), channel_id=1, source_target_pairs={{0,1},{1,0},{2,3},{3,2},{4,5},{5,4},{6,7},{7,6},{8,9},{9,8},{10,11... | collective-permute-start | bytes 442376 | tf_op jit(solution)/shard_map/ppermute | solution.py:487
  19.9 1.4 %collective-permute-start.24 = (bf16[144,512]{1,0:T(8,128)(2,1)S(1)}, bf16[144,512]{1,0:T(8,128)(2,1)S(1)}, u32[]{:S(2)}, u32[]{:S(2)}) collective-permute-start(bf16[144,512]{1,0:T(8,128)(2,1)S(1)} %collective-permute-done.23.refs_4_), channel_id=1, source_target_pairs={{0,1},{1,0},{2,3},{3,2},{4,5},{5,4},{6,7},{7,6},{8,9},{9,8},{10,11... | collective-permute-start | bytes 442376 | tf_op jit(solution)/shard_map/ppermute | solution.py:487
  19.9 1.6 %collective-permute-start.22 = (bf16[144,512]{1,0:T(8,128)(2,1)S(1)}, bf16[144,512]{1,0:T(8,128)(2,1)S(1)}, u32[]{:S(2)}, u32[]{:S(2)}) collective-permute-start(bf16[144,512]{1,0:T(8,128)(2,1)S(1)} %collective-permute-done.21.refs_2_), channel_id=1, source_target_pairs={{0,1},{1,0},{2,3},{3,2},{4,5},{5,4},{6,7},{7,6},{8,9},{9,8},{10,11... | collective-permute-start | bytes 442376 | tf_op jit(solution)/shard_map/ppermute | solution.py:487
  20.4 15.4 %slice-start = ((s8[12582912]{0:T(1024)(128)(4,1)}), s8[4194304]{0:T(1024)(128)(4,1)S(1)}, s32[]{:S(2)}) async-start(s8[12582912]{0:T(1024)(128)(4,1)} %bitcast.95), calls=%async_computation | async-start | bytes 8388608
  20.5 15.3 %slice-start.1 = ((s8[12582912]{0:T(1024)(128)(4,1)}), s8[4194304]{0:T(1024)(128)(4,1)S(1)}, s32[]{:S(2)}) async-start(s8[12582912]{0:T(1024)(128)(4,1)} %bitcast.95), calls=%async_computation.1 | async-start | bytes 8388608
  20.5 15.3 %slice-start.2 = ((s8[12582912]{0:T(1024)(128)(4,1)}), s8[4194304]{0:T(1024)(128)(4,1)S(1)}, s32[]{:S(2)}) async-start(s8[12582912]{0:T(1024)(128)(4,1)} %bitcast.95), calls=%async_computation.2 | async-start | bytes 8388608
  32.7 13.5 %collective-permute-start.27 = (bf16[2,320,384]{2,1,0:T(8,128)(2,1)S(1)}, bf16[2,320,384]{2,1,0:T(8,128)(2,1)S(1)}, u32[]{:S(2)}, u32[]{:S(2)}) collective-permute-start(bf16[2,320,384]{2,1,0:T(8,128)(2,1)S(1)} %get-tuple-element.104), channel_id=1, source_target_pairs={{0,8},{8,0},{16,24},{24,16},{1,9},{9,1},{17,25},{25,17},{2,10},{10... | collective-permute-start | bytes 1474568 | tf_op jit(solution)/shard_map/ppermute | solution.py:487
  34.2 13.6 %collective-permute-start.28 = (bf16[2,320,384]{2,1,0:T(8,128)(2,1)S(1)}, bf16[2,320,384]{2,1,0:T(8,128)(2,1)S(1)}, u32[]{:S(2)}, u32[]{:S(2)}) collective-permute-start(bf16[2,320,384]{2,1,0:T(8,128)(2,1)S(1)} %get-tuple-element.105), channel_id=1, source_target_pairs={{0,16},{8,24},{16,0},{24,8},{1,17},{9,25},{17,1},{25,9},{2,18},{10... | collective-permute-start | bytes 1474568 | tf_op jit(solution)/shard_map/ppermute | solution.py:487
  44.2 14.2 %collective-permute-start.35 = (bf16[2,320,384]{2,1,0:T(8,128)(2,1)S(1)}, bf16[2,320,384]{2,1,0:T(8,128)(2,1)S(1)}, u32[]{:S(2)}, u32[]{:S(2)}) collective-permute-start(bf16[2,320,384]{2,1,0:T(8,128)(2,1)S(1)} %get-tuple-element.124), channel_id=1, source_target_pairs={{0,8},{8,0},{16,24},{24,16},{1,9},{9,1},{17,25},{25,17},{2,10},{10... | collective-permute-start | bytes 1474568 | tf_op jit(solution)/shard_map/ppermute | solution.py:487
  44.8 14.2 %collective-permute-start.37 = (bf16[2,320,384]{2,1,0:T(8,128)(2,1)S(1)}, bf16[2,320,384]{2,1,0:T(8,128)(2,1)S(1)}, u32[]{:S(2)}, u32[]{:S(2)}) collective-permute-start(bf16[2,320,384]{2,1,0:T(8,128)(2,1)S(1)} %get-tuple-element.127), channel_id=1, source_target_pairs={{0,16},{8,24},{16,0},{24,8},{1,17},{9,25},{17,1},{25,9},{2,18},{10... | collective-permute-start | bytes 1474568 | tf_op jit(solution)/shard_map/ppermute | solution.py:487
  47.9 16.9 %collective-permute-start.29 = (bf16[320,384]{1,0:T(8,128)(2,1)S(1)}, bf16[320,384]{1,0:T(8,128)(2,1)S(1)}, u32[]{:S(2)}, u32[]{:S(2)}) collective-permute-start(bf16[320,384]{1,0:T(8,128)(2,1)S(1)} %fusion.25), channel_id=1, source_target_pairs={{0,16},{8,24},{16,0},{24,8},{1,17},{9,25},{17,1},{25,9},{2,18},{10... | collective-permute-start | bytes 737288 | tf_op jit(solution)/shard_map/ppermute | solution.py:487
  50.0 14.7 %collective-permute-start.30 = (bf16[320,384]{1,0:T(8,128)(2,1)S(1)}, bf16[320,384]{1,0:T(8,128)(2,1)S(1)}, u32[]{:S(2)}, u32[]{:S(2)}) collective-permute-start(bf16[320,384]{1,0:T(8,128)(2,1)S(1)} %fusion.21), channel_id=1, source_target_pairs={{0,8},{8,0},{16,24},{24,16},{1,9},{9,1},{17,25},{25,17},{2,10},{10... | collective-permute-start | bytes 737288 | tf_op jit(solution)/shard_map/ppermute | solution.py:487
  58.5 11.1 %collective-permute-start.36 = (bf16[320,384]{1,0:T(8,128)(2,1)S(1)}, bf16[320,384]{1,0:T(8,128)(2,1)S(1)}, u32[]{:S(2)}, u32[]{:S(2)}) collective-permute-start(bf16[320,384]{1,0:T(8,128)(2,1)S(1)} %fusion.19), channel_id=1, source_target_pairs={{0,16},{8,24},{16,0},{24,8},{1,17},{9,25},{17,1},{25,9},{2,18},{10... | collective-permute-start | bytes 737288 | tf_op jit(solution)/shard_map/ppermute | solution.py:487
  59.1 10.4 %collective-permute-start.38 = (bf16[320,384]{1,0:T(8,128)(2,1)S(1)}, bf16[320,384]{1,0:T(8,128)(2,1)S(1)}, u32[]{:S(2)}, u32[]{:S(2)}) collective-permute-start(bf16[320,384]{1,0:T(8,128)(2,1)S(1)} %fusion.15), channel_id=1, source_target_pairs={{0,8},{8,0},{16,24},{24,16},{1,9},{9,1},{17,25},{25,17},{2,10},{10... | collective-permute-start | bytes 737288 | tf_op jit(solution)/shard_map/ppermute | solution.py:487
  65.0 9.8 %collective-permute-start.32 = (bf16[320,384]{1,0:T(8,128)(2,1)S(1)}, bf16[320,384]{1,0:T(8,128)(2,1)S(1)}, u32[]{:S(2)}, u32[]{:S(2)}) collective-permute-start(bf16[320,384]{1,0:T(8,128)(2,1)S(1)} %fusion.24.refs_0_), channel_id=1, source_target_pairs={{0,16},{8,24},{16,0},{24,8},{1,17},{9,25},{17,1},{25,9},{2,18},{10... | collective-permute-start | bytes 737288 | tf_op jit(solution)/shard_map/ppermute | solution.py:487
  66.0 10.4 %collective-permute-start.31 = (bf16[320,384]{1,0:T(8,128)(2,1)S(1)}, bf16[320,384]{1,0:T(8,128)(2,1)S(1)}, u32[]{:S(2)}, u32[]{:S(2)}) collective-permute-start(bf16[320,384]{1,0:T(8,128)(2,1)S(1)} %fusion.24.refs_0_), channel_id=1, source_target_pairs={{0,8},{8,0},{16,24},{24,16},{1,9},{9,1},{17,25},{25,17},{2,10},{10... | collective-permute-start | bytes 737288 | tf_op jit(solution)/shard_map/ppermute | solution.py:487
  69.8 10.3 %collective-permute-start.40 = (bf16[320,384]{1,0:T(8,128)(2,1)S(1)}, bf16[320,384]{1,0:T(8,128)(2,1)S(1)}, u32[]{:S(2)}, u32[]{:S(2)}) collective-permute-start(bf16[320,384]{1,0:T(8,128)(2,1)S(1)} %fusion.18.refs_5_), channel_id=1, source_target_pairs={{0,16},{8,24},{16,0},{24,8},{1,17},{9,25},{17,1},{25,9},{2,18},{10... | collective-permute-start | bytes 737288 | tf_op jit(solution)/shard_map/ppermute | solution.py:487
  71.2 10.1 %collective-permute-start.39 = (bf16[320,384]{1,0:T(8,128)(2,1)S(1)}, bf16[320,384]{1,0:T(8,128)(2,1)S(1)}, u32[]{:S(2)}, u32[]{:S(2)}) collective-permute-start(bf16[320,384]{1,0:T(8,128)(2,1)S(1)} %fusion.18.refs_5_), channel_id=1, source_target_pairs={{0,8},{8,0},{16,24},{24,16},{1,9},{9,1},{17,25},{25,17},{2,10},{10... | collective-permute-start | bytes 737288 | tf_op jit(solution)/shard_map/ppermute | solution.py:487
  74.8 7.4 %collective-permute-start.34 = (bf16[160,384]{1,0:T(8,128)(2,1)S(1)}, bf16[160,384]{1,0:T(8,128)(2,1)S(1)}, u32[]{:S(2)}, u32[]{:S(2)}) collective-permute-start(bf16[160,384]{1,0:T(8,128)(2,1)S(1)} %slice.131), channel_id=1, source_target_pairs={{0,8},{8,0},{16,24},{24,16},{1,9},{9,1},{17,25},{25,17},{2,10},{10... | collective-permute-start | bytes 368648 | tf_op jit(solution)/shard_map/ppermute | solution.py:487
  76.4 5.8 %collective-permute-start.33 = (bf16[160,384]{1,0:T(8,128)(2,1)S(1)}, bf16[160,384]{1,0:T(8,128)(2,1)S(1)}, u32[]{:S(2)}, u32[]{:S(2)}) collective-permute-start(bf16[160,384]{1,0:T(8,128)(2,1)S(1)} %slice.130), channel_id=1, source_target_pairs={{0,16},{8,24},{16,0},{24,8},{1,17},{9,25},{17,1},{25,9},{2,18},{10... | collective-permute-start | bytes 368648 | tf_op jit(solution)/shard_map/ppermute | solution.py:487
  80.1 4.9 %collective-permute-start.42 = (bf16[160,384]{1,0:T(8,128)(2,1)S(1)}, bf16[160,384]{1,0:T(8,128)(2,1)S(1)}, u32[]{:S(2)}, u32[]{:S(2)}) collective-permute-start(bf16[160,384]{1,0:T(8,128)(2,1)S(1)} %slice.137), channel_id=1, source_target_pairs={{0,8},{8,0},{16,24},{24,16},{1,9},{9,1},{17,25},{25,17},{2,10},{10... | collective-permute-start | bytes 368648 | tf_op jit(solution)/shard_map/ppermute | solution.py:487
  81.4 4.9 %collective-permute-start.41 = (bf16[160,384]{1,0:T(8,128)(2,1)S(1)}, bf16[160,384]{1,0:T(8,128)(2,1)S(1)}, u32[]{:S(2)}, u32[]{:S(2)}) collective-permute-start(bf16[160,384]{1,0:T(8,128)(2,1)S(1)} %slice.136), channel_id=1, source_target_pairs={{0,16},{8,24},{16,0},{24,8},{1,17},{9,25},{17,1},{25,9},{2,18},{10... | collective-permute-start | bytes 368648 | tf_op jit(solution)/shard_map/ppermute | solution.py:487
  94.5 2.0 %collective-permute-start.43 = (bf16[4,128,512]{2,1,0:T(8,128)(2,1)S(1)}, bf16[4,128,512]{2,1,0:T(8,128)(2,1)S(1)}, u32[]{:S(2)}, u32[]{:S(2)}) collective-permute-start(bf16[4,128,512]{2,1,0:T(8,128)(2,1)S(1)} %get-tuple-element.130), channel_id=1, source_target_pairs={{0,1},{1,0},{2,3},{3,2},{4,5},{5,4},{6,7},{7,6},{8,9},{9,8},{10,11... | collective-permute-start | bytes 1572872 | tf_op jit(solution)/shard_map/ppermute | solution.py:487
  96.7 8.3 %collective-permute-start.44 = (bf16[128,512]{1,0:T(8,128)(2,1)S(1)}, bf16[128,512]{1,0:T(8,128)(2,1)S(1)}, u32[]{:S(2)}, u32[]{:S(2)}) collective-permute-start(bf16[128,512]{1,0:T(8,128)(2,1)S(1)} %get-tuple-element.139), channel_id=1, source_target_pairs={{0,6},{1,7},{2,4},{3,5},{4,2},{5,3},{6,0},{7,1},{8,14},{9,15},{10,... | collective-permute-start | bytes 393224 | tf_op jit(solution)/shard_map/ppermute | solution.py:487
  99.3 10.5 %collective-permute-start.46 = (bf16[128,512]{1,0:T(8,128)(2,1)S(1)}, bf16[128,512]{1,0:T(8,128)(2,1)S(1)}, u32[]{:S(2)}, u32[]{:S(2)}) collective-permute-start(bf16[128,512]{1,0:T(8,128)(2,1)S(1)} %get-tuple-element.140), channel_id=1, source_target_pairs={{0,2},{1,3},{2,0},{3,1},{4,6},{5,7},{6,4},{7,5},{8,10},{9,11},{10,... | collective-permute-start | bytes 393224 | tf_op jit(solution)/shard_map/ppermute | solution.py:487
  99.3 10.6 %collective-permute-start.45 = (bf16[128,512]{1,0:T(8,128)(2,1)S(1)}, bf16[128,512]{1,0:T(8,128)(2,1)S(1)}, u32[]{:S(2)}, u32[]{:S(2)}) collective-permute-start(bf16[128,512]{1,0:T(8,128)(2,1)S(1)} %get-tuple-element.141), channel_id=1, source_target_pairs={{0,4},{1,5},{2,6},{3,7},{4,0},{5,1},{6,2},{7,3},{8,12},{9,13},{10,... | collective-permute-start | bytes 393224 | tf_op jit(solution)/shard_map/ppermute | solution.py:487
  110.2 0.7 copy-start.4
